TPU v7x, 32 devices: a whole 2x2x4 slice. The times are simulated.
32 devices in a mesh: dom: 2 (over y), expert: 4 (over z), dp: 2 (over x), sub: 2 (over core).
Axes of the slice: x: 2, y: 2, z: 4, core: 2. Of those that a mesh axis runs over, the one named last changes fastest.
Arguments:
- tokens: bfloat16 [1024, 2048], P(('dom', 'expert', 'dp'), 'sub'), parts along dimension 0, may hold values from -6 to 6
- out_grad: bfloat16 [1024, 2048], P(('dom', 'expert', 'dp'), 'sub'), parts along dimension 0, may hold values from -6 to 6
- gates: float32 [1024, 8], P(('dom', 'expert', 'dp')), parts along dimension 0, may hold values from 0.1 to 1
- expert_ids: int32 [1024, 8], P(('dom', 'expert', 'dp')), parts along dimension 0, may hold values from 0 to 63, as said below
- slots: int32 [1024, 8], P(('dom', 'expert', 'dp')), parts along dimension 0, may hold values from 0 to 9, as said below
- gate_weight: bfloat16 [64, 2048, 768], P('expert', 'dp', 'sub'), may hold values from -0.125 to 0.125
- up_weight: bfloat16 [64, 2048, 768], P('expert', 'dp', 'sub'), may hold values from -0.125 to 0.125
- down_weight: bfloat16 [64, 768, 2048], P('expert', 'sub', 'dp'), may hold values from -0.21875 to 0.21875
Outputs:
- scores: float32 [128, 768], P(('dom', 'expert'), 'sub'), parts along dimension 0
- input_grad: bfloat16 [1024, 2048], P(('dom', 'expert', 'dp'), 'sub'), parts along dimension 0
There are 2 independent parts, one for each index of `dom`. A program takes and returns all parts, laid end to end along the dimension named above; an argument that names none is the same for every part. Nothing has to cross between parts.
Inputs may be any that keep to these rules, and one draw needn't show every extreme that they name: `expert_ids`: A row names 8 different experts; in each aligned block of 64 rows (the rows of one index pair of expert and dp) no expert is named by more than 10 rows, every expert is named, and some expert is named by exactly 10 rows in every block. Within one aligned block of 64 rows, the routes to one expert have different slots.
All inputs are finite; a program needn't handle non-finite values.
Results may differ from a plain program's by a relative error of at most 0.0085.
Values may be sent and summed in bfloat16 or wider, within the bound.
No kernel may reach another device: no remote copies, remote signals or barrier semaphores. Data moves between devices by JAX's collectives and lax.ppermute only.
A program may use at most 256 MiB of HBM per device.

v0:
```python
import jax
import jax.numpy as jnp
from jax import lax
from jax.sharding import PartitionSpec as P

LOCAL_EXPERTS = 64
TOPK = 8
CAP = 10


def local(tokens, out_grad, gates, expert_ids, slots, gate_weight, up_weight, down_weight):
    expert_count = lax.axis_size("expert")
    group_count = lax.axis_size("dp")
    local_count = gate_weight.shape[0]
    tok_rows = tokens.shape[0]
    half_width = tokens.shape[1]
    slot_count = local_count * expert_count * CAP
    target_dev = expert_ids // local_count
    local_expert = expert_ids % local_count
    slot_rows = ((local_expert * expert_count + target_dev) * CAP + slots).reshape(-1)
    scaled = (gates[:, :, None] * out_grad[:, None, :].astype(jnp.float32)).astype(jnp.bfloat16)
    scaled = scaled.reshape(tok_rows * TOPK, half_width)
    repeated = jnp.repeat(tokens, TOPK, axis=0)
    x_send = jnp.zeros((slot_count, half_width), jnp.bfloat16).at[slot_rows].add(repeated)
    x_send = x_send.reshape(local_count, expert_count, CAP, half_width)
    grad_send = jnp.zeros((slot_count, half_width), jnp.bfloat16).at[slot_rows].add(scaled)
    grad_send = grad_send.reshape(local_count, expert_count, CAP, half_width)
    x_recv, grad_recv = (
        lax.all_to_all(x_send, "expert", split_axis=1, concat_axis=1, tiled=True),
        lax.all_to_all(grad_send, "expert", split_axis=1, concat_axis=1, tiled=True),
    )
    x_full, grad_full = (
        lax.all_gather(x_recv, "sub", axis=3, tiled=True),
        lax.all_gather(grad_recv, "sub", axis=3, tiled=True),
    )
    width = x_full.shape[3]
    expert_rows = expert_count * CAP
    x_full = x_full.reshape(local_count, expert_rows, width)
    grad_full = grad_full.reshape(local_count, expert_rows, width)
    gate_full, up_full = (
        lax.all_gather(gate_weight, "dp", axis=1, tiled=True),
        lax.all_gather(up_weight, "dp", axis=1, tiled=True),
    )
    gate_pre = jnp.einsum("erd,edf->erf", x_full, gate_full, preferred_element_type=jnp.float32)
    up_pre = jnp.einsum("erd,edf->erf", x_full, up_full, preferred_element_type=jnp.float32)
    hidden_grad = jnp.einsum(
        "erd,efd->erf",
        grad_full,
        lax.all_gather(down_weight, "dp", axis=2, tiled=True),
        preferred_element_type=jnp.float32,
    )
    gating = jax.nn.sigmoid(gate_pre)
    activated = gate_pre * gating
    hidden = activated * up_pre
    channel = lax.psum(jnp.sum(hidden * hidden_grad, axis=1), "dp")
    scale = LOCAL_EXPERTS / (tok_rows * expert_count * group_count * TOPK)
    scores = channel * channel * scale
    gate_grad = (hidden_grad * up_pre * gating * (1.0 + gate_pre * (1.0 - gating))).astype(
        jnp.bfloat16
    )
    up_grad = (hidden_grad * activated).astype(jnp.bfloat16)
    parts_out = jnp.einsum("erf,edf->erd", gate_grad, gate_full, preferred_element_type=jnp.float32)
    parts_out = parts_out + jnp.einsum(
        "erf,edf->erd", up_grad, up_full, preferred_element_type=jnp.float32
    )
    parts_out = parts_out.astype(jnp.bfloat16)
    widened = lax.optimization_barrier(parts_out).astype(jnp.float32)
    summed = lax.psum_scatter(
        widened.astype(jnp.bfloat16), "sub", scatter_dimension=2, tiled=True
    ).astype(jnp.float32)
    summed = summed.reshape(local_count, expert_count, CAP, half_width)
    returned = lax.all_to_all(
        summed.astype(jnp.bfloat16), "expert", split_axis=1, concat_axis=1, tiled=True
    ).astype(summed.dtype)
    picked = returned.reshape(slot_count, half_width)[slot_rows].reshape(tok_rows, TOPK, half_width)
    token_grad = jnp.sum(picked, axis=1)
    return (scores, token_grad.astype(jnp.bfloat16))


def solution(mesh):
    in_specs = (
        P(("dom", "expert", "dp"), "sub"),
        P(("dom", "expert", "dp"), "sub"),
        P(("dom", "expert", "dp"), None),
        P(("dom", "expert", "dp"), None),
        P(("dom", "expert", "dp"), None),
        P("expert", "dp", "sub"),
        P("expert", "dp", "sub"),
        P("expert", "sub", "dp"),
    )
    out_specs = (P(("dom", "expert"), "sub"), P(("dom", "expert", "dp"), "sub"))
    return jax.shard_map(local, mesh=mesh, in_specs=in_specs, out_specs=out_specs, check_vma=False)
```

profile of v0, /device:TPU:1, one launch (start us, length us, event | category | flops | bytes accessed | tf_op | source)
XLA Modules:
  0.0 1084.9 jit_solution(605266737010587557)
XLA Ops:
  7.2 0.7 fusion.23
  8.2 5.3 scatter_custom_fusion
  14.0 0.7 copy.20
  14.7 35.8 %all_to_all.15 = bf16[16,4,10,1024]{3,0,2,1:T(8,128)(2,1)} all-to-all(bf16[16,4,10,1024]{3,0,2,1:T(8,128)(2,1)S(1)} %copy.20), channel_id=1, replica_groups=mesh['dom'=2,'expert'=4,'dp'=2,'sub'=2] {'expert'}, dimensions={1} | all-to-all | bytes 2621440 | tf_op jit(solution)/shard_map/all_to_all | solution.py:29
  52.4 5.6 scatter_custom_fusion.1
  58.5 0.7 copy.24
  59.2 33.6 %all_to_all.16 = bf16[16,4,10,1024]{3,0,2,1:T(8,128)(2,1)} all-to-all(bf16[16,4,10,1024]{3,0,2,1:T(8,128)(2,1)S(1)} %copy.24), channel_id=1, replica_groups=mesh['dom'=2,'expert'=4,'dp'=2,'sub'=2] {'expert'}, dimensions={1} | all-to-all | bytes 2621440 | tf_op jit(solution)/shard_map/all_to_all | solution.py:30
  93.5 267.1 %all-gather.8.cloned.1.call-done = bf16[16,2048,384]{2,1,0:T(8,128)(2,1)} async-done(((bf16[16,1024,384]{2,1,0:T(8,128)(2,1)}), bf16[16,2048,384]{2,1,0:T(8,128)(2,1)}) %all-gather.8.cloned.1.call-update) | async-done | bytes 25165840 | tf_op jit(solution)/shard_map/all_gather | solution.py:41
  360.6 14.9 %fusion.4 = f32[16,40,384]{2,1,0:T(8,128)S(1)} fusion(bf16[16,2048,384]{2,1,0:T(8,128)(2,1)} %all-gather.8.cloned.1.call-done, bf16[16,40,2048]{2,0,1:T(8,128)(2,1)} %bitcast.19), kind=kOutput, calls=%fused_computation.8 | convolution fusion | flops 1006632960 | bytes 28770304 | tf_op jit(solution)/shard_map/erd,edf->erf/dot_general | solution.py:44
  375.5 282.3 %all-gather.10.cloned.1.call-done = bf16[16,2048,384]{2,1,0:T(8,128)(2,1)} async-done(((bf16[16,1024,384]{2,1,0:T(8,128)(2,1)}), bf16[16,2048,384]{2,1,0:T(8,128)(2,1)}) %all-gather.10.cloned.1.call-update) | async-done | bytes 25165840 | tf_op jit(solution)/shard_map/all_gather | solution.py:42
  657.8 14.5 %fusion.2 = f32[16,40,384]{2,1,0:T(8,128)S(1)} fusion(bf16[16,2048,384]{2,1,0:T(8,128)(2,1)} %all-gather.10.cloned.1.call-done, bf16[16,40,2048]{2,0,1:T(8,128)(2,1)} %bitcast.20), kind=kOutput, calls=%fused_computation.6 | convolution fusion | flops 1006632960 | bytes 28770304 | tf_op jit(solution)/shard_map/erd,edf->erf/dot_general | solution.py:45
  672.3 294.6 %all-gather.14.cloned.1.call-done = bf16[16,384,2048]{2,1,0:T(8,128)(2,1)} async-done(((bf16[16,384,1024]{2,1,0:T(8,128)(2,1)}), bf16[16,384,2048]{2,1,0:T(8,128)(2,1)}) %all-gather.14.cloned.1.call-update) | async-done | bytes 25165840 | tf_op jit(solution)/shard_map/all_gather | solution.py:49
  966.9 12.6 %multiply_reduce_fusion = (f32[16,384]{1,0:T(8,128)S(1)}, f32[16,40,384]{2,1,0:T(8,128)S(1)}) fusion(f32[16,40,384]{2,1,0:T(8,128)S(1)} %fusion.2, f32[16,40,384]{2,1,0:T(8,128)S(1)} %fusion.4, bf16[16,384,2048]{2,1,0:T(8,128)(2,1)} %all-gather.14.cloned.1.call-done, bf16[16,40,2048]{2,0,1:T(8,128)(2,1)} %bitcast.21), kind=kOutput, calls=%fused_computation.20 | convolution fusion | flops 1008347136 | bytes 30760960 | tf_op jit(solution)/shard_map/erd,efd->erf/dot_general | solution.py:46
  979.4 16.1 %fusion.17 = f32[16,40,2048]{2,1,0:T(8,128)} fusion(bf16[16,2048,384]{2,1,0:T(8,128)(2,1)} %all-gather.8.cloned.1.call-done, f32[16,40,384]{2,1,0:T(8,128)S(1)} %fusion.4, f32[16,40,384]{2,1,0:T(8,128)S(1)} %get-tuple-element.3, f32[16,40,384]{2,1,0:T(8,128)S(1)} %fusion.2), kind=kOutput, calls=%fused_computation.26 | convolution fusion | flops 1009090560 | bytes 33357824 | tf_op jit(solution)/shard_map/erf,edf->erd/dot_general | solution.py:62
  995.6 21.6 %add_convert_fusion = bf16[16,40,2048]{2,1,0:T(8,128)(2,1)} fusion(f32[16,40,2048]{2,1,0:T(8,128)} %fusion.17, bf16[16,2048,384]{2,1,0:T(8,128)(2,1)} %all-gather.10.cloned.1.call-done, f32[16,40,384]{2,1,0:T(8,128)S(1)} %get-tuple-element.3, f32[16,40,384]{2,1,0:T(8,128)S(1)} %fusion.4), kind=kOutput, calls=%fused_computation.3 | convolution fusion | flops 1010728960 | bytes 34996224 | tf_op jit(solution)/shard_map/erf,edf->erd/dot_general | solution.py:63
  1017.2 10.8 reduce-scatter.2.cloned.1.call-done
  1028.0 3.1 copy.26
  1031.1 4.6 all-to-all-start.2
  1035.7 6.9 psum.7
  1043.2 23.4 %all-to-all-done.2 = bf16[16,4,10,1024]{3,0,2,1:T(8,128)(2,1)S(1)} async-done(((bf16[16,4,10,1024]{3,0,2,1:T(8,128)(2,1)}), bf16[16,4,10,1024]{3,0,2,1:T(8,128)(2,1)S(1)}, u32[]{:S(2)}, u32[]{:S(2)}) %all-to-all-start.2) | async-done | bytes 1310752 | tf_op jit(solution)/shard_map/all_to_all | solution.py:72
  1066.6 2.9 copy.27
  1069.5 3.0 reshape.78
  1072.5 2.7 gather_fusion
  1075.2 2.8 bitcast_reduce_fusion
  (32 shorter events, 4.3 us)
Async XLA Ops:
  7.2 1.0 copy-start
  7.2 86.3 %all-gather.6.cloned.1.call-start = ((), (), s32[]{:S(2)}) async-start(), calls=%async_computation.4 | async-start | bytes 3932160 | tf_op jit(solution)/shard_map/all_gather | solution.py:33
  50.6 310.1 %all-gather.8.cloned.1.call-start = ((), (), s32[]{:S(2)}) async-start(), calls=%async_computation.5 | async-start | bytes 37748736 | tf_op jit(solution)/shard_map/all_gather | solution.py:41
  51.3 0.9 copy-start.2
  51.3 0.9 copy-start.3
  51.3 606.4 %all-gather.10.cloned.1.call-start = ((), (), s32[]{:S(2)}) async-start(), calls=%async_computation.6 | async-start | bytes 37748736 | tf_op jit(solution)/shard_map/all_gather | solution.py:42
  52.1 620.2 %all-gather.12.cloned.1.call-start = ((), (), s32[]{:S(2)}) async-start(), calls=%async_computation.7 | async-start | bytes 3932160 | tf_op jit(solution)/shard_map/all_gather | solution.py:34
  92.8 874.0 %all-gather.14.cloned.1.call-start = ((), (), s32[]{:S(2)}) async-start(), calls=%async_computation.8 | async-start | bytes 37748736 | tf_op jit(solution)/shard_map/all_gather | solution.py:49
  93.4 934.6 %reduce-scatter.2.cloned.1.call-start = ((), (), s32[]{:S(2)}) async-start(), calls=%async_computation.9 | async-start | bytes 3932160 | tf_op jit(solution)/shard_map/reduce_scatter | solution.py:68
  1031.1 35.5 %all-to-all-start.2 = ((bf16[16,4,10,1024]{3,0,2,1:T(8,128)(2,1)}), bf16[16,4,10,1024]{3,0,2,1:T(8,128)(2,1)S(1)}, u32[]{:S(2)}, u32[]{:S(2)}) async-start(bf16[16,4,10,1024]{3,0,2,1:T(8,128)(2,1)} %bitcast.5), calls=%async_computation.3 | async-start | bytes 2621440 | tf_op jit(solution)/shard_map/all_to_all | solution.py:72
  1072.5 5.5 copy-start.1
Sparse Core Ops, SparseCore 0:
  50.7 11.9 all-gather.5
  64.3 296.3 all-gather.7
  362.2 295.5 all-gather.9
  659.1 11.7 all-gather.11
  672.3 294.4 all-gather.13
  1017.4 10.6 reduce-scatter.1
where the time goes:
time: 1090 us; the launch traced here: 1080 us
  waiting for transfers between devices  880 us (81%)
  matrix products  79.7 us (7%)
  blocking collectives  76.3 us (7%)
  other arithmetic  15.1 us (1%)
  local copies, waits for them, and re-layouts  14.6 us (1%)
  between operations  14.3 us (1%)
    all_gather x1, waiting for transfers between devices, local(): lax.all_gather(down_weight, 'dp', axis=2, tiled=True)  295 us
    all_gather x1, waiting for transfers between devices, local(): lax.all_gather(up_weight, 'dp', axis=1, tiled=True)  282 us
    all_gather x1, waiting for transfers between devices, local(): lax.all_gather(gate_weight, 'dp', axis=1, tiled=True)  267 us
    all_to_all x1, blocking collectives, local(): lax.all_to_all(x_send, 'expert', split_axis=1, concat_axis=1, tiled=True)  35.8 us
    all_to_all x1, blocking collectives, local(): lax.all_to_all(grad_send, 'expert', split_axis=1, concat_axis=1, tiled=True)  33.6 us
    all_to_all x1, waiting for transfers between devices, local(): lax.all_to_all(summed.astype(jnp.bfloat16), 'expert', split_axis=1, conca...  23.4 us
  transfers between devices with their start and end apart: 7, of which 5 were waited for; matrix products, arithmetic and copies ran while one was open for 3% of the time, Pallas kernels for 0%

commit v1 on v0

v1 whole, which is shorter than its diff:
```python
import functools

import jax
import jax.numpy as jnp
from jax import lax
from jax.experimental import pallas as pl
from jax.experimental.pallas import tpu as pltpu
from jax.sharding import PartitionSpec as P

LOCAL_EXPERTS = 64
TOPK = 8
CAP = 10
F32 = jnp.float32
BF16 = jnp.bfloat16
NT = (((1,), (1,)), ((), ()))
TN = (((0,), (0,)), ((), ()))
PARAMS = dict(vmem_limit_bytes=48 * 1024 * 1024)


def gathered(tokens, out_grad, gates, expert_ids, slots, gate_weight, up_weight, down_weight):
    expert_count = lax.axis_size("expert")
    group_count = lax.axis_size("dp")
    local_count = gate_weight.shape[0]
    tok_rows = tokens.shape[0]
    half_width = tokens.shape[1]
    slot_count = local_count * expert_count * CAP
    target_dev = expert_ids // local_count
    local_expert = expert_ids % local_count
    slot_rows = ((local_expert * expert_count + target_dev) * CAP + slots).reshape(-1)
    scaled = (gates[:, :, None] * out_grad[:, None, :].astype(F32)).astype(BF16)
    scaled = scaled.reshape(tok_rows * TOPK, half_width)
    repeated = jnp.repeat(tokens, TOPK, axis=0)

    def route(rows):
        send = jnp.zeros((slot_count, half_width), BF16).at[slot_rows].add(rows)
        send = send.reshape(local_count, expert_count, CAP, half_width)
        recv = lax.all_to_all(send, "expert", split_axis=1, concat_axis=1, tiled=True)
        full = lax.all_gather(recv, "sub", axis=3, tiled=True)
        return full.reshape(local_count, expert_count * CAP, full.shape[3])

    x_full, grad_full = route(repeated), route(scaled)
    gate_full = lax.all_gather(gate_weight, "dp", axis=1, tiled=True)
    up_full = lax.all_gather(up_weight, "dp", axis=1, tiled=True)
    down_full = lax.all_gather(down_weight, "dp", axis=2, tiled=True)
    gate_pre = jnp.einsum("erd,edf->erf", x_full, gate_full, preferred_element_type=F32)
    up_pre = jnp.einsum("erd,edf->erf", x_full, up_full, preferred_element_type=F32)
    hidden_grad = jnp.einsum("erd,efd->erf", grad_full, down_full, preferred_element_type=F32)
    gating = jax.nn.sigmoid(gate_pre)
    activated = gate_pre * gating
    channel = lax.psum(jnp.sum(activated * up_pre * hidden_grad, axis=1), "dp")
    scale = LOCAL_EXPERTS / (tok_rows * expert_count * group_count * TOPK)
    scores = channel * channel * scale
    gate_grad = (hidden_grad * up_pre * gating * (1.0 + gate_pre * (1.0 - gating))).astype(BF16)
    up_grad = (hidden_grad * activated).astype(BF16)
    parts = jnp.einsum("erf,edf->erd", gate_grad, gate_full, preferred_element_type=F32)
    parts = parts + jnp.einsum("erf,edf->erd", up_grad, up_full, preferred_element_type=F32)
    summed = lax.psum_scatter(parts.astype(BF16), "sub", scatter_dimension=2, tiled=True)
    summed = summed.reshape(local_count, expert_count, CAP, half_width)
    returned = lax.all_to_all(summed, "expert", split_axis=1, concat_axis=1, tiled=True)
    picked = returned.reshape(slot_count, half_width)[slot_rows].astype(F32)
    token_grad = jnp.sum(picked.reshape(tok_rows, TOPK, half_width), axis=1)
    return (scores, token_grad.astype(BF16))


def one_hot(rows, place):
    index = lax.broadcasted_iota(jnp.int32, (rows, place.shape[1]), 0).astype(F32)
    return jnp.where(index == place, 1.0, 0.0)


def fill(tok_ref, own_refs, other_refs, side, tok):
    for d, (own, other) in enumerate(zip(own_refs, other_refs)):
        tok_ref[pl.ds(2 * d * tok + side * tok, tok), :] = own[...]
        tok_ref[pl.ds(2 * d * tok + (1 - side) * tok, tok), :] = other[...]


def dispatch(rows, experts, group, place_ref, tok_ref, hot_ref, out_ref, level_ref=None):
    def body(g, carry):
        levels = []
        for j in range(group):
            e = g * group + j
            hot = one_hot(rows, place_ref[pl.ds(e, 1), :])
            hot_ref[pl.ds(j * rows, rows), :] = hot.astype(BF16)
            if level_ref is not None:
                levels.append(jnp.sum(hot * level_ref[pl.ds(e, 1), :], axis=1, keepdims=True))
        got = jnp.dot(hot_ref[...], tok_ref[...], preferred_element_type=F32)
        if level_ref is not None:
            got = got * jnp.concatenate(levels, axis=0)
        out_ref[pl.ds(pl.multiple_of(g * group * rows, group * rows), group * rows), :] = got.astype(BF16)
        return carry

    lax.fori_loop(0, experts // group, body, 0)


def places(zs, tok, cap, experts, meta_refs, place_ref, level_ref, first):
    lane = lax.broadcasted_iota(jnp.int32, (TOPK, 2 * tok), 1)
    rows, codes, levels = [], [], []
    for d in range(zs):
        code = meta_refs[d][0:TOPK, :]
        expert = jnp.floor((code + 0.5) * (1.0 / cap))
        block = 2 * d + (lane >= tok).astype(jnp.int32)
        rows.append(code - expert * cap + block.astype(F32) * cap)
        codes.append(expert)
        levels.append(meta_refs[d][TOPK : 2 * TOPK, :])
    row, expert, level = (jnp.concatenate(v, axis=1) for v in (rows, codes, levels))
    for e in range(experts):
        hit = expert == (first + e).astype(F32)
        place_ref[e : e + 1, :] = jnp.max(jnp.where(hit, row, -1.0), axis=0, keepdims=True)
        level_ref[e : e + 1, :] = jnp.sum(jnp.where(hit, level, 0.0), axis=0, keepdims=True)


def x_kernel(cfg, s_ref, *refs):
    zs, tok, experts, rows, group = cfg
    own, other, meta = refs[:zs], refs[zs : 2 * zs], refs[2 * zs : 3 * zs]
    gate_ref, up_ref, au_ref, xin_ref, place_ref, level_ref, tok_ref, hot_ref = refs[3 * zs :]
    j = pl.program_id(0)

    @pl.when(j == 0)
    def _():
        places(zs, tok, CAP, experts, meta, place_ref, level_ref, s_ref[2])
        fill(tok_ref, own, other, s_ref[1], tok)
        dispatch(rows, experts, group, place_ref, tok_ref, hot_ref, xin_ref)

    e = s_ref[0] + j
    x = xin_ref[pl.ds(pl.multiple_of(e * rows, rows), rows), :]
    au_ref[0, 0:rows, :] = jnp.dot(x, gate_ref[0], preferred_element_type=F32).astype(BF16)
    au_ref[0, rows:, :] = jnp.dot(x, up_ref[0], preferred_element_type=F32).astype(BF16)


def x2_kernel(rows, s_ref, x_ref, gate_ref, up_ref, au_ref):
    x = x_ref[...]
    au_ref[0, 0:rows, :] = jnp.dot(x, gate_ref[0], preferred_element_type=F32).astype(BF16)
    au_ref[0, rows:, :] = jnp.dot(x, up_ref[0], preferred_element_type=F32).astype(BF16)


def y_kernel(cfg, s_ref, *refs):
    zs, tok, experts, rows, group = cfg
    own, other = refs[:zs], refs[zs : 2 * zs]
    place_ref, level_ref, down_ref, dh_ref, yin_ref, tok_ref, hot_ref = refs[2 * zs :]
    j = pl.program_id(0)

    @pl.when(j == 0)
    def _():
        fill(tok_ref, own, other, s_ref[1], tok)
        dispatch(rows, experts, group, place_ref, tok_ref, hot_ref, yin_ref, level_ref)

    e = s_ref[0] + j
    y = yin_ref[pl.ds(pl.multiple_of(e * rows, rows), rows), :]
    dh_ref[0] = lax.dot_general(y, down_ref[0], NT, preferred_element_type=F32).astype(BF16)


def combine(rows, count, first, place_ref, part_ref, hot_ref):
    for j in range(count):
        hot_ref[j * rows : (j + 1) * rows, :] = one_hot(rows, place_ref[pl.ds(first + j, 1), :]).astype(BF16)
    return lax.dot_general(hot_ref[...], part_ref[...], TN, preferred_element_type=F32)


def mine_kernel(rows, count, scale, has_acc, s_ref, *refs):
    x_ref, y_ref, au_ref, dhr_ref, gate_ref, up_ref, down_ref, place_ref = refs[:8]
    acc_in = refs[8] if has_acc else None
    d_ref, score_ref, acc_ref, part_ref, hot_ref = refs[8 + has_acc :]
    j = pl.program_id(0)
    x, y = x_ref[...], y_ref[...]
    gate, up = gate_ref[0], up_ref[0]
    a = jnp.dot(x, gate, preferred_element_type=F32) + au_ref[0, 0:rows, :].astype(F32)
    u = jnp.dot(x, up, preferred_element_type=F32) + au_ref[0, rows:, :].astype(F32)
    dh = lax.dot_general(y, down_ref[0], NT, preferred_element_type=F32) + dhr_ref[0].astype(F32)
    sig = jax.nn.sigmoid(a)
    act = a * sig
    channel = jnp.sum(act * u * dh, axis=0, keepdims=True)
    score_ref[0] = channel * channel * scale
    da = (dh * u * sig * (1.0 + a * (1.0 - sig))).astype(BF16)
    du = (dh * act).astype(BF16)
    d_ref[0, 0:rows, :] = da
    d_ref[0, rows:, :] = du
    part = lax.dot_general(da, gate, NT, preferred_element_type=F32)
    part = part + lax.dot_general(du, up, NT, preferred_element_type=F32)
    part_ref[pl.ds(pl.multiple_of(j * rows, rows), rows), :] = part.astype(BF16)

    @pl.when(j == count - 1)
    def _():
        total = combine(rows, count, s_ref[0], place_ref, part_ref, hot_ref)
        acc_ref[...] = total + acc_in[...] if has_acc else total


def other_kernel(cfg, last, s_ref, *refs):
    rows, count, zs, tok = cfg
    d_ref, gate_ref, up_ref, place_ref, acc_in = refs[:5]
    j = pl.program_id(0)
    part_ref, hot_ref = refs[-2:]
    part = lax.dot_general(d_ref[0, 0:rows, :], gate_ref[0], NT, preferred_element_type=F32)
    part = part + lax.dot_general(d_ref[0, rows:, :], up_ref[0], NT, preferred_element_type=F32)
    part_ref[pl.ds(pl.multiple_of(j * rows, rows), rows), :] = part.astype(BF16)

    @pl.when(j == count - 1)
    def _():
        total = combine(rows, count, s_ref[0], place_ref, part_ref, hot_ref) + acc_in[...]
        if not last:
            refs[5][...] = total
        else:
            keep_ref, send_ref, acc = refs[5], refs[6], refs[7]
            acc[...] = total
            side = s_ref[1]
            for d in range(zs):
                keep_ref[d] = acc[pl.ds(2 * d * tok + side * tok, tok), :]
                send_ref[d] = acc[pl.ds(2 * d * tok + (1 - side) * tok, tok), :].astype(BF16)


def stationary(tokens, out_grad, gates, expert_ids, slots, gate_weight, up_weight, down_weight):
    zs = lax.axis_size("expert")
    tok, width = tokens.shape
    experts, _, ff = gate_weight.shape
    rows = 2 * zs * CAP
    all_tok = 2 * zs * tok
    half = experts // 2
    chunks = 2 if half % 2 == 0 else 1
    count = half // chunks
    group = count
    p, s, z = lax.axis_index("dp"), lax.axis_index("sub"), lax.axis_index("expert")
    mine0, other0 = half * p, half * (1 - p)

    def swap(v):
        return lax.ppermute(v, ("dp", "sub"), [(0, 0), (1, 2), (2, 1), (3, 3)])

    def flip(v, axis):
        return lax.ppermute(v, axis, [(0, 1), (1, 0)])

    def shift(v, d):
        return lax.ppermute(v, "expert", [(i, (i + d) % zs) for i in range(zs)])

    meta = jnp.concatenate([(expert_ids * CAP + slots).astype(F32).T, gates.T], axis=0)
    meta_other = flip(meta, "dp")
    pair = jnp.concatenate(
        [jnp.where(p == 0, meta, meta_other), jnp.where(p == 0, meta_other, meta)], axis=1
    )
    metas = [pair] + [shift(pair, d) for d in range(1, zs)]

    def spread(v):
        v = swap(v)
        own = [v] + [shift(v, d) for d in range(1, zs)]
        return own, [flip(w, "sub") for w in own]

    x_own, x_other = spread(tokens)
    y_own, y_other = spread(out_grad)

    def info(first):
        return jnp.stack([first, s, z * experts]).astype(jnp.int32)

    def whole(shape):
        return pl.BlockSpec(shape, lambda j, m: (0,) * len(shape))

    def per(shape):
        return pl.BlockSpec((1,) + shape, lambda j, m: (j,) + (0,) * len(shape))

    def pick(shape):
        return pl.BlockSpec((1,) + shape, lambda j, m: (m[0] + j,) + (0,) * len(shape))

    def sds(shape, dtype):
        return jax.ShapeDtypeStruct(shape, dtype)

    rows_spec = pl.BlockSpec((rows, width), lambda j, m: (m[0] + j, 0))
    up_spec, down_spec = pick((width, ff)), pick((ff, width))
    blocks = [whole((tok, width))] * zs

    def call(body, first, ins, args, outs, out_specs, scratch, steps, cost):
        return pl.pallas_call(
            body,
            out_shape=outs,
            grid_spec=pltpu.PrefetchScalarGridSpec(
                num_scalar_prefetch=1, grid=(steps,), in_specs=ins, out_specs=out_specs, scratch_shapes=scratch
            ),
            compiler_params=pltpu.CompilerParams(**PARAMS),
            cost_estimate=pl.CostEstimate(flops=cost[0], bytes_accessed=cost[1], transcendentals=0),
        )(info(first), *args)

    wbytes = width * ff * 2
    flop = 2 * rows * width * ff
    dflop = 2 * experts * rows * all_tok * width
    cfg = (zs, tok, experts, rows, group)
    hot = pltpu.VMEM((group * rows, all_tok), BF16)
    tok_scratch = pltpu.VMEM((all_tok, width), BF16)
    au0, xin, place, level = call(
        functools.partial(x_kernel, cfg),
        other0,
        blocks * 2 + [whole((2 * TOPK, 2 * tok))] * zs + [up_spec, up_spec],
        (*x_own, *x_other, *metas, gate_weight, up_weight),
        [
            sds((count, 2 * rows, ff), BF16),
            sds((experts * rows, width), BF16),
            sds((experts, all_tok), F32),
            sds((experts, all_tok), F32),
        ],
        [per((2 * rows, ff)), whole((experts * rows, width)), whole((experts, all_tok)), whole((experts, all_tok))],
        [tok_scratch, hot],
        count,
        (2 * count * flop + dflop, 2 * count * wbytes),
    )
    au_send = [au0]
    for c in range(1, chunks):
        au_send.append(
            call(
                functools.partial(x2_kernel, rows),
                other0 + c * count,
                [rows_spec, up_spec, up_spec],
                (xin, gate_weight, up_weight),
                sds((count, 2 * rows, ff), BF16),
                per((2 * rows, ff)),
                [],
                count,
                (2 * count * flop, 2 * count * wbytes),
            )
        )
    au_recv = [flip(v, "dp") for v in au_send]
    dh_send, yin = call(
        functools.partial(y_kernel, cfg),
        other0,
        blocks * 2 + [whole((experts, all_tok))] * 2 + [down_spec],
        (*y_own, *y_other, place, level, down_weight),
        [sds((half, rows, ff), BF16), sds((experts * rows, width), BF16)],
        [per((rows, ff)), whole((experts * rows, width))],
        [tok_scratch, hot],
        half,
        (half * flop + dflop, half * wbytes),
    )
    dh_recv = [flip(dh_send[c * count : (c + 1) * count], "dp") for c in range(chunks)]
    scale = LOCAL_EXPERTS / (all_tok * TOPK)
    part_scratch = pltpu.VMEM((count * rows, width), BF16)
    place_spec = whole((experts, all_tok))
    acc_spec, acc_shape = whole((all_tok, width)), sds((all_tok, width), F32)
    acc = None
    back, scores = [], []
    for c in range(chunks):
        has_acc = acc is not None
        d, sc, acc = call(
            functools.partial(mine_kernel, rows, count, scale, has_acc),
            mine0 + c * count,
            [rows_spec, rows_spec, per((2 * rows, ff)), per((rows, ff)), up_spec, up_spec, down_spec, place_spec]
            + [acc_spec] * has_acc,
            (xin, yin, au_recv[c], dh_recv[c], gate_weight, up_weight, down_weight, place) + (acc,) * has_acc,
            [sds((count, 2 * rows, ff), BF16), sds((count, 1, ff), F32), acc_shape],
            [per((2 * rows, ff)), per((1, ff)), acc_spec],
            [part_scratch, hot],
            count,
            (5 * count * flop, 3 * count * wbytes),
        )
        back.append(flip(d, "dp"))
        scores.append(sc)
    for c in range(chunks):
        last = c == chunks - 1
        zshape = (zs, tok, width)
        res = call(
            functools.partial(other_kernel, (rows, count, zs, tok), last),
            other0 + c * count,
            [per((2 * rows, ff)), up_spec, up_spec, place_spec, acc_spec],
            (back[c], gate_weight, up_weight, place, acc),
            [sds(zshape, F32), sds(zshape, BF16)] if last else acc_shape,
            [whole(zshape), whole(zshape)] if last else acc_spec,
            ([pltpu.VMEM((all_tok, width), F32)] if last else []) + [part_scratch, hot],
            count,
            (2 * count * flop, 2 * count * wbytes),
        )
        if not last:
            acc = res
    keep, send = res
    summed = (keep + flip(send, "sub").astype(F32)).astype(BF16)
    total = summed[0].astype(F32)
    for d in range(1, zs):
        total = total + shift(summed[d], -d).astype(F32)
    token_grad = swap(total.astype(BF16))
    score = jnp.concatenate(scores, axis=0).reshape(half, ff)
    score_other = flip(score, "dp")
    scores = jnp.concatenate(
        [jnp.where(p == 0, score, score_other), jnp.where(p == 0, score_other, score)], axis=0
    )
    return (scores, token_grad)


def solution(mesh):
    in_specs = (
        P(("dom", "expert", "dp"), "sub"),
        P(("dom", "expert", "dp"), "sub"),
        P(("dom", "expert", "dp"), None),
        P(("dom", "expert", "dp"), None),
        P(("dom", "expert", "dp"), None),
        P("expert", "dp", "sub"),
        P("expert", "dp", "sub"),
        P("expert", "sub", "dp"),
    )
    out_specs = (P(("dom", "expert"), "sub"), P(("dom", "expert", "dp"), "sub"))
    pairs = mesh.shape["dp"] == 2 and mesh.shape["sub"] == 2
    split = (LOCAL_EXPERTS // mesh.shape["expert"]) % 2 == 0
    local = stationary if pairs and split else gathered
    return jax.shard_map(local, mesh=mesh, in_specs=in_specs, out_specs=out_specs, check_vma=False)
```

time: 1090 us -> 153 us (0.14)
  waiting for transfers between devices: 880 us -> 49.1 us
  matrix products: 79.7 us -> 0 us
  blocking collectives: 76.3 us -> 0 us
  Pallas kernels: 0 us -> 52.5 us
  starting transfers between devices: 4.83 us -> 37.4 us
  between operations: 14.3 us -> 0.83 us
  other arithmetic: 15.1 us -> 3.34 us
    all_gather x5 -> x0, waiting for transfers between devices: 844 us -> none  [the longest x1 295 us: local(): lax.all_gather(down_weight, 'dp', axis=2, tiled=True)]
    dot_general x5 -> x0, matrix products: 79.7 us -> none  [the longest x1 21.6 us: local(): jnp.einsum('erf,edf->erd', up_grad, up_full, preferred_element_type=jnp.f...]
    all_to_all x2 -> x0, blocking collectives: 69.4 us -> none  [the longest x1 35.8 us: local(): lax.all_to_all(x_send, 'expert', split_axis=1, concat_axis=1, tiled=True)]
    pallas_call x0 -> x7, Pallas kernels: none -> 52.5 us  [call(): pl.pallas_call(body, out_shape=outs, grid_spec=pltpu.PrefetchScalarGridSp...]
    ppermute x0 -> x32, waiting for transfers between devices: none -> 49.1 us  [the longest x12 26.7 us: shift(): return lax.ppermute(v, 'expert', [(i, (i + d) % zs) for i in range(zs)])]
    ppermute x0 -> x32, starting transfers between devices: none -> 37.4 us  [the longest x12 14.4 us: shift(): return lax.ppermute(v, 'expert', [(i, (i + d) % zs) for i in range(zs)])]
    all_to_all x1 -> x0, waiting for transfers between devices: 23.4 us -> none  [local(): lax.all_to_all(summed.astype(jnp.bfloat16), 'expert', split_axis=1, conca...]
  transfers between devices with their start and end apart: 7 -> 32, of which waited for: 5 -> 12; matrix products, arithmetic and copies ran while one was open for 3% -> 2% of each run, Pallas kernels for 0% -> 30%
where the time goes in v1:
time: 153 us; the launch traced here: 152 us
  Pallas kernels  52.5 us (34%)
  waiting for transfers between devices  49.1 us (32%)
  starting transfers between devices  37.4 us (24%)
  local copies, waits for them, and re-layouts  9.26 us (6%)
  other arithmetic  3.34 us (2%)
    pallas_call x7, Pallas kernels, call(): pl.pallas_call(body, out_shape=outs, grid_spec=pltpu.PrefetchScalarGridSp...  52.5 us
    ppermute x12, waiting for transfers between devices, shift(): return lax.ppermute(v, 'expert', [(i, (i + d) % zs) for i in range(zs)])  26.7 us
    ppermute x17, waiting for transfers between devices, flip(): return lax.ppermute(v, axis, [(0, 1), (1, 0)])  20.4 us
    ppermute x12, starting transfers between devices, shift(): return lax.ppermute(v, 'expert', [(i, (i + d) % zs) for i in range(zs)])  14.4 us
    ppermute x17, starting transfers between devices, flip(): return lax.ppermute(v, axis, [(0, 1), (1, 0)])  13.7 us
    ppermute x3, starting transfers between devices, swap(): return lax.ppermute(v, ('dp', 'sub'), [(0, 0), (1, 2), (2, 1), (3, 3)])  9.32 us
    unnamed x22, local copies, waits for them, and re-layouts  8.4 us
  transfers between devices with their start and end apart: 32, of which 12 were waited for; matrix products, arithmetic and copies ran while one was open for 2% of the time, Pallas kernels for 30%

profile of v1, /device:TPU:1, one launch (start us, length us, event | category | flops | bytes accessed | tf_op | source)
XLA Modules:
  0.0 152.4 jit_solution(17077035727001314421)
XLA Ops:
  2.0 2.0 %collective-permute-start.8 = (f32[16,64]{1,0:T(8,128)S(1)}, f32[16,64]{1,0:T(8,128)S(1)}, u32[]{:S(2)}, u32[]{:S(2)}) collective-permute-start(f32[16,64]{1,0:T(8,128)S(1)} %pad_maximum_fusion.2), channel_id=1, source_target_pairs={{0,2},{2,0},{1,3},{3,1},{4,6},{6,4},{5,7},{7,5},{8,10},{10,8},{9,1... | collective-permute-start | bytes 12296 | tf_op jit(solution)/shard_map/ppermute | solution.py:225
  4.1 2.5 %collective-permute-start = (bf16[64,1024]{1,0:T(8,128)(2,1)}, bf16[64,1024]{1,0:T(8,128)(2,1)S(1)}, u32[]{:S(2)}, u32[]{:S(2)}) collective-permute-start(bf16[64,1024]{1,0:T(8,128)(2,1)} %param.8), channel_id=1, source_target_pairs={{0,0},{1,2},{2,1},{3,3},{4,4},{5,6},{6,5},{7,7},{8,8},{9,10},{10,9... | collective-permute-start | bytes 393224 | tf_op jit(solution)/shard_map/ppermute | solution.py:222
  6.5 3.1 %collective-permute-start.12 = (bf16[64,1024]{1,0:T(8,128)(2,1)}, bf16[64,1024]{1,0:T(8,128)(2,1)S(1)}, u32[]{:S(2)}, u32[]{:S(2)}) collective-permute-start(bf16[64,1024]{1,0:T(8,128)(2,1)} %param.9), channel_id=1, source_target_pairs={{0,0},{1,2},{2,1},{3,3},{4,4},{5,6},{6,5},{7,7},{8,8},{9,10},{10,9... | collective-permute-start | bytes 393224 | tf_op jit(solution)/shard_map/ppermute | solution.py:222
  10.4 3.3 %collective-permute-start.11 = (f32[16,128]{1,0:T(8,128)S(1)}, f32[16,128]{1,0:T(8,128)S(1)}, u32[]{:S(2)}, u32[]{:S(2)}) collective-permute-start(f32[16,128]{1,0:T(8,128)S(1)} %pad_maximum_fusion.3.refs_8_), channel_id=1, source_target_pairs={{0,12},{4,0},{8,4},{12,8},{1,13},{5,1},{9,5},{13,9},{2,14},{6,2},{... | collective-permute-start | bytes 24584 | tf_op jit(solution)/shard_map/ppermute | solution.py:228
  14.6 3.5 %collective-permute-start.3 = (bf16[64,1024]{1,0:T(8,128)(2,1)S(1)}, bf16[64,1024]{1,0:T(8,128)(2,1)S(1)}, u32[]{:S(2)}, u32[]{:S(2)}) collective-permute-start(bf16[64,1024]{1,0:T(8,128)(2,1)S(1)} %collective-permute-done.refs_0_), channel_id=1, source_target_pairs={{0,12},{4,0},{8,4},{12,8},{1,13},{5,1},{9,5},{13,9},{2,14},{6,2},{... | collective-permute-start | bytes 393224 | tf_op jit(solution)/shard_map/ppermute | solution.py:228
  18.4 3.0 %collective-permute-start.15 = (bf16[64,1024]{1,0:T(8,128)(2,1)S(1)}, bf16[64,1024]{1,0:T(8,128)(2,1)S(1)}, u32[]{:S(2)}, u32[]{:S(2)}) collective-permute-start(bf16[64,1024]{1,0:T(8,128)(2,1)S(1)} %collective-permute-done.12.refs_0_), channel_id=1, source_target_pairs={{0,12},{4,0},{8,4},{12,8},{1,13},{5,1},{9,5},{13,9},{2,14},{6,2},{... | collective-permute-start | bytes 393224 | tf_op jit(solution)/shard_map/ppermute | solution.py:228
  22.0 7.8 %collective-permute-done.2.refs_2_ = bf16[64,1024]{1,0:T(8,128)(2,1)S(1)} collective-permute-done((bf16[64,1024]{1,0:T(8,128)(2,1)S(1)}, bf16[64,1024]{1,0:T(8,128)(2,1)S(1)}, u32[]{:S(2)}, u32[]{:S(2)}) %collective-permute-start.2) | collective-permute-done | bytes 131104 | tf_op jit(solution)/shard_map/ppermute | solution.py:228
  32.1 9.0 %collective-permute-done.14.refs_2_ = bf16[64,1024]{1,0:T(8,128)(2,1)} collective-permute-done((bf16[64,1024]{1,0:T(8,128)(2,1)S(1)}, bf16[64,1024]{1,0:T(8,128)(2,1)}, u32[]{:S(2)}, u32[]{:S(2)}) %collective-permute-start.14) | collective-permute-done | bytes 131104 | tf_op jit(solution)/shard_map/ppermute | solution.py:228
  48.0 7.7 %shard_map.95 = (bf16[4,160,384]{2,1,0:T(8,128)(2,1)}, bf16[1280,1024]{1,0:T(8,128)(2,1)S(1)}, f32[16,512]{1,0:T(8,128)S(1)}, f32[16,512]{1,0:T(8,128)S(1)}) custom-call(s32[3]{0:T(128)S(1)} %add_add_fusion.1.s_ref, bf16[64,1024]{1,0:T(8,128)(2,1)S(1)} %collective-permute-done.refs_0_, bf16[64,1024]{1,0:T(8,128)(2,1)S(1)} %copy-done.3, ...), custom_call_target="tpu_custom_call" | custom-call | flops 1845493760 | bytes 6291456 | tf_op jit(solution)/shard_map/pallas_call | solution.py:265
  55.7 5.9 %shard_map.98 = bf16[4,160,384]{2,1,0:T(8,128)(2,1)} custom-call(s32[3]{0:T(128)S(1)} %add_add_fusion.3.s_ref, bf16[1280,1024]{1,0:T(8,128)(2,1)S(1)} %get-tuple-element.16.refs_0_.x_ref, bf16[16,1024,384]{2,1,0:T(8,128)(2,1)} %refs_1_.3, bf16[16,1024,384]{2,1,0:T(8,128)(2,1)} %refs_2_.3), custom_call_target="tpu_custom_call" | custom-call | flops 503316480 | bytes 6291456 | tf_op jit(solution)/shard_map/pallas_call | solution.py:265
  61.6 2.0 %collective-permute-start.22 = (bf16[4,160,384]{2,1,0:T(8,128)(2,1)}, bf16[4,160,384]{2,1,0:T(8,128)(2,1)S(1)}, u32[]{:S(2)}, u32[]{:S(2)}) collective-permute-start(bf16[4,160,384]{2,1,0:T(8,128)(2,1)} %shard_map.98), channel_id=1, source_target_pairs={{0,2},{2,0},{1,3},{3,1},{4,6},{6,4},{5,7},{7,5},{8,10},{10,8},{9,1... | collective-permute-start | bytes 1474568 | tf_op jit(solution)/shard_map/ppermute | solution.py:225
  63.7 9.7 %shard_map.96 = (bf16[8,80,384]{2,1,0:T(8,128)(2,1)S(1)}, bf16[1280,1024]{1,0:T(8,128)(2,1)S(1)}) custom-call(s32[3]{0:T(128)S(1)} %add_add_fusion.1.s_ref, bf16[64,1024]{1,0:T(8,128)(2,1)S(1)} %collective-permute-done.12.refs_0_, bf16[64,1024]{1,0:T(8,128)(2,1)} %collective-permute-done.13.refs_1_, bf16[64,1024]{1,0:T(8,128)(2,1)} %collective-permute-done.14.refs_2_, ...), custom_call_target="tpu_custom_call" | custom-call | flops 1845493760 | bytes 6291456 | tf_op jit(solution)/shard_map/pallas_call | solution.py:265
  77.3 13.5 %collective-permute-done.21.refs_3_ = bf16[4,80,384]{2,1,0:T(8,128)(2,1)} collective-permute-done((bf16[4,80,384]{2,1,0:T(8,128)(2,1)}, bf16[4,80,384]{2,1,0:T(8,128)(2,1)}, u32[]{:S(2)}, u32[]{:S(2)}) %collective-permute-start.21) | collective-permute-done | bytes 245792 | tf_op jit(solution)/shard_map/ppermute | solution.py:225
  90.8 8.5 %shard_map.97 = (bf16[4,160,384]{2,1,0:T(8,128)(2,1)S(1)}, f32[4,1,384]{2,1,0:T(1,128)S(1)}, f32[512,1024]{1,0:T(8,128)S(1)}) custom-call(s32[3]{0:T(128)S(1)} %add_add_fusion.s_ref, bf16[1280,1024]{1,0:T(8,128)(2,1)S(1)} %get-tuple-element.16.refs_0_.x_ref, bf16[1280,1024]{1,0:T(8,128)(2,1)} %copy-done.1, ...), custom_call_target="tpu_custom_call" | custom-call | flops 1258291200 | bytes 9437184 | tf_op jit(solution)/shard_map/pallas_call | solution.py:265
  100.6 8.5 %shard_map.99 = (bf16[4,160,384]{2,1,0:T(8,128)(2,1)S(1)}, f32[4,1,384]{2,1,0:T(1,128)S(1)}, f32[512,1024]{1,0:T(8,128)S(1)}) custom-call(s32[3]{0:T(128)S(1)} %add_add_fusion.2.s_ref, bf16[1280,1024]{1,0:T(8,128)(2,1)} %copy-done, bf16[1280,1024]{1,0:T(8,128)(2,1)} %copy-done.1, bf16[4,160,384]{2,1,0:T(8,128)(2,1)S(1)} %collective-permute-done.22.refs_2_, ...), custom_call_target="tpu_custom_call" | custom-call | flops 1258291200 | bytes 9437184 | tf_op jit(solution)/shard_map/pallas_call | solution.py:265
  110.4 6.1 %shard_map.100.refs_4_ = f32[512,1024]{1,0:T(8,128)S(1)} custom-call(s32[3]{0:T(128)S(1)} %add_add_fusion.1.s_ref, bf16[4,160,384]{2,1,0:T(8,128)(2,1)S(1)} %collective-permute-done.26.refs_0_, bf16[16,1024,384]{2,1,0:T(8,128)(2,1)} %refs_1_.3, bf16[16,1024,384]{2,1,0:T(8,128)(2,1)} %refs_2_.3, f32[16,512]{1,0:T(8,128)S(1)} %get-tuple-element.17.refs_8_.refs_7_.refs_3_, ...), custom_call_target="tpu_custom_call" | custom-call | flops 503316480 | bytes 6291456 | tf_op jit(solution)/shard_map/pallas_call | solution.py:265
  116.5 4.4 %collective-permute-done.25.refs_0_ = bf16[4,160,384]{2,1,0:T(8,128)(2,1)S(1)} collective-permute-done((bf16[4,160,384]{2,1,0:T(8,128)(2,1)S(1)}, bf16[4,160,384]{2,1,0:T(8,128)(2,1)S(1)}, u32[]{:S(2)}, u32[]{:S(2)}) %collective-permute-start.25) | collective-permute-done | bytes 491552 | tf_op jit(solution)/shard_map/ppermute | solution.py:225
  120.9 6.2 %shard_map.101 = (f32[4,64,1024]{2,1,0:T(8,128)S(1)}, bf16[4,64,1024]{2,1,0:T(8,128)(2,1)S(1)}) custom-call(s32[3]{0:T(128)S(1)} %add_add_fusion.3.s_ref, bf16[4,160,384]{2,1,0:T(8,128)(2,1)S(1)} %collective-permute-done.25.refs_0_, bf16[16,1024,384]{2,1,0:T(8,128)(2,1)} %refs_1_.3, bf16[16,1024,384]{2,1,0:T(8,128)(2,1)} %refs_2_.3, ...), custom_call_target="tpu_custom_call" | custom-call | flops 503316480 | bytes 6291456 | tf_op jit(solution)/shard_map/pallas_call | solution.py:265
  127.0 2.8 %collective-permute-start.27 = (bf16[4,64,1024]{2,1,0:T(8,128)(2,1)S(1)}, bf16[4,64,1024]{2,1,0:T(8,128)(2,1)S(1)}, u32[]{:S(2)}, u32[]{:S(2)}) collective-permute-start(bf16[4,64,1024]{2,1,0:T(8,128)(2,1)S(1)} %get-tuple-element.29), channel_id=1, source_target_pairs={{0,1},{1,0},{2,3},{3,2},{4,5},{5,4},{6,7},{7,6},{8,9},{9,8},{10,11... | collective-permute-start | bytes 1572872 | tf_op jit(solution)/shard_map/ppermute | solution.py:225
  133.1 1.7 %collective-permute-start.29 = (bf16[64,1024]{1,0:T(8,128)(2,1)S(1)}, bf16[64,1024]{1,0:T(8,128)(2,1)S(1)}, u32[]{:S(2)}, u32[]{:S(2)}) collective-permute-start(bf16[64,1024]{1,0:T(8,128)(2,1)S(1)} %get-tuple-element.32), channel_id=1, source_target_pairs={{0,8},{4,12},{8,0},{12,4},{1,9},{5,13},{9,1},{13,5},{2,10},{6,14},... | collective-permute-start | bytes 393224 | tf_op jit(solution)/shard_map/ppermute | solution.py:228
  136.3 4.3 %collective-permute-done.30 = bf16[64,1024]{1,0:T(8,128)(2,1)S(1)} collective-permute-done((bf16[64,1024]{1,0:T(8,128)(2,1)S(1)}, bf16[64,1024]{1,0:T(8,128)(2,1)S(1)}, u32[]{:S(2)}, u32[]{:S(2)}) %collective-permute-start.30) | collective-permute-done | bytes 131104 | tf_op jit(solution)/shard_map/ppermute | solution.py:228
  140.6 4.6 %collective-permute-done.29 = bf16[64,1024]{1,0:T(8,128)(2,1)S(1)} collective-permute-done((bf16[64,1024]{1,0:T(8,128)(2,1)S(1)}, bf16[64,1024]{1,0:T(8,128)(2,1)S(1)}, u32[]{:S(2)}, u32[]{:S(2)}) %collective-permute-start.29) | collective-permute-done | bytes 131104 | tf_op jit(solution)/shard_map/ppermute | solution.py:228
  145.3 3.8 %collective-permute-start.31 = (bf16[64,1024]{1,0:T(8,128)(2,1)S(1)}, bf16[64,1024]{1,0:T(8,128)(2,1)S(1)}, u32[]{:S(2)}, u32[]{:S(2)}) collective-permute-start(bf16[64,1024]{1,0:T(8,128)(2,1)S(1)} %fusion.2), channel_id=1, source_target_pairs={{0,0},{1,2},{2,1},{3,3},{4,4},{5,6},{6,5},{7,7},{8,8},{9,10},{10,9... | collective-permute-start | bytes 393224 | tf_op jit(solution)/shard_map/ppermute | solution.py:222
  149.7 2.0 %collective-permute-done.31 = bf16[64,1024]{1,0:T(8,128)(2,1)S(1)} collective-permute-done((bf16[64,1024]{1,0:T(8,128)(2,1)S(1)}, bf16[64,1024]{1,0:T(8,128)(2,1)S(1)}, u32[]{:S(2)}, u32[]{:S(2)}) %collective-permute-start.31) | collective-permute-done | bytes 131104 | tf_op jit(solution)/shard_map/ppermute | solution.py:222
  (84 shorter events, 25.6 us)
Async XLA Ops:
  2.0 7.6 %collective-permute-start.8 = (f32[16,64]{1,0:T(8,128)S(1)}, f32[16,64]{1,0:T(8,128)S(1)}, u32[]{:S(2)}, u32[]{:S(2)}) collective-permute-start(f32[16,64]{1,0:T(8,128)S(1)} %pad_maximum_fusion.2), channel_id=1, source_target_pairs={{0,2},{2,0},{1,3},{3,1},{4,6},{6,4},{5,7},{7,5},{8,10},{10,8},{9,1... | collective-permute-start | bytes 12296 | tf_op jit(solution)/shard_map/ppermute | solution.py:225
  4.1 10.1 %collective-permute-start = (bf16[64,1024]{1,0:T(8,128)(2,1)}, bf16[64,1024]{1,0:T(8,128)(2,1)S(1)}, u32[]{:S(2)}, u32[]{:S(2)}) collective-permute-start(bf16[64,1024]{1,0:T(8,128)(2,1)} %param.8), channel_id=1, source_target_pairs={{0,0},{1,2},{2,1},{3,3},{4,4},{5,6},{6,5},{7,7},{8,8},{9,10},{10,9... | collective-permute-start | bytes 393224 | tf_op jit(solution)/shard_map/ppermute | solution.py:222
  6.5 11.8 %collective-permute-start.12 = (bf16[64,1024]{1,0:T(8,128)(2,1)}, bf16[64,1024]{1,0:T(8,128)(2,1)S(1)}, u32[]{:S(2)}, u32[]{:S(2)}) collective-permute-start(bf16[64,1024]{1,0:T(8,128)(2,1)} %param.9), channel_id=1, source_target_pairs={{0,0},{1,2},{2,1},{3,3},{4,4},{5,6},{6,5},{7,7},{8,8},{9,10},{10,9... | collective-permute-start | bytes 393224 | tf_op jit(solution)/shard_map/ppermute | solution.py:222
  18.1 11.7 %collective-permute-start.2 = (bf16[64,1024]{1,0:T(8,128)(2,1)S(1)}, bf16[64,1024]{1,0:T(8,128)(2,1)S(1)}, u32[]{:S(2)}, u32[]{:S(2)}) collective-permute-start(bf16[64,1024]{1,0:T(8,128)(2,1)S(1)} %collective-permute-done.refs_0_), channel_id=1, source_target_pairs={{0,8},{4,12},{8,0},{12,4},{1,9},{5,13},{9,1},{13,5},{2,10},{6,14},... | collective-permute-start | bytes 393224 | tf_op jit(solution)/shard_map/ppermute | solution.py:228
  18.2 12.6 %collective-permute-start.1 = (bf16[64,1024]{1,0:T(8,128)(2,1)S(1)}, bf16[64,1024]{1,0:T(8,128)(2,1)S(1)}, u32[]{:S(2)}, u32[]{:S(2)}) collective-permute-start(bf16[64,1024]{1,0:T(8,128)(2,1)S(1)} %collective-permute-done.refs_0_), channel_id=1, source_target_pairs={{0,4},{4,8},{8,12},{12,0},{1,5},{5,9},{9,13},{13,1},{2,6},{6,10},{... | collective-permute-start | bytes 393224 | tf_op jit(solution)/shard_map/ppermute | solution.py:228
  18.4 12.4 %collective-permute-start.15 = (bf16[64,1024]{1,0:T(8,128)(2,1)S(1)}, bf16[64,1024]{1,0:T(8,128)(2,1)S(1)}, u32[]{:S(2)}, u32[]{:S(2)}) collective-permute-start(bf16[64,1024]{1,0:T(8,128)(2,1)S(1)} %collective-permute-done.12.refs_0_), channel_id=1, source_target_pairs={{0,12},{4,0},{8,4},{12,8},{1,13},{5,1},{9,5},{13,9},{2,14},{6,2},{... | collective-permute-start | bytes 393224 | tf_op jit(solution)/shard_map/ppermute | solution.py:228
  21.4 19.7 %collective-permute-start.14 = (bf16[64,1024]{1,0:T(8,128)(2,1)S(1)}, bf16[64,1024]{1,0:T(8,128)(2,1)}, u32[]{:S(2)}, u32[]{:S(2)}) collective-permute-start(bf16[64,1024]{1,0:T(8,128)(2,1)S(1)} %collective-permute-done.12.refs_0_), channel_id=1, source_target_pairs={{0,8},{4,12},{8,0},{12,4},{1,9},{5,13},{9,1},{13,5},{2,10},{6,14},... | collective-permute-start | bytes 393224 | tf_op jit(solution)/shard_map/ppermute | solution.py:228
  21.9 19.9 %collective-permute-start.13 = (bf16[64,1024]{1,0:T(8,128)(2,1)S(1)}, bf16[64,1024]{1,0:T(8,128)(2,1)}, u32[]{:S(2)}, u32[]{:S(2)}) collective-permute-start(bf16[64,1024]{1,0:T(8,128)(2,1)S(1)} %collective-permute-done.12.refs_0_), channel_id=1, source_target_pairs={{0,4},{4,8},{8,12},{12,0},{1,5},{5,9},{9,13},{13,1},{2,6},{6,10},{... | collective-permute-start | bytes 393224 | tf_op jit(solution)/shard_map/ppermute | solution.py:228
  29.8 12.0 %collective-permute-start.7 = (bf16[64,1024]{1,0:T(8,128)(2,1)S(1)}, bf16[64,1024]{1,0:T(8,128)(2,1)S(1)}, u32[]{:S(2)}, u32[]{:S(2)}) collective-permute-start(bf16[64,1024]{1,0:T(8,128)(2,1)S(1)} %collective-permute-done.3.refs_3_), channel_id=1, source_target_pairs={{0,1},{1,0},{2,3},{3,2},{4,5},{5,4},{6,7},{7,6},{8,9},{9,8},{10,11... | collective-permute-start | bytes 393224 | tf_op jit(solution)/shard_map/ppermute | solution.py:225
  30.8 12.2 %collective-permute-start.6 = (bf16[64,1024]{1,0:T(8,128)(2,1)S(1)}, bf16[64,1024]{1,0:T(8,128)(2,1)S(1)}, u32[]{:S(2)}, u32[]{:S(2)}) collective-permute-start(bf16[64,1024]{1,0:T(8,128)(2,1)S(1)} %collective-permute-done.2.refs_2_), channel_id=1, source_target_pairs={{0,1},{1,0},{2,3},{3,2},{4,5},{5,4},{6,7},{7,6},{8,9},{9,8},{10,11... | collective-permute-start | bytes 393224 | tf_op jit(solution)/shard_map/ppermute | solution.py:225
  30.8 12.9 %collective-permute-start.5 = (bf16[64,1024]{1,0:T(8,128)(2,1)S(1)}, bf16[64,1024]{1,0:T(8,128)(2,1)S(1)}, u32[]{:S(2)}, u32[]{:S(2)}) collective-permute-start(bf16[64,1024]{1,0:T(8,128)(2,1)S(1)} %collective-permute-done.1.refs_1_), channel_id=1, source_target_pairs={{0,1},{1,0},{2,3},{3,2},{4,5},{5,4},{6,7},{7,6},{8,9},{9,8},{10,11... | collective-permute-start | bytes 393224 | tf_op jit(solution)/shard_map/ppermute | solution.py:225
  41.2 22.4 %collective-permute-start.16 = (bf16[64,1024]{1,0:T(8,128)(2,1)S(1)}, bf16[64,1024]{1,0:T(8,128)(2,1)S(1)}, u32[]{:S(2)}, u32[]{:S(2)}) collective-permute-start(bf16[64,1024]{1,0:T(8,128)(2,1)S(1)} %collective-permute-done.12.refs_0_), channel_id=1, source_target_pairs={{0,1},{1,0},{2,3},{3,2},{4,5},{5,4},{6,7},{7,6},{8,9},{9,8},{10,11... | collective-permute-start | bytes 393224 | tf_op jit(solution)/shard_map/ppermute | solution.py:225
  41.9 21.8 %collective-permute-start.19 = (bf16[64,1024]{1,0:T(8,128)(2,1)S(1)}, bf16[64,1024]{1,0:T(8,128)(2,1)S(1)}, u32[]{:S(2)}, u32[]{:S(2)}) collective-permute-start(bf16[64,1024]{1,0:T(8,128)(2,1)S(1)} %collective-permute-done.15.refs_3_), channel_id=1, source_target_pairs={{0,1},{1,0},{2,3},{3,2},{4,5},{5,4},{6,7},{7,6},{8,9},{9,8},{10,11... | collective-permute-start | bytes 393224 | tf_op jit(solution)/shard_map/ppermute | solution.py:225
  42.5 21.1 %collective-permute-start.18 = (bf16[64,1024]{1,0:T(8,128)(2,1)}, bf16[64,1024]{1,0:T(8,128)(2,1)S(1)}, u32[]{:S(2)}, u32[]{:S(2)}) collective-permute-start(bf16[64,1024]{1,0:T(8,128)(2,1)} %collective-permute-done.14.refs_2_), channel_id=1, source_target_pairs={{0,1},{1,0},{2,3},{3,2},{4,5},{5,4},{6,7},{7,6},{8,9},{9,8},{10,11... | collective-permute-start | bytes 393224 | tf_op jit(solution)/shard_map/ppermute | solution.py:225
  43.7 20.0 %collective-permute-start.17 = (bf16[64,1024]{1,0:T(8,128)(2,1)}, bf16[64,1024]{1,0:T(8,128)(2,1)S(1)}, u32[]{:S(2)}, u32[]{:S(2)}) collective-permute-start(bf16[64,1024]{1,0:T(8,128)(2,1)} %collective-permute-done.13.refs_1_), channel_id=1, source_target_pairs={{0,1},{1,0},{2,3},{3,2},{4,5},{5,4},{6,7},{7,6},{8,9},{9,8},{10,11... | collective-permute-start | bytes 393224 | tf_op jit(solution)/shard_map/ppermute | solution.py:225
  61.6 39.0 %collective-permute-start.22 = (bf16[4,160,384]{2,1,0:T(8,128)(2,1)}, bf16[4,160,384]{2,1,0:T(8,128)(2,1)S(1)}, u32[]{:S(2)}, u32[]{:S(2)}) collective-permute-start(bf16[4,160,384]{2,1,0:T(8,128)(2,1)} %shard_map.98), channel_id=1, source_target_pairs={{0,2},{2,0},{1,3},{3,1},{4,6},{6,4},{5,7},{7,5},{8,10},{10,8},{9,1... | collective-permute-start | bytes 1474568 | tf_op jit(solution)/shard_map/ppermute | solution.py:225
  63.6 27.3 %collective-permute-start.20 = (bf16[4,160,384]{2,1,0:T(8,128)(2,1)}, bf16[4,160,384]{2,1,0:T(8,128)(2,1)}, u32[]{:S(2)}, u32[]{:S(2)}) collective-permute-start(bf16[4,160,384]{2,1,0:T(8,128)(2,1)} %get-tuple-element.20), channel_id=1, source_target_pairs={{0,2},{2,0},{1,3},{3,1},{4,6},{6,4},{5,7},{7,5},{8,10},{10,8},{9,1... | collective-permute-start | bytes 1474568 | tf_op jit(solution)/shard_map/ppermute | solution.py:225
  75.7 15.1 %collective-permute-start.21 = (bf16[4,80,384]{2,1,0:T(8,128)(2,1)}, bf16[4,80,384]{2,1,0:T(8,128)(2,1)}, u32[]{:S(2)}, u32[]{:S(2)}) collective-permute-start(bf16[4,80,384]{2,1,0:T(8,128)(2,1)} %get-tuple-element.33), channel_id=1, source_target_pairs={{0,2},{2,0},{1,3},{3,1},{4,6},{6,4},{5,7},{7,5},{8,10},{10,8},{9,1... | collective-permute-start | bytes 737288 | tf_op jit(solution)/shard_map/ppermute | solution.py:225
  77.1 23.5 %collective-permute-start.23 = (bf16[4,80,384]{2,1,0:T(8,128)(2,1)}, bf16[4,80,384]{2,1,0:T(8,128)(2,1)S(1)}, u32[]{:S(2)}, u32[]{:S(2)}) collective-permute-start(bf16[4,80,384]{2,1,0:T(8,128)(2,1)} %get-tuple-element.34), channel_id=1, source_target_pairs={{0,2},{2,0},{1,3},{3,1},{4,6},{6,4},{5,7},{7,5},{8,10},{10,8},{9,1... | collective-permute-start | bytes 737288 | tf_op jit(solution)/shard_map/ppermute | solution.py:225
  99.4 11.1 %collective-permute-start.26 = (bf16[4,160,384]{2,1,0:T(8,128)(2,1)S(1)}, bf16[4,160,384]{2,1,0:T(8,128)(2,1)S(1)}, u32[]{:S(2)}, u32[]{:S(2)}) collective-permute-start(bf16[4,160,384]{2,1,0:T(8,128)(2,1)S(1)} %get-tuple-element.26), channel_id=1, source_target_pairs={{0,2},{2,0},{1,3},{3,1},{4,6},{6,4},{5,7},{7,5},{8,10},{10,8},{9,1... | collective-permute-start | bytes 1474568 | tf_op jit(solution)/shard_map/ppermute | solution.py:225
  109.1 11.8 %collective-permute-start.25 = (bf16[4,160,384]{2,1,0:T(8,128)(2,1)S(1)}, bf16[4,160,384]{2,1,0:T(8,128)(2,1)S(1)}, u32[]{:S(2)}, u32[]{:S(2)}) collective-permute-start(bf16[4,160,384]{2,1,0:T(8,128)(2,1)S(1)} %get-tuple-element.25), channel_id=1, source_target_pairs={{0,2},{2,0},{1,3},{3,1},{4,6},{6,4},{5,7},{7,5},{8,10},{10,8},{9,1... | collective-permute-start | bytes 1474568 | tf_op jit(solution)/shard_map/ppermute | solution.py:225
  131.6 9.0 %collective-permute-start.30 = (bf16[64,1024]{1,0:T(8,128)(2,1)S(1)}, bf16[64,1024]{1,0:T(8,128)(2,1)S(1)}, u32[]{:S(2)}, u32[]{:S(2)}) collective-permute-start(bf16[64,1024]{1,0:T(8,128)(2,1)S(1)} %get-tuple-element.31), channel_id=1, source_target_pairs={{0,4},{4,8},{8,12},{12,0},{1,5},{5,9},{9,13},{13,1},{2,6},{6,10},{... | collective-permute-start | bytes 393224 | tf_op jit(solution)/shard_map/ppermute | solution.py:228
  133.1 12.1 %collective-permute-start.29 = (bf16[64,1024]{1,0:T(8,128)(2,1)S(1)}, bf16[64,1024]{1,0:T(8,128)(2,1)S(1)}, u32[]{:S(2)}, u32[]{:S(2)}) collective-permute-start(bf16[64,1024]{1,0:T(8,128)(2,1)S(1)} %get-tuple-element.32), channel_id=1, source_target_pairs={{0,8},{4,12},{8,0},{12,4},{1,9},{5,13},{9,1},{13,5},{2,10},{6,14},... | collective-permute-start | bytes 393224 | tf_op jit(solution)/shard_map/ppermute | solution.py:228
  134.8 14.2 %collective-permute-start.24 = (f32[8,384]{1,0:T(8,128)S(1)}, f32[8,384]{1,0:T(8,128)S(1)}, u32[]{:S(2)}, u32[]{:S(2)}) collective-permute-start(f32[8,384]{1,0:T(8,128)S(1)} %bitcast.29), channel_id=1, source_target_pairs={{0,2},{2,0},{1,3},{3,1},{4,6},{6,4},{5,7},{7,5},{8,10},{10,8},{9,1... | collective-permute-start | bytes 36872 | tf_op jit(solution)/shard_map/ppermute | solution.py:225
  (18 other events, 85.9 us)

commit v2 on v0

v2 whole, which is shorter than its diff:
```python
import functools

import jax
import jax.numpy as jnp
from jax import lax
from jax.experimental import pallas as pl
from jax.experimental.pallas import tpu as pltpu
from jax.sharding import PartitionSpec as P

LOCAL_EXPERTS = 64
TOPK = 8
CAP = 10
F32 = jnp.float32
BF16 = jnp.bfloat16
NT = (((1,), (1,)), ((), ()))
TN = (((0,), (0,)), ((), ()))
VMEM_LIMIT = 40 * 1024 * 1024


def gathered(tokens, out_grad, gates, expert_ids, slots, gate_weight, up_weight, down_weight):
    expert_count = lax.axis_size("expert")
    group_count = lax.axis_size("dp")
    local_count = gate_weight.shape[0]
    tok_rows = tokens.shape[0]
    half_width = tokens.shape[1]
    slot_count = local_count * expert_count * CAP
    target_dev = expert_ids // local_count
    local_expert = expert_ids % local_count
    slot_rows = ((local_expert * expert_count + target_dev) * CAP + slots).reshape(-1)
    scaled = (gates[:, :, None] * out_grad[:, None, :].astype(F32)).astype(BF16)
    scaled = scaled.reshape(tok_rows * TOPK, half_width)
    repeated = jnp.repeat(tokens, TOPK, axis=0)

    def route(rows):
        send = jnp.zeros((slot_count, half_width), BF16).at[slot_rows].add(rows)
        send = send.reshape(local_count, expert_count, CAP, half_width)
        recv = lax.all_to_all(send, "expert", split_axis=1, concat_axis=1, tiled=True)
        full = lax.all_gather(recv, "sub", axis=3, tiled=True)
        return full.reshape(local_count, expert_count * CAP, full.shape[3])

    x_full, grad_full = route(repeated), route(scaled)
    gate_full = lax.all_gather(gate_weight, "dp", axis=1, tiled=True)
    up_full = lax.all_gather(up_weight, "dp", axis=1, tiled=True)
    down_full = lax.all_gather(down_weight, "dp", axis=2, tiled=True)
    gate_pre = jnp.einsum("erd,edf->erf", x_full, gate_full, preferred_element_type=F32)
    up_pre = jnp.einsum("erd,edf->erf", x_full, up_full, preferred_element_type=F32)
    hidden_grad = jnp.einsum("erd,efd->erf", grad_full, down_full, preferred_element_type=F32)
    gating = jax.nn.sigmoid(gate_pre)
    activated = gate_pre * gating
    channel = lax.psum(jnp.sum(activated * up_pre * hidden_grad, axis=1), "dp")
    scale = LOCAL_EXPERTS / (tok_rows * expert_count * group_count * TOPK)
    scores = channel * channel * scale
    gate_grad = (hidden_grad * up_pre * gating * (1.0 + gate_pre * (1.0 - gating))).astype(BF16)
    up_grad = (hidden_grad * activated).astype(BF16)
    parts = jnp.einsum("erf,edf->erd", gate_grad, gate_full, preferred_element_type=F32)
    parts = parts + jnp.einsum("erf,edf->erd", up_grad, up_full, preferred_element_type=F32)
    summed = lax.psum_scatter(parts.astype(BF16), "sub", scatter_dimension=2, tiled=True)
    summed = summed.reshape(local_count, expert_count, CAP, half_width)
    returned = lax.all_to_all(summed, "expert", split_axis=1, concat_axis=1, tiled=True)
    picked = returned.reshape(slot_count, half_width)[slot_rows].astype(F32)
    token_grad = jnp.sum(picked.reshape(tok_rows, TOPK, half_width), axis=1)
    return (scores, token_grad.astype(BF16))


ROUTE_ROWS = 16


def load(sources, first, count, buffers, sem):
    copies = []
    for j in range(count):
        line = []
        for n, (source, buffer) in enumerate(zip(sources, buffers)):
            copy = pltpu.make_async_copy(source.at[first + j], buffer.at[j], sem.at[j * len(sources) + n])
            copy.start()
            line.append(copy)
        copies.append(line)
    return copies


def ready(line):
    for copy in line:
        copy.wait()


def one_hot(rows, place):
    index = lax.broadcasted_iota(jnp.int32, (rows, place.shape[1]), 0).astype(F32)
    return jnp.where(index == place, 1.0, 0.0)


def fill(tok_ref, token_refs, side, tok, sem, meta_ref=None):
    copies = []
    zs = len(token_refs) // 2
    for n, ref in enumerate(token_refs):
        d, part = n % zs, side if n < zs else 1 - side
        start = pl.multiple_of(2 * d * tok + part * tok, tok)
        copies.append(pltpu.make_async_copy(ref.at[pl.ds(0, tok)], tok_ref.at[pl.ds(start, tok)], sem.at[n]))
        copies[-1].start()
    routes = []
    if meta_ref is not None:
        for n, ref in enumerate(token_refs):
            source = ref.at[pl.ds(tok, ROUTE_ROWS)]
            routes.append(pltpu.make_async_copy(source, meta_ref.at[n], sem.at[2 * zs + n]))
            routes[-1].start()
    return copies, routes


def dispatch(rows, experts, group, place_ref, tok_ref, hot_ref, out_ref, level_ref=None):
    def body(g, carry):
        levels = []
        for j in range(group):
            e = g * group + j
            hot = one_hot(rows, place_ref[pl.ds(e, 1), :])
            hot_ref[pl.ds(j * rows, rows), :] = hot.astype(BF16)
            if level_ref is not None:
                levels.append(jnp.sum(hot * level_ref[pl.ds(e, 1), :], axis=1, keepdims=True))
        got = jnp.dot(hot_ref[...], tok_ref[...], preferred_element_type=F32)
        if level_ref is not None:
            got = got * jnp.concatenate(levels, axis=0)
        out_ref[pl.ds(pl.multiple_of(g * group * rows, group * rows), group * rows), :] = got.astype(BF16)
        return carry

    lax.fori_loop(0, experts // group, body, 0)


def places(zs, tok, experts, meta_ref, place_ref, level_ref, first):
    lane = lax.broadcasted_iota(jnp.int32, (TOPK, 2 * tok), 1)
    rows, ids, levels = [], [], []
    for d in range(zs):
        meta = meta_ref[d].astype(F32) + meta_ref[zs + d].astype(F32)
        kinds = [meta[0:TOPK, 2 * tok * n : 2 * tok * (n + 1)] for n in range(5)]
        block = 2 * d + (lane >= tok).astype(jnp.int32)
        rows.append(kinds[1] + block.astype(F32) * CAP)
        ids.append(kinds[0])
        levels.append(kinds[2] + kinds[3] + kinds[4])
    row, expert, level = (jnp.concatenate(v, axis=1) for v in (rows, ids, levels))
    for e in range(experts):
        hit = expert == (first + e).astype(F32)
        place_ref[e : e + 1, :] = jnp.max(jnp.where(hit, row, -1.0), axis=0, keepdims=True)
        level_ref[e : e + 1, :] = jnp.sum(jnp.where(hit, level, 0.0), axis=0, keepdims=True)


def expert_rows(ref, rows, e):
    return ref[pl.ds(pl.multiple_of(e * rows, rows), rows), :]


def forward(rows, count, first, copies, xin_ref, bufs, out_ref):
    for j in range(count):
        x = expert_rows(xin_ref, rows, first + j)
        ready(copies[j])
        for n, buf in enumerate(bufs):
            got = jnp.dot(x, buf[j], preferred_element_type=F32)
            out_ref[j, n * rows : (n + 1) * rows, :] = got.astype(out_ref.dtype)


def x_kernel(cfg, count, s_ref, *refs):
    zs, tok, experts, rows, group = cfg
    tokens = refs[: 2 * zs]
    gate_ref, up_ref, au_ref, xin_ref, place_ref, level_ref = refs[2 * zs : 2 * zs + 6]
    tok_ref, hot_ref, meta_ref, gate, up, sem, tok_sem = refs[2 * zs + 6 :]
    filling, routes = fill(tok_ref, tokens, s_ref[1], tok, tok_sem, meta_ref)
    copies = load((gate_ref, up_ref), s_ref[0], count, (gate, up), sem)
    ready(routes)
    places(zs, tok, experts, meta_ref, place_ref, level_ref, s_ref[2])
    ready(filling)
    dispatch(rows, experts, group, place_ref, tok_ref, hot_ref, xin_ref)
    forward(rows, count, s_ref[0], copies, xin_ref, (gate, up), au_ref)


def x2_kernel(rows, count, s_ref, xin_ref, gate_ref, up_ref, au_ref, gate, up, sem):
    copies = load((gate_ref, up_ref), s_ref[0], count, (gate, up), sem)
    forward(rows, count, s_ref[0], copies, xin_ref, (gate, up), au_ref)


def back_dots(rows, count, first, copies, yin_ref, down, out_ref):
    for j in range(count):
        y = expert_rows(yin_ref, rows, first + j)
        ready(copies[j])
        out_ref[j] = lax.dot_general(y, down[j], NT, preferred_element_type=F32).astype(out_ref.dtype)


def y_kernel(cfg, count, s_ref, *refs):
    zs, tok, experts, rows, group = cfg
    tokens = refs[: 2 * zs]
    place_ref, level_ref, down_ref, dh_ref, yin_ref, tok_ref, hot_ref, down, sem, tok_sem = refs[2 * zs :]
    filling, _ = fill(tok_ref, tokens, s_ref[1], tok, tok_sem)
    copies = load((down_ref,), s_ref[0], count, (down,), sem)
    ready(filling)
    dispatch(rows, experts, group, place_ref, tok_ref, hot_ref, yin_ref, level_ref)
    back_dots(rows, count, s_ref[0], copies, yin_ref, down, dh_ref)


def y2_kernel(rows, count, s_ref, yin_ref, down_ref, dh_ref, down, sem):
    copies = load((down_ref,), s_ref[0], count, (down,), sem)
    back_dots(rows, count, s_ref[0], copies, yin_ref, down, dh_ref)


def final_kernel(rows, scale, at, au_index, dh_index, s_ref, *refs):
    aus, dhs = sorted({n for n, _ in au_index}), sorted({n for n, _ in dh_index})
    au_m, dh_m = refs[:2]
    au_r = dict(zip(aus, refs[2:]))
    dh_r = dict(zip(dhs, refs[2 + len(aus) :]))
    d_ref, score_ref = refs[2 + len(aus) + len(dhs) :]
    for j, ((na, ia), (nd, idx)) in enumerate(zip(au_index, dh_index)):
        au = au_m[at + j] + au_r[na][ia].astype(F32)
        a, u = au[0:rows], au[rows:]
        dh = dh_m[at + j] + dh_r[nd][idx].astype(F32)
        sig = jax.nn.sigmoid(a)
        act = a * sig
        channel = jnp.sum(act * u * dh, axis=0, keepdims=True)
        score_ref[j] = channel * channel * scale
        d_ref[j, 0:rows, :] = (dh * u * sig * (1.0 + a * (1.0 - sig))).astype(BF16)
        d_ref[j, rows:, :] = (dh * act).astype(BF16)


def gradient_rows(rows, d_refs, sizes, copies, gate, up, part_ref, at=0):
    j = 0
    for d_ref, size in zip(d_refs, sizes):
        for i in range(size):
            ready(copies[j])
            part = lax.dot_general(d_ref[i, 0:rows, :], gate[j], NT, preferred_element_type=F32)
            part = part + lax.dot_general(d_ref[i, rows:, :], up[j], NT, preferred_element_type=F32)
            start = at + j * rows
            part_ref[start : start + rows, :] = part.astype(BF16)
            j += 1


def mine_parts_kernel(rows, sizes, s_ref, *refs):
    n = len(sizes)
    gate_ref, up_ref, part_ref, gate, up, sem = refs[n:]
    copies = load((gate_ref, up_ref), s_ref[0], sum(sizes), (gate, up), sem)
    gradient_rows(rows, refs[:n], sizes, copies, gate, up, part_ref)


def early_kernel(rows, zs, tok, half, sizes, s_ref, *refs):
    n = len(sizes)
    count = sum(sizes)
    gate_ref, up_ref, place_ref, mine_ref, keep_ref, send_ref = refs[n : n + 6]
    gate, up, part_ref, hot_ref, acc, sem = refs[n + 6 :]
    first = s_ref[0]
    copies = load((gate_ref, up_ref), first, count, (gate, up), sem)
    start = half - first
    for j in range(half + count):
        e = start + j if j < half else first + j - half
        hot = one_hot(rows, place_ref[pl.ds(e, 1), :])
        hot_ref[j * rows : (j + 1) * rows, :] = hot.astype(BF16)
    cut = half * rows
    acc[...] = lax.dot_general(hot_ref[0:cut, :], mine_ref[...], TN, preferred_element_type=F32)
    gradient_rows(rows, refs[:n], sizes, copies, gate, up, part_ref)
    acc[...] += lax.dot_general(hot_ref[cut:, :], part_ref[...], TN, preferred_element_type=F32)
    side = s_ref[1]
    for d in range(zs):
        keep_ref[d] = acc[pl.ds(pl.multiple_of(2 * d * tok + side * tok, tok), tok), :]
        send_ref[d] = acc[pl.ds(pl.multiple_of(2 * d * tok + (1 - side) * tok, tok), tok), :].astype(BF16)


def late_kernel(rows, zs, pad, count, s_ref, d_ref, gate_ref, up_ref, keep_ref, send_ref, gate, up, part_ref, sem):
    copies = load((gate_ref, up_ref), s_ref[0], count, (gate, up), sem)
    gradient_rows(rows, [d_ref], [count], copies, gate, up, part_ref)
    shape = (zs * pad, count * rows)
    out = lax.broadcasted_iota(jnp.int32, shape, 0)
    source = lax.broadcasted_iota(jnp.int32, shape, 1)
    dist, place = out // pad, out % pad
    expert, slot = place // CAP, place % CAP
    for ref, side in ((keep_ref, s_ref[1]), (send_ref, 1 - s_ref[1])):
        want = expert * rows + (2 * dist + side) * CAP + slot
        want = jnp.where(expert < count, want, -1)
        move = jnp.where(want == source, 1.0, 0.0).astype(BF16)
        got = jnp.dot(move, part_ref[...], preferred_element_type=F32)
        for d in range(zs):
            ref[d] = got[d * pad : (d + 1) * pad].astype(ref.dtype)


def home_kernel(zs, pad, count, experts, s_ref, code_ref, *refs):
    early, late, (out_ref, late_ref) = refs[:zs], refs[zs : 2 * zs], refs[2 * zs :]
    tok = out_ref.shape[0]
    column = lax.broadcasted_iota(jnp.int32, (tok, zs * pad), 1)
    hot = jnp.zeros((tok, zs * pad), F32)
    for d in range(zs):
        late_ref[d * pad : (d + 1) * pad, :] = late[d][...]
        base = ((s_ref[2] + d) % zs * experts + s_ref[0]) * CAP
        for k in range(TOPK):
            at = code_ref[:, k : k + 1] - base
            at = jnp.where((at >= 0) & (at < count * CAP), at + d * pad, -1)
            hot = hot + jnp.where(at == column, 1.0, 0.0)
    total = jnp.dot(hot.astype(BF16), late_ref[...], preferred_element_type=F32)
    for ref in early:
        total = total + ref[...].astype(F32)
    out_ref[...] = total.astype(BF16)


def split(total, sizes):
    ends = [total * sum(sizes[: n + 1]) // sum(sizes) for n in range(len(sizes))]
    return [b - a for a, b in zip([0] + ends[:-1], ends) if b > a]


def locate(sizes, e):
    for n, size in enumerate(sizes):
        if e < size:
            return n, e
        e -= size


def stationary(tokens, out_grad, gates, expert_ids, slots, gate_weight, up_weight, down_weight):
    zs = lax.axis_size("expert")
    tok, width = tokens.shape
    experts, _, ff = gate_weight.shape
    rows = 2 * zs * CAP
    all_tok = 2 * zs * tok
    half = experts // 2
    group = 4 if experts % 4 == 0 else 1
    p, s, z = lax.axis_index("dp"), lax.axis_index("sub"), lax.axis_index("expert")
    mine0, other0 = half * p, half * (1 - p)
    au_sizes, dh_sizes, d_sizes = split(half, (1, 3)), split(half, (1, 1)), split(half, (2, 1, 1))

    def flip(v, axis):
        return lax.ppermute(v, axis, [(0, 1), (1, 0)])

    def turn(v, d):
        pairs = [
            ((i * 2 + a) * 2 + b, (((i + d) % zs) * 2 + b) * 2 + a)
            for i in range(zs)
            for a in range(2)
            for b in range(2)
        ]
        return lax.ppermute(v, ("expert", "dp", "sub"), pairs)

    levels, left = [], gates
    for _ in range(3):
        levels.append(lax.reduce_precision(left, 8, 7))
        left = left - levels[-1]
    kinds = jnp.stack([expert_ids.astype(F32), slots.astype(F32)] + levels).transpose(2, 0, 1)
    none = jnp.zeros_like(kinds)
    kinds = jnp.concatenate([jnp.where(p == 0, kinds, none), jnp.where(p == 0, none, kinds)], axis=2)
    kinds = kinds.reshape(TOPK, 10 * tok).astype(BF16)
    kinds = jnp.pad(kinds, ((0, ROUTE_ROWS - TOPK), (0, width - 10 * tok)))
    loaded = jnp.concatenate([tokens, kinds], axis=0)
    x_own = [turn(loaded, d) for d in range(zs)]
    x_other = [flip(v, "sub") for v in x_own]

    def sds(shape, dtype):
        return jax.ShapeDtypeStruct(shape, dtype)

    vmem, anywhere = pl.BlockSpec(memory_space=pltpu.VMEM), pl.BlockSpec(memory_space=pl.ANY)
    smem = pl.BlockSpec(memory_space=pltpu.SMEM)
    dma = pltpu.SemaphoreType.DMA

    def call(body, first, args, outs, scratch, flops, moved, name):
        ins = [spec for spec, group in args for _ in group]
        arrays = [v for _, group in args for v in group]
        info = jnp.stack([first, s, z * experts]).astype(jnp.int32)
        return pl.pallas_call(
            body,
            out_shape=outs,
            in_specs=[smem] + ins,
            out_specs=jax.tree.map(lambda _: vmem, outs),
            scratch_shapes=scratch,
            compiler_params=pltpu.CompilerParams(vmem_limit_bytes=VMEM_LIMIT),
            cost_estimate=pl.CostEstimate(flops=int(flops), bytes_accessed=int(moved), transcendentals=0),
            name=name,
        )(info, *arrays)

    wbytes = width * ff * 2
    flop = 2 * rows * width * ff
    dflop = 2 * experts * rows * all_tok * width
    cfg = (zs, tok, experts, rows, group)
    hot = pltpu.VMEM((group * rows, all_tok), BF16)
    tok_scratch = pltpu.VMEM((all_tok, width), BF16)

    def wide(count):
        return pltpu.VMEM((count, width, ff), BF16)

    def tall(count):
        return pltpu.VMEM((count, ff, width), BF16)

    place_shape = sds((experts, all_tok), F32)
    rows_shape = sds((experts * rows, width), BF16)
    n = au_sizes[0]
    au0, xin, place, level = call(
        functools.partial(x_kernel, cfg, n),
        other0,
        [(anywhere, (*x_own, *x_other, gate_weight, up_weight))],
        [sds((n, 2 * rows, ff), BF16), rows_shape, place_shape, place_shape],
        [tok_scratch, hot, pltpu.VMEM((2 * zs, ROUTE_ROWS, width), BF16), wide(n), wide(n)]
        + [dma((2 * n,)), dma((4 * zs,))],
        2 * n * flop + dflop,
        2 * n * wbytes,
        "x_first",
    )

    out_grad, au0 = lax.optimization_barrier((out_grad, au0))
    y_own = [turn(out_grad, d) for d in range(zs)]

    def x_call(first, n, dtype, name):
        return call(
            functools.partial(x2_kernel, rows, n),
            first,
            [(vmem, (xin,)), (anywhere, (gate_weight, up_weight))],
            sds((n, 2 * rows, ff), dtype),
            [wide(n), wide(n), dma((2 * n,))],
            2 * n * flop,
            2 * n * wbytes,
            name,
        )

    au_send = [au0]
    at = au_sizes[0]
    for n in au_sizes[1:]:
        au_send.append(x_call(other0 + at, n, BF16, "x_other"))
        at += n
    au_recv = [flip(v, "dp") for v in au_send]
    au_mine = x_call(mine0, half, F32, "x_mine")
    y_other = [flip(v, "sub") for v in y_own]
    n = dh_sizes[0]
    dh0, yin = call(
        functools.partial(y_kernel, cfg, n),
        other0,
        [(anywhere, (*y_own, *y_other)), (vmem, (place, level)), (anywhere, (down_weight,))],
        [sds((n, rows, ff), BF16), rows_shape],
        [tok_scratch, hot, tall(n), dma((n,)), dma((2 * zs,))],
        n * flop + dflop,
        n * wbytes,
        "y_first",
    )

    def y_call(first, n, dtype, name):
        return call(
            functools.partial(y2_kernel, rows, n),
            first,
            [(vmem, (yin,)), (anywhere, (down_weight,))],
            sds((n, rows, ff), dtype),
            [tall(n), dma((n,))],
            n * flop,
            n * wbytes,
            name,
        )

    dh_send, at = [dh0], n
    for n in dh_sizes[1:]:
        dh_send.append(y_call(other0 + at, n, BF16, "y_other"))
        at += n
    dh_recv = [flip(v, "dp") for v in dh_send]
    dh_mine = y_call(mine0, half, F32, "y_mine")
    scale = LOCAL_EXPERTS / (all_tok * TOPK)
    grads, back, scores, at = [], [], [], 0
    for n in d_sizes:
        au_index = [locate(au_sizes, e) for e in range(at, at + n)]
        dh_index = [locate(dh_sizes, e) for e in range(at, at + n)]
        aus = [au_recv[k] for k in sorted({k for k, _ in au_index})]
        dhs = [dh_recv[k] for k in sorted({k for k, _ in dh_index})]
        d, score = call(
            functools.partial(final_kernel, rows, scale, at, au_index, dh_index),
            mine0,
            [(vmem, (au_mine, dh_mine, *aus, *dhs))],
            [sds((n, 2 * rows, ff), BF16), sds((n, 1, ff), F32)],
            [],
            n * rows * ff * 40,
            n * rows * ff * 30,
            "final",
        )
        grads.append(d)
        scores.append(score)
        back.append(flip(d, "dp"))
        at += n

    score = jnp.concatenate(scores, axis=0).reshape(half, ff)
    score_other = flip(score, "dp")
    scores = jnp.concatenate(
        [jnp.where(p == 0, score, score_other), jnp.where(p == 0, score_other, score)], axis=0
    )
    weights = (anywhere, (gate_weight, up_weight))

    def parts_scratch(n):
        return [wide(n), wide(n), pltpu.VMEM((n * rows, width), BF16)]

    mine_parts = call(
        functools.partial(mine_parts_kernel, rows, d_sizes),
        mine0,
        [(vmem, grads), weights],
        sds((half * rows, width), BF16),
        parts_scratch(half)[:2] + [dma((2 * half,))],
        2 * half * flop,
        2 * half * wbytes,
        "mine_parts",
    )
    n_last = d_sizes[-1]
    n = half - n_last
    zshape = (zs, tok, width)
    keep, send = call(
        functools.partial(early_kernel, rows, zs, tok, half, d_sizes[:-1]),
        other0,
        [(vmem, back[:-1]), weights, (vmem, (place, mine_parts))],
        [sds(zshape, F32), sds(zshape, BF16)],
        parts_scratch(n)
        + [pltpu.VMEM(((half + n) * rows, all_tok), BF16), pltpu.VMEM((all_tok, width), F32), dma((2 * n,))],
        2 * n * flop + 2 * (half + n) * rows * width * all_tok,
        2 * n * wbytes,
        "early",
    )
    pad = -(-n_last * CAP // 16) * 16
    late_shape = (zs, pad, width)
    keep_late, send_late = call(
        functools.partial(late_kernel, rows, zs, pad, n_last),
        other0 + n,
        [(vmem, (back[-1],)), weights],
        [sds(late_shape, F32), sds(late_shape, BF16)],
        parts_scratch(n_last) + [dma((2 * n_last,))],
        2 * n_last * flop,
        2 * n_last * wbytes,
        "late",
    )

    def home(keep, send):
        summed = (keep + flip(send, "sub").astype(F32)).astype(BF16)
        return [turn(summed[d], -d) for d in range(zs)]

    early = home(keep, send)
    late = home(keep_late, send_late)
    info = jnp.stack([half * (1 - s) + n, s, z]).astype(jnp.int32)
    token_grad = pl.pallas_call(
        functools.partial(home_kernel, zs, pad, n_last, experts),
        out_shape=sds((tok, width), BF16),
        in_specs=[smem] + [vmem] * (1 + 2 * zs),
        out_specs=vmem,
        scratch_shapes=[pltpu.VMEM((zs * pad, width), BF16)],
        compiler_params=pltpu.CompilerParams(vmem_limit_bytes=VMEM_LIMIT),
        name="home",
    )(info, expert_ids * CAP + slots, *early, *late)
    return (scores, token_grad)


def solution(mesh):
    in_specs = (
        P(("dom", "expert", "dp"), "sub"),
        P(("dom", "expert", "dp"), "sub"),
        P(("dom", "expert", "dp"), None),
        P(("dom", "expert", "dp"), None),
        P(("dom", "expert", "dp"), None),
        P("expert", "dp", "sub"),
        P("expert", "dp", "sub"),
        P("expert", "sub", "dp"),
    )
    out_specs = (P(("dom", "expert"), "sub"), P(("dom", "expert", "dp"), "sub"))
    pairs = mesh.shape["dp"] == 2 and mesh.shape["sub"] == 2
    split = (LOCAL_EXPERTS // mesh.shape["expert"]) % 2 == 0
    local = stationary if pairs and split else gathered
    return jax.shard_map(local, mesh=mesh, in_specs=in_specs, out_specs=out_specs, check_vma=False)
```

time: 1090 us -> 155 us (0.14)
  waiting for transfers between devices: 880 us -> 31.9 us
  matrix products: 79.7 us -> 0 us
  blocking collectives: 76.3 us -> 0 us
  Pallas kernels: 0 us -> 53.8 us
  starting transfers between devices: 4.83 us -> 51.7 us
  between operations: 14.3 us -> 0.95 us
    all_gather x5 -> x0, waiting for transfers between devices: 844 us -> none  [the longest x1 295 us: local(): lax.all_gather(down_weight, 'dp', axis=2, tiled=True)]
    dot_general x5 -> x0, matrix products: 79.7 us -> none  [the longest x1 21.6 us: local(): jnp.einsum('erf,edf->erd', up_grad, up_full, preferred_element_type=jnp.f...]
    all_to_all x2 -> x0, blocking collectives: 69.4 us -> none  [the longest x1 35.8 us: local(): lax.all_to_all(x_send, 'expert', split_axis=1, concat_axis=1, tiled=True)]
    pallas_call x0 -> x13, Pallas kernels: none -> 53.8 us  [the longest x12 52 us: call(): pl.pallas_call(body, out_shape=outs, in_specs=[smem] + ins, out_specs=jax...]
    ppermute x0 -> x34, starting transfers between devices: none -> 51.7 us  [the longest x16 38 us: turn(): return lax.ppermute(v, ('expert', 'dp', 'sub'), pairs)]
    ppermute x0 -> x34, waiting for transfers between devices: none -> 31.9 us  [the longest x16 26.5 us: turn(): return lax.ppermute(v, ('expert', 'dp', 'sub'), pairs)]
    all_to_all x1 -> x0, waiting for transfers between devices: 23.4 us -> none  [local(): lax.all_to_all(summed.astype(jnp.bfloat16), 'expert', split_axis=1, conca...]
  transfers between devices with their start and end apart: 7 -> 34, of which waited for: 5 -> 9; matrix products, arithmetic and copies ran while one was open for 3% -> 1% of each run, Pallas kernels for 0% -> 26%
where the time goes in v2:
time: 155 us
  Pallas kernels  53.8 us (35%)
  starting transfers between devices  51.7 us (33%)
  waiting for transfers between devices  31.9 us (21%)
  local copies, waits for them, and re-layouts  10.8 us (7%)
  other arithmetic  5.76 us (4%)
    pallas_call x12, Pallas kernels, call(): pl.pallas_call(body, out_shape=outs, in_specs=[smem] + ins, out_specs=jax...  52 us
    ppermute x16, starting transfers between devices, turn(): return lax.ppermute(v, ('expert', 'dp', 'sub'), pairs)  38 us
    ppermute x16, waiting for transfers between devices, turn(): return lax.ppermute(v, ('expert', 'dp', 'sub'), pairs)  26.5 us
    ppermute x18, starting transfers between devices, flip(): return lax.ppermute(v, axis, [(0, 1), (1, 0)])  13.7 us
    unnamed x33, local copies, waits for them, and re-layouts  10.6 us
    ppermute x18, waiting for transfers between devices, flip(): return lax.ppermute(v, axis, [(0, 1), (1, 0)])  5.4 us
  transfers between devices with their start and end apart: 34, of which 9 were waited for; matrix products, arithmetic and copies ran while one was open for 1% of the time, Pallas kernels for 26%

profile of v2, /device:TPU:1, one launch (start us, length us, event | category | flops | bytes accessed | tf_op | source)
XLA Modules:
  0.0 155.0 jit_solution(10336048572882054202)
XLA Ops:
  5.1 4.5 %collective-permute-start = (bf16[80,1024]{1,0:T(8,128)(2,1)S(1)}, bf16[80,1024]{1,0:T(8,128)(2,1)S(1)}, u32[]{:S(2)}, u32[]{:S(2)}) collective-permute-start(bf16[80,1024]{1,0:T(8,128)(2,1)S(1)} %fusion.1), channel_id=1, source_target_pairs={{0,0},{1,2},{2,1},{3,3},{4,4},{5,6},{6,5},{7,7},{8,8},{9,10},{10,9... | collective-permute-start | bytes 491528 | tf_op jit(solution)/shard_map/ppermute | solution.py:325
  10.7 3.8 %collective-permute-start.2 = (bf16[80,1024]{1,0:T(8,128)(2,1)S(1)}, bf16[80,1024]{1,0:T(8,128)(2,1)S(1)}, u32[]{:S(2)}, u32[]{:S(2)}) collective-permute-start(bf16[80,1024]{1,0:T(8,128)(2,1)S(1)} %fusion.1), channel_id=1, source_target_pairs={{0,8},{1,10},{2,9},{3,11},{4,12},{5,14},{6,13},{7,15},{8,0},{9,2},... | collective-permute-start | bytes 491528 | tf_op jit(solution)/shard_map/ppermute | solution.py:325
  15.3 3.7 %collective-permute-done.1.refs_1_ = bf16[80,1024]{1,0:T(8,128)(2,1)S(1)} collective-permute-done((bf16[80,1024]{1,0:T(8,128)(2,1)S(1)}, bf16[80,1024]{1,0:T(8,128)(2,1)S(1)}, u32[]{:S(2)}, u32[]{:S(2)}) %collective-permute-start.1) | collective-permute-done | bytes 163872 | tf_op jit(solution)/shard_map/ppermute | solution.py:325
  19.0 3.6 %collective-permute-done.2.refs_2_ = bf16[80,1024]{1,0:T(8,128)(2,1)S(1)} collective-permute-done((bf16[80,1024]{1,0:T(8,128)(2,1)S(1)}, bf16[80,1024]{1,0:T(8,128)(2,1)S(1)}, u32[]{:S(2)}, u32[]{:S(2)}) %collective-permute-start.2) | collective-permute-done | bytes 163872 | tf_op jit(solution)/shard_map/ppermute | solution.py:325
  28.1 5.4 %x_first.1 = (bf16[2,160,384]{2,1,0:T(8,128)(2,1)S(1)}, bf16[1280,1024]{1,0:T(8,128)(2,1)S(1)}, f32[16,512]{1,0:T(8,128)S(1)}, f32[16,512]{1,0:T(8,128)S(1)}) custom-call(s32[3]{0:T(128)S(1)} %add_add_fusion.1.s_ref, bf16[80,1024]{1,0:T(8,128)(2,1)S(1)} %collective-permute-done.refs_0_, bf16[80,1024]{1,0:T(8,128)(2,1)S(1)} %collective-permute-done.1.refs_1_, ...), custom_call_target="tpu_custom_call" | custom-call | flops 1593835520 | bytes 3145728 | tf_op jit(solution)/shard_map/x_first/pallas_call | solution.py:351
  33.6 5.6 %x_other.1 = bf16[6,160,384]{2,1,0:T(8,128)(2,1)} custom-call(s32[3]{0:T(128)S(1)} %add_add_fusion.2.s_ref, bf16[1280,1024]{1,0:T(8,128)(2,1)S(1)} %get-tuple-element.20.xin_ref, bf16[16,1024,384]{2,1,0:T(8,128)(2,1)} %gate_ref.5, bf16[16,1024,384]{2,1,0:T(8,128)(2,1)} %up_ref.5), custom_call_target="tpu_custom_call" | custom-call | flops 754974720 | bytes 9437184 | tf_op jit(solution)/shard_map/x_other/pallas_call | solution.py:351
  43.1 4.5 %collective-permute-start.9 = (bf16[64,1024]{1,0:T(8,128)(2,1)S(1)}, bf16[64,1024]{1,0:T(8,128)(2,1)}, u32[]{:S(2)}, u32[]{:S(2)}) collective-permute-start(bf16[64,1024]{1,0:T(8,128)(2,1)S(1)} %copy-done.15), channel_id=1, source_target_pairs={{0,4},{1,6},{2,5},{3,7},{4,8},{5,10},{6,9},{7,11},{8,12},{9,14},{1... | collective-permute-start | bytes 393224 | tf_op jit(solution)/shard_map/ppermute | solution.py:325
  50.6 12.8 %collective-permute-done.8.refs_0_ = bf16[64,1024]{1,0:T(8,128)(2,1)S(1)} collective-permute-done((bf16[64,1024]{1,0:T(8,128)(2,1)S(1)}, bf16[64,1024]{1,0:T(8,128)(2,1)S(1)}, u32[]{:S(2)}, u32[]{:S(2)}) %collective-permute-start.8) | collective-permute-done | bytes 131104 | tf_op jit(solution)/shard_map/ppermute | solution.py:325
  67.4 6.9 %y_first.1 = (bf16[4,80,384]{2,1,0:T(8,128)(2,1)S(1)}, bf16[1280,1024]{1,0:T(8,128)(2,1)S(1)}) custom-call(s32[3]{0:T(128)S(1)} %copy-done.10, bf16[64,1024]{1,0:T(8,128)(2,1)S(1)} %collective-permute-done.8.refs_0_, bf16[64,1024]{1,0:T(8,128)(2,1)} %collective-permute-done.9.refs_1_, bf16[64,1024]{1,0:T(8,128)(2,1)} %collective-permute-done.10.refs_2_, ...), custom_call_target="tpu_custom_call" | custom-call | flops 1593835520 | bytes 3145728 | tf_op jit(solution)/shard_map/y_first/pallas_call | solution.py:351
  75.4 5.7 %x_mine.1.refs_0_ = f32[8,160,384]{2,1,0:T(8,128)S(1)} custom-call(s32[3]{0:T(128)S(1)} %add_add_fusion.s_ref, bf16[1280,1024]{1,0:T(8,128)(2,1)S(1)} %get-tuple-element.20.xin_ref, bf16[16,1024,384]{2,1,0:T(8,128)(2,1)} %gate_ref.5, bf16[16,1024,384]{2,1,0:T(8,128)(2,1)} %up_ref.5), custom_call_target="tpu_custom_call" | custom-call | flops 1006632960 | bytes 12582912 | tf_op jit(solution)/shard_map/x_mine/pallas_call | solution.py:351
  81.1 3.4 %y_other.1 = bf16[4,80,384]{2,1,0:T(8,128)(2,1)S(1)} custom-call(s32[3]{0:T(128)S(1)} %add_add_fusion.3.s_ref, bf16[1280,1024]{1,0:T(8,128)(2,1)S(1)} %get-tuple-element.25.yin_ref, bf16[16,384,1024]{2,1,0:T(8,128)(2,1)} %down_ref.3), custom_call_target="tpu_custom_call" | custom-call | flops 251658240 | bytes 3145728 | tf_op jit(solution)/shard_map/y_other/pallas_call | solution.py:351
  85.1 5.2 %y_mine.1.refs_1_ = f32[8,80,384]{2,1,0:T(8,128)S(1)} custom-call(s32[3]{0:T(128)S(1)} %add_add_fusion.s_ref, bf16[1280,1024]{1,0:T(8,128)(2,1)S(1)} %get-tuple-element.25.yin_ref, bf16[16,384,1024]{2,1,0:T(8,128)(2,1)} %down_ref.3), custom_call_target="tpu_custom_call" | custom-call | flops 503316480 | bytes 6291456 | tf_op jit(solution)/shard_map/y_mine/pallas_call | solution.py:351
  96.4 6.9 %mine_parts.1.refs_5_ = bf16[640,1024]{1,0:T(8,128)(2,1)S(1)} custom-call(s32[3]{0:T(128)S(1)} %copy-done.8, bf16[4,160,384]{2,1,0:T(8,128)(2,1)S(1)} %get-tuple-element.31.refs_0_, bf16[2,160,384]{2,1,0:T(8,128)(2,1)S(1)} %get-tuple-element.32.refs_1_, bf16[2,160,384]{2,1,0:T(8,128)(2,1)S(1)} %get-tuple-element.33.refs_2_, bf16[16,1024,384]{2,1,0:T(8,128)(2,1)} %gate_ref.5, ...), custom_call_target="tpu_custom_call" | custom-call | flops 1006632960 | bytes 12582912 | tf_op jit(solution)/shard_map/mine_parts/pallas_call | solution.py:351
  103.3 4.8 %collective-permute-done.28.d_ref = bf16[2,160,384]{2,1,0:T(8,128)(2,1)S(1)} collective-permute-done((bf16[2,160,384]{2,1,0:T(8,128)(2,1)S(1)}, bf16[2,160,384]{2,1,0:T(8,128)(2,1)S(1)}, u32[]{:S(2)}, u32[]{:S(2)}) %collective-permute-start.28) | collective-permute-done | bytes 245792 | tf_op jit(solution)/shard_map/ppermute | solution.py:316
  108.1 4.6 %copy-done = bf16[16,1024,384]{2,1,0:T(8,128)(2,1)S(1)} copy-done((bf16[16,1024,384]{2,1,0:T(8,128)(2,1)S(1)}, bf16[16,1024,384]{2,1,0:T(8,128)(2,1)}, u32[]{:S(2)}) %copy-start) | copy-done | bytes 12582936
  112.7 3.2 %late.1 = (f32[4,32,1024]{2,1,0:T(8,128)S(1)}, bf16[4,32,1024]{2,1,0:T(8,128)(2,1)S(1)}) custom-call(s32[3]{0:T(128)S(1)} %add_add_fusion.4.s_ref, bf16[2,160,384]{2,1,0:T(8,128)(2,1)S(1)} %collective-permute-done.28.d_ref, bf16[16,1024,384]{2,1,0:T(8,128)(2,1)S(1)} %copy-done, bf16[16,1024,384]{2,1,0:T(8,128)(2,1)} %up_ref.5), custom_call_target="tpu_custom_call" | custom-call | flops 251658240 | bytes 3145728 | tf_op jit(solution)/shard_map/late/pallas_call | solution.py:351
  116.0 4.0 %collective-permute-start.29 = (bf16[4,32,1024]{2,1,0:T(8,128)(2,1)S(1)}, bf16[4,32,1024]{2,1,0:T(8,128)(2,1)S(1)}, u32[]{:S(2)}, u32[]{:S(2)}) collective-permute-start(bf16[4,32,1024]{2,1,0:T(8,128)(2,1)S(1)} %get-tuple-element.37), channel_id=1, source_target_pairs={{0,1},{1,0},{2,3},{3,2},{4,5},{5,4},{6,7},{7,6},{8,9},{9,8},{10,11... | collective-permute-start | bytes 786440 | tf_op jit(solution)/shard_map/ppermute | solution.py:316
  120.0 7.1 %early.1 = (f32[4,64,1024]{2,1,0:T(8,128)S(1)}, bf16[4,64,1024]{2,1,0:T(8,128)(2,1)S(1)}) custom-call(s32[3]{0:T(128)S(1)} %copy-done.11, bf16[4,160,384]{2,1,0:T(8,128)(2,1)S(1)} %collective-permute-done.21.refs_0_, bf16[2,160,384]{2,1,0:T(8,128)(2,1)S(1)} %collective-permute-done.22.refs_1_, bf16[16,1024,384]{2,1,0:T(8,128)(2,1)} %gate_ref.5, ...), custom_call_target="tpu_custom_call" | custom-call | flops 1929379840 | bytes 9437184 | tf_op jit(solution)/shard_map/early/pallas_call | solution.py:351
  127.8 3.6 %collective-permute-start.30 = (bf16[32,1024]{1,0:T(8,128)(2,1)S(1)}, bf16[32,1024]{1,0:T(8,128)(2,1)S(1)}, u32[]{:S(2)}, u32[]{:S(2)}) collective-permute-start(bf16[32,1024]{1,0:T(8,128)(2,1)S(1)} %get-tuple-element.45), channel_id=1, source_target_pairs={{0,0},{1,2},{2,1},{3,3},{4,4},{5,6},{6,5},{7,7},{8,8},{9,10},{10,9... | collective-permute-start | bytes 196616 | tf_op jit(solution)/shard_map/ppermute | solution.py:325
  131.4 4.7 %collective-permute-start.31 = (bf16[32,1024]{1,0:T(8,128)(2,1)S(1)}, bf16[32,1024]{1,0:T(8,128)(2,1)S(1)}, u32[]{:S(2)}, u32[]{:S(2)}) collective-permute-start(bf16[32,1024]{1,0:T(8,128)(2,1)S(1)} %get-tuple-element.44), channel_id=1, source_target_pairs={{0,12},{1,14},{2,13},{3,15},{4,0},{5,2},{6,1},{7,3},{8,4},{9,6},{1... | collective-permute-start | bytes 196616 | tf_op jit(solution)/shard_map/ppermute | solution.py:325
  137.3 2.6 %collective-permute-start.24 = (bf16[64,1024]{1,0:T(8,128)(2,1)S(1)}, bf16[64,1024]{1,0:T(8,128)(2,1)S(1)}, u32[]{:S(2)}, u32[]{:S(2)}) collective-permute-start(bf16[64,1024]{1,0:T(8,128)(2,1)S(1)} %get-tuple-element.41), channel_id=1, source_target_pairs={{0,0},{1,2},{2,1},{3,3},{4,4},{5,6},{6,5},{7,7},{8,8},{9,10},{10,9... | collective-permute-start | bytes 393224 | tf_op jit(solution)/shard_map/ppermute | solution.py:325
  140.4 3.2 %collective-permute-start.26 = (bf16[64,1024]{1,0:T(8,128)(2,1)S(1)}, bf16[64,1024]{1,0:T(8,128)(2,1)S(1)}, u32[]{:S(2)}, u32[]{:S(2)}) collective-permute-start(bf16[64,1024]{1,0:T(8,128)(2,1)S(1)} %get-tuple-element.39), channel_id=1, source_target_pairs={{0,8},{1,10},{2,9},{3,11},{4,12},{5,14},{6,13},{7,15},{8,0},{9,2},... | collective-permute-start | bytes 393224 | tf_op jit(solution)/shard_map/ppermute | solution.py:325
  143.6 2.6 %collective-permute-start.27 = (bf16[64,1024]{1,0:T(8,128)(2,1)S(1)}, bf16[64,1024]{1,0:T(8,128)(2,1)S(1)}, u32[]{:S(2)}, u32[]{:S(2)}) collective-permute-start(bf16[64,1024]{1,0:T(8,128)(2,1)S(1)} %get-tuple-element.38), channel_id=1, source_target_pairs={{0,4},{1,6},{2,5},{3,7},{4,8},{5,10},{6,9},{7,11},{8,12},{9,14},{1... | collective-permute-start | bytes 393224 | tf_op jit(solution)/shard_map/ppermute | solution.py:325
  146.8 5.9 %collective-permute-done.33.refs_7_ = bf16[32,1024]{1,0:T(8,128)(2,1)S(1)} collective-permute-done((bf16[32,1024]{1,0:T(8,128)(2,1)S(1)}, bf16[32,1024]{1,0:T(8,128)(2,1)S(1)}, u32[]{:S(2)}, u32[]{:S(2)}) %collective-permute-start.33) | collective-permute-done | bytes 65568 | tf_op jit(solution)/shard_map/ppermute | solution.py:325
  (113 shorter events, 35.8 us)
Async XLA Ops:
  5.1 10.2 %collective-permute-start = (bf16[80,1024]{1,0:T(8,128)(2,1)S(1)}, bf16[80,1024]{1,0:T(8,128)(2,1)S(1)}, u32[]{:S(2)}, u32[]{:S(2)}) collective-permute-start(bf16[80,1024]{1,0:T(8,128)(2,1)S(1)} %fusion.1), channel_id=1, source_target_pairs={{0,0},{1,2},{2,1},{3,3},{4,4},{5,6},{6,5},{7,7},{8,8},{9,10},{10,9... | collective-permute-start | bytes 491528 | tf_op jit(solution)/shard_map/ppermute | solution.py:325
  9.6 9.4 %collective-permute-start.1 = (bf16[80,1024]{1,0:T(8,128)(2,1)S(1)}, bf16[80,1024]{1,0:T(8,128)(2,1)S(1)}, u32[]{:S(2)}, u32[]{:S(2)}) collective-permute-start(bf16[80,1024]{1,0:T(8,128)(2,1)S(1)} %fusion.1), channel_id=1, source_target_pairs={{0,4},{1,6},{2,5},{3,7},{4,8},{5,10},{6,9},{7,11},{8,12},{9,14},{1... | collective-permute-start | bytes 491528 | tf_op jit(solution)/shard_map/ppermute | solution.py:325
  10.7 11.9 %collective-permute-start.2 = (bf16[80,1024]{1,0:T(8,128)(2,1)S(1)}, bf16[80,1024]{1,0:T(8,128)(2,1)S(1)}, u32[]{:S(2)}, u32[]{:S(2)}) collective-permute-start(bf16[80,1024]{1,0:T(8,128)(2,1)S(1)} %fusion.1), channel_id=1, source_target_pairs={{0,8},{1,10},{2,9},{3,11},{4,12},{5,14},{6,13},{7,15},{8,0},{9,2},... | collective-permute-start | bytes 491528 | tf_op jit(solution)/shard_map/ppermute | solution.py:325
  14.5 8.4 %collective-permute-start.3 = (bf16[80,1024]{1,0:T(8,128)(2,1)S(1)}, bf16[80,1024]{1,0:T(8,128)(2,1)S(1)}, u32[]{:S(2)}, u32[]{:S(2)}) collective-permute-start(bf16[80,1024]{1,0:T(8,128)(2,1)S(1)} %fusion.1), channel_id=1, source_target_pairs={{0,12},{1,14},{2,13},{3,15},{4,0},{5,2},{6,1},{7,3},{8,4},{9,6},{1... | collective-permute-start | bytes 491528 | tf_op jit(solution)/shard_map/ppermute | solution.py:325
  39.2 51.1 %collective-permute-start.17 = (bf16[6,160,384]{2,1,0:T(8,128)(2,1)}, bf16[6,160,384]{2,1,0:T(8,128)(2,1)S(1)}, u32[]{:S(2)}, u32[]{:S(2)}) collective-permute-start(bf16[6,160,384]{2,1,0:T(8,128)(2,1)} %x_other.1), channel_id=1, source_target_pairs={{0,2},{2,0},{1,3},{3,1},{4,6},{6,4},{5,7},{7,5},{8,10},{10,8},{9,1... | collective-permute-start | bytes 2211848 | tf_op jit(solution)/shard_map/ppermute | solution.py:316
  40.8 22.6 %collective-permute-start.8 = (bf16[64,1024]{1,0:T(8,128)(2,1)S(1)}, bf16[64,1024]{1,0:T(8,128)(2,1)S(1)}, u32[]{:S(2)}, u32[]{:S(2)}) collective-permute-start(bf16[64,1024]{1,0:T(8,128)(2,1)S(1)} %copy-done.15), channel_id=1, source_target_pairs={{0,0},{1,2},{2,1},{3,3},{4,4},{5,6},{6,5},{7,7},{8,8},{9,10},{10,9... | collective-permute-start | bytes 393224 | tf_op jit(solution)/shard_map/ppermute | solution.py:325
  43.1 20.3 %collective-permute-start.9 = (bf16[64,1024]{1,0:T(8,128)(2,1)S(1)}, bf16[64,1024]{1,0:T(8,128)(2,1)}, u32[]{:S(2)}, u32[]{:S(2)}) collective-permute-start(bf16[64,1024]{1,0:T(8,128)(2,1)S(1)} %copy-done.15), channel_id=1, source_target_pairs={{0,4},{1,6},{2,5},{3,7},{4,8},{5,10},{6,9},{7,11},{8,12},{9,14},{1... | collective-permute-start | bytes 393224 | tf_op jit(solution)/shard_map/ppermute | solution.py:325
  47.6 16.3 %collective-permute-start.10 = (bf16[64,1024]{1,0:T(8,128)(2,1)S(1)}, bf16[64,1024]{1,0:T(8,128)(2,1)}, u32[]{:S(2)}, u32[]{:S(2)}) collective-permute-start(bf16[64,1024]{1,0:T(8,128)(2,1)S(1)} %copy-done.15), channel_id=1, source_target_pairs={{0,8},{1,10},{2,9},{3,11},{4,12},{5,14},{6,13},{7,15},{8,0},{9,2},... | collective-permute-start | bytes 393224 | tf_op jit(solution)/shard_map/ppermute | solution.py:325
  49.4 14.6 %collective-permute-start.11 = (bf16[64,1024]{1,0:T(8,128)(2,1)S(1)}, bf16[64,1024]{1,0:T(8,128)(2,1)}, u32[]{:S(2)}, u32[]{:S(2)}) collective-permute-start(bf16[64,1024]{1,0:T(8,128)(2,1)S(1)} %copy-done.15), channel_id=1, source_target_pairs={{0,12},{1,14},{2,13},{3,15},{4,0},{5,2},{6,1},{7,3},{8,4},{9,6},{1... | collective-permute-start | bytes 393224 | tf_op jit(solution)/shard_map/ppermute | solution.py:325
  65.0 25.3 %collective-permute-start.16 = (bf16[2,160,384]{2,1,0:T(8,128)(2,1)}, bf16[2,160,384]{2,1,0:T(8,128)(2,1)S(1)}, u32[]{:S(2)}, u32[]{:S(2)}) collective-permute-start(bf16[2,160,384]{2,1,0:T(8,128)(2,1)} %copy-done.12), channel_id=1, source_target_pairs={{0,2},{2,0},{1,3},{3,1},{4,6},{6,4},{5,7},{7,5},{8,10},{10,8},{9,1... | collective-permute-start | bytes 737288 | tf_op jit(solution)/shard_map/ppermute | solution.py:316
  74.3 16.0 %collective-permute-start.18 = (bf16[4,80,384]{2,1,0:T(8,128)(2,1)S(1)}, bf16[4,80,384]{2,1,0:T(8,128)(2,1)S(1)}, u32[]{:S(2)}, u32[]{:S(2)}) collective-permute-start(bf16[4,80,384]{2,1,0:T(8,128)(2,1)S(1)} %get-tuple-element.27), channel_id=1, source_target_pairs={{0,2},{2,0},{1,3},{3,1},{4,6},{6,4},{5,7},{7,5},{8,10},{10,8},{9,1... | collective-permute-start | bytes 737288 | tf_op jit(solution)/shard_map/ppermute | solution.py:316
  91.3 28.6 %collective-permute-start.21 = (bf16[4,160,384]{2,1,0:T(8,128)(2,1)S(1)}, bf16[4,160,384]{2,1,0:T(8,128)(2,1)S(1)}, u32[]{:S(2)}, u32[]{:S(2)}) collective-permute-start(bf16[4,160,384]{2,1,0:T(8,128)(2,1)S(1)} %get-tuple-element.31.refs_0_), channel_id=1, source_target_pairs={{0,2},{2,0},{1,3},{3,1},{4,6},{6,4},{5,7},{7,5},{8,10},{10,8},{9,1... | collective-permute-start | bytes 1474568 | tf_op jit(solution)/shard_map/ppermute | solution.py:316
  93.2 15.0 %collective-permute-start.28 = (bf16[2,160,384]{2,1,0:T(8,128)(2,1)S(1)}, bf16[2,160,384]{2,1,0:T(8,128)(2,1)S(1)}, u32[]{:S(2)}, u32[]{:S(2)}) collective-permute-start(bf16[2,160,384]{2,1,0:T(8,128)(2,1)S(1)} %get-tuple-element.33.refs_2_), channel_id=1, source_target_pairs={{0,2},{2,0},{1,3},{3,1},{4,6},{6,4},{5,7},{7,5},{8,10},{10,8},{9,1... | collective-permute-start | bytes 737288 | tf_op jit(solution)/shard_map/ppermute | solution.py:316
  94.5 25.5 %collective-permute-start.22 = (bf16[2,160,384]{2,1,0:T(8,128)(2,1)S(1)}, bf16[2,160,384]{2,1,0:T(8,128)(2,1)S(1)}, u32[]{:S(2)}, u32[]{:S(2)}) collective-permute-start(bf16[2,160,384]{2,1,0:T(8,128)(2,1)S(1)} %get-tuple-element.32.refs_1_), channel_id=1, source_target_pairs={{0,2},{2,0},{1,3},{3,1},{4,6},{6,4},{5,7},{7,5},{8,10},{10,8},{9,1... | collective-permute-start | bytes 737288 | tf_op jit(solution)/shard_map/ppermute | solution.py:316
  116.0 11.8 %collective-permute-start.29 = (bf16[4,32,1024]{2,1,0:T(8,128)(2,1)S(1)}, bf16[4,32,1024]{2,1,0:T(8,128)(2,1)S(1)}, u32[]{:S(2)}, u32[]{:S(2)}) collective-permute-start(bf16[4,32,1024]{2,1,0:T(8,128)(2,1)S(1)} %get-tuple-element.37), channel_id=1, source_target_pairs={{0,1},{1,0},{2,3},{3,2},{4,5},{5,4},{6,7},{7,6},{8,9},{9,8},{10,11... | collective-permute-start | bytes 786440 | tf_op jit(solution)/shard_map/ppermute | solution.py:316
  127.1 10.1 %collective-permute-start.23 = (bf16[4,64,1024]{2,1,0:T(8,128)(2,1)S(1)}, bf16[4,64,1024]{2,1,0:T(8,128)(2,1)S(1)}, u32[]{:S(2)}, u32[]{:S(2)}) collective-permute-start(bf16[4,64,1024]{2,1,0:T(8,128)(2,1)S(1)} %get-tuple-element.35), channel_id=1, source_target_pairs={{0,1},{1,0},{2,3},{3,2},{4,5},{5,4},{6,7},{7,6},{8,9},{9,8},{10,11... | collective-permute-start | bytes 1572872 | tf_op jit(solution)/shard_map/ppermute | solution.py:316
  127.2 12.7 %collective-permute-start.20 = (f32[8,384]{1,0:T(8,128)S(1)}, f32[8,384]{1,0:T(8,128)S(1)}, u32[]{:S(2)}, u32[]{:S(2)}) collective-permute-start(f32[8,384]{1,0:T(8,128)S(1)} %bitcast.54), channel_id=1, source_target_pairs={{0,2},{2,0},{1,3},{3,1},{4,6},{6,4},{5,7},{7,5},{8,10},{10,8},{9,1... | collective-permute-start | bytes 36872 | tf_op jit(solution)/shard_map/ppermute | solution.py:316
  127.8 12.6 %collective-permute-start.30 = (bf16[32,1024]{1,0:T(8,128)(2,1)S(1)}, bf16[32,1024]{1,0:T(8,128)(2,1)S(1)}, u32[]{:S(2)}, u32[]{:S(2)}) collective-permute-start(bf16[32,1024]{1,0:T(8,128)(2,1)S(1)} %get-tuple-element.45), channel_id=1, source_target_pairs={{0,0},{1,2},{2,1},{3,3},{4,4},{5,6},{6,5},{7,7},{8,8},{9,10},{10,9... | collective-permute-start | bytes 196616 | tf_op jit(solution)/shard_map/ppermute | solution.py:325
  131.4 12.2 %collective-permute-start.31 = (bf16[32,1024]{1,0:T(8,128)(2,1)S(1)}, bf16[32,1024]{1,0:T(8,128)(2,1)S(1)}, u32[]{:S(2)}, u32[]{:S(2)}) collective-permute-start(bf16[32,1024]{1,0:T(8,128)(2,1)S(1)} %get-tuple-element.44), channel_id=1, source_target_pairs={{0,12},{1,14},{2,13},{3,15},{4,0},{5,2},{6,1},{7,3},{8,4},{9,6},{1... | collective-permute-start | bytes 196616 | tf_op jit(solution)/shard_map/ppermute | solution.py:325
  136.1 10.1 %collective-permute-start.32 = (bf16[32,1024]{1,0:T(8,128)(2,1)S(1)}, bf16[32,1024]{1,0:T(8,128)(2,1)S(1)}, u32[]{:S(2)}, u32[]{:S(2)}) collective-permute-start(bf16[32,1024]{1,0:T(8,128)(2,1)S(1)} %get-tuple-element.43), channel_id=1, source_target_pairs={{0,8},{1,10},{2,9},{3,11},{4,12},{5,14},{6,13},{7,15},{8,0},{9,2},... | collective-permute-start | bytes 196616 | tf_op jit(solution)/shard_map/ppermute | solution.py:325
  137.3 15.4 %collective-permute-start.24 = (bf16[64,1024]{1,0:T(8,128)(2,1)S(1)}, bf16[64,1024]{1,0:T(8,128)(2,1)S(1)}, u32[]{:S(2)}, u32[]{:S(2)}) collective-permute-start(bf16[64,1024]{1,0:T(8,128)(2,1)S(1)} %get-tuple-element.41), channel_id=1, source_target_pairs={{0,0},{1,2},{2,1},{3,3},{4,4},{5,6},{6,5},{7,7},{8,8},{9,10},{10,9... | collective-permute-start | bytes 393224 | tf_op jit(solution)/shard_map/ppermute | solution.py:325
  139.9 12.8 %collective-permute-start.25 = (bf16[64,1024]{1,0:T(8,128)(2,1)S(1)}, bf16[64,1024]{1,0:T(8,128)(2,1)S(1)}, u32[]{:S(2)}, u32[]{:S(2)}) collective-permute-start(bf16[64,1024]{1,0:T(8,128)(2,1)S(1)} %get-tuple-element.40), channel_id=1, source_target_pairs={{0,12},{1,14},{2,13},{3,15},{4,0},{5,2},{6,1},{7,3},{8,4},{9,6},{1... | collective-permute-start | bytes 393224 | tf_op jit(solution)/shard_map/ppermute | solution.py:325
  140.4 12.8 %collective-permute-start.26 = (bf16[64,1024]{1,0:T(8,128)(2,1)S(1)}, bf16[64,1024]{1,0:T(8,128)(2,1)S(1)}, u32[]{:S(2)}, u32[]{:S(2)}) collective-permute-start(bf16[64,1024]{1,0:T(8,128)(2,1)S(1)} %get-tuple-element.39), channel_id=1, source_target_pairs={{0,8},{1,10},{2,9},{3,11},{4,12},{5,14},{6,13},{7,15},{8,0},{9,2},... | collective-permute-start | bytes 393224 | tf_op jit(solution)/shard_map/ppermute | solution.py:325
  143.6 9.6 %collective-permute-start.27 = (bf16[64,1024]{1,0:T(8,128)(2,1)S(1)}, bf16[64,1024]{1,0:T(8,128)(2,1)S(1)}, u32[]{:S(2)}, u32[]{:S(2)}) collective-permute-start(bf16[64,1024]{1,0:T(8,128)(2,1)S(1)} %get-tuple-element.38), channel_id=1, source_target_pairs={{0,4},{1,6},{2,5},{3,7},{4,8},{5,10},{6,9},{7,11},{8,12},{9,14},{1... | collective-permute-start | bytes 393224 | tf_op jit(solution)/shard_map/ppermute | solution.py:325
  (26 other events, 114.9 us)

commit v3 on v2

v3 whole, which is shorter than its diff:
```python
import functools

import jax
import jax.numpy as jnp
from jax import lax
from jax.experimental import pallas as pl
from jax.experimental.pallas import tpu as pltpu
from jax.sharding import PartitionSpec as P

LOCAL_EXPERTS = 64
TOPK = 8
CAP = 10
F32 = jnp.float32
BF16 = jnp.bfloat16
NT = (((1,), (1,)), ((), ()))
TN = (((0,), (0,)), ((), ()))
VMEM_LIMIT = 52 * 1024 * 1024


def gathered(tokens, out_grad, gates, expert_ids, slots, gate_weight, up_weight, down_weight):
    expert_count = lax.axis_size("expert")
    group_count = lax.axis_size("dp")
    local_count = gate_weight.shape[0]
    tok_rows = tokens.shape[0]
    half_width = tokens.shape[1]
    slot_count = local_count * expert_count * CAP
    target_dev = expert_ids // local_count
    local_expert = expert_ids % local_count
    slot_rows = ((local_expert * expert_count + target_dev) * CAP + slots).reshape(-1)
    scaled = (gates[:, :, None] * out_grad[:, None, :].astype(F32)).astype(BF16)
    scaled = scaled.reshape(tok_rows * TOPK, half_width)
    repeated = jnp.repeat(tokens, TOPK, axis=0)

    def route(rows):
        send = jnp.zeros((slot_count, half_width), BF16).at[slot_rows].add(rows)
        send = send.reshape(local_count, expert_count, CAP, half_width)
        recv = lax.all_to_all(send, "expert", split_axis=1, concat_axis=1, tiled=True)
        full = lax.all_gather(recv, "sub", axis=3, tiled=True)
        return full.reshape(local_count, expert_count * CAP, full.shape[3])

    x_full, grad_full = route(repeated), route(scaled)
    gate_full = lax.all_gather(gate_weight, "dp", axis=1, tiled=True)
    up_full = lax.all_gather(up_weight, "dp", axis=1, tiled=True)
    down_full = lax.all_gather(down_weight, "dp", axis=2, tiled=True)
    gate_pre = jnp.einsum("erd,edf->erf", x_full, gate_full, preferred_element_type=F32)
    up_pre = jnp.einsum("erd,edf->erf", x_full, up_full, preferred_element_type=F32)
    hidden_grad = jnp.einsum("erd,efd->erf", grad_full, down_full, preferred_element_type=F32)
    gating = jax.nn.sigmoid(gate_pre)
    activated = gate_pre * gating
    channel = lax.psum(jnp.sum(activated * up_pre * hidden_grad, axis=1), "dp")
    scale = LOCAL_EXPERTS / (tok_rows * expert_count * group_count * TOPK)
    scores = channel * channel * scale
    gate_grad = (hidden_grad * up_pre * gating * (1.0 + gate_pre * (1.0 - gating))).astype(BF16)
    up_grad = (hidden_grad * activated).astype(BF16)
    parts = jnp.einsum("erf,edf->erd", gate_grad, gate_full, preferred_element_type=F32)
    parts = parts + jnp.einsum("erf,edf->erd", up_grad, up_full, preferred_element_type=F32)
    summed = lax.psum_scatter(parts.astype(BF16), "sub", scatter_dimension=2, tiled=True)
    summed = summed.reshape(local_count, expert_count, CAP, half_width)
    returned = lax.all_to_all(summed, "expert", split_axis=1, concat_axis=1, tiled=True)
    picked = returned.reshape(slot_count, half_width)[slot_rows].astype(F32)
    token_grad = jnp.sum(picked.reshape(tok_rows, TOPK, half_width), axis=1)
    return (scores, token_grad.astype(BF16))


COST = 1.0


ROUTE_ROWS = 16


def each(count, body):
    def step(j, carry):
        body(j)
        return carry

    lax.fori_loop(0, count, step, 0)


def load(sources, first, count, buffers, sem):
    def copies(j):
        return [
            pltpu.make_async_copy(source.at[first + j], buffer.at[j], sem.at[j * len(sources) + n])
            for n, (source, buffer) in enumerate(zip(sources, buffers))
        ]

    def start(j):
        for copy in copies(j):
            copy.start()

    each(count, start)
    return lambda j: ready(copies(j))


def ready(line):
    for copy in line:
        copy.wait()


def one_hot(rows, place):
    index = lax.broadcasted_iota(jnp.int32, (rows, place.shape[1]), 0).astype(F32)
    return jnp.where(index == place, 1.0, 0.0)


def pack_kernel(p_ref, tokens_ref, ids_ref, slots_ref, gates_ref, out_ref):
    tok = tokens_ref.shape[0]
    out_ref[0:tok, :] = tokens_ref[...]
    out_ref[tok:, :] = jnp.zeros((ROUTE_ROWS, out_ref.shape[1]), BF16)
    lane = lax.broadcasted_iota(jnp.int32, (tok, 2 * tok), 1)
    row = lax.broadcasted_iota(jnp.int32, (tok, 2 * tok), 0) + p_ref[0] * tok
    place = jnp.where(lane == row, 1.0, 0.0).astype(BF16)
    left = gates_ref[...]
    kinds = [ids_ref[...].astype(F32), slots_ref[...].astype(F32)]
    for _ in range(3):
        kinds.append(left.astype(BF16).astype(F32))
        left = left - kinds[-1]
    kinds = jnp.concatenate(kinds, axis=0).astype(BF16)
    moved = jnp.dot(kinds, place, preferred_element_type=F32)
    none = jnp.zeros((ROUTE_ROWS - TOPK, 2 * tok), F32)
    for n in range(5):
        block = jnp.concatenate([moved[n * TOPK : (n + 1) * TOPK], none], axis=0)
        out_ref[tok:, 2 * tok * n : 2 * tok * (n + 1)] = block.astype(BF16)


def fill(tok_ref, token_refs, side, tok, sem, meta_ref=None):
    copies = []
    zs = len(token_refs) // 2
    for n, ref in enumerate(token_refs):
        d, part = n % zs, side if n < zs else 1 - side
        start = pl.multiple_of(2 * d * tok + part * tok, tok)
        copies.append(pltpu.make_async_copy(ref.at[pl.ds(0, tok)], tok_ref.at[pl.ds(start, tok)], sem.at[n]))
        copies[-1].start()
    routes = []
    if meta_ref is not None:
        for n, ref in enumerate(token_refs):
            source = ref.at[pl.ds(tok, ROUTE_ROWS)]
            routes.append(pltpu.make_async_copy(source, meta_ref.at[n], sem.at[2 * zs + n]))
            routes[-1].start()
    return copies, routes


def dispatch(rows, experts, group, place_ref, tok_ref, hot_ref, out_ref, level_ref=None):
    def body(g, carry):
        levels = []
        for j in range(group):
            e = g * group + j
            hot = one_hot(rows, place_ref[pl.ds(e, 1), :])
            hot_ref[pl.ds(j * rows, rows), :] = hot.astype(BF16)
            if level_ref is not None:
                levels.append(jnp.sum(hot * level_ref[pl.ds(e, 1), :], axis=1, keepdims=True))
        got = jnp.dot(hot_ref[...], tok_ref[...], preferred_element_type=F32)
        if level_ref is not None:
            got = got * jnp.concatenate(levels, axis=0)
        out_ref[pl.ds(pl.multiple_of(g * group * rows, group * rows), group * rows), :] = got.astype(BF16)
        return carry

    lax.fori_loop(0, experts // group, body, 0)


def places(zs, tok, experts, meta_ref, place_ref, level_ref, first):
    lane = lax.broadcasted_iota(jnp.int32, (TOPK, 2 * tok), 1)
    rows, ids, levels = [], [], []
    for d in range(zs):
        meta = meta_ref[d].astype(F32) + meta_ref[zs + d].astype(F32)
        kinds = [meta[0:TOPK, 2 * tok * n : 2 * tok * (n + 1)] for n in range(5)]
        block = 2 * d + (lane >= tok).astype(jnp.int32)
        rows.append(kinds[1] + block.astype(F32) * CAP)
        ids.append(kinds[0])
        levels.append(kinds[2] + kinds[3] + kinds[4])
    row, expert, level = (jnp.concatenate(v, axis=1) for v in (rows, ids, levels))
    for e in range(experts):
        hit = expert == (first + e).astype(F32)
        place_ref[e : e + 1, :] = jnp.max(jnp.where(hit, row, -1.0), axis=0, keepdims=True)
        level_ref[e : e + 1, :] = jnp.sum(jnp.where(hit, level, 0.0), axis=0, keepdims=True)


def expert_rows(ref, rows, e):
    return ref[pl.ds(pl.multiple_of(e * rows, rows), rows), :]


def at_rows(rows, j):
    return pl.ds(pl.multiple_of(j * rows, rows), rows)


def forward(rows, count, first, arrived, xin_ref, bufs, out_ref):
    def body(j):
        x = expert_rows(xin_ref, rows, first + j)
        arrived(j)
        for n, buf in enumerate(bufs):
            got = jnp.dot(x, buf[j], preferred_element_type=F32)
            out_ref[j, n * rows : (n + 1) * rows, :] = got.astype(out_ref.dtype)

    each(count, body)


def x_kernel(cfg, count, s_ref, *refs):
    zs, tok, experts, rows, group = cfg
    tokens = refs[: 2 * zs]
    gate_ref, up_ref, au_ref, xin_ref, place_ref, level_ref = refs[2 * zs : 2 * zs + 6]
    tok_ref, hot_ref, meta_ref, gate, up, sem, tok_sem = refs[2 * zs + 6 :]
    filling, routes = fill(tok_ref, tokens, s_ref[1], tok, tok_sem, meta_ref)
    copies = load((gate_ref, up_ref), s_ref[0], count, (gate, up), sem)
    ready(routes)
    places(zs, tok, experts, meta_ref, place_ref, level_ref, s_ref[2])
    ready(filling)
    dispatch(rows, experts, group, place_ref, tok_ref, hot_ref, xin_ref)
    forward(rows, count, s_ref[0], copies, xin_ref, (gate, up), au_ref)


def x2_kernel(rows, counts, s_ref, xin_ref, gate_ref, up_ref, au_ref, mine_ref, gate, up, gate_m, up_m, sem, sem_m):
    copies = load((gate_ref, up_ref), s_ref[0], counts[0], (gate, up), sem)
    copies_m = load((gate_ref, up_ref), s_ref[1], counts[1], (gate_m, up_m), sem_m)
    forward(rows, counts[0], s_ref[0], copies, xin_ref, (gate, up), au_ref)
    forward(rows, counts[1], s_ref[1], copies_m, xin_ref, (gate_m, up_m), mine_ref)


def back_dots(rows, count, first, arrived, yin_ref, down, out_ref):
    def body(j):
        y = expert_rows(yin_ref, rows, first + j)
        arrived(j)
        out_ref[j] = lax.dot_general(y, down[j], NT, preferred_element_type=F32).astype(out_ref.dtype)

    each(count, body)


def y_kernel(cfg, count, s_ref, *refs):
    zs, tok, experts, rows, group = cfg
    tokens = refs[: 2 * zs]
    place_ref, level_ref, down_ref, dh_ref, yin_ref, tok_ref, hot_ref, down, sem, tok_sem = refs[2 * zs :]
    filling, _ = fill(tok_ref, tokens, s_ref[1], tok, tok_sem)
    copies = load((down_ref,), s_ref[0], count, (down,), sem)
    ready(filling)
    dispatch(rows, experts, group, place_ref, tok_ref, hot_ref, yin_ref, level_ref)
    back_dots(rows, count, s_ref[0], copies, yin_ref, down, dh_ref)


def y2_kernel(rows, counts, s_ref, yin_ref, down_ref, dh_ref, mine_ref, down, down_m, sem, sem_m):
    copies = load((down_ref,), s_ref[0], counts[0], (down,), sem)
    copies_m = load((down_ref,), s_ref[1], counts[1], (down_m,), sem_m)
    back_dots(rows, counts[0], s_ref[0], copies, yin_ref, down, dh_ref)
    back_dots(rows, counts[1], s_ref[1], copies_m, yin_ref, down_m, mine_ref)


def final_kernel(rows, scale, at, s_ref, au_m, dh_m, au_r, dh_r, d_ref, score_ref):
    def body(j):
        au = au_m[at + j] + au_r[j].astype(F32)
        a, u = au[0:rows], au[rows:]
        dh = dh_m[at + j] + dh_r[j].astype(F32)
        sig = jax.nn.sigmoid(a)
        act = a * sig
        channel = jnp.sum(act * u * dh, axis=0, keepdims=True)
        score_ref[j] = channel * channel * scale
        d_ref[j, 0:rows, :] = (dh * u * sig * (1.0 + a * (1.0 - sig))).astype(BF16)
        d_ref[j, rows:, :] = (dh * act).astype(BF16)

    each(d_ref.shape[0], body)


def gradient_rows(rows, d_ref, arrived, gate, up, part_ref, at=0):
    def body(j):
        arrived(at + j)
        part = lax.dot_general(d_ref[j, 0:rows, :], gate[at + j], NT, preferred_element_type=F32)
        part = part + lax.dot_general(d_ref[j, rows:, :], up[at + j], NT, preferred_element_type=F32)
        part_ref[at_rows(rows, at + j), :] = part.astype(BF16)

    each(d_ref.shape[0], body)


def mine_parts_kernel(rows, sizes, s_ref, *refs):
    n = len(sizes)
    gate_ref, up_ref, part_ref, gate, up, sem = refs[n:]
    arrived = load((gate_ref, up_ref), s_ref[0], sum(sizes), (gate, up), sem)
    at = 0
    for d_ref, size in zip(refs[:n], sizes):
        gradient_rows(rows, d_ref, arrived, gate, up, part_ref, at)
        at += size


def combine_kernel(rows, zs, tok, half, at, count, s_ref, d_ref, gate_ref, up_ref, place_ref, *refs):
    first = s_ref[0] + at
    if at == 0:
        mine_ref, acc, gate, up, part_ref, hot_ref, sem = refs
    else:
        acc_in, keep_ref, send_ref, gate, up, part_ref, hot_ref, acc, sem = refs
    copies = load((gate_ref, up_ref), first, count, (gate, up), sem)

    def mark(start, e, n):
        def body(j):
            hot = one_hot(rows, place_ref[pl.ds(e + j, 1), :])
            hot_ref[at_rows(rows, start + j), :] = hot.astype(BF16)

        each(n, body)

    mark(half if at == 0 else 0, first, count)
    if at == 0:
        mark(0, half - s_ref[0], half)
    cut = half * rows if at == 0 else 0
    if at == 0:
        acc[...] = lax.dot_general(hot_ref[0:cut, :], mine_ref[...], TN, preferred_element_type=F32)
    gradient_rows(rows, d_ref, copies, gate, up, part_ref)
    total = lax.dot_general(hot_ref[cut:, :], part_ref[...], TN, preferred_element_type=F32)
    if at == 0:
        acc[...] += total
        return
    acc[...] = total + acc_in[...]
    side = s_ref[1]
    for d in range(zs):
        keep_ref[d] = acc[pl.ds(pl.multiple_of(2 * d * tok + side * tok, tok), tok), :]
        send_ref[d] = acc[pl.ds(pl.multiple_of(2 * d * tok + (1 - side) * tok, tok), tok), :].astype(BF16)


def stationary(tokens, out_grad, gates, expert_ids, slots, gate_weight, up_weight, down_weight):
    zs = lax.axis_size("expert")
    tok, width = tokens.shape
    experts, _, ff = gate_weight.shape
    rows = 2 * zs * CAP
    all_tok = 2 * zs * tok
    half = experts // 2
    group = 4 if experts % 4 == 0 else 1
    p, s, z = lax.axis_index("dp"), lax.axis_index("sub"), lax.axis_index("expert")
    mine0, other0 = half * p, half * (1 - p)
    first = half // 2
    rest = half - first
    sizes = [first, rest]

    def flip(v, axis):
        return lax.ppermute(v, axis, [(0, 1), (1, 0)])

    def turn(v, d):
        pairs = [
            ((i * 2 + a) * 2 + b, (((i + d) % zs) * 2 + b) * 2 + a)
            for i in range(zs)
            for a in range(2)
            for b in range(2)
        ]
        return lax.ppermute(v, ("expert", "dp", "sub"), pairs)

    def shift(v, d):
        return lax.ppermute(v, "expert", [(i, (i + d) % zs) for i in range(zs)])

    def sds(shape, dtype):
        return jax.ShapeDtypeStruct(shape, dtype)

    vmem, anywhere = pl.BlockSpec(memory_space=pltpu.VMEM), pl.BlockSpec(memory_space=pltpu.HBM)
    smem = pl.BlockSpec(memory_space=pltpu.SMEM)
    dma = pltpu.SemaphoreType.DMA

    def call(body, first, second, args, outs, scratch, flops, moved, name):
        ins = [spec for spec, group in args for _ in group]
        arrays = [v for _, group in args for v in group]
        info = jnp.stack([jnp.int32(first), jnp.int32(second), jnp.int32(z * experts)])
        return pl.pallas_call(
            body,
            out_shape=outs,
            in_specs=[smem] + ins,
            out_specs=jax.tree.map(lambda _: vmem, outs),
            scratch_shapes=scratch,
            compiler_params=pltpu.CompilerParams(vmem_limit_bytes=VMEM_LIMIT),
            cost_estimate=pl.CostEstimate(flops=int(flops * COST), bytes_accessed=int(moved * COST), transcendentals=0),
            name=name,
        )(info, *arrays)

    loaded = pl.pallas_call(
        pack_kernel,
        out_shape=sds((tok + ROUTE_ROWS, width), BF16),
        in_specs=[smem] + [vmem] * 4,
        out_specs=vmem,
        name="pack",
    )(jnp.stack([p]).astype(jnp.int32), tokens, expert_ids.T, slots.T, gates.T)
    x_own = [turn(loaded, d) for d in range(zs)]
    x_other = [flip(v, "sub") for v in x_own]
    out_grad, _ = lax.optimization_barrier((out_grad, loaded))
    y_here = turn(out_grad, 0)
    wbytes = width * ff * 2
    flop = 2 * rows * width * ff
    dflop = 2 * experts * rows * all_tok * width
    cfg = (zs, tok, experts, rows, group)
    hot = pltpu.VMEM((group * rows, all_tok), BF16)
    tok_scratch = pltpu.VMEM((all_tok, width), BF16)

    def wide(count):
        return pltpu.VMEM((count, width, ff), BF16)

    def tall(count):
        return pltpu.VMEM((count, ff, width), BF16)

    place_shape = sds((experts, all_tok), F32)
    rows_shape = sds((experts * rows, width), BF16)
    weights = (anywhere, (gate_weight, up_weight))
    au_first, xin, place, level = call(
        functools.partial(x_kernel, cfg, first),
        other0,
        s,
        [(anywhere, (*x_own, *x_other)), weights],
        [sds((first, 2 * rows, ff), BF16), rows_shape, place_shape, place_shape],
        [tok_scratch, hot, pltpu.VMEM((2 * zs, ROUTE_ROWS, width), BF16), wide(first), wide(first)]
        + [dma((2 * first,)), dma((4 * zs,))],
        2 * first * flop + dflop,
        2 * first * wbytes,
        "x_first",
    )
    y_here, au_first = lax.optimization_barrier((y_here, au_first))
    y_own = [y_here] + [shift(y_here, d) for d in range(1, zs)]
    au_rest, au_mine = call(
        functools.partial(x2_kernel, rows, (rest, half)),
        other0 + first,
        mine0,
        [(vmem, (xin,)), weights],
        [sds((rest, 2 * rows, ff), BF16), sds((half, 2 * rows, ff), F32)],
        [wide(rest), wide(rest), wide(half), wide(half), dma((2 * rest,)), dma((2 * half,))],
        2 * (rest + half) * flop,
        2 * (rest + half) * wbytes,
        "x_rest",
    )
    au_recv = [flip(v, "dp") for v in (au_first, au_rest)]
    *y_own, au_mine = lax.optimization_barrier((*y_own, au_mine))
    y_other = [flip(v, "sub") for v in y_own]
    dh_first, yin = call(
        functools.partial(y_kernel, cfg, first),
        other0,
        s,
        [(anywhere, (*y_own, *y_other)), (vmem, (place, level)), (anywhere, (down_weight,))],
        [sds((first, rows, ff), BF16), rows_shape],
        [tok_scratch, hot, tall(first), dma((first,)), dma((2 * zs,))],
        first * flop + dflop,
        first * wbytes,
        "y_first",
    )
    dh_rest, dh_mine = call(
        functools.partial(y2_kernel, rows, (rest, half)),
        other0 + first,
        mine0,
        [(vmem, (yin,)), (anywhere, (down_weight,))],
        [sds((rest, rows, ff), BF16), sds((half, rows, ff), F32)],
        [tall(rest), tall(half), dma((rest,)), dma((half,))],
        (rest + half) * flop,
        (rest + half) * wbytes,
        "y_rest",
    )
    dh_recv = [flip(v, "dp") for v in (dh_first, dh_rest)]
    scale = LOCAL_EXPERTS / (all_tok * TOPK)
    grads, back, scores = [], [], []
    for k, n in enumerate(sizes):
        d, score = call(
            functools.partial(final_kernel, rows, scale, k * first),
            mine0,
            s,
            [(vmem, (au_mine, dh_mine, au_recv[k], dh_recv[k]))],
            [sds((n, 2 * rows, ff), BF16), sds((n, 1, ff), F32)],
            [],
            n * rows * ff * 40,
            n * rows * ff * 30,
            "final",
        )
        dh_mine, d = lax.optimization_barrier((dh_mine, d))
        grads.append(d)
        scores.append(score)
        back.append(flip(d, "dp"))
    score = jnp.concatenate(scores, axis=0).reshape(half, ff)
    score_other = flip(score, "dp")
    scores = jnp.concatenate(
        [jnp.where(p == 0, score, score_other), jnp.where(p == 0, score_other, score)], axis=0
    )
    back[0], scores = lax.optimization_barrier((back[0], scores))
    mine_parts = call(
        functools.partial(mine_parts_kernel, rows, sizes),
        mine0,
        s,
        [(vmem, grads), weights],
        sds((half * rows, width), BF16),
        [wide(half), wide(half), dma((2 * half,))],
        2 * half * flop,
        2 * half * wbytes,
        "mine_parts",
    )
    acc_shape, zshape = (all_tok, width), (zs, tok, width)
    given = mine_parts
    for k, n in enumerate(sizes):
        used = n + half * (k == 0)
        given = call(
            functools.partial(combine_kernel, rows, zs, tok, half, k * first, n),
            other0,
            s,
            [(vmem, (back[k],)), weights, (vmem, (place, given))],
            sds(acc_shape, F32) if k == 0 else [sds(zshape, F32), sds(zshape, BF16)],
            [wide(n), wide(n), pltpu.VMEM((n * rows, width), BF16), pltpu.VMEM((used * rows, all_tok), BF16)]
            + ([] if k == 0 else [pltpu.VMEM(acc_shape, F32)])
            + [dma((2 * n,))],
            2 * n * flop + 2 * used * rows * width * all_tok,
            2 * n * wbytes,
            "combine",
        )
    keep, send = given
    summed = (keep + flip(send, "sub").astype(F32)).astype(BF16)
    total = turn(summed[0], 0).astype(F32)
    for d in range(1, zs):
        total = total + turn(summed[d], -d).astype(F32)
    return (scores, total.astype(BF16))


def solution(mesh):
    in_specs = (
        P(("dom", "expert", "dp"), "sub"),
        P(("dom", "expert", "dp"), "sub"),
        P(("dom", "expert", "dp"), None),
        P(("dom", "expert", "dp"), None),
        P(("dom", "expert", "dp"), None),
        P("expert", "dp", "sub"),
        P("expert", "dp", "sub"),
        P("expert", "sub", "dp"),
    )
    out_specs = (P(("dom", "expert"), "sub"), P(("dom", "expert", "dp"), "sub"))
    pairs = mesh.shape["dp"] == 2 and mesh.shape["sub"] == 2
    split = (LOCAL_EXPERTS // mesh.shape["expert"]) % 2 == 0
    local = stationary if pairs and split else gathered
    return jax.shard_map(local, mesh=mesh, in_specs=in_specs, out_specs=out_specs, check_vma=False)
```

time: 155 us -> 136 us (0.88)
  starting transfers between devices: 51.7 us -> 32.7 us
  local copies, waits for them, and re-layouts: 10.8 us -> 2.31 us
  Pallas kernels: 53.8 us -> 60.2 us
  waiting for transfers between devices: 31.9 us -> 35.7 us
  other arithmetic: 5.76 us -> 2.87 us
    ppermute x16 -> x9, starting transfers between devices: 38 us -> 19.3 us  [turn(): return lax.ppermute(v, ('expert', 'dp', 'sub'), pairs)]
    ppermute x18 -> x16, waiting for transfers between devices: 5.4 us -> 18.7 us  [flip(): return lax.ppermute(v, axis, [(0, 1), (1, 0)])]
    ppermute x16 -> x9, waiting for transfers between devices: 26.5 us -> 17 us  [turn(): return lax.ppermute(v, ('expert', 'dp', 'sub'), pairs)]
    unnamed x33 -> x5, local copies, waits for them, and re-layouts: 10.6 us -> 2.27 us
    pallas_call x12 -> x9, Pallas kernels: 52 us -> 58.5 us  [call(): pl.pallas_call(body, out_shape=outs, in_specs=[smem] + ins, out_specs=jax...]
    ppermute x18 -> x16, starting transfers between devices: 13.7 us -> 9.27 us  [flip(): return lax.ppermute(v, axis, [(0, 1), (1, 0)])]
    ppermute x0 -> x3, starting transfers between devices: none -> 4.1 us  [shift(): return lax.ppermute(v, 'expert', [(i, (i + d) % zs) for i in range(zs)])]
    unnamed x4 -> x0, other arithmetic: 2.78 us -> none
  transfers between devices with their start and end apart: 34 -> 28, of which waited for: 9 -> 9; matrix products, arithmetic and copies ran while one was open for 1% -> 1% of each run, Pallas kernels for 26% -> 36%
where the time goes in v3:
time: 136 us; the launch traced here: 135 us
  Pallas kernels  60.2 us (44%)
  waiting for transfers between devices  35.7 us (26%)
  starting transfers between devices  32.7 us (24%)
  other arithmetic  2.87 us (2%)
  local copies, waits for them, and re-layouts  2.31 us (2%)
    pallas_call x9, Pallas kernels, call(): pl.pallas_call(body, out_shape=outs, in_specs=[smem] + ins, out_specs=jax...  58.5 us
    ppermute x9, starting transfers between devices, turn(): return lax.ppermute(v, ('expert', 'dp', 'sub'), pairs)  19.3 us
    ppermute x16, waiting for transfers between devices, flip(): return lax.ppermute(v, axis, [(0, 1), (1, 0)])  18.7 us
    ppermute x9, waiting for transfers between devices, turn(): return lax.ppermute(v, ('expert', 'dp', 'sub'), pairs)  17 us
    ppermute x16, starting transfers between devices, flip(): return lax.ppermute(v, axis, [(0, 1), (1, 0)])  9.27 us
    ppermute x3, starting transfers between devices, shift(): return lax.ppermute(v, 'expert', [(i, (i + d) % zs) for i in range(zs)])  4.1 us
  transfers between devices with their start and end apart: 28, of which 9 were waited for; matrix products, arithmetic and copies ran while one was open for 1% of the time, Pallas kernels for 36%

profile of v3, /device:TPU:1, one launch (start us, length us, event | category | flops | bytes accessed | tf_op | source)
XLA Modules:
  0.0 134.6 jit_solution(2345817921816670692)
XLA Ops:
  0.6 1.7 %pack.1 = bf16[80,1024]{1,0:T(8,128)(2,1)} custom-call(s32[1]{0:T(128)} %bitcast.5.p_ref, bf16[64,1024]{1,0:T(8,128)(2,1)} %tokens_ref.1, s32[8,64]{1,0:T(8,128)} %bitcast.25, s32[8,64]{1,0:T(8,128)} %bitcast.26, f32[8,64]{1,0:T(8,128)} %bitcast.27), custom_call_target="tpu_custom_call" | custom-call | tf_op jit(solution)/shard_map/pack/pallas_call | solution.py:362
  2.3 5.6 %collective-permute-start.4 = (bf16[80,1024]{1,0:T(8,128)(2,1)}, bf16[80,1024]{1,0:T(8,128)(2,1)S(1)}, u32[]{:S(2)}, u32[]{:S(2)}) collective-permute-start(bf16[80,1024]{1,0:T(8,128)(2,1)} %pack.1), channel_id=1, source_target_pairs={{0,12},{1,14},{2,13},{3,15},{4,0},{5,2},{6,1},{7,3},{8,4},{9,6},{1... | collective-permute-start | bytes 491528 | tf_op jit(solution)/shard_map/ppermute | solution.py:335
  9.6 2.0 %collective-permute-start.1 = (bf16[80,1024]{1,0:T(8,128)(2,1)}, bf16[80,1024]{1,0:T(8,128)(2,1)S(1)}, u32[]{:S(2)}, u32[]{:S(2)}) collective-permute-start(bf16[80,1024]{1,0:T(8,128)(2,1)} %pack.1), channel_id=1, source_target_pairs={{0,0},{1,2},{2,1},{3,3},{4,4},{5,6},{6,5},{7,7},{8,8},{9,10},{10,9... | collective-permute-start | bytes 491528 | tf_op jit(solution)/shard_map/ppermute | solution.py:335
  12.3 9.5 %collective-permute-done.3.refs_2_ = bf16[80,1024]{1,0:T(8,128)(2,1)S(1)} collective-permute-done((bf16[80,1024]{1,0:T(8,128)(2,1)}, bf16[80,1024]{1,0:T(8,128)(2,1)S(1)}, u32[]{:S(2)}, u32[]{:S(2)}) %collective-permute-start.3) | collective-permute-done | bytes 163872 | tf_op jit(solution)/shard_map/ppermute | solution.py:335
  23.2 3.0 %collective-permute-start = (bf16[64,1024]{1,0:T(8,128)(2,1)}, bf16[64,1024]{1,0:T(8,128)(2,1)S(1)}, u32[]{:S(2)}, u32[]{:S(2)}) collective-permute-start(bf16[64,1024]{1,0:T(8,128)(2,1)} %param.9), channel_id=1, source_target_pairs={{0,0},{1,2},{2,1},{3,3},{4,4},{5,6},{6,5},{7,7},{8,8},{9,10},{10,9... | collective-permute-start | bytes 393224 | tf_op jit(solution)/shard_map/ppermute | solution.py:335
  26.3 7.4 %x_first.1 = (bf16[4,160,384]{2,1,0:T(8,128)(2,1)S(1)}, bf16[1280,1024]{1,0:T(8,128)(2,1)}, f32[16,512]{1,0:T(8,128)S(1)}, f32[16,512]{1,0:T(8,128)S(1)}) custom-call(s32[3]{0:T(128)S(1)} %get-tuple-element.67.s_ref, bf16[80,1024]{1,0:T(8,128)(2,1)S(1)} %collective-permute-done.1.refs_0_, bf16[80,1024]{1,0:T(8,128)(2,1)S(1)} %collective-permute-done.2.refs_1_, ...), custom_call_target="tpu_custom_call" | custom-call | flops 1845493760 | bytes 6291456 | tf_op jit(solution)/shard_map/x_first/pallas_call | solution.py:351
  33.9 2.6 %collective-permute-start.10 = (bf16[64,1024]{1,0:T(8,128)(2,1)S(1)}, bf16[64,1024]{1,0:T(8,128)(2,1)S(1)}, u32[]{:S(2)}, u32[]{:S(2)}) collective-permute-start(bf16[64,1024]{1,0:T(8,128)(2,1)S(1)} %collective-permute-done.refs_0_), channel_id=1, source_target_pairs={{0,8},{4,12},{8,0},{12,4},{1,9},{5,13},{9,1},{13,5},{2,10},{6,14},... | collective-permute-start | bytes 393224 | tf_op jit(solution)/shard_map/ppermute | solution.py:338
  37.9 10.1 %x_rest.1 = (bf16[4,160,384]{2,1,0:T(8,128)(2,1)S(1)}, f32[8,160,384]{2,1,0:T(8,128)}) custom-call(s32[3]{0:T(128)S(1)} %get-tuple-element.66.s_ref, bf16[1280,1024]{1,0:T(8,128)(2,1)} %get-tuple-element.34.xin_ref, bf16[16,1024,384]{2,1,0:T(8,128)(2,1)} %gate_ref.5, bf16[16,1024,384]{2,1,0:T(8,128)(2,1)} %up_ref.5), custom_call_target="tpu_custom_call" | custom-call | flops 1509949440 | bytes 18874368 | tf_op jit(solution)/shard_map/x_rest/pallas_call | solution.py:351
  50.6 7.1 %y_first.1 = (bf16[4,80,384]{2,1,0:T(8,128)(2,1)S(1)}, bf16[1280,1024]{1,0:T(8,128)(2,1)}) custom-call(s32[3]{0:T(128)S(1)} %get-tuple-element.67.s_ref, bf16[64,1024]{1,0:T(8,128)(2,1)S(1)} %collective-permute-done.refs_0_, bf16[64,1024]{1,0:T(8,128)(2,1)S(1)} %collective-permute-done.9.refs_1_, bf16[64,1024]{1,0:T(8,128)(2,1)S(1)} %collective-permute-done.10.refs_2_, ...), custom_call_target="tpu_custom_call" | custom-call | flops 1593835520 | bytes 3145728 | tf_op jit(solution)/shard_map/y_first/pallas_call | solution.py:351
  58.5 7.5 %y_rest.1 = (bf16[4,80,384]{2,1,0:T(8,128)(2,1)S(1)}, f32[8,80,384]{2,1,0:T(8,128)S(1)}) custom-call(s32[3]{0:T(128)S(1)} %get-tuple-element.66.s_ref, bf16[1280,1024]{1,0:T(8,128)(2,1)} %get-tuple-element.42.yin_ref, bf16[16,384,1024]{2,1,0:T(8,128)(2,1)} %down_ref.1), custom_call_target="tpu_custom_call" | custom-call | flops 754974720 | bytes 9437184 | tf_op jit(solution)/shard_map/y_rest/pallas_call | solution.py:351
  67.8 9.9 %collective-permute-done.17.dh_r = bf16[4,80,384]{2,1,0:T(8,128)(2,1)S(1)} collective-permute-done((bf16[4,80,384]{2,1,0:T(8,128)(2,1)S(1)}, bf16[4,80,384]{2,1,0:T(8,128)(2,1)S(1)}, u32[]{:S(2)}, u32[]{:S(2)}) %collective-permute-start.17) | collective-permute-done | bytes 245792 | tf_op jit(solution)/shard_map/ppermute | solution.py:326
  77.7 2.2 %final.2 = (bf16[4,160,384]{2,1,0:T(8,128)(2,1)S(1)}, f32[4,1,384]{2,1,0:T(1,128)S(1)}) custom-call(s32[3]{0:T(128)S(1)} %add_add_fusion.2.s_ref, f32[8,160,384]{2,1,0:T(8,128)} %get-tuple-element.44.au_m, f32[8,80,384]{2,1,0:T(8,128)} %copy-done.1, bf16[4,160,384]{2,1,0:T(8,128)(2,1)S(1)} %collective-permute-done.16.au_r, ...), custom_call_target="tpu_custom_call" | custom-call | flops 4915200 | bytes 3686400 | tf_op jit(solution)/shard_map/final/pallas_call | solution.py:351
  79.9 3.0 %collective-permute-done.20.dh_r = bf16[4,80,384]{2,1,0:T(8,128)(2,1)S(1)} collective-permute-done((bf16[4,80,384]{2,1,0:T(8,128)(2,1)S(1)}, bf16[4,80,384]{2,1,0:T(8,128)(2,1)S(1)}, u32[]{:S(2)}, u32[]{:S(2)}) %collective-permute-start.20) | collective-permute-done | bytes 245792 | tf_op jit(solution)/shard_map/ppermute | solution.py:326
  82.9 2.2 %final.3 = (bf16[4,160,384]{2,1,0:T(8,128)(2,1)S(1)}, f32[4,1,384]{2,1,0:T(1,128)S(1)}) custom-call(s32[3]{0:T(128)S(1)} %add_add_fusion.2.s_ref, f32[8,160,384]{2,1,0:T(8,128)} %get-tuple-element.44.au_m, f32[8,80,384]{2,1,0:T(8,128)} %copy-done.1, bf16[4,160,384]{2,1,0:T(8,128)(2,1)S(1)} %collective-permute-done.19.au_r, ...), custom_call_target="tpu_custom_call" | custom-call | flops 4915200 | bytes 3686400 | tf_op jit(solution)/shard_map/final/pallas_call | solution.py:351
  87.2 8.1 %mine_parts.1.refs_0_ = bf16[640,1024]{1,0:T(8,128)(2,1)} custom-call(s32[3]{0:T(128)S(1)} %add_add_fusion.2.s_ref, bf16[4,160,384]{2,1,0:T(8,128)(2,1)S(1)} %get-tuple-element.48.refs_0_, bf16[4,160,384]{2,1,0:T(8,128)(2,1)S(1)} %get-tuple-element.56.refs_1_, bf16[16,1024,384]{2,1,0:T(8,128)(2,1)} %gate_ref.5, bf16[16,1024,384]{2,1,0:T(8,128)(2,1)} %up_ref.5), custom_call_target="tpu_custom_call" | custom-call | flops 1006632960 | bytes 12582912 | tf_op jit(solution)/shard_map/mine_parts/pallas_call | solution.py:351
  95.2 2.2 %collective-permute-done.21 = f32[8,384]{1,0:T(8,128)S(1)} collective-permute-done((f32[8,384]{1,0:T(8,128)S(1)}, f32[8,384]{1,0:T(8,128)S(1)}, u32[]{:S(2)}, u32[]{:S(2)}) %collective-permute-start.21) | collective-permute-done | bytes 12320 | tf_op jit(solution)/shard_map/ppermute | solution.py:326
  99.3 6.5 %combine.2.refs_0_ = f32[512,1024]{1,0:T(8,128)} custom-call(s32[3]{0:T(128)S(1)} %get-tuple-element.67.s_ref, bf16[4,160,384]{2,1,0:T(8,128)(2,1)S(1)} %collective-permute-done.18.d_ref, bf16[16,1024,384]{2,1,0:T(8,128)(2,1)} %gate_ref.5, bf16[16,1024,384]{2,1,0:T(8,128)(2,1)} %up_ref.5, f32[16,512]{1,0:T(8,128)S(1)} %get-tuple-element.40.refs_8_.place_ref, ...), custom_call_target="tpu_custom_call" | custom-call | flops 1509949440 | bytes 6291456 | tf_op jit(solution)/shard_map/combine/pallas_call | solution.py:351
  105.9 2.1 %collective-permute-done.22.d_ref = bf16[4,160,384]{2,1,0:T(8,128)(2,1)S(1)} collective-permute-done((bf16[4,160,384]{2,1,0:T(8,128)(2,1)S(1)}, bf16[4,160,384]{2,1,0:T(8,128)(2,1)S(1)}, u32[]{:S(2)}, u32[]{:S(2)}) %collective-permute-start.22) | collective-permute-done | bytes 491552 | tf_op jit(solution)/shard_map/ppermute | solution.py:326
  107.9 7.3 %combine.3 = (f32[4,64,1024]{2,1,0:T(8,128)}, bf16[4,64,1024]{2,1,0:T(8,128)(2,1)S(1)}) custom-call(s32[3]{0:T(128)S(1)} %get-tuple-element.67.s_ref, bf16[4,160,384]{2,1,0:T(8,128)(2,1)S(1)} %collective-permute-done.22.d_ref, bf16[16,1024,384]{2,1,0:T(8,128)(2,1)} %gate_ref.5, bf16[16,1024,384]{2,1,0:T(8,128)(2,1)} %up_ref.5, ...), custom_call_target="tpu_custom_call" | custom-call | flops 838860800 | bytes 6291456 | tf_op jit(solution)/shard_map/combine/pallas_call | solution.py:351
  115.3 1.8 %collective-permute-start.23 = (bf16[4,64,1024]{2,1,0:T(8,128)(2,1)S(1)}, bf16[4,64,1024]{2,1,0:T(8,128)(2,1)S(1)}, u32[]{:S(2)}, u32[]{:S(2)}) collective-permute-start(bf16[4,64,1024]{2,1,0:T(8,128)(2,1)S(1)} %get-tuple-element.59), channel_id=1, source_target_pairs={{0,1},{1,0},{2,3},{3,2},{4,5},{5,4},{6,7},{7,6},{8,9},{9,8},{10,11... | collective-permute-start | bytes 1572872 | tf_op jit(solution)/shard_map/ppermute | solution.py:326
  120.0 2.5 %collective-permute-start.24 = (bf16[64,1024]{1,0:T(8,128)(2,1)S(1)}, bf16[64,1024]{1,0:T(8,128)(2,1)S(1)}, u32[]{:S(2)}, u32[]{:S(2)}) collective-permute-start(bf16[64,1024]{1,0:T(8,128)(2,1)S(1)} %get-tuple-element.60), channel_id=1, source_target_pairs={{0,0},{1,2},{2,1},{3,3},{4,4},{5,6},{6,5},{7,7},{8,8},{9,10},{10,9... | collective-permute-start | bytes 393224 | tf_op jit(solution)/shard_map/ppermute | solution.py:335
  123.4 2.2 %collective-permute-start.26 = (bf16[64,1024]{1,0:T(8,128)(2,1)S(1)}, bf16[64,1024]{1,0:T(8,128)(2,1)S(1)}, u32[]{:S(2)}, u32[]{:S(2)}) collective-permute-start(bf16[64,1024]{1,0:T(8,128)(2,1)S(1)} %get-tuple-element.62), channel_id=1, source_target_pairs={{0,8},{1,10},{2,9},{3,11},{4,12},{5,14},{6,13},{7,15},{8,0},{9,2},... | collective-permute-start | bytes 393224 | tf_op jit(solution)/shard_map/ppermute | solution.py:335
  127.1 3.6 %collective-permute-done.27 = bf16[64,1024]{1,0:T(8,128)(2,1)S(1)} collective-permute-done((bf16[64,1024]{1,0:T(8,128)(2,1)S(1)}, bf16[64,1024]{1,0:T(8,128)(2,1)S(1)}, u32[]{:S(2)}, u32[]{:S(2)}) %collective-permute-start.27) | collective-permute-done | bytes 131104 | tf_op jit(solution)/shard_map/ppermute | solution.py:335
  130.7 3.2 %collective-permute-done.26 = bf16[64,1024]{1,0:T(8,128)(2,1)S(1)} collective-permute-done((bf16[64,1024]{1,0:T(8,128)(2,1)S(1)}, bf16[64,1024]{1,0:T(8,128)(2,1)S(1)}, u32[]{:S(2)}, u32[]{:S(2)}) %collective-permute-start.26) | collective-permute-done | bytes 131104 | tf_op jit(solution)/shard_map/ppermute | solution.py:335
  (55 shorter events, 20.3 us)
Async XLA Ops:
  2.3 10.0 %collective-permute-start.4 = (bf16[80,1024]{1,0:T(8,128)(2,1)}, bf16[80,1024]{1,0:T(8,128)(2,1)S(1)}, u32[]{:S(2)}, u32[]{:S(2)}) collective-permute-start(bf16[80,1024]{1,0:T(8,128)(2,1)} %pack.1), channel_id=1, source_target_pairs={{0,12},{1,14},{2,13},{3,15},{4,0},{5,2},{6,1},{7,3},{8,4},{9,6},{1... | collective-permute-start | bytes 491528 | tf_op jit(solution)/shard_map/ppermute | solution.py:335
  8.0 13.8 %collective-permute-start.3 = (bf16[80,1024]{1,0:T(8,128)(2,1)}, bf16[80,1024]{1,0:T(8,128)(2,1)S(1)}, u32[]{:S(2)}, u32[]{:S(2)}) collective-permute-start(bf16[80,1024]{1,0:T(8,128)(2,1)} %pack.1), channel_id=1, source_target_pairs={{0,8},{1,10},{2,9},{3,11},{4,12},{5,14},{6,13},{7,15},{8,0},{9,2},... | collective-permute-start | bytes 491528 | tf_op jit(solution)/shard_map/ppermute | solution.py:335
  8.0 14.7 %collective-permute-start.2 = (bf16[80,1024]{1,0:T(8,128)(2,1)}, bf16[80,1024]{1,0:T(8,128)(2,1)S(1)}, u32[]{:S(2)}, u32[]{:S(2)}) collective-permute-start(bf16[80,1024]{1,0:T(8,128)(2,1)} %pack.1), channel_id=1, source_target_pairs={{0,4},{1,6},{2,5},{3,7},{4,8},{5,10},{6,9},{7,11},{8,12},{9,14},{1... | collective-permute-start | bytes 491528 | tf_op jit(solution)/shard_map/ppermute | solution.py:335
  9.6 13.1 %collective-permute-start.1 = (bf16[80,1024]{1,0:T(8,128)(2,1)}, bf16[80,1024]{1,0:T(8,128)(2,1)S(1)}, u32[]{:S(2)}, u32[]{:S(2)}) collective-permute-start(bf16[80,1024]{1,0:T(8,128)(2,1)} %pack.1), channel_id=1, source_target_pairs={{0,0},{1,2},{2,1},{3,3},{4,4},{5,6},{6,5},{7,7},{8,8},{9,10},{10,9... | collective-permute-start | bytes 491528 | tf_op jit(solution)/shard_map/ppermute | solution.py:335
  12.3 14.0 %collective-permute-start.8 = (bf16[80,1024]{1,0:T(8,128)(2,1)S(1)}, bf16[80,1024]{1,0:T(8,128)(2,1)S(1)}, u32[]{:S(2)}, u32[]{:S(2)}) collective-permute-start(bf16[80,1024]{1,0:T(8,128)(2,1)S(1)} %collective-permute-done.4.refs_3_), channel_id=1, source_target_pairs={{0,1},{1,0},{2,3},{3,2},{4,5},{5,4},{6,7},{7,6},{8,9},{9,8},{10,11... | collective-permute-start | bytes 491528 | tf_op jit(solution)/shard_map/ppermute | solution.py:326
  21.8 4.5 %collective-permute-start.7 = (bf16[80,1024]{1,0:T(8,128)(2,1)S(1)}, bf16[80,1024]{1,0:T(8,128)(2,1)S(1)}, u32[]{:S(2)}, u32[]{:S(2)}) collective-permute-start(bf16[80,1024]{1,0:T(8,128)(2,1)S(1)} %collective-permute-done.3.refs_2_), channel_id=1, source_target_pairs={{0,1},{1,0},{2,3},{3,2},{4,5},{5,4},{6,7},{7,6},{8,9},{9,8},{10,11... | collective-permute-start | bytes 491528 | tf_op jit(solution)/shard_map/ppermute | solution.py:326
  22.7 3.6 %collective-permute-start.6 = (bf16[80,1024]{1,0:T(8,128)(2,1)S(1)}, bf16[80,1024]{1,0:T(8,128)(2,1)S(1)}, u32[]{:S(2)}, u32[]{:S(2)}) collective-permute-start(bf16[80,1024]{1,0:T(8,128)(2,1)S(1)} %collective-permute-done.2.refs_1_), channel_id=1, source_target_pairs={{0,1},{1,0},{2,3},{3,2},{4,5},{5,4},{6,7},{7,6},{8,9},{9,8},{10,11... | collective-permute-start | bytes 491528 | tf_op jit(solution)/shard_map/ppermute | solution.py:326
  22.7 3.6 %collective-permute-start.5 = (bf16[80,1024]{1,0:T(8,128)(2,1)S(1)}, bf16[80,1024]{1,0:T(8,128)(2,1)S(1)}, u32[]{:S(2)}, u32[]{:S(2)}) collective-permute-start(bf16[80,1024]{1,0:T(8,128)(2,1)S(1)} %collective-permute-done.1.refs_0_), channel_id=1, source_target_pairs={{0,1},{1,0},{2,3},{3,2},{4,5},{5,4},{6,7},{7,6},{8,9},{9,8},{10,11... | collective-permute-start | bytes 491528 | tf_op jit(solution)/shard_map/ppermute | solution.py:326
  23.2 10.5 %collective-permute-start = (bf16[64,1024]{1,0:T(8,128)(2,1)}, bf16[64,1024]{1,0:T(8,128)(2,1)S(1)}, u32[]{:S(2)}, u32[]{:S(2)}) collective-permute-start(bf16[64,1024]{1,0:T(8,128)(2,1)} %param.9), channel_id=1, source_target_pairs={{0,0},{1,2},{2,1},{3,3},{4,4},{5,6},{6,5},{7,7},{8,8},{9,10},{10,9... | collective-permute-start | bytes 393224 | tf_op jit(solution)/shard_map/ppermute | solution.py:335
  33.8 14.2 %collective-permute-start.11 = (bf16[64,1024]{1,0:T(8,128)(2,1)S(1)}, bf16[64,1024]{1,0:T(8,128)(2,1)S(1)}, u32[]{:S(2)}, u32[]{:S(2)}) collective-permute-start(bf16[64,1024]{1,0:T(8,128)(2,1)S(1)} %collective-permute-done.refs_0_), channel_id=1, source_target_pairs={{0,12},{4,0},{8,4},{12,8},{1,13},{5,1},{9,5},{13,9},{2,14},{6,2},{... | collective-permute-start | bytes 393224 | tf_op jit(solution)/shard_map/ppermute | solution.py:338
  33.9 14.1 %collective-permute-start.10 = (bf16[64,1024]{1,0:T(8,128)(2,1)S(1)}, bf16[64,1024]{1,0:T(8,128)(2,1)S(1)}, u32[]{:S(2)}, u32[]{:S(2)}) collective-permute-start(bf16[64,1024]{1,0:T(8,128)(2,1)S(1)} %collective-permute-done.refs_0_), channel_id=1, source_target_pairs={{0,8},{4,12},{8,0},{12,4},{1,9},{5,13},{9,1},{13,5},{2,10},{6,14},... | collective-permute-start | bytes 393224 | tf_op jit(solution)/shard_map/ppermute | solution.py:338
  36.5 11.5 %collective-permute-start.9 = (bf16[64,1024]{1,0:T(8,128)(2,1)S(1)}, bf16[64,1024]{1,0:T(8,128)(2,1)S(1)}, u32[]{:S(2)}, u32[]{:S(2)}) collective-permute-start(bf16[64,1024]{1,0:T(8,128)(2,1)S(1)} %collective-permute-done.refs_0_), channel_id=1, source_target_pairs={{0,4},{4,8},{8,12},{12,0},{1,5},{5,9},{9,13},{13,1},{2,6},{6,10},{... | collective-permute-start | bytes 393224 | tf_op jit(solution)/shard_map/ppermute | solution.py:338
  49.1 18.7 %collective-permute-start.16 = (bf16[4,160,384]{2,1,0:T(8,128)(2,1)S(1)}, bf16[4,160,384]{2,1,0:T(8,128)(2,1)S(1)}, u32[]{:S(2)}, u32[]{:S(2)}) collective-permute-start(bf16[4,160,384]{2,1,0:T(8,128)(2,1)S(1)} %get-tuple-element.45), channel_id=1, source_target_pairs={{0,2},{2,0},{1,3},{3,1},{4,6},{6,4},{5,7},{7,5},{8,10},{10,8},{9,1... | collective-permute-start | bytes 1474568 | tf_op jit(solution)/shard_map/ppermute | solution.py:326
  49.9 30.1 %collective-permute-start.19 = (bf16[4,160,384]{2,1,0:T(8,128)(2,1)S(1)}, bf16[4,160,384]{2,1,0:T(8,128)(2,1)S(1)}, u32[]{:S(2)}, u32[]{:S(2)}) collective-permute-start(bf16[4,160,384]{2,1,0:T(8,128)(2,1)S(1)} %get-tuple-element.51), channel_id=1, source_target_pairs={{0,2},{2,0},{1,3},{3,1},{4,6},{6,4},{5,7},{7,5},{8,10},{10,8},{9,1... | collective-permute-start | bytes 1474568 | tf_op jit(solution)/shard_map/ppermute | solution.py:326
  57.6 20.0 %collective-permute-start.17 = (bf16[4,80,384]{2,1,0:T(8,128)(2,1)S(1)}, bf16[4,80,384]{2,1,0:T(8,128)(2,1)S(1)}, u32[]{:S(2)}, u32[]{:S(2)}) collective-permute-start(bf16[4,80,384]{2,1,0:T(8,128)(2,1)S(1)} %get-tuple-element.46), channel_id=1, source_target_pairs={{0,2},{2,0},{1,3},{3,1},{4,6},{6,4},{5,7},{7,5},{8,10},{10,8},{9,1... | collective-permute-start | bytes 737288 | tf_op jit(solution)/shard_map/ppermute | solution.py:326
  67.0 15.9 %collective-permute-start.20 = (bf16[4,80,384]{2,1,0:T(8,128)(2,1)S(1)}, bf16[4,80,384]{2,1,0:T(8,128)(2,1)S(1)}, u32[]{:S(2)}, u32[]{:S(2)}) collective-permute-start(bf16[4,80,384]{2,1,0:T(8,128)(2,1)S(1)} %get-tuple-element.52), channel_id=1, source_target_pairs={{0,2},{2,0},{1,3},{3,1},{4,6},{6,4},{5,7},{7,5},{8,10},{10,8},{9,1... | collective-permute-start | bytes 737288 | tf_op jit(solution)/shard_map/ppermute | solution.py:326
  85.2 12.8 %collective-permute-start.18 = (bf16[4,160,384]{2,1,0:T(8,128)(2,1)S(1)}, bf16[4,160,384]{2,1,0:T(8,128)(2,1)S(1)}, u32[]{:S(2)}, u32[]{:S(2)}) collective-permute-start(bf16[4,160,384]{2,1,0:T(8,128)(2,1)S(1)} %get-tuple-element.48.refs_0_), channel_id=1, source_target_pairs={{0,2},{2,0},{1,3},{3,1},{4,6},{6,4},{5,7},{7,5},{8,10},{10,8},{9,1... | collective-permute-start | bytes 1474568 | tf_op jit(solution)/shard_map/ppermute | solution.py:326
  85.6 11.8 %collective-permute-start.21 = (f32[8,384]{1,0:T(8,128)S(1)}, f32[8,384]{1,0:T(8,128)S(1)}, u32[]{:S(2)}, u32[]{:S(2)}) collective-permute-start(f32[8,384]{1,0:T(8,128)S(1)} %bitcast.24), channel_id=1, source_target_pairs={{0,2},{2,0},{1,3},{3,1},{4,6},{6,4},{5,7},{7,5},{8,10},{10,8},{9,1... | collective-permute-start | bytes 36872 | tf_op jit(solution)/shard_map/ppermute | solution.py:326
  86.8 21.1 %collective-permute-start.22 = (bf16[4,160,384]{2,1,0:T(8,128)(2,1)S(1)}, bf16[4,160,384]{2,1,0:T(8,128)(2,1)S(1)}, u32[]{:S(2)}, u32[]{:S(2)}) collective-permute-start(bf16[4,160,384]{2,1,0:T(8,128)(2,1)S(1)} %get-tuple-element.56.refs_1_), channel_id=1, source_target_pairs={{0,2},{2,0},{1,3},{3,1},{4,6},{6,4},{5,7},{7,5},{8,10},{10,8},{9,1... | collective-permute-start | bytes 1474568 | tf_op jit(solution)/shard_map/ppermute | solution.py:326
  115.3 3.4 %collective-permute-start.23 = (bf16[4,64,1024]{2,1,0:T(8,128)(2,1)S(1)}, bf16[4,64,1024]{2,1,0:T(8,128)(2,1)S(1)}, u32[]{:S(2)}, u32[]{:S(2)}) collective-permute-start(bf16[4,64,1024]{2,1,0:T(8,128)(2,1)S(1)} %get-tuple-element.59), channel_id=1, source_target_pairs={{0,1},{1,0},{2,3},{3,2},{4,5},{5,4},{6,7},{7,6},{8,9},{9,8},{10,11... | collective-permute-start | bytes 1572872 | tf_op jit(solution)/shard_map/ppermute | solution.py:326
  120.0 7.0 %collective-permute-start.24 = (bf16[64,1024]{1,0:T(8,128)(2,1)S(1)}, bf16[64,1024]{1,0:T(8,128)(2,1)S(1)}, u32[]{:S(2)}, u32[]{:S(2)}) collective-permute-start(bf16[64,1024]{1,0:T(8,128)(2,1)S(1)} %get-tuple-element.60), channel_id=1, source_target_pairs={{0,0},{1,2},{2,1},{3,3},{4,4},{5,6},{6,5},{7,7},{8,8},{9,10},{10,9... | collective-permute-start | bytes 393224 | tf_op jit(solution)/shard_map/ppermute | solution.py:335
  122.6 8.1 %collective-permute-start.27 = (bf16[64,1024]{1,0:T(8,128)(2,1)S(1)}, bf16[64,1024]{1,0:T(8,128)(2,1)S(1)}, u32[]{:S(2)}, u32[]{:S(2)}) collective-permute-start(bf16[64,1024]{1,0:T(8,128)(2,1)S(1)} %get-tuple-element.61), channel_id=1, source_target_pairs={{0,4},{1,6},{2,5},{3,7},{4,8},{5,10},{6,9},{7,11},{8,12},{9,14},{1... | collective-permute-start | bytes 393224 | tf_op jit(solution)/shard_map/ppermute | solution.py:335
  123.4 10.5 %collective-permute-start.26 = (bf16[64,1024]{1,0:T(8,128)(2,1)S(1)}, bf16[64,1024]{1,0:T(8,128)(2,1)S(1)}, u32[]{:S(2)}, u32[]{:S(2)}) collective-permute-start(bf16[64,1024]{1,0:T(8,128)(2,1)S(1)} %get-tuple-element.62), channel_id=1, source_target_pairs={{0,8},{1,10},{2,9},{3,11},{4,12},{5,14},{6,13},{7,15},{8,0},{9,2},... | collective-permute-start | bytes 393224 | tf_op jit(solution)/shard_map/ppermute | solution.py:335
  125.7 8.2 %collective-permute-start.25 = (bf16[64,1024]{1,0:T(8,128)(2,1)S(1)}, bf16[64,1024]{1,0:T(8,128)(2,1)S(1)}, u32[]{:S(2)}, u32[]{:S(2)}) collective-permute-start(bf16[64,1024]{1,0:T(8,128)(2,1)S(1)} %get-tuple-element.63), channel_id=1, source_target_pairs={{0,12},{1,14},{2,13},{3,15},{4,0},{5,2},{6,1},{7,3},{8,4},{9,6},{1... | collective-permute-start | bytes 393224 | tf_op jit(solution)/shard_map/ppermute | solution.py:335
  (6 other events, 10.6 us)

commit v4 on v3

--- a/solution.py
+++ b/solution.py
@@ -14,7 +14,7 @@
 BF16 = jnp.bfloat16
 NT = (((1,), (1,)), ((), ()))
 TN = (((0,), (0,)), ((), ()))
-VMEM_LIMIT = 52 * 1024 * 1024
+VMEM_LIMIT = 32 * 1024 * 1024
 
 
 def gathered(tokens, out_grad, gates, expert_ids, slots, gate_weight, up_weight, down_weight):
@@ -62,6 +62,9 @@
     return (scores, token_grad.astype(BF16))
 
 
+MINE_COST = 1
+PART_COST = 1
+SIZES = (1, 1)
 COST = 1.0
 
 
@@ -206,11 +209,9 @@
     forward(rows, count, s_ref[0], copies, xin_ref, (gate, up), au_ref)
 
 
-def x2_kernel(rows, counts, s_ref, xin_ref, gate_ref, up_ref, au_ref, mine_ref, gate, up, gate_m, up_m, sem, sem_m):
-    copies = load((gate_ref, up_ref), s_ref[0], counts[0], (gate, up), sem)
-    copies_m = load((gate_ref, up_ref), s_ref[1], counts[1], (gate_m, up_m), sem_m)
-    forward(rows, counts[0], s_ref[0], copies, xin_ref, (gate, up), au_ref)
-    forward(rows, counts[1], s_ref[1], copies_m, xin_ref, (gate_m, up_m), mine_ref)
+def x2_kernel(rows, count, s_ref, xin_ref, gate_ref, up_ref, au_ref, gate, up, sem):
+    copies = load((gate_ref, up_ref), s_ref[0], count, (gate, up), sem)
+    forward(rows, count, s_ref[0], copies, xin_ref, (gate, up), au_ref)
 
 
 def back_dots(rows, count, first, arrived, yin_ref, down, out_ref):
@@ -265,20 +266,15 @@
     each(d_ref.shape[0], body)
 
 
-def mine_parts_kernel(rows, sizes, s_ref, *refs):
-    n = len(sizes)
-    gate_ref, up_ref, part_ref, gate, up, sem = refs[n:]
-    arrived = load((gate_ref, up_ref), s_ref[0], sum(sizes), (gate, up), sem)
-    at = 0
-    for d_ref, size in zip(refs[:n], sizes):
-        gradient_rows(rows, d_ref, arrived, gate, up, part_ref, at)
-        at += size
+def mine_parts_kernel(rows, s_ref, d_ref, gate_ref, up_ref, part_ref, gate, up, sem):
+    arrived = load((gate_ref, up_ref), s_ref[0], d_ref.shape[0], (gate, up), sem)
+    gradient_rows(rows, d_ref, arrived, gate, up, part_ref)
 
 
 def combine_kernel(rows, zs, tok, half, at, count, s_ref, d_ref, gate_ref, up_ref, place_ref, *refs):
     first = s_ref[0] + at
     if at == 0:
-        mine_ref, acc, gate, up, part_ref, hot_ref, sem = refs
+        *mine_refs, acc, gate, up, part_ref, hot_ref, sem = refs
     else:
         acc_in, keep_ref, send_ref, gate, up, part_ref, hot_ref, acc, sem = refs
     copies = load((gate_ref, up_ref), first, count, (gate, up), sem)
@@ -293,9 +289,13 @@
     mark(half if at == 0 else 0, first, count)
     if at == 0:
         mark(0, half - s_ref[0], half)
-    cut = half * rows if at == 0 else 0
+    cut = 0
     if at == 0:
-        acc[...] = lax.dot_general(hot_ref[0:cut, :], mine_ref[...], TN, preferred_element_type=F32)
+        for n, mine_ref in enumerate(mine_refs):
+            size = mine_ref.shape[0]
+            own = lax.dot_general(hot_ref[cut : cut + size, :], mine_ref[...], TN, preferred_element_type=F32)
+            acc[...] = own if n == 0 else acc[...] + own
+            cut += size
     gradient_rows(rows, d_ref, copies, gate, up, part_ref)
     total = lax.dot_general(hot_ref[cut:, :], part_ref[...], TN, preferred_element_type=F32)
     if at == 0:
@@ -344,7 +344,7 @@
     smem = pl.BlockSpec(memory_space=pltpu.SMEM)
     dma = pltpu.SemaphoreType.DMA
 
-    def call(body, first, second, args, outs, scratch, flops, moved, name):
+    def call(body, first, second, args, outs, scratch, flops, moved, name, factor=1):
         ins = [spec for spec, group in args for _ in group]
         arrays = [v for _, group in args for v in group]
         info = jnp.stack([jnp.int32(first), jnp.int32(second), jnp.int32(z * experts)])
@@ -355,7 +355,7 @@
             out_specs=jax.tree.map(lambda _: vmem, outs),
             scratch_shapes=scratch,
             compiler_params=pltpu.CompilerParams(vmem_limit_bytes=VMEM_LIMIT),
-            cost_estimate=pl.CostEstimate(flops=int(flops * COST), bytes_accessed=int(moved * COST), transcendentals=0),
+            cost_estimate=pl.CostEstimate(flops=int(flops * COST * factor), bytes_accessed=int(moved * COST * factor), transcendentals=0),
             name=name,
         )(info, *arrays)
 
@@ -385,12 +385,16 @@
 
     place_shape = sds((experts, all_tok), F32)
     rows_shape = sds((experts * rows, width), BF16)
-    weights = (anywhere, (gate_weight, up_weight))
+    def pinned(*arrays):
+        return tuple(pltpu.with_memory_space_constraint(v, pltpu.HBM) for v in arrays)
+
+    weights = (anywhere, pinned(gate_weight, up_weight))
+    down_weight, = pinned(down_weight)
     au_first, xin, place, level = call(
         functools.partial(x_kernel, cfg, first),
         other0,
         s,
-        [(anywhere, (*x_own, *x_other)), weights],
+        [(anywhere, pinned(*x_own, *x_other)), weights],
         [sds((first, 2 * rows, ff), BF16), rows_shape, place_shape, place_shape],
         [tok_scratch, hot, pltpu.VMEM((2 * zs, ROUTE_ROWS, width), BF16), wide(first), wide(first)]
         + [dma((2 * first,)), dma((4 * zs,))],
@@ -400,31 +404,40 @@
     )
     y_here, au_first = lax.optimization_barrier((y_here, au_first))
     y_own = [y_here] + [shift(y_here, d) for d in range(1, zs)]
-    au_rest, au_mine = call(
-        functools.partial(x2_kernel, rows, (rest, half)),
-        other0 + first,
-        mine0,
-        [(vmem, (xin,)), weights],
-        [sds((rest, 2 * rows, ff), BF16), sds((half, 2 * rows, ff), F32)],
-        [wide(rest), wide(rest), wide(half), wide(half), dma((2 * rest,)), dma((2 * half,))],
-        2 * (rest + half) * flop,
-        2 * (rest + half) * wbytes,
-        "x_rest",
-    )
+
+    def x_call(first, n, dtype, name, factor):
+        return call(
+            functools.partial(x2_kernel, rows, n),
+            first,
+            s,
+            [(vmem, (xin,)), weights],
+            sds((n, 2 * rows, ff), dtype),
+            [wide(n), wide(n), dma((2 * n,))],
+            2 * n * flop,
+            2 * n * wbytes,
+            name,
+            factor,
+        )
+
+    au_rest = x_call(other0 + first, rest, BF16, "x_other", 1)
+    xin, au_rest = lax.optimization_barrier((xin, au_rest))
+    au_mine = x_call(mine0, half, F32, "x_mine", MINE_COST)
     au_recv = [flip(v, "dp") for v in (au_first, au_rest)]
     *y_own, au_mine = lax.optimization_barrier((*y_own, au_mine))
+    place, au_recv[0] = lax.optimization_barrier((place, au_recv[0]))
     y_other = [flip(v, "sub") for v in y_own]
     dh_first, yin = call(
         functools.partial(y_kernel, cfg, first),
         other0,
         s,
-        [(anywhere, (*y_own, *y_other)), (vmem, (place, level)), (anywhere, (down_weight,))],
+        [(anywhere, pinned(*y_own, *y_other)), (vmem, (place, level)), (anywhere, (down_weight,))],
         [sds((first, rows, ff), BF16), rows_shape],
         [tok_scratch, hot, tall(first), dma((first,)), dma((2 * zs,))],
         first * flop + dflop,
         first * wbytes,
         "y_first",
     )
+    yin, au_recv[1] = lax.optimization_barrier((yin, au_recv[1]))
     dh_rest, dh_mine = call(
         functools.partial(y2_kernel, rows, (rest, half)),
         other0 + first,
@@ -438,7 +451,7 @@
     )
     dh_recv = [flip(v, "dp") for v in (dh_first, dh_rest)]
     scale = LOCAL_EXPERTS / (all_tok * TOPK)
-    grads, back, scores = [], [], []
+    given, back, scores = [], [], []
     for k, n in enumerate(sizes):
         d, score = call(
             functools.partial(final_kernel, rows, scale, k * first),
@@ -451,36 +464,32 @@
             n * rows * ff * 30,
             "final",
         )
-        dh_mine, d = lax.optimization_barrier((dh_mine, d))
-        grads.append(d)
         scores.append(score)
         back.append(flip(d, "dp"))
+        part = call(
+            functools.partial(mine_parts_kernel, rows),
+            mine0 + k * first,
+            s,
+            [(vmem, (d,)), weights],
+            sds((n * rows, width), BF16),
+            [wide(n), wide(n), dma((2 * n,))],
+            2 * n * flop,
+            2 * n * wbytes,
+            "mine_parts",
+            PART_COST,
+        )
+        dh_mine, part = lax.optimization_barrier((dh_mine, part))
+        given.append(part)
     score = jnp.concatenate(scores, axis=0).reshape(half, ff)
     score_other = flip(score, "dp")
-    scores = jnp.concatenate(
-        [jnp.where(p == 0, score, score_other), jnp.where(p == 0, score_other, score)], axis=0
-    )
-    back[0], scores = lax.optimization_barrier((back[0], scores))
-    mine_parts = call(
-        functools.partial(mine_parts_kernel, rows, sizes),
-        mine0,
-        s,
-        [(vmem, grads), weights],
-        sds((half * rows, width), BF16),
-        [wide(half), wide(half), dma((2 * half,))],
-        2 * half * flop,
-        2 * half * wbytes,
-        "mine_parts",
-    )
     acc_shape, zshape = (all_tok, width), (zs, tok, width)
-    given = mine_parts
     for k, n in enumerate(sizes):
         used = n + half * (k == 0)
         given = call(
             functools.partial(combine_kernel, rows, zs, tok, half, k * first, n),
             other0,
             s,
-            [(vmem, (back[k],)), weights, (vmem, (place, given))],
+            [(vmem, (back[k],)), weights, (vmem, (place, *given))],
             sds(acc_shape, F32) if k == 0 else [sds(zshape, F32), sds(zshape, BF16)],
             [wide(n), wide(n), pltpu.VMEM((n * rows, width), BF16), pltpu.VMEM((used * rows, all_tok), BF16)]
             + ([] if k == 0 else [pltpu.VMEM(acc_shape, F32)])
@@ -489,8 +498,13 @@
             2 * n * wbytes,
             "combine",
         )
+        given = [given] if k == 0 else given
     keep, send = given
     summed = (keep + flip(send, "sub").astype(F32)).astype(BF16)
+    summed, score_other = lax.optimization_barrier((summed, score_other))
+    scores = jnp.concatenate(
+        [jnp.where(p == 0, score, score_other), jnp.where(p == 0, score_other, score)], axis=0
+    )
     total = turn(summed[0], 0).astype(F32)
     for d in range(1, zs):
         total = total + turn(summed[d], -d).astype(F32)

time: 136 us -> 120 us (0.88)
  Pallas kernels: 60.2 us -> 51.5 us
  waiting for transfers between devices: 35.7 us -> 29.1 us
    pallas_call x9 -> x11, Pallas kernels: 58.5 us -> 49.7 us  [call(): pl.pallas_call(body, out_shape=outs, in_specs=[smem] + ins, out_specs=jax...]
    ppermute x16, waiting for transfers between devices: 18.7 us -> 13.5 us  [flip(): return lax.ppermute(v, axis, [(0, 1), (1, 0)])]
    ppermute x9, waiting for transfers between devices: 17 us -> 15.6 us  [turn(): return lax.ppermute(v, ('expert', 'dp', 'sub'), pairs)]
  transfers between devices with their start and end apart: 28 -> 28, of which waited for: 9 -> 13; matrix products, arithmetic and copies ran while one was open for 1% -> 1% of each run, Pallas kernels for 36% -> 38%
where the time goes in v4:
time: 120 us; the launch traced here: 118 us
  Pallas kernels  51.5 us (43%)
  starting transfers between devices  33.1 us (28%)
  waiting for transfers between devices  29.1 us (24%)
  local copies, waits for them, and re-layouts  2.08 us (2%)
  other arithmetic  1.8 us (2%)
    pallas_call x11, Pallas kernels, call(): pl.pallas_call(body, out_shape=outs, in_specs=[smem] + ins, out_specs=jax...  49.7 us
    ppermute x9, starting transfers between devices, turn(): return lax.ppermute(v, ('expert', 'dp', 'sub'), pairs)  20 us
    ppermute x9, waiting for transfers between devices, turn(): return lax.ppermute(v, ('expert', 'dp', 'sub'), pairs)  15.6 us
    ppermute x16, waiting for transfers between devices, flip(): return lax.ppermute(v, axis, [(0, 1), (1, 0)])  13.5 us
    ppermute x16, starting transfers between devices, flip(): return lax.ppermute(v, axis, [(0, 1), (1, 0)])  9.3 us
    ppermute x3, starting transfers between devices, shift(): return lax.ppermute(v, 'expert', [(i, (i + d) % zs) for i in range(zs)])  3.83 us
  transfers between devices with their start and end apart: 28, of which 13 were waited for; matrix products, arithmetic and copies ran while one was open for 1% of the time, Pallas kernels for 38%

profile of v4, /device:TPU:1, one launch (start us, length us, event | category | flops | bytes accessed | tf_op | source)
XLA Modules:
  0.0 118.5 jit_solution(8042304671826322158)
XLA Ops:
  0.6 1.7 %pack.1 = bf16[80,1024]{1,0:T(8,128)(2,1)} custom-call(s32[1]{0:T(128)} %bitcast.3.p_ref, bf16[64,1024]{1,0:T(8,128)(2,1)} %tokens_ref.1, s32[8,64]{1,0:T(8,128)} %bitcast.26, s32[8,64]{1,0:T(8,128)} %bitcast.27, f32[8,64]{1,0:T(8,128)} %bitcast.28), custom_call_target="tpu_custom_call" | custom-call | tf_op jit(solution)/shard_map/pack/pallas_call | solution.py:362
  2.4 5.6 %collective-permute-start.4 = (bf16[80,1024]{1,0:T(8,128)(2,1)}, bf16[80,1024]{1,0:T(8,128)(2,1)S(1)}, u32[]{:S(2)}, u32[]{:S(2)}) collective-permute-start(bf16[80,1024]{1,0:T(8,128)(2,1)} %pack.1), channel_id=1, source_target_pairs={{0,12},{1,14},{2,13},{3,15},{4,0},{5,2},{6,1},{7,3},{8,4},{9,6},{1... | collective-permute-start | bytes 491528 | tf_op jit(solution)/shard_map/ppermute | solution.py:335
  8.0 1.6 %collective-permute-start.2 = (bf16[80,1024]{1,0:T(8,128)(2,1)}, bf16[80,1024]{1,0:T(8,128)(2,1)S(1)}, u32[]{:S(2)}, u32[]{:S(2)}) collective-permute-start(bf16[80,1024]{1,0:T(8,128)(2,1)} %pack.1), channel_id=1, source_target_pairs={{0,4},{1,6},{2,5},{3,7},{4,8},{5,10},{6,9},{7,11},{8,12},{9,14},{1... | collective-permute-start | bytes 491528 | tf_op jit(solution)/shard_map/ppermute | solution.py:335
  9.6 2.0 %collective-permute-start.1 = (bf16[80,1024]{1,0:T(8,128)(2,1)}, bf16[80,1024]{1,0:T(8,128)(2,1)S(1)}, u32[]{:S(2)}, u32[]{:S(2)}) collective-permute-start(bf16[80,1024]{1,0:T(8,128)(2,1)} %pack.1), channel_id=1, source_target_pairs={{0,0},{1,2},{2,1},{3,3},{4,4},{5,6},{6,5},{7,7},{8,8},{9,10},{10,9... | collective-permute-start | bytes 491528 | tf_op jit(solution)/shard_map/ppermute | solution.py:335
  12.3 9.5 %collective-permute-done.3.refs_2_ = bf16[80,1024]{1,0:T(8,128)(2,1)S(1)} collective-permute-done((bf16[80,1024]{1,0:T(8,128)(2,1)}, bf16[80,1024]{1,0:T(8,128)(2,1)S(1)}, u32[]{:S(2)}, u32[]{:S(2)}) %collective-permute-start.3) | collective-permute-done | bytes 163872 | tf_op jit(solution)/shard_map/ppermute | solution.py:335
  23.2 3.0 %collective-permute-start = (bf16[64,1024]{1,0:T(8,128)(2,1)}, bf16[64,1024]{1,0:T(8,128)(2,1)}, u32[]{:S(2)}, u32[]{:S(2)}) collective-permute-start(bf16[64,1024]{1,0:T(8,128)(2,1)} %param.9), channel_id=1, source_target_pairs={{0,0},{1,2},{2,1},{3,3},{4,4},{5,6},{6,5},{7,7},{8,8},{9,10},{10,9... | collective-permute-start | bytes 393224 | tf_op jit(solution)/shard_map/ppermute | solution.py:335
  27.8 6.6 %x_first.1 = (bf16[4,160,384]{2,1,0:T(8,128)(2,1)}, bf16[1280,1024]{1,0:T(8,128)(2,1)S(1)}, f32[16,512]{1,0:T(8,128)S(1)}, f32[16,512]{1,0:T(8,128)S(1)}) custom-call(s32[3]{0:T(128)S(1)} %get-tuple-element.74.s_ref, bf16[80,1024]{1,0:T(8,128)(2,1)} %copy-done.3, bf16[80,1024]{1,0:T(8,128)(2,1)} %copy-done.2, bf16[80,1024]{1,0:T(8,128)(2,1)} %copy-done.1, ...), custom_call_target="tpu_custom_call" | custom-call | flops 1845493760 | bytes 6291456 | tf_op jit(solution)/shard_map/x_first/pallas_call | solution.py:351
  34.7 2.4 %collective-permute-start.10 = (bf16[64,1024]{1,0:T(8,128)(2,1)}, bf16[64,1024]{1,0:T(8,128)(2,1)S(1)}, u32[]{:S(2)}, u32[]{:S(2)}) collective-permute-start(bf16[64,1024]{1,0:T(8,128)(2,1)} %collective-permute-done.refs_0_), channel_id=1, source_target_pairs={{0,8},{4,12},{8,0},{12,4},{1,9},{5,13},{9,1},{13,5},{2,10},{6,14},... | collective-permute-start | bytes 393224 | tf_op jit(solution)/shard_map/ppermute | solution.py:338
  38.5 3.8 %x_other.1 = bf16[4,160,384]{2,1,0:T(8,128)(2,1)S(1)} custom-call(s32[3]{0:T(128)S(1)} %get-tuple-element.75.s_ref, bf16[1280,1024]{1,0:T(8,128)(2,1)S(1)} %get-tuple-element.39.xin_ref, bf16[16,1024,384]{2,1,0:T(8,128)(2,1)} %gate_ref.11, bf16[16,1024,384]{2,1,0:T(8,128)(2,1)} %up_ref.11), custom_call_target="tpu_custom_call" | custom-call | flops 503316480 | bytes 6291456 | tf_op jit(solution)/shard_map/x_other/pallas_call | solution.py:351
  42.4 1.4 %collective-permute-start.17 = (bf16[4,160,384]{2,1,0:T(8,128)(2,1)S(1)}, bf16[4,160,384]{2,1,0:T(8,128)(2,1)S(1)}, u32[]{:S(2)}, u32[]{:S(2)}) collective-permute-start(bf16[4,160,384]{2,1,0:T(8,128)(2,1)S(1)} %x_other.1), channel_id=1, source_target_pairs={{0,2},{2,0},{1,3},{3,1},{4,6},{6,4},{5,7},{7,5},{8,10},{10,8},{9,1... | collective-permute-start | bytes 1474568 | tf_op jit(solution)/shard_map/ppermute | solution.py:326
  43.9 5.7 %x_mine.1.au_m = f32[8,160,384]{2,1,0:T(8,128)S(1)} custom-call(s32[3]{0:T(128)S(1)} %add_add_fusion.s_ref, bf16[1280,1024]{1,0:T(8,128)(2,1)S(1)} %get-tuple-element.39.xin_ref, bf16[16,1024,384]{2,1,0:T(8,128)(2,1)} %gate_ref.11, bf16[16,1024,384]{2,1,0:T(8,128)(2,1)} %up_ref.11), custom_call_target="tpu_custom_call" | custom-call | flops 1006632960 | bytes 12582912 | tf_op jit(solution)/shard_map/x_mine/pallas_call | solution.py:351
  52.9 5.8 %y_first.1 = (bf16[4,80,384]{2,1,0:T(8,128)(2,1)S(1)}, bf16[1280,1024]{1,0:T(8,128)(2,1)S(1)}) custom-call(s32[3]{0:T(128)S(1)} %get-tuple-element.74.s_ref, bf16[64,1024]{1,0:T(8,128)(2,1)} %collective-permute-done.refs_0_, bf16[64,1024]{1,0:T(8,128)(2,1)} %copy-done.10, bf16[64,1024]{1,0:T(8,128)(2,1)} %copy-done.9, bf16[64,1024]{1,0:T(8,128)(2,1)} %copy-done.8, ...), custom_call_target="tpu_custom_call" | custom-call | flops 1593835520 | bytes 3145728 | tf_op jit(solution)/shard_map/y_first/pallas_call | solution.py:351
  60.1 6.3 %y_rest.1 = (bf16[4,80,384]{2,1,0:T(8,128)(2,1)S(1)}, f32[8,80,384]{2,1,0:T(8,128)S(1)}) custom-call(s32[3]{0:T(128)S(1)} %add_add_fusion.3.s_ref, bf16[1280,1024]{1,0:T(8,128)(2,1)S(1)} %get-tuple-element.51.yin_ref, bf16[16,384,1024]{2,1,0:T(8,128)(2,1)} %down_ref.1), custom_call_target="tpu_custom_call" | custom-call | flops 754974720 | bytes 9437184 | tf_op jit(solution)/shard_map/y_rest/pallas_call | solution.py:351
  69.0 4.4 %mine_parts.2.refs_0_ = bf16[320,1024]{1,0:T(8,128)(2,1)S(1)} custom-call(s32[3]{0:T(128)S(1)} %add_add_fusion.s_ref, bf16[4,160,384]{2,1,0:T(8,128)(2,1)S(1)} %get-tuple-element.56.d_ref, bf16[16,1024,384]{2,1,0:T(8,128)(2,1)} %gate_ref.11, bf16[16,1024,384]{2,1,0:T(8,128)(2,1)} %up_ref.11), custom_call_target="tpu_custom_call" | custom-call | flops 503316480 | bytes 6291456 | tf_op jit(solution)/shard_map/mine_parts/pallas_call | solution.py:351
  74.9 4.5 %mine_parts.3.refs_1_ = bf16[320,1024]{1,0:T(8,128)(2,1)S(1)} custom-call(s32[3]{0:T(128)S(1)} %add_add_fusion.4.s_ref, bf16[4,160,384]{2,1,0:T(8,128)(2,1)S(1)} %get-tuple-element.61.d_ref, bf16[16,1024,384]{2,1,0:T(8,128)(2,1)} %gate_ref.11, bf16[16,1024,384]{2,1,0:T(8,128)(2,1)} %up_ref.11), custom_call_target="tpu_custom_call" | custom-call | flops 503316480 | bytes 6291456 | tf_op jit(solution)/shard_map/mine_parts/pallas_call | solution.py:351
  79.4 4.7 %collective-permute-done.21.d_ref = bf16[4,160,384]{2,1,0:T(8,128)(2,1)S(1)} collective-permute-done((bf16[4,160,384]{2,1,0:T(8,128)(2,1)S(1)}, bf16[4,160,384]{2,1,0:T(8,128)(2,1)S(1)}, u32[]{:S(2)}, u32[]{:S(2)}) %collective-permute-start.21) | collective-permute-done | bytes 491552 | tf_op jit(solution)/shard_map/ppermute | solution.py:326
  84.1 5.3 %combine.2.refs_0_ = f32[512,1024]{1,0:T(8,128)S(1)} custom-call(s32[3]{0:T(128)S(1)} %get-tuple-element.74.s_ref, bf16[4,160,384]{2,1,0:T(8,128)(2,1)S(1)} %collective-permute-done.21.d_ref, bf16[16,1024,384]{2,1,0:T(8,128)(2,1)} %gate_ref.11, bf16[16,1024,384]{2,1,0:T(8,128)(2,1)} %up_ref.11, f32[16,512]{1,0:T(8,128)S(1)} %get-tuple-element.47.refs_8_.place_ref, ...), custom_call_target="tpu_custom_call" | custom-call | flops 1509949440 | bytes 6291456 | tf_op jit(solution)/shard_map/combine/pallas_call | solution.py:351
  89.4 5.2 %collective-permute-done.20.d_ref = bf16[4,160,384]{2,1,0:T(8,128)(2,1)S(1)} collective-permute-done((bf16[4,160,384]{2,1,0:T(8,128)(2,1)S(1)}, bf16[4,160,384]{2,1,0:T(8,128)(2,1)S(1)}, u32[]{:S(2)}, u32[]{:S(2)}) %collective-permute-start.20) | collective-permute-done | bytes 491552 | tf_op jit(solution)/shard_map/ppermute | solution.py:326
  94.6 5.3 %combine.3 = (f32[4,64,1024]{2,1,0:T(8,128)S(1)}, bf16[4,64,1024]{2,1,0:T(8,128)(2,1)S(1)}) custom-call(s32[3]{0:T(128)S(1)} %get-tuple-element.74.s_ref, bf16[4,160,384]{2,1,0:T(8,128)(2,1)S(1)} %collective-permute-done.20.d_ref, bf16[16,1024,384]{2,1,0:T(8,128)(2,1)} %gate_ref.11, bf16[16,1024,384]{2,1,0:T(8,128)(2,1)} %up_ref.11, ...), custom_call_target="tpu_custom_call" | custom-call | flops 838860800 | bytes 6291456 | tf_op jit(solution)/shard_map/combine/pallas_call | solution.py:351
  103.9 3.2 %collective-permute-start.24 = (bf16[64,1024]{1,0:T(8,128)(2,1)S(1)}, bf16[64,1024]{1,0:T(8,128)(2,1)S(1)}, u32[]{:S(2)}, u32[]{:S(2)}) collective-permute-start(bf16[64,1024]{1,0:T(8,128)(2,1)S(1)} %get-tuple-element.68), channel_id=1, source_target_pairs={{0,0},{1,2},{2,1},{3,3},{4,4},{5,6},{6,5},{7,7},{8,8},{9,10},{10,9... | collective-permute-start | bytes 393224 | tf_op jit(solution)/shard_map/ppermute | solution.py:335
  107.2 3.0 %collective-permute-start.26 = (bf16[64,1024]{1,0:T(8,128)(2,1)S(1)}, bf16[64,1024]{1,0:T(8,128)(2,1)S(1)}, u32[]{:S(2)}, u32[]{:S(2)}) collective-permute-start(bf16[64,1024]{1,0:T(8,128)(2,1)S(1)} %get-tuple-element.70), channel_id=1, source_target_pairs={{0,8},{1,10},{2,9},{3,11},{4,12},{5,14},{6,13},{7,15},{8,0},{9,2},... | collective-permute-start | bytes 393224 | tf_op jit(solution)/shard_map/ppermute | solution.py:335
  110.2 1.5 %collective-permute-start.25 = (bf16[64,1024]{1,0:T(8,128)(2,1)S(1)}, bf16[64,1024]{1,0:T(8,128)(2,1)S(1)}, u32[]{:S(2)}, u32[]{:S(2)}) collective-permute-start(bf16[64,1024]{1,0:T(8,128)(2,1)S(1)} %get-tuple-element.71), channel_id=1, source_target_pairs={{0,12},{1,14},{2,13},{3,15},{4,0},{5,2},{6,1},{7,3},{8,4},{9,6},{1... | collective-permute-start | bytes 393224 | tf_op jit(solution)/shard_map/ppermute | solution.py:335
  112.3 2.4 %collective-permute-done.27 = bf16[64,1024]{1,0:T(8,128)(2,1)S(1)} collective-permute-done((bf16[64,1024]{1,0:T(8,128)(2,1)S(1)}, bf16[64,1024]{1,0:T(8,128)(2,1)S(1)}, u32[]{:S(2)}, u32[]{:S(2)}) %collective-permute-start.27) | collective-permute-done | bytes 131104 | tf_op jit(solution)/shard_map/ppermute | solution.py:335
  114.6 3.1 %collective-permute-done.26 = bf16[64,1024]{1,0:T(8,128)(2,1)S(1)} collective-permute-done((bf16[64,1024]{1,0:T(8,128)(2,1)S(1)}, bf16[64,1024]{1,0:T(8,128)(2,1)S(1)}, u32[]{:S(2)}, u32[]{:S(2)}) %collective-permute-start.26) | collective-permute-done | bytes 131104 | tf_op jit(solution)/shard_map/ppermute | solution.py:335
  (85 shorter events, 19.5 us)
Async XLA Ops:
  2.4 10.0 %collective-permute-start.4 = (bf16[80,1024]{1,0:T(8,128)(2,1)}, bf16[80,1024]{1,0:T(8,128)(2,1)S(1)}, u32[]{:S(2)}, u32[]{:S(2)}) collective-permute-start(bf16[80,1024]{1,0:T(8,128)(2,1)} %pack.1), channel_id=1, source_target_pairs={{0,12},{1,14},{2,13},{3,15},{4,0},{5,2},{6,1},{7,3},{8,4},{9,6},{1... | collective-permute-start | bytes 491528 | tf_op jit(solution)/shard_map/ppermute | solution.py:335
  8.0 13.8 %collective-permute-start.3 = (bf16[80,1024]{1,0:T(8,128)(2,1)}, bf16[80,1024]{1,0:T(8,128)(2,1)S(1)}, u32[]{:S(2)}, u32[]{:S(2)}) collective-permute-start(bf16[80,1024]{1,0:T(8,128)(2,1)} %pack.1), channel_id=1, source_target_pairs={{0,8},{1,10},{2,9},{3,11},{4,12},{5,14},{6,13},{7,15},{8,0},{9,2},... | collective-permute-start | bytes 491528 | tf_op jit(solution)/shard_map/ppermute | solution.py:335
  8.0 14.7 %collective-permute-start.2 = (bf16[80,1024]{1,0:T(8,128)(2,1)}, bf16[80,1024]{1,0:T(8,128)(2,1)S(1)}, u32[]{:S(2)}, u32[]{:S(2)}) collective-permute-start(bf16[80,1024]{1,0:T(8,128)(2,1)} %pack.1), channel_id=1, source_target_pairs={{0,4},{1,6},{2,5},{3,7},{4,8},{5,10},{6,9},{7,11},{8,12},{9,14},{1... | collective-permute-start | bytes 491528 | tf_op jit(solution)/shard_map/ppermute | solution.py:335
  9.6 13.2 %collective-permute-start.1 = (bf16[80,1024]{1,0:T(8,128)(2,1)}, bf16[80,1024]{1,0:T(8,128)(2,1)S(1)}, u32[]{:S(2)}, u32[]{:S(2)}) collective-permute-start(bf16[80,1024]{1,0:T(8,128)(2,1)} %pack.1), channel_id=1, source_target_pairs={{0,0},{1,2},{2,1},{3,3},{4,4},{5,6},{6,5},{7,7},{8,8},{9,10},{10,9... | collective-permute-start | bytes 491528 | tf_op jit(solution)/shard_map/ppermute | solution.py:335
  12.3 14.0 %collective-permute-start.8 = (bf16[80,1024]{1,0:T(8,128)(2,1)S(1)}, bf16[80,1024]{1,0:T(8,128)(2,1)S(1)}, u32[]{:S(2)}, u32[]{:S(2)}) collective-permute-start(bf16[80,1024]{1,0:T(8,128)(2,1)S(1)} %collective-permute-done.4.refs_3_), channel_id=1, source_target_pairs={{0,1},{1,0},{2,3},{3,2},{4,5},{5,4},{6,7},{7,6},{8,9},{9,8},{10,11... | collective-permute-start | bytes 491528 | tf_op jit(solution)/shard_map/ppermute | solution.py:326
  21.8 4.5 %collective-permute-start.7 = (bf16[80,1024]{1,0:T(8,128)(2,1)S(1)}, bf16[80,1024]{1,0:T(8,128)(2,1)S(1)}, u32[]{:S(2)}, u32[]{:S(2)}) collective-permute-start(bf16[80,1024]{1,0:T(8,128)(2,1)S(1)} %collective-permute-done.3.refs_2_), channel_id=1, source_target_pairs={{0,1},{1,0},{2,3},{3,2},{4,5},{5,4},{6,7},{7,6},{8,9},{9,8},{10,11... | collective-permute-start | bytes 491528 | tf_op jit(solution)/shard_map/ppermute | solution.py:326
  22.7 3.6 %collective-permute-start.6 = (bf16[80,1024]{1,0:T(8,128)(2,1)S(1)}, bf16[80,1024]{1,0:T(8,128)(2,1)S(1)}, u32[]{:S(2)}, u32[]{:S(2)}) collective-permute-start(bf16[80,1024]{1,0:T(8,128)(2,1)S(1)} %collective-permute-done.2.refs_1_), channel_id=1, source_target_pairs={{0,1},{1,0},{2,3},{3,2},{4,5},{5,4},{6,7},{7,6},{8,9},{9,8},{10,11... | collective-permute-start | bytes 491528 | tf_op jit(solution)/shard_map/ppermute | solution.py:326
  22.8 3.6 %collective-permute-start.5 = (bf16[80,1024]{1,0:T(8,128)(2,1)S(1)}, bf16[80,1024]{1,0:T(8,128)(2,1)S(1)}, u32[]{:S(2)}, u32[]{:S(2)}) collective-permute-start(bf16[80,1024]{1,0:T(8,128)(2,1)S(1)} %collective-permute-done.1.refs_0_), channel_id=1, source_target_pairs={{0,1},{1,0},{2,3},{3,2},{4,5},{5,4},{6,7},{7,6},{8,9},{9,8},{10,11... | collective-permute-start | bytes 491528 | tf_op jit(solution)/shard_map/ppermute | solution.py:326
  23.2 11.2 %collective-permute-start = (bf16[64,1024]{1,0:T(8,128)(2,1)}, bf16[64,1024]{1,0:T(8,128)(2,1)}, u32[]{:S(2)}, u32[]{:S(2)}) collective-permute-start(bf16[64,1024]{1,0:T(8,128)(2,1)} %param.9), channel_id=1, source_target_pairs={{0,0},{1,2},{2,1},{3,3},{4,4},{5,6},{6,5},{7,7},{8,8},{9,10},{10,9... | collective-permute-start | bytes 393224 | tf_op jit(solution)/shard_map/ppermute | solution.py:335
  34.4 16.5 %collective-permute-start.16 = (bf16[4,160,384]{2,1,0:T(8,128)(2,1)}, bf16[4,160,384]{2,1,0:T(8,128)(2,1)S(1)}, u32[]{:S(2)}, u32[]{:S(2)}) collective-permute-start(bf16[4,160,384]{2,1,0:T(8,128)(2,1)} %get-tuple-element.46), channel_id=1, source_target_pairs={{0,2},{2,0},{1,3},{3,1},{4,6},{6,4},{5,7},{7,5},{8,10},{10,8},{9,1... | collective-permute-start | bytes 1474568 | tf_op jit(solution)/shard_map/ppermute | solution.py:326
  34.7 14.9 %collective-permute-start.11 = (bf16[64,1024]{1,0:T(8,128)(2,1)}, bf16[64,1024]{1,0:T(8,128)(2,1)S(1)}, u32[]{:S(2)}, u32[]{:S(2)}) collective-permute-start(bf16[64,1024]{1,0:T(8,128)(2,1)} %collective-permute-done.refs_0_), channel_id=1, source_target_pairs={{0,12},{4,0},{8,4},{12,8},{1,13},{5,1},{9,5},{13,9},{2,14},{6,2},{... | collective-permute-start | bytes 393224 | tf_op jit(solution)/shard_map/ppermute | solution.py:338
  34.7 14.8 %collective-permute-start.10 = (bf16[64,1024]{1,0:T(8,128)(2,1)}, bf16[64,1024]{1,0:T(8,128)(2,1)S(1)}, u32[]{:S(2)}, u32[]{:S(2)}) collective-permute-start(bf16[64,1024]{1,0:T(8,128)(2,1)} %collective-permute-done.refs_0_), channel_id=1, source_target_pairs={{0,8},{4,12},{8,0},{12,4},{1,9},{5,13},{9,1},{13,5},{2,10},{6,14},... | collective-permute-start | bytes 393224 | tf_op jit(solution)/shard_map/ppermute | solution.py:338
  37.2 12.5 %collective-permute-start.9 = (bf16[64,1024]{1,0:T(8,128)(2,1)}, bf16[64,1024]{1,0:T(8,128)(2,1)S(1)}, u32[]{:S(2)}, u32[]{:S(2)}) collective-permute-start(bf16[64,1024]{1,0:T(8,128)(2,1)} %collective-permute-done.refs_0_), channel_id=1, source_target_pairs={{0,4},{4,8},{8,12},{12,0},{1,5},{5,9},{9,13},{13,1},{2,6},{6,10},{... | collective-permute-start | bytes 393224 | tf_op jit(solution)/shard_map/ppermute | solution.py:338
  42.4 17.7 %collective-permute-start.17 = (bf16[4,160,384]{2,1,0:T(8,128)(2,1)S(1)}, bf16[4,160,384]{2,1,0:T(8,128)(2,1)S(1)}, u32[]{:S(2)}, u32[]{:S(2)}) collective-permute-start(bf16[4,160,384]{2,1,0:T(8,128)(2,1)S(1)} %x_other.1), channel_id=1, source_target_pairs={{0,2},{2,0},{1,3},{3,1},{4,6},{6,4},{5,7},{7,5},{8,10},{10,8},{9,1... | collective-permute-start | bytes 1474568 | tf_op jit(solution)/shard_map/ppermute | solution.py:326
  58.7 8.0 %collective-permute-start.18 = (bf16[4,80,384]{2,1,0:T(8,128)(2,1)S(1)}, bf16[4,80,384]{2,1,0:T(8,128)(2,1)S(1)}, u32[]{:S(2)}, u32[]{:S(2)}) collective-permute-start(bf16[4,80,384]{2,1,0:T(8,128)(2,1)S(1)} %get-tuple-element.54), channel_id=1, source_target_pairs={{0,2},{2,0},{1,3},{3,1},{4,6},{6,4},{5,7},{7,5},{8,10},{10,8},{9,1... | collective-permute-start | bytes 737288 | tf_op jit(solution)/shard_map/ppermute | solution.py:326
  66.4 7.1 %collective-permute-start.19 = (bf16[4,80,384]{2,1,0:T(8,128)(2,1)S(1)}, bf16[4,80,384]{2,1,0:T(8,128)(2,1)S(1)}, u32[]{:S(2)}, u32[]{:S(2)}) collective-permute-start(bf16[4,80,384]{2,1,0:T(8,128)(2,1)S(1)} %get-tuple-element.59), channel_id=1, source_target_pairs={{0,2},{2,0},{1,3},{3,1},{4,6},{6,4},{5,7},{7,5},{8,10},{10,8},{9,1... | collective-permute-start | bytes 737288 | tf_op jit(solution)/shard_map/ppermute | solution.py:326
  67.7 16.4 %collective-permute-start.21 = (bf16[4,160,384]{2,1,0:T(8,128)(2,1)S(1)}, bf16[4,160,384]{2,1,0:T(8,128)(2,1)S(1)}, u32[]{:S(2)}, u32[]{:S(2)}) collective-permute-start(bf16[4,160,384]{2,1,0:T(8,128)(2,1)S(1)} %get-tuple-element.56.d_ref), channel_id=1, source_target_pairs={{0,2},{2,0},{1,3},{3,1},{4,6},{6,4},{5,7},{7,5},{8,10},{10,8},{9,1... | collective-permute-start | bytes 1474568 | tf_op jit(solution)/shard_map/ppermute | solution.py:326
  74.5 20.1 %collective-permute-start.20 = (bf16[4,160,384]{2,1,0:T(8,128)(2,1)S(1)}, bf16[4,160,384]{2,1,0:T(8,128)(2,1)S(1)}, u32[]{:S(2)}, u32[]{:S(2)}) collective-permute-start(bf16[4,160,384]{2,1,0:T(8,128)(2,1)S(1)} %get-tuple-element.61.d_ref), channel_id=1, source_target_pairs={{0,2},{2,0},{1,3},{3,1},{4,6},{6,4},{5,7},{7,5},{8,10},{10,8},{9,1... | collective-permute-start | bytes 1474568 | tf_op jit(solution)/shard_map/ppermute | solution.py:326
  99.9 2.9 %collective-permute-start.22 = (bf16[4,64,1024]{2,1,0:T(8,128)(2,1)S(1)}, bf16[4,64,1024]{2,1,0:T(8,128)(2,1)S(1)}, u32[]{:S(2)}, u32[]{:S(2)}) collective-permute-start(bf16[4,64,1024]{2,1,0:T(8,128)(2,1)S(1)} %get-tuple-element.65), channel_id=1, source_target_pairs={{0,1},{1,0},{2,3},{3,2},{4,5},{5,4},{6,7},{7,6},{8,9},{9,8},{10,11... | collective-permute-start | bytes 1572872 | tf_op jit(solution)/shard_map/ppermute | solution.py:326
  101.3 2.6 %collective-permute-start.23 = (f32[8,384]{1,0:T(8,128)S(1)}, f32[8,384]{1,0:T(8,128)S(1)}, u32[]{:S(2)}, u32[]{:S(2)}) collective-permute-start(f32[8,384]{1,0:T(8,128)S(1)} %bitcast.25), channel_id=1, source_target_pairs={{0,2},{2,0},{1,3},{3,1},{4,6},{6,4},{5,7},{7,5},{8,10},{10,8},{9,1... | collective-permute-start | bytes 36872 | tf_op jit(solution)/shard_map/ppermute | solution.py:326
  103.9 8.3 %collective-permute-start.24 = (bf16[64,1024]{1,0:T(8,128)(2,1)S(1)}, bf16[64,1024]{1,0:T(8,128)(2,1)S(1)}, u32[]{:S(2)}, u32[]{:S(2)}) collective-permute-start(bf16[64,1024]{1,0:T(8,128)(2,1)S(1)} %get-tuple-element.68), channel_id=1, source_target_pairs={{0,0},{1,2},{2,1},{3,3},{4,4},{5,6},{6,5},{7,7},{8,8},{9,10},{10,9... | collective-permute-start | bytes 393224 | tf_op jit(solution)/shard_map/ppermute | solution.py:335
  107.1 7.5 %collective-permute-start.27 = (bf16[64,1024]{1,0:T(8,128)(2,1)S(1)}, bf16[64,1024]{1,0:T(8,128)(2,1)S(1)}, u32[]{:S(2)}, u32[]{:S(2)}) collective-permute-start(bf16[64,1024]{1,0:T(8,128)(2,1)S(1)} %get-tuple-element.69), channel_id=1, source_target_pairs={{0,4},{1,6},{2,5},{3,7},{4,8},{5,10},{6,9},{7,11},{8,12},{9,14},{1... | collective-permute-start | bytes 393224 | tf_op jit(solution)/shard_map/ppermute | solution.py:335
  107.2 10.5 %collective-permute-start.26 = (bf16[64,1024]{1,0:T(8,128)(2,1)S(1)}, bf16[64,1024]{1,0:T(8,128)(2,1)S(1)}, u32[]{:S(2)}, u32[]{:S(2)}) collective-permute-start(bf16[64,1024]{1,0:T(8,128)(2,1)S(1)} %get-tuple-element.70), channel_id=1, source_target_pairs={{0,8},{1,10},{2,9},{3,11},{4,12},{5,14},{6,13},{7,15},{8,0},{9,2},... | collective-permute-start | bytes 393224 | tf_op jit(solution)/shard_map/ppermute | solution.py:335
  110.2 7.6 %collective-permute-start.25 = (bf16[64,1024]{1,0:T(8,128)(2,1)S(1)}, bf16[64,1024]{1,0:T(8,128)(2,1)S(1)}, u32[]{:S(2)}, u32[]{:S(2)}) collective-permute-start(bf16[64,1024]{1,0:T(8,128)(2,1)S(1)} %get-tuple-element.71), channel_id=1, source_target_pairs={{0,12},{1,14},{2,13},{3,15},{4,0},{5,2},{6,1},{7,3},{8,4},{9,6},{1... | collective-permute-start | bytes 393224 | tf_op jit(solution)/shard_map/ppermute | solution.py:335
  (19 other events, 51.4 us)

commit v5 on v4

--- a/solution.py
+++ b/solution.py
@@ -64,7 +64,6 @@
 
 MINE_COST = 1
 PART_COST = 1
-SIZES = (1, 1)
 COST = 1.0
 
 
@@ -153,7 +152,7 @@
         got = jnp.dot(hot_ref[...], tok_ref[...], preferred_element_type=F32)
         if level_ref is not None:
             got = got * jnp.concatenate(levels, axis=0)
-        out_ref[pl.ds(pl.multiple_of(g * group * rows, group * rows), group * rows), :] = got.astype(BF16)
+        out_ref[pl.ds(g * group, group)] = got.astype(BF16).reshape(group, rows, got.shape[1])
         return carry
 
     lax.fori_loop(0, experts // group, body, 0)
@@ -176,18 +175,14 @@
         level_ref[e : e + 1, :] = jnp.sum(jnp.where(hit, level, 0.0), axis=0, keepdims=True)
 
 
-def expert_rows(ref, rows, e):
-    return ref[pl.ds(pl.multiple_of(e * rows, rows), rows), :]
-
-
 def at_rows(rows, j):
     return pl.ds(pl.multiple_of(j * rows, rows), rows)
 
 
-def forward(rows, count, first, arrived, xin_ref, bufs, out_ref):
+def forward(rows, count, first, arrived, xs, bufs, out_ref):
     def body(j):
-        x = expert_rows(xin_ref, rows, first + j)
         arrived(j)
+        x = xs[first + j]
         for n, buf in enumerate(bufs):
             got = jnp.dot(x, buf[j], preferred_element_type=F32)
             out_ref[j, n * rows : (n + 1) * rows, :] = got.astype(out_ref.dtype)
@@ -199,26 +194,28 @@
     zs, tok, experts, rows, group = cfg
     tokens = refs[: 2 * zs]
     gate_ref, up_ref, au_ref, xin_ref, place_ref, level_ref = refs[2 * zs : 2 * zs + 6]
-    tok_ref, hot_ref, meta_ref, gate, up, sem, tok_sem = refs[2 * zs + 6 :]
+    tok_ref, hot_ref, meta_ref, rows_ref, gate, up, sem, tok_sem, out_sem = refs[2 * zs + 6 :]
     filling, routes = fill(tok_ref, tokens, s_ref[1], tok, tok_sem, meta_ref)
     copies = load((gate_ref, up_ref), s_ref[0], count, (gate, up), sem)
     ready(routes)
     places(zs, tok, experts, meta_ref, place_ref, level_ref, s_ref[2])
     ready(filling)
-    dispatch(rows, experts, group, place_ref, tok_ref, hot_ref, xin_ref)
-    forward(rows, count, s_ref[0], copies, xin_ref, (gate, up), au_ref)
-
-
-def x2_kernel(rows, count, s_ref, xin_ref, gate_ref, up_ref, au_ref, gate, up, sem):
-    copies = load((gate_ref, up_ref), s_ref[0], count, (gate, up), sem)
-    forward(rows, count, s_ref[0], copies, xin_ref, (gate, up), au_ref)
-
-
-def back_dots(rows, count, first, arrived, yin_ref, down, out_ref):
+    dispatch(rows, experts, group, place_ref, tok_ref, hot_ref, rows_ref)
+    leaving = pltpu.make_async_copy(rows_ref, xin_ref, out_sem)
+    leaving.start()
+    forward(rows, count, s_ref[0], copies, rows_ref, (gate, up), au_ref)
+    leaving.wait()
+
+
+def x2_kernel(rows, count, s_ref, xin_ref, gate_ref, up_ref, au_ref, xs, gate, up, sem):
+    arrived = load((xin_ref, gate_ref, up_ref), s_ref[0], count, (xs, gate, up), sem)
+    forward(rows, count, 0, arrived, xs, (gate, up), au_ref)
+
+
+def back_dots(count, first, arrived, ys, down, out_ref):
     def body(j):
-        y = expert_rows(yin_ref, rows, first + j)
         arrived(j)
-        out_ref[j] = lax.dot_general(y, down[j], NT, preferred_element_type=F32).astype(out_ref.dtype)
+        out_ref[j] = lax.dot_general(ys[first + j], down[j], NT, preferred_element_type=F32).astype(out_ref.dtype)
 
     each(count, body)
 
@@ -226,26 +223,28 @@
 def y_kernel(cfg, count, s_ref, *refs):
     zs, tok, experts, rows, group = cfg
     tokens = refs[: 2 * zs]
-    place_ref, level_ref, down_ref, dh_ref, yin_ref, tok_ref, hot_ref, down, sem, tok_sem = refs[2 * zs :]
+    place_ref, level_ref, down_ref, dh_ref, yin_ref = refs[2 * zs : 2 * zs + 5]
+    tok_ref, hot_ref, rows_ref, down, sem, tok_sem, out_sem = refs[2 * zs + 5 :]
     filling, _ = fill(tok_ref, tokens, s_ref[1], tok, tok_sem)
     copies = load((down_ref,), s_ref[0], count, (down,), sem)
     ready(filling)
-    dispatch(rows, experts, group, place_ref, tok_ref, hot_ref, yin_ref, level_ref)
-    back_dots(rows, count, s_ref[0], copies, yin_ref, down, dh_ref)
-
-
-def y2_kernel(rows, counts, s_ref, yin_ref, down_ref, dh_ref, mine_ref, down, down_m, sem, sem_m):
-    copies = load((down_ref,), s_ref[0], counts[0], (down,), sem)
-    copies_m = load((down_ref,), s_ref[1], counts[1], (down_m,), sem_m)
-    back_dots(rows, counts[0], s_ref[0], copies, yin_ref, down, dh_ref)
-    back_dots(rows, counts[1], s_ref[1], copies_m, yin_ref, down_m, mine_ref)
-
-
-def final_kernel(rows, scale, at, s_ref, au_m, dh_m, au_r, dh_r, d_ref, score_ref):
+    dispatch(rows, experts, group, place_ref, tok_ref, hot_ref, rows_ref, level_ref)
+    leaving = pltpu.make_async_copy(rows_ref, yin_ref, out_sem)
+    leaving.start()
+    back_dots(count, s_ref[0], copies, rows_ref, down, dh_ref)
+    leaving.wait()
+
+
+def y2_kernel(count, s_ref, yin_ref, down_ref, dh_ref, ys, down, sem):
+    arrived = load((yin_ref, down_ref), s_ref[0], count, (ys, down), sem)
+    back_dots(count, 0, arrived, ys, down, dh_ref)
+
+
+def final_kernel(rows, scale, at, off, s_ref, au_m, dh_m, au_r, dh_r, d_ref, score_ref):
     def body(j):
-        au = au_m[at + j] + au_r[j].astype(F32)
+        au = au_m[at + j] + au_r[at + j].astype(F32)
         a, u = au[0:rows], au[rows:]
-        dh = dh_m[at + j] + dh_r[j].astype(F32)
+        dh = dh_m[at + j] + dh_r[off + j].astype(F32)
         sig = jax.nn.sigmoid(a)
         act = a * sig
         channel = jnp.sum(act * u * dh, axis=0, keepdims=True)
@@ -266,17 +265,24 @@
     each(d_ref.shape[0], body)
 
 
-def mine_parts_kernel(rows, s_ref, d_ref, gate_ref, up_ref, part_ref, gate, up, sem):
-    arrived = load((gate_ref, up_ref), s_ref[0], d_ref.shape[0], (gate, up), sem)
-    gradient_rows(rows, d_ref, arrived, gate, up, part_ref)
-
-
-def combine_kernel(rows, zs, tok, half, at, count, s_ref, d_ref, gate_ref, up_ref, place_ref, *refs):
+def mine_parts_kernel(rows, sizes, s_ref, *refs):
+    n = len(sizes)
+    gate_ref, up_ref, part_ref, gate, up, sem = refs[n:]
+    arrived = load((gate_ref, up_ref), s_ref[0], sum(sizes), (gate, up), sem)
+    at = 0
+    for d_ref, size in zip(refs[:n], sizes):
+        gradient_rows(rows, d_ref, arrived, gate, up, part_ref, at)
+        at += size
+
+
+def combine_kernel(rows, zs, tok, half, at, count, last, s_ref, d_ref, gate_ref, up_ref, place_ref, *refs):
     first = s_ref[0] + at
     if at == 0:
         *mine_refs, acc, gate, up, part_ref, hot_ref, sem = refs
+    elif last:
+        acc_in, keep_ref, send_ref, gate, up, part_ref, hot_ref, acc, sem = refs
     else:
-        acc_in, keep_ref, send_ref, gate, up, part_ref, hot_ref, acc, sem = refs
+        acc_in, acc, gate, up, part_ref, hot_ref, sem = refs
     copies = load((gate_ref, up_ref), first, count, (gate, up), sem)
 
     def mark(start, e, n):
@@ -302,6 +308,8 @@
         acc[...] += total
         return
     acc[...] = total + acc_in[...]
+    if not last:
+        return
     side = s_ref[1]
     for d in range(zs):
         keep_ref[d] = acc[pl.ds(pl.multiple_of(2 * d * tok + side * tok, tok), tok), :]
@@ -352,7 +360,7 @@
             body,
             out_shape=outs,
             in_specs=[smem] + ins,
-            out_specs=jax.tree.map(lambda _: vmem, outs),
+            out_specs=jax.tree.map(lambda v: anywhere if v is rows_shape else vmem, outs),
             scratch_shapes=scratch,
             compiler_params=pltpu.CompilerParams(vmem_limit_bytes=VMEM_LIMIT),
             cost_estimate=pl.CostEstimate(flops=int(flops * COST * factor), bytes_accessed=int(moved * COST * factor), transcendentals=0),
@@ -367,9 +375,10 @@
         name="pack",
     )(jnp.stack([p]).astype(jnp.int32), tokens, expert_ids.T, slots.T, gates.T)
     x_own = [turn(loaded, d) for d in range(zs)]
-    x_other = [flip(v, "sub") for v in x_own]
     out_grad, _ = lax.optimization_barrier((out_grad, loaded))
     y_here = turn(out_grad, 0)
+    *x_own, y_here = lax.optimization_barrier((*x_own, y_here))
+    x_other = [flip(v, "sub") for v in x_own]
     wbytes = width * ff * 2
     flop = 2 * rows * width * ff
     dflop = 2 * experts * rows * all_tok * width
@@ -384,25 +393,26 @@
         return pltpu.VMEM((count, ff, width), BF16)
 
     place_shape = sds((experts, all_tok), F32)
-    rows_shape = sds((experts * rows, width), BF16)
+    rows_shape = pltpu.HBM((experts, rows, width), BF16)
+    rows_scratch = pltpu.VMEM((experts, rows, width), BF16)
     def pinned(*arrays):
         return tuple(pltpu.with_memory_space_constraint(v, pltpu.HBM) for v in arrays)
 
     weights = (anywhere, pinned(gate_weight, up_weight))
     down_weight, = pinned(down_weight)
-    au_first, xin, place, level = call(
-        functools.partial(x_kernel, cfg, first),
+    au_send, xin, place, level = call(
+        functools.partial(x_kernel, cfg, half),
         other0,
         s,
         [(anywhere, pinned(*x_own, *x_other)), weights],
-        [sds((first, 2 * rows, ff), BF16), rows_shape, place_shape, place_shape],
-        [tok_scratch, hot, pltpu.VMEM((2 * zs, ROUTE_ROWS, width), BF16), wide(first), wide(first)]
-        + [dma((2 * first,)), dma((4 * zs,))],
-        2 * first * flop + dflop,
-        2 * first * wbytes,
+        [sds((half, 2 * rows, ff), BF16), rows_shape, place_shape, place_shape],
+        [tok_scratch, hot, pltpu.VMEM((2 * zs, ROUTE_ROWS, width), BF16), rows_scratch, wide(half), wide(half)]
+        + [dma((2 * half,)), dma((4 * zs,)), dma],
+        2 * half * flop + dflop,
+        2 * half * wbytes,
         "x_first",
     )
-    y_here, au_first = lax.optimization_barrier((y_here, au_first))
+    y_here, au_send = lax.optimization_barrier((y_here, au_send))
     y_own = [y_here] + [shift(y_here, d) for d in range(1, zs)]
 
     def x_call(first, n, dtype, name, factor):
@@ -410,21 +420,18 @@
             functools.partial(x2_kernel, rows, n),
             first,
             s,
-            [(vmem, (xin,)), weights],
+            [(anywhere, pinned(xin)), weights],
             sds((n, 2 * rows, ff), dtype),
-            [wide(n), wide(n), dma((2 * n,))],
+            [pltpu.VMEM((n, rows, width), BF16), wide(n), wide(n), dma((3 * n,))],
             2 * n * flop,
             2 * n * wbytes,
             name,
             factor,
         )
 
-    au_rest = x_call(other0 + first, rest, BF16, "x_other", 1)
-    xin, au_rest = lax.optimization_barrier((xin, au_rest))
     au_mine = x_call(mine0, half, F32, "x_mine", MINE_COST)
-    au_recv = [flip(v, "dp") for v in (au_first, au_rest)]
+    au_recv = flip(au_send, "dp")
     *y_own, au_mine = lax.optimization_barrier((*y_own, au_mine))
-    place, au_recv[0] = lax.optimization_barrier((place, au_recv[0]))
     y_other = [flip(v, "sub") for v in y_own]
     dh_first, yin = call(
         functools.partial(y_kernel, cfg, first),
@@ -432,32 +439,41 @@
         s,
         [(anywhere, pinned(*y_own, *y_other)), (vmem, (place, level)), (anywhere, (down_weight,))],
         [sds((first, rows, ff), BF16), rows_shape],
-        [tok_scratch, hot, tall(first), dma((first,)), dma((2 * zs,))],
+        [tok_scratch, hot, rows_scratch, tall(first), dma((first,)), dma((2 * zs,)), dma],
         first * flop + dflop,
         first * wbytes,
         "y_first",
     )
-    yin, au_recv[1] = lax.optimization_barrier((yin, au_recv[1]))
-    dh_rest, dh_mine = call(
-        functools.partial(y2_kernel, rows, (rest, half)),
-        other0 + first,
-        mine0,
-        [(vmem, (yin,)), (anywhere, (down_weight,))],
-        [sds((rest, rows, ff), BF16), sds((half, rows, ff), F32)],
-        [tall(rest), tall(half), dma((rest,)), dma((half,))],
-        (rest + half) * flop,
-        (rest + half) * wbytes,
-        "y_rest",
-    )
+
+    def y_call(first, n, dtype, name):
+        return call(
+            functools.partial(y2_kernel, n),
+            first,
+            s,
+            [(anywhere, pinned(yin, down_weight))],
+            sds((n, rows, ff), dtype),
+            [pltpu.VMEM((n, rows, width), BF16), tall(n), dma((2 * n,))],
+            n * flop,
+            n * wbytes,
+            name,
+        )
+
+    yin, au_recv = lax.optimization_barrier((yin, au_recv))
+    dh_rest = y_call(other0 + first, rest, BF16, "y_other")
+    yin, dh_rest = lax.optimization_barrier((yin, dh_rest))
+    dh_mine = y_call(mine0, half, F32, "y_mine")
     dh_recv = [flip(v, "dp") for v in (dh_first, dh_rest)]
     scale = LOCAL_EXPERTS / (all_tok * TOPK)
-    given, back, scores = [], [], []
-    for k, n in enumerate(sizes):
+    last = 0
+    chunks = [(0, 0, first)] + [(1, at, n) for at, n in ((0, rest - last), (rest - last, last)) if n]
+    back, scores = [], []
+
+    def final_call(k, at, n):
         d, score = call(
-            functools.partial(final_kernel, rows, scale, k * first),
+            functools.partial(final_kernel, rows, scale, k * first + at, at),
             mine0,
             s,
-            [(vmem, (au_mine, dh_mine, au_recv[k], dh_recv[k]))],
+            [(vmem, (au_mine, dh_mine, au_recv, dh_recv[k]))],
             [sds((n, 2 * rows, ff), BF16), sds((n, 1, ff), F32)],
             [],
             n * rows * ff * 40,
@@ -465,12 +481,21 @@
             "final",
         )
         scores.append(score)
-        back.append(flip(d, "dp"))
-        part = call(
-            functools.partial(mine_parts_kernel, rows),
-            mine0 + k * first,
+        if k == 0:
+            sent, dh_recv[1] = lax.optimization_barrier((d, dh_recv[1]))
+        else:
+            sent = d
+        back.append(flip(sent, "dp"))
+        return d
+
+    def parts_call(start, ds):
+        counts = [d.shape[0] for d in ds]
+        n = sum(counts)
+        return call(
+            functools.partial(mine_parts_kernel, rows, counts),
+            mine0 + start,
             s,
-            [(vmem, (d,)), weights],
+            [(vmem, ds), weights],
             sds((n * rows, width), BF16),
             [wide(n), wide(n), dma((2 * n,))],
             2 * n * flop,
@@ -478,33 +503,39 @@
             "mine_parts",
             PART_COST,
         )
-        dh_mine, part = lax.optimization_barrier((dh_mine, part))
-        given.append(part)
+
+    given = [parts_call(0, [final_call(*chunks[0])])]
+    dh_mine, given[0] = lax.optimization_barrier((dh_mine, given[0]))
+    ds = []
+    for chunk in chunks[1:]:
+        ds.append(final_call(*chunk))
+        dh_mine, ds[-1] = lax.optimization_barrier((dh_mine, ds[-1]))
+    given.append(parts_call(first, ds))
     score = jnp.concatenate(scores, axis=0).reshape(half, ff)
     score_other = flip(score, "dp")
     acc_shape, zshape = (all_tok, width), (zs, tok, width)
-    for k, n in enumerate(sizes):
-        used = n + half * (k == 0)
+    for k, (part, at, n) in enumerate(chunks):
+        used, final = n + half * (k == 0), k == len(chunks) - 1
         given = call(
-            functools.partial(combine_kernel, rows, zs, tok, half, k * first, n),
+            functools.partial(combine_kernel, rows, zs, tok, half, part * first + at, n, final),
             other0,
             s,
             [(vmem, (back[k],)), weights, (vmem, (place, *given))],
-            sds(acc_shape, F32) if k == 0 else [sds(zshape, F32), sds(zshape, BF16)],
+            [sds(zshape, F32), sds(zshape, BF16)] if final else [sds(acc_shape, F32)],
             [wide(n), wide(n), pltpu.VMEM((n * rows, width), BF16), pltpu.VMEM((used * rows, all_tok), BF16)]
-            + ([] if k == 0 else [pltpu.VMEM(acc_shape, F32)])
+            + ([pltpu.VMEM(acc_shape, F32)] if final else [])
             + [dma((2 * n,))],
             2 * n * flop + 2 * used * rows * width * all_tok,
             2 * n * wbytes,
             "combine",
         )
-        given = [given] if k == 0 else given
+        if k == len(chunks) - 2:
+            *given, score_other = lax.optimization_barrier((*given, score_other))
+            scores = jnp.concatenate(
+                [jnp.where(p == 0, score, score_other), jnp.where(p == 0, score_other, score)], axis=0
+            )
     keep, send = given
     summed = (keep + flip(send, "sub").astype(F32)).astype(BF16)
-    summed, score_other = lax.optimization_barrier((summed, score_other))
-    scores = jnp.concatenate(
-        [jnp.where(p == 0, score, score_other), jnp.where(p == 0, score_other, score)], axis=0
-    )
     total = turn(summed[0], 0).astype(F32)
     for d in range(1, zs):
         total = total + turn(summed[d], -d).astype(F32)

time: 120 us -> 118 us (0.983)
  waiting for transfers between devices: 29.1 us -> 26 us
  Pallas kernels: 51.5 us -> 53.6 us
    ppermute x16 -> x15, waiting for transfers between devices: 13.5 us -> 9.35 us  [flip(): return lax.ppermute(v, axis, [(0, 1), (1, 0)])]
    ppermute x3, waiting for transfers between devices: 0.01 us -> 4.08 us  [shift(): return lax.ppermute(v, 'expert', [(i, (i + d) % zs) for i in range(zs)])]
    ppermute x9, waiting for transfers between devices: 15.6 us -> 12.6 us  [turn(): return lax.ppermute(v, ('expert', 'dp', 'sub'), pairs)]
    pallas_call x11, Pallas kernels: 49.7 us -> 51.8 us  [call(): pl.pallas_call(body, out_shape=outs, in_specs=[smem] + ins, out_specs=jax...]
    ppermute x16 -> x15, starting transfers between devices: 9.3 us -> 10 us  [flip(): return lax.ppermute(v, axis, [(0, 1), (1, 0)])]
  transfers between devices with their start and end apart: 28 -> 27, of which waited for: 13 -> 16; matrix products, arithmetic and copies ran while one was open for 1% -> 1% of each run, Pallas kernels for 38% -> 33%
where the time goes in v5:
time: 118 us; the launch traced here: 117 us
  Pallas kernels  53.6 us (45%)
  starting transfers between devices  34 us (29%)
  waiting for transfers between devices  26 us (22%)
  other arithmetic  1.82 us (2%)
    pallas_call x11, Pallas kernels, call(): pl.pallas_call(body, out_shape=outs, in_specs=[smem] + ins, out_specs=jax...  51.8 us
    ppermute x9, starting transfers between devices, turn(): return lax.ppermute(v, ('expert', 'dp', 'sub'), pairs)  19.9 us
    ppermute x9, waiting for transfers between devices, turn(): return lax.ppermute(v, ('expert', 'dp', 'sub'), pairs)  12.6 us
    ppermute x15, starting transfers between devices, flip(): return lax.ppermute(v, axis, [(0, 1), (1, 0)])  10 us
    ppermute x15, waiting for transfers between devices, flip(): return lax.ppermute(v, axis, [(0, 1), (1, 0)])  9.35 us
    ppermute x3, starting transfers between devices, shift(): return lax.ppermute(v, 'expert', [(i, (i + d) % zs) for i in range(zs)])  4.1 us
    ppermute x3, waiting for transfers between devices, shift(): return lax.ppermute(v, 'expert', [(i, (i + d) % zs) for i in range(zs)])  4.08 us
  transfers between devices with their start and end apart: 27, of which 16 were waited for; matrix products, arithmetic and copies ran while one was open for 1% of the time, Pallas kernels for 33%

profile of v5, /device:TPU:1, one launch (start us, length us, event | category | flops | bytes accessed | tf_op | source)
XLA Modules:
  0.0 117.4 jit_solution(3035731808341223336)
XLA Ops:
  0.6 1.7 %pack.1 = bf16[80,1024]{1,0:T(8,128)(2,1)} custom-call(s32[1]{0:T(128)} %bitcast.3.p_ref, bf16[64,1024]{1,0:T(8,128)(2,1)} %tokens_ref.1, s32[8,64]{1,0:T(8,128)} %bitcast.26, s32[8,64]{1,0:T(8,128)} %bitcast.27, f32[8,64]{1,0:T(8,128)} %bitcast.28), custom_call_target="tpu_custom_call" | custom-call | tf_op jit(solution)/shard_map/pack/pallas_call | solution.py:370
  2.4 5.6 %collective-permute-start.3 = (bf16[80,1024]{1,0:T(8,128)(2,1)}, bf16[80,1024]{1,0:T(8,128)(2,1)S(1)}, u32[]{:S(2)}, u32[]{:S(2)}) collective-permute-start(bf16[80,1024]{1,0:T(8,128)(2,1)} %pack.1), channel_id=1, source_target_pairs={{0,12},{1,14},{2,13},{3,15},{4,0},{5,2},{6,1},{7,3},{8,4},{9,6},{1... | collective-permute-start | bytes 491528 | tf_op jit(solution)/shard_map/ppermute | solution.py:343
  9.6 2.0 %collective-permute-start = (bf16[80,1024]{1,0:T(8,128)(2,1)}, bf16[80,1024]{1,0:T(8,128)(2,1)S(1)}, u32[]{:S(2)}, u32[]{:S(2)}) collective-permute-start(bf16[80,1024]{1,0:T(8,128)(2,1)} %pack.1), channel_id=1, source_target_pairs={{0,0},{1,2},{2,1},{3,3},{4,4},{5,6},{6,5},{7,7},{8,8},{9,10},{10,9... | collective-permute-start | bytes 491528 | tf_op jit(solution)/shard_map/ppermute | solution.py:343
  11.7 3.5 %collective-permute-start.4 = (bf16[64,1024]{1,0:T(8,128)(2,1)}, bf16[64,1024]{1,0:T(8,128)(2,1)S(1)}, u32[]{:S(2)}, u32[]{:S(2)}) collective-permute-start(bf16[64,1024]{1,0:T(8,128)(2,1)} %param.9), channel_id=1, source_target_pairs={{0,0},{1,2},{2,1},{3,3},{4,4},{5,6},{6,5},{7,7},{8,8},{9,10},{10,9... | collective-permute-start | bytes 393224 | tf_op jit(solution)/shard_map/ppermute | solution.py:343
  15.2 5.3 %collective-permute-done.4.refs_0_ = bf16[64,1024]{1,0:T(8,128)(2,1)S(1)} collective-permute-done((bf16[64,1024]{1,0:T(8,128)(2,1)}, bf16[64,1024]{1,0:T(8,128)(2,1)S(1)}, u32[]{:S(2)}, u32[]{:S(2)}) %collective-permute-start.4) | collective-permute-done | bytes 131104 | tf_op jit(solution)/shard_map/ppermute | solution.py:343
  25.8 8.3 %x_first.1 = (bf16[8,160,384]{2,1,0:T(8,128)(2,1)}, bf16[16,80,1024]{2,1,0:T(8,128)(2,1)}, f32[16,512]{1,0:T(8,128)S(1)}, f32[16,512]{1,0:T(8,128)S(1)}) custom-call(s32[3]{0:T(128)S(1)} %add_add_fusion.1.s_ref, bf16[80,1024]{1,0:T(8,128)(2,1)} %copy-done.5, bf16[80,1024]{1,0:T(8,128)(2,1)} %copy-done.4, bf16[80,1024]{1,0:T(8,128)(2,1)} %copy-done.3, ...), custom_call_target="tpu_custom_call" | custom-call | flops 2348810240 | bytes 12582912 | tf_op jit(solution)/shard_map/x_first/pallas_call | solution.py:359
  35.6 2.4 %collective-permute-start.10 = (bf16[64,1024]{1,0:T(8,128)(2,1)S(1)}, bf16[64,1024]{1,0:T(8,128)(2,1)S(1)}, u32[]{:S(2)}, u32[]{:S(2)}) collective-permute-start(bf16[64,1024]{1,0:T(8,128)(2,1)S(1)} %collective-permute-done.4.refs_0_), channel_id=1, source_target_pairs={{0,8},{4,12},{8,0},{12,4},{1,9},{5,13},{9,1},{13,5},{2,10},{6,14},... | collective-permute-start | bytes 393224 | tf_op jit(solution)/shard_map/ppermute | solution.py:346
  39.5 6.1 %x_mine.1.au_m = f32[8,160,384]{2,1,0:T(8,128)S(1)} custom-call(s32[3]{0:T(128)S(1)} %add_add_fusion.s_ref, bf16[16,80,1024]{2,1,0:T(8,128)(2,1)} %get-tuple-element.46.xin_ref, bf16[16,1024,384]{2,1,0:T(8,128)(2,1)} %gate_ref.5, bf16[16,1024,384]{2,1,0:T(8,128)(2,1)} %up_ref.5), custom_call_target="tpu_custom_call" | custom-call | flops 1006632960 | bytes 12582912 | tf_op jit(solution)/shard_map/x_mine/pallas_call | solution.py:359
  45.7 4.1 %collective-permute-done.10.refs_2_ = bf16[64,1024]{1,0:T(8,128)(2,1)S(1)} collective-permute-done((bf16[64,1024]{1,0:T(8,128)(2,1)S(1)}, bf16[64,1024]{1,0:T(8,128)(2,1)S(1)}, u32[]{:S(2)}, u32[]{:S(2)}) %collective-permute-start.10) | collective-permute-done | bytes 131104 | tf_op jit(solution)/shard_map/ppermute | solution.py:346
  52.9 5.8 %y_first.1 = (bf16[4,80,384]{2,1,0:T(8,128)(2,1)S(1)}, bf16[16,80,1024]{2,1,0:T(8,128)(2,1)}) custom-call(s32[3]{0:T(128)S(1)} %add_add_fusion.1.s_ref, bf16[64,1024]{1,0:T(8,128)(2,1)} %copy-done.10, bf16[64,1024]{1,0:T(8,128)(2,1)} %copy-done.13, bf16[64,1024]{1,0:T(8,128)(2,1)} %copy-done.12, bf16[64,1024]{1,0:T(8,128)(2,1)} %copy-done.11, ...), custom_call_target="tpu_custom_call" | custom-call | flops 1593835520 | bytes 3145728 | tf_op jit(solution)/shard_map/y_first/pallas_call | solution.py:359
  59.2 3.3 %y_other.1 = bf16[4,80,384]{2,1,0:T(8,128)(2,1)S(1)} custom-call(s32[3]{0:T(128)S(1)} %add_add_fusion.2.s_ref, bf16[16,80,1024]{2,1,0:T(8,128)(2,1)} %get-tuple-element.57.yin_ref, bf16[16,384,1024]{2,1,0:T(8,128)(2,1)} %down_ref.3), custom_call_target="tpu_custom_call" | custom-call | flops 251658240 | bytes 3145728 | tf_op jit(solution)/shard_map/y_other/pallas_call | solution.py:359
  63.7 4.9 %y_mine.1.dh_m = f32[8,80,384]{2,1,0:T(8,128)S(1)} custom-call(s32[3]{0:T(128)S(1)} %add_add_fusion.s_ref, bf16[16,80,1024]{2,1,0:T(8,128)(2,1)} %get-tuple-element.57.yin_ref, bf16[16,384,1024]{2,1,0:T(8,128)(2,1)} %down_ref.3), custom_call_target="tpu_custom_call" | custom-call | flops 503316480 | bytes 6291456 | tf_op jit(solution)/shard_map/y_mine/pallas_call | solution.py:359
  69.6 1.9 %collective-permute-done.18.dh_r = bf16[4,80,384]{2,1,0:T(8,128)(2,1)S(1)} collective-permute-done((bf16[4,80,384]{2,1,0:T(8,128)(2,1)S(1)}, bf16[4,80,384]{2,1,0:T(8,128)(2,1)S(1)}, u32[]{:S(2)}, u32[]{:S(2)}) %collective-permute-start.18) | collective-permute-done | bytes 245792 | tf_op jit(solution)/shard_map/ppermute | solution.py:334
  71.9 4.4 %mine_parts.2.refs_0_ = bf16[320,1024]{1,0:T(8,128)(2,1)S(1)} custom-call(s32[3]{0:T(128)S(1)} %add_add_fusion.s_ref, bf16[4,160,384]{2,1,0:T(8,128)(2,1)S(1)} %get-tuple-element.66.refs_0_, bf16[16,1024,384]{2,1,0:T(8,128)(2,1)} %gate_ref.5, bf16[16,1024,384]{2,1,0:T(8,128)(2,1)} %up_ref.5), custom_call_target="tpu_custom_call" | custom-call | flops 503316480 | bytes 6291456 | tf_op jit(solution)/shard_map/mine_parts/pallas_call | solution.py:359
  76.3 1.8 %final.3 = (bf16[4,160,384]{2,1,0:T(8,128)(2,1)}, f32[4,1,384]{2,1,0:T(1,128)S(1)}) custom-call(s32[3]{0:T(128)S(1)} %add_add_fusion.s_ref, f32[8,160,384]{2,1,0:T(8,128)S(1)} %x_mine.1.au_m, f32[8,80,384]{2,1,0:T(8,128)S(1)} %y_mine.1.dh_m, bf16[8,160,384]{2,1,0:T(8,128)(2,1)S(1)} %collective-permute-done.16.au_r, ...), custom_call_target="tpu_custom_call" | custom-call | flops 4915200 | bytes 3686400 | tf_op jit(solution)/shard_map/final/pallas_call | solution.py:359
  79.8 4.9 %mine_parts.3.refs_1_ = bf16[320,1024]{1,0:T(8,128)(2,1)S(1)} custom-call(s32[3]{0:T(128)S(1)} %add_add_fusion.3.s_ref, bf16[4,160,384]{2,1,0:T(8,128)(2,1)} %get-tuple-element.69.refs_0_, bf16[16,1024,384]{2,1,0:T(8,128)(2,1)} %gate_ref.5, bf16[16,1024,384]{2,1,0:T(8,128)(2,1)} %up_ref.5), custom_call_target="tpu_custom_call" | custom-call | flops 503316480 | bytes 6291456 | tf_op jit(solution)/shard_map/mine_parts/pallas_call | solution.py:359
  84.7 5.8 %combine.2.refs_0_ = f32[512,1024]{1,0:T(8,128)S(1)} custom-call(s32[3]{0:T(128)S(1)} %add_add_fusion.1.s_ref, bf16[4,160,384]{2,1,0:T(8,128)(2,1)} %collective-permute-done.19.d_ref, bf16[16,1024,384]{2,1,0:T(8,128)(2,1)} %gate_ref.5, bf16[16,1024,384]{2,1,0:T(8,128)(2,1)} %up_ref.5, f32[16,512]{1,0:T(8,128)S(1)} %get-tuple-element.52.refs_8_.place_ref, ...), custom_call_target="tpu_custom_call" | custom-call | flops 1509949440 | bytes 6291456 | tf_op jit(solution)/shard_map/combine/pallas_call | solution.py:359
  90.6 3.4 %collective-permute-done.20 = f32[8,384]{1,0:T(8,128)S(1)} collective-permute-done((f32[8,384]{1,0:T(8,128)S(1)}, f32[8,384]{1,0:T(8,128)S(1)}, u32[]{:S(2)}, u32[]{:S(2)}) %collective-permute-start.20) | collective-permute-done | bytes 12320 | tf_op jit(solution)/shard_map/ppermute | solution.py:334
  94.0 5.3 %combine.3 = (f32[4,64,1024]{2,1,0:T(8,128)S(1)}, bf16[4,64,1024]{2,1,0:T(8,128)(2,1)S(1)}) custom-call(s32[3]{0:T(128)S(1)} %add_add_fusion.1.s_ref, bf16[4,160,384]{2,1,0:T(8,128)(2,1)S(1)} %collective-permute-done.21.d_ref, bf16[16,1024,384]{2,1,0:T(8,128)(2,1)} %gate_ref.5, bf16[16,1024,384]{2,1,0:T(8,128)(2,1)} %up_ref.5, ...), custom_call_target="tpu_custom_call" | custom-call | flops 838860800 | bytes 6291456 | tf_op jit(solution)/shard_map/combine/pallas_call | solution.py:359
  99.3 2.0 %collective-permute-start.22 = (bf16[4,64,1024]{2,1,0:T(8,128)(2,1)S(1)}, bf16[4,64,1024]{2,1,0:T(8,128)(2,1)S(1)}, u32[]{:S(2)}, u32[]{:S(2)}) collective-permute-start(bf16[4,64,1024]{2,1,0:T(8,128)(2,1)S(1)} %get-tuple-element.73), channel_id=1, source_target_pairs={{0,1},{1,0},{2,3},{3,2},{4,5},{5,4},{6,7},{7,6},{8,9},{9,8},{10,11... | collective-permute-start | bytes 1572872 | tf_op jit(solution)/shard_map/ppermute | solution.py:334
  103.0 2.6 %collective-permute-start.23 = (bf16[64,1024]{1,0:T(8,128)(2,1)S(1)}, bf16[64,1024]{1,0:T(8,128)(2,1)S(1)}, u32[]{:S(2)}, u32[]{:S(2)}) collective-permute-start(bf16[64,1024]{1,0:T(8,128)(2,1)S(1)} %get-tuple-element.74), channel_id=1, source_target_pairs={{0,0},{1,2},{2,1},{3,3},{4,4},{5,6},{6,5},{7,7},{8,8},{9,10},{10,9... | collective-permute-start | bytes 393224 | tf_op jit(solution)/shard_map/ppermute | solution.py:343
  105.8 4.3 %collective-permute-start.24 = (bf16[64,1024]{1,0:T(8,128)(2,1)S(1)}, bf16[64,1024]{1,0:T(8,128)(2,1)S(1)}, u32[]{:S(2)}, u32[]{:S(2)}) collective-permute-start(bf16[64,1024]{1,0:T(8,128)(2,1)S(1)} %get-tuple-element.77), channel_id=1, source_target_pairs={{0,12},{1,14},{2,13},{3,15},{4,0},{5,2},{6,1},{7,3},{8,4},{9,6},{1... | collective-permute-start | bytes 393224 | tf_op jit(solution)/shard_map/ppermute | solution.py:343
  110.7 3.0 %collective-permute-done.26 = bf16[64,1024]{1,0:T(8,128)(2,1)S(1)} collective-permute-done((bf16[64,1024]{1,0:T(8,128)(2,1)S(1)}, bf16[64,1024]{1,0:T(8,128)(2,1)S(1)}, u32[]{:S(2)}, u32[]{:S(2)}) %collective-permute-start.26) | collective-permute-done | bytes 131104 | tf_op jit(solution)/shard_map/ppermute | solution.py:343
  113.7 2.9 %collective-permute-done.25 = bf16[64,1024]{1,0:T(8,128)(2,1)S(1)} collective-permute-done((bf16[64,1024]{1,0:T(8,128)(2,1)S(1)}, bf16[64,1024]{1,0:T(8,128)(2,1)S(1)}, u32[]{:S(2)}, u32[]{:S(2)}) %collective-permute-start.25) | collective-permute-done | bytes 131104 | tf_op jit(solution)/shard_map/ppermute | solution.py:343
  (81 shorter events, 20.9 us)
Async XLA Ops:
  2.4 18.1 %collective-permute-start.3 = (bf16[80,1024]{1,0:T(8,128)(2,1)}, bf16[80,1024]{1,0:T(8,128)(2,1)S(1)}, u32[]{:S(2)}, u32[]{:S(2)}) collective-permute-start(bf16[80,1024]{1,0:T(8,128)(2,1)} %pack.1), channel_id=1, source_target_pairs={{0,12},{1,14},{2,13},{3,15},{4,0},{5,2},{6,1},{7,3},{8,4},{9,6},{1... | collective-permute-start | bytes 491528 | tf_op jit(solution)/shard_map/ppermute | solution.py:343
  8.0 13.8 %collective-permute-start.2 = (bf16[80,1024]{1,0:T(8,128)(2,1)}, bf16[80,1024]{1,0:T(8,128)(2,1)S(1)}, u32[]{:S(2)}, u32[]{:S(2)}) collective-permute-start(bf16[80,1024]{1,0:T(8,128)(2,1)} %pack.1), channel_id=1, source_target_pairs={{0,8},{1,10},{2,9},{3,11},{4,12},{5,14},{6,13},{7,15},{8,0},{9,2},... | collective-permute-start | bytes 491528 | tf_op jit(solution)/shard_map/ppermute | solution.py:343
  8.0 13.8 %collective-permute-start.1 = (bf16[80,1024]{1,0:T(8,128)(2,1)}, bf16[80,1024]{1,0:T(8,128)(2,1)S(1)}, u32[]{:S(2)}, u32[]{:S(2)}) collective-permute-start(bf16[80,1024]{1,0:T(8,128)(2,1)} %pack.1), channel_id=1, source_target_pairs={{0,4},{1,6},{2,5},{3,7},{4,8},{5,10},{6,9},{7,11},{8,12},{9,14},{1... | collective-permute-start | bytes 491528 | tf_op jit(solution)/shard_map/ppermute | solution.py:343
  9.6 12.2 %collective-permute-start = (bf16[80,1024]{1,0:T(8,128)(2,1)}, bf16[80,1024]{1,0:T(8,128)(2,1)S(1)}, u32[]{:S(2)}, u32[]{:S(2)}) collective-permute-start(bf16[80,1024]{1,0:T(8,128)(2,1)} %pack.1), channel_id=1, source_target_pairs={{0,0},{1,2},{2,1},{3,3},{4,4},{5,6},{6,5},{7,7},{8,8},{9,10},{10,9... | collective-permute-start | bytes 491528 | tf_op jit(solution)/shard_map/ppermute | solution.py:343
  11.7 8.8 %collective-permute-start.4 = (bf16[64,1024]{1,0:T(8,128)(2,1)}, bf16[64,1024]{1,0:T(8,128)(2,1)S(1)}, u32[]{:S(2)}, u32[]{:S(2)}) collective-permute-start(bf16[64,1024]{1,0:T(8,128)(2,1)} %param.9), channel_id=1, source_target_pairs={{0,0},{1,2},{2,1},{3,3},{4,4},{5,6},{6,5},{7,7},{8,8},{9,10},{10,9... | collective-permute-start | bytes 393224 | tf_op jit(solution)/shard_map/ppermute | solution.py:343
  21.8 2.0 %collective-permute-start.5 = (bf16[80,1024]{1,0:T(8,128)(2,1)S(1)}, bf16[80,1024]{1,0:T(8,128)(2,1)S(1)}, u32[]{:S(2)}, u32[]{:S(2)}) collective-permute-start(bf16[80,1024]{1,0:T(8,128)(2,1)S(1)} %collective-permute-done.refs_0_), channel_id=1, source_target_pairs={{0,1},{1,0},{2,3},{3,2},{4,5},{5,4},{6,7},{7,6},{8,9},{9,8},{10,11... | collective-permute-start | bytes 491528 | tf_op jit(solution)/shard_map/ppermute | solution.py:334
  22.9 1.6 %collective-permute-start.7 = (bf16[80,1024]{1,0:T(8,128)(2,1)S(1)}, bf16[80,1024]{1,0:T(8,128)(2,1)S(1)}, u32[]{:S(2)}, u32[]{:S(2)}) collective-permute-start(bf16[80,1024]{1,0:T(8,128)(2,1)S(1)} %collective-permute-done.2.refs_2_), channel_id=1, source_target_pairs={{0,1},{1,0},{2,3},{3,2},{4,5},{5,4},{6,7},{7,6},{8,9},{9,8},{10,11... | collective-permute-start | bytes 491528 | tf_op jit(solution)/shard_map/ppermute | solution.py:334
  34.1 25.1 %collective-permute-start.16 = (bf16[8,160,384]{2,1,0:T(8,128)(2,1)}, bf16[8,160,384]{2,1,0:T(8,128)(2,1)S(1)}, u32[]{:S(2)}, u32[]{:S(2)}) collective-permute-start(bf16[8,160,384]{2,1,0:T(8,128)(2,1)} %get-tuple-element.55), channel_id=1, source_target_pairs={{0,2},{2,0},{1,3},{3,1},{4,6},{6,4},{5,7},{7,5},{8,10},{10,8},{9,1... | collective-permute-start | bytes 2949128 | tf_op jit(solution)/shard_map/ppermute | solution.py:334
  35.3 10.3 %collective-permute-start.11 = (bf16[64,1024]{1,0:T(8,128)(2,1)S(1)}, bf16[64,1024]{1,0:T(8,128)(2,1)S(1)}, u32[]{:S(2)}, u32[]{:S(2)}) collective-permute-start(bf16[64,1024]{1,0:T(8,128)(2,1)S(1)} %collective-permute-done.4.refs_0_), channel_id=1, source_target_pairs={{0,12},{4,0},{8,4},{12,8},{1,13},{5,1},{9,5},{13,9},{2,14},{6,2},{... | collective-permute-start | bytes 393224 | tf_op jit(solution)/shard_map/ppermute | solution.py:346
  35.6 14.2 %collective-permute-start.10 = (bf16[64,1024]{1,0:T(8,128)(2,1)S(1)}, bf16[64,1024]{1,0:T(8,128)(2,1)S(1)}, u32[]{:S(2)}, u32[]{:S(2)}) collective-permute-start(bf16[64,1024]{1,0:T(8,128)(2,1)S(1)} %collective-permute-done.4.refs_0_), channel_id=1, source_target_pairs={{0,8},{4,12},{8,0},{12,4},{1,9},{5,13},{9,1},{13,5},{2,10},{6,14},... | collective-permute-start | bytes 393224 | tf_op jit(solution)/shard_map/ppermute | solution.py:346
  38.0 11.8 %collective-permute-start.9 = (bf16[64,1024]{1,0:T(8,128)(2,1)S(1)}, bf16[64,1024]{1,0:T(8,128)(2,1)S(1)}, u32[]{:S(2)}, u32[]{:S(2)}) collective-permute-start(bf16[64,1024]{1,0:T(8,128)(2,1)S(1)} %collective-permute-done.4.refs_0_), channel_id=1, source_target_pairs={{0,4},{4,8},{8,12},{12,0},{1,5},{5,9},{9,13},{13,1},{2,6},{6,10},{... | collective-permute-start | bytes 393224 | tf_op jit(solution)/shard_map/ppermute | solution.py:346
  49.8 2.3 %collective-permute-start.12 = (bf16[64,1024]{1,0:T(8,128)(2,1)S(1)}, bf16[64,1024]{1,0:T(8,128)(2,1)}, u32[]{:S(2)}, u32[]{:S(2)}) collective-permute-start(bf16[64,1024]{1,0:T(8,128)(2,1)S(1)} %collective-permute-done.4.refs_0_), channel_id=1, source_target_pairs={{0,1},{1,0},{2,3},{3,2},{4,5},{5,4},{6,7},{7,6},{8,9},{9,8},{10,11... | collective-permute-start | bytes 393224 | tf_op jit(solution)/shard_map/ppermute | solution.py:334
  50.9 1.5 %collective-permute-start.13 = (bf16[64,1024]{1,0:T(8,128)(2,1)S(1)}, bf16[64,1024]{1,0:T(8,128)(2,1)}, u32[]{:S(2)}, u32[]{:S(2)}) collective-permute-start(bf16[64,1024]{1,0:T(8,128)(2,1)S(1)} %collective-permute-done.9.refs_1_), channel_id=1, source_target_pairs={{0,1},{1,0},{2,3},{3,2},{4,5},{5,4},{6,7},{7,6},{8,9},{9,8},{10,11... | collective-permute-start | bytes 393224 | tf_op jit(solution)/shard_map/ppermute | solution.py:334
  51.0 1.6 %collective-permute-start.14 = (bf16[64,1024]{1,0:T(8,128)(2,1)S(1)}, bf16[64,1024]{1,0:T(8,128)(2,1)}, u32[]{:S(2)}, u32[]{:S(2)}) collective-permute-start(bf16[64,1024]{1,0:T(8,128)(2,1)S(1)} %collective-permute-done.10.refs_2_), channel_id=1, source_target_pairs={{0,1},{1,0},{2,3},{3,2},{4,5},{5,4},{6,7},{7,6},{8,9},{9,8},{10,11... | collective-permute-start | bytes 393224 | tf_op jit(solution)/shard_map/ppermute | solution.py:334
  58.7 9.9 %collective-permute-start.17 = (bf16[4,80,384]{2,1,0:T(8,128)(2,1)S(1)}, bf16[4,80,384]{2,1,0:T(8,128)(2,1)S(1)}, u32[]{:S(2)}, u32[]{:S(2)}) collective-permute-start(bf16[4,80,384]{2,1,0:T(8,128)(2,1)S(1)} %get-tuple-element.59), channel_id=1, source_target_pairs={{0,2},{2,0},{1,3},{3,1},{4,6},{6,4},{5,7},{7,5},{8,10},{10,8},{9,1... | collective-permute-start | bytes 737288 | tf_op jit(solution)/shard_map/ppermute | solution.py:334
  62.6 8.9 %collective-permute-start.18 = (bf16[4,80,384]{2,1,0:T(8,128)(2,1)S(1)}, bf16[4,80,384]{2,1,0:T(8,128)(2,1)S(1)}, u32[]{:S(2)}, u32[]{:S(2)}) collective-permute-start(bf16[4,80,384]{2,1,0:T(8,128)(2,1)S(1)} %y_other.1), channel_id=1, source_target_pairs={{0,2},{2,0},{1,3},{3,1},{4,6},{6,4},{5,7},{7,5},{8,10},{10,8},{9,1... | collective-permute-start | bytes 737288 | tf_op jit(solution)/shard_map/ppermute | solution.py:334
  71.5 13.3 %collective-permute-start.19 = (bf16[4,160,384]{2,1,0:T(8,128)(2,1)S(1)}, bf16[4,160,384]{2,1,0:T(8,128)(2,1)}, u32[]{:S(2)}, u32[]{:S(2)}) collective-permute-start(bf16[4,160,384]{2,1,0:T(8,128)(2,1)S(1)} %get-tuple-element.66.refs_0_), channel_id=1, source_target_pairs={{0,2},{2,0},{1,3},{3,1},{4,6},{6,4},{5,7},{7,5},{8,10},{10,8},{9,1... | collective-permute-start | bytes 1474568 | tf_op jit(solution)/shard_map/ppermute | solution.py:334
  78.1 15.9 %collective-permute-start.21 = (bf16[4,160,384]{2,1,0:T(8,128)(2,1)}, bf16[4,160,384]{2,1,0:T(8,128)(2,1)S(1)}, u32[]{:S(2)}, u32[]{:S(2)}) collective-permute-start(bf16[4,160,384]{2,1,0:T(8,128)(2,1)} %get-tuple-element.69.refs_0_), channel_id=1, source_target_pairs={{0,2},{2,0},{1,3},{3,1},{4,6},{6,4},{5,7},{7,5},{8,10},{10,8},{9,1... | collective-permute-start | bytes 1474568 | tf_op jit(solution)/shard_map/ppermute | solution.py:334
  79.3 14.7 %collective-permute-start.20 = (f32[8,384]{1,0:T(8,128)S(1)}, f32[8,384]{1,0:T(8,128)S(1)}, u32[]{:S(2)}, u32[]{:S(2)}) collective-permute-start(f32[8,384]{1,0:T(8,128)S(1)} %bitcast.25), channel_id=1, source_target_pairs={{0,2},{2,0},{1,3},{3,1},{4,6},{6,4},{5,7},{7,5},{8,10},{10,8},{9,1... | collective-permute-start | bytes 36872 | tf_op jit(solution)/shard_map/ppermute | solution.py:334
  99.3 3.5 %collective-permute-start.22 = (bf16[4,64,1024]{2,1,0:T(8,128)(2,1)S(1)}, bf16[4,64,1024]{2,1,0:T(8,128)(2,1)S(1)}, u32[]{:S(2)}, u32[]{:S(2)}) collective-permute-start(bf16[4,64,1024]{2,1,0:T(8,128)(2,1)S(1)} %get-tuple-element.73), channel_id=1, source_target_pairs={{0,1},{1,0},{2,3},{3,2},{4,5},{5,4},{6,7},{7,6},{8,9},{9,8},{10,11... | collective-permute-start | bytes 1572872 | tf_op jit(solution)/shard_map/ppermute | solution.py:334
  103.0 7.7 %collective-permute-start.23 = (bf16[64,1024]{1,0:T(8,128)(2,1)S(1)}, bf16[64,1024]{1,0:T(8,128)(2,1)S(1)}, u32[]{:S(2)}, u32[]{:S(2)}) collective-permute-start(bf16[64,1024]{1,0:T(8,128)(2,1)S(1)} %get-tuple-element.74), channel_id=1, source_target_pairs={{0,0},{1,2},{2,1},{3,3},{4,4},{5,6},{6,5},{7,7},{8,8},{9,10},{10,9... | collective-permute-start | bytes 393224 | tf_op jit(solution)/shard_map/ppermute | solution.py:343
  105.6 8.1 %collective-permute-start.26 = (bf16[64,1024]{1,0:T(8,128)(2,1)S(1)}, bf16[64,1024]{1,0:T(8,128)(2,1)S(1)}, u32[]{:S(2)}, u32[]{:S(2)}) collective-permute-start(bf16[64,1024]{1,0:T(8,128)(2,1)S(1)} %get-tuple-element.75), channel_id=1, source_target_pairs={{0,4},{1,6},{2,5},{3,7},{4,8},{5,10},{6,9},{7,11},{8,12},{9,14},{1... | collective-permute-start | bytes 393224 | tf_op jit(solution)/shard_map/ppermute | solution.py:343
  105.6 11.0 %collective-permute-start.25 = (bf16[64,1024]{1,0:T(8,128)(2,1)S(1)}, bf16[64,1024]{1,0:T(8,128)(2,1)S(1)}, u32[]{:S(2)}, u32[]{:S(2)}) collective-permute-start(bf16[64,1024]{1,0:T(8,128)(2,1)S(1)} %get-tuple-element.76), channel_id=1, source_target_pairs={{0,8},{1,10},{2,9},{3,11},{4,12},{5,14},{6,13},{7,15},{8,0},{9,2},... | collective-permute-start | bytes 393224 | tf_op jit(solution)/shard_map/ppermute | solution.py:343
  105.8 10.9 %collective-permute-start.24 = (bf16[64,1024]{1,0:T(8,128)(2,1)S(1)}, bf16[64,1024]{1,0:T(8,128)(2,1)S(1)}, u32[]{:S(2)}, u32[]{:S(2)}) collective-permute-start(bf16[64,1024]{1,0:T(8,128)(2,1)S(1)} %get-tuple-element.77), channel_id=1, source_target_pairs={{0,12},{1,14},{2,13},{3,15},{4,0},{5,2},{6,1},{7,3},{8,4},{9,6},{1... | collective-permute-start | bytes 393224 | tf_op jit(solution)/shard_map/ppermute | solution.py:343
  (17 other events, 70.2 us)

commit v6 on v5

--- a/solution.py
+++ b/solution.py
@@ -62,7 +62,6 @@
     return (scores, token_grad.astype(BF16))
 
 
-MINE_COST = 1
 PART_COST = 1
 COST = 1.0
 
@@ -140,11 +139,11 @@
     return copies, routes
 
 
-def dispatch(rows, experts, group, place_ref, tok_ref, hot_ref, out_ref, level_ref=None):
+def dispatch(rows, first, count, group, place_ref, tok_ref, hot_ref, out_ref, level_ref=None):
     def body(g, carry):
         levels = []
         for j in range(group):
-            e = g * group + j
+            e = first + g * group + j
             hot = one_hot(rows, place_ref[pl.ds(e, 1), :])
             hot_ref[pl.ds(j * rows, rows), :] = hot.astype(BF16)
             if level_ref is not None:
@@ -155,7 +154,7 @@
         out_ref[pl.ds(g * group, group)] = got.astype(BF16).reshape(group, rows, got.shape[1])
         return carry
 
-    lax.fori_loop(0, experts // group, body, 0)
+    lax.fori_loop(0, count // group, body, 0)
 
 
 def places(zs, tok, experts, meta_ref, place_ref, level_ref, first):
@@ -193,23 +192,25 @@
 def x_kernel(cfg, count, s_ref, *refs):
     zs, tok, experts, rows, group = cfg
     tokens = refs[: 2 * zs]
-    gate_ref, up_ref, au_ref, xin_ref, place_ref, level_ref = refs[2 * zs : 2 * zs + 6]
-    tok_ref, hot_ref, meta_ref, rows_ref, gate, up, sem, tok_sem, out_sem = refs[2 * zs + 6 :]
+    gate_ref, up_ref, au_ref, place_ref, level_ref = refs[2 * zs : 2 * zs + 5]
+    tok_ref, hot_ref, meta_ref, rows_ref, gate, up, sem, tok_sem = refs[2 * zs + 5 :]
     filling, routes = fill(tok_ref, tokens, s_ref[1], tok, tok_sem, meta_ref)
     copies = load((gate_ref, up_ref), s_ref[0], count, (gate, up), sem)
     ready(routes)
     places(zs, tok, experts, meta_ref, place_ref, level_ref, s_ref[2])
     ready(filling)
-    dispatch(rows, experts, group, place_ref, tok_ref, hot_ref, rows_ref)
-    leaving = pltpu.make_async_copy(rows_ref, xin_ref, out_sem)
-    leaving.start()
-    forward(rows, count, s_ref[0], copies, rows_ref, (gate, up), au_ref)
-    leaving.wait()
-
-
-def x2_kernel(rows, count, s_ref, xin_ref, gate_ref, up_ref, au_ref, xs, gate, up, sem):
-    arrived = load((xin_ref, gate_ref, up_ref), s_ref[0], count, (xs, gate, up), sem)
-    forward(rows, count, 0, arrived, xs, (gate, up), au_ref)
+    dispatch(rows, s_ref[0], count, group, place_ref, tok_ref, hot_ref, rows_ref)
+    forward(rows, count, 0, copies, rows_ref, (gate, up), au_ref)
+
+
+def x2_kernel(cfg, count, s_ref, *refs):
+    zs, tok, experts, rows, group = cfg
+    place_ref, gate_ref, up_ref, au_ref, tok_ref, hot_ref, rows_ref, gate, up, sem, tok_sem = refs[2 * zs :]
+    filling, _ = fill(tok_ref, refs[: 2 * zs], s_ref[1], tok, tok_sem)
+    copies = load((gate_ref, up_ref), s_ref[0], count, (gate, up), sem)
+    ready(filling)
+    dispatch(rows, s_ref[0], count, group, place_ref, tok_ref, hot_ref, rows_ref)
+    forward(rows, count, 0, copies, rows_ref, (gate, up), au_ref)
 
 
 def back_dots(count, first, arrived, ys, down, out_ref):
@@ -228,7 +229,7 @@
     filling, _ = fill(tok_ref, tokens, s_ref[1], tok, tok_sem)
     copies = load((down_ref,), s_ref[0], count, (down,), sem)
     ready(filling)
-    dispatch(rows, experts, group, place_ref, tok_ref, hot_ref, rows_ref, level_ref)
+    dispatch(rows, 0, experts, group, place_ref, tok_ref, hot_ref, rows_ref, level_ref)
     leaving = pltpu.make_async_copy(rows_ref, yin_ref, out_sem)
     leaving.start()
     back_dots(count, s_ref[0], copies, rows_ref, down, dh_ref)
@@ -323,7 +324,7 @@
     rows = 2 * zs * CAP
     all_tok = 2 * zs * tok
     half = experts // 2
-    group = 4 if experts % 4 == 0 else 1
+    group = 4 if half % 4 == 0 else 1
     p, s, z = lax.axis_index("dp"), lax.axis_index("sub"), lax.axis_index("expert")
     mine0, other0 = half * p, half * (1 - p)
     first = half // 2
@@ -394,42 +395,39 @@
 
     place_shape = sds((experts, all_tok), F32)
     rows_shape = pltpu.HBM((experts, rows, width), BF16)
+    half_rows = pltpu.VMEM((half, rows, width), BF16)
     rows_scratch = pltpu.VMEM((experts, rows, width), BF16)
     def pinned(*arrays):
         return tuple(pltpu.with_memory_space_constraint(v, pltpu.HBM) for v in arrays)
 
     weights = (anywhere, pinned(gate_weight, up_weight))
     down_weight, = pinned(down_weight)
-    au_send, xin, place, level = call(
+    au_send, place, level = call(
         functools.partial(x_kernel, cfg, half),
         other0,
         s,
         [(anywhere, pinned(*x_own, *x_other)), weights],
-        [sds((half, 2 * rows, ff), BF16), rows_shape, place_shape, place_shape],
-        [tok_scratch, hot, pltpu.VMEM((2 * zs, ROUTE_ROWS, width), BF16), rows_scratch, wide(half), wide(half)]
-        + [dma((2 * half,)), dma((4 * zs,)), dma],
-        2 * half * flop + dflop,
+        [sds((half, 2 * rows, ff), BF16), place_shape, place_shape],
+        [tok_scratch, hot, pltpu.VMEM((2 * zs, ROUTE_ROWS, width), BF16), half_rows, wide(half), wide(half)]
+        + [dma((2 * half,)), dma((4 * zs,))],
+        2 * half * flop + dflop // 2,
         2 * half * wbytes,
         "x_first",
     )
     y_here, au_send = lax.optimization_barrier((y_here, au_send))
     y_own = [y_here] + [shift(y_here, d) for d in range(1, zs)]
 
-    def x_call(first, n, dtype, name, factor):
-        return call(
-            functools.partial(x2_kernel, rows, n),
-            first,
-            s,
-            [(anywhere, pinned(xin)), weights],
-            sds((n, 2 * rows, ff), dtype),
-            [pltpu.VMEM((n, rows, width), BF16), wide(n), wide(n), dma((3 * n,))],
-            2 * n * flop,
-            2 * n * wbytes,
-            name,
-            factor,
-        )
-
-    au_mine = x_call(mine0, half, F32, "x_mine", MINE_COST)
+    au_mine = call(
+        functools.partial(x2_kernel, cfg, half),
+        mine0,
+        s,
+        [(anywhere, pinned(*x_own, *x_other)), (vmem, (place,)), weights],
+        sds((half, 2 * rows, ff), F32),
+        [tok_scratch, hot, half_rows, wide(half), wide(half), dma((2 * half,)), dma((2 * zs,))],
+        2 * half * flop + dflop // 2,
+        2 * half * wbytes,
+        "x_mine",
+    )
     au_recv = flip(au_send, "dp")
     *y_own, au_mine = lax.optimization_barrier((*y_own, au_mine))
     y_other = [flip(v, "sub") for v in y_own]

time: 118 us -> 117 us (level)
  no operation moved by 1% of the time
where the time goes in v6:
time: 117 us; the launch traced here: 116 us
  Pallas kernels  52.5 us (45%)
  starting transfers between devices  34 us (29%)
  waiting for transfers between devices  26.1 us (22%)
  other arithmetic  1.82 us (2%)
    pallas_call x11, Pallas kernels, call(): pl.pallas_call(body, out_shape=outs, in_specs=[smem] + ins, out_specs=jax...  50.8 us
    ppermute x9, starting transfers between devices, turn(): return lax.ppermute(v, ('expert', 'dp', 'sub'), pairs)  19.9 us
    ppermute x9, waiting for transfers between devices, turn(): return lax.ppermute(v, ('expert', 'dp', 'sub'), pairs)  12.6 us
    ppermute x15, starting transfers between devices, flip(): return lax.ppermute(v, axis, [(0, 1), (1, 0)])  10 us
    ppermute x15, waiting for transfers between devices, flip(): return lax.ppermute(v, axis, [(0, 1), (1, 0)])  9.35 us
    ppermute x3, waiting for transfers between devices, shift(): return lax.ppermute(v, 'expert', [(i, (i + d) % zs) for i in range(zs)])  4.15 us
    ppermute x3, starting transfers between devices, shift(): return lax.ppermute(v, 'expert', [(i, (i + d) % zs) for i in range(zs)])  4.1 us
  transfers between devices with their start and end apart: 27, of which 16 were waited for; matrix products, arithmetic and copies ran while one was open for 1% of the time, Pallas kernels for 33%

profile of v6, /device:TPU:1, one launch (start us, length us, event | category | flops | bytes accessed | tf_op | source)
XLA Modules:
  0.0 116.4 jit_solution(5594262092580765271)
XLA Ops:
  0.6 1.7 %pack.1 = bf16[80,1024]{1,0:T(8,128)(2,1)} custom-call(s32[1]{0:T(128)} %bitcast.3.p_ref, bf16[64,1024]{1,0:T(8,128)(2,1)} %tokens_ref.1, s32[8,64]{1,0:T(8,128)} %bitcast.26, s32[8,64]{1,0:T(8,128)} %bitcast.27, f32[8,64]{1,0:T(8,128)} %bitcast.28), custom_call_target="tpu_custom_call" | custom-call | tf_op jit(solution)/shard_map/pack/pallas_call | solution.py:371
  2.4 5.6 %collective-permute-start.3 = (bf16[80,1024]{1,0:T(8,128)(2,1)}, bf16[80,1024]{1,0:T(8,128)(2,1)S(1)}, u32[]{:S(2)}, u32[]{:S(2)}) collective-permute-start(bf16[80,1024]{1,0:T(8,128)(2,1)} %pack.1), channel_id=1, source_target_pairs={{0,12},{1,14},{2,13},{3,15},{4,0},{5,2},{6,1},{7,3},{8,4},{9,6},{1... | collective-permute-start | bytes 491528 | tf_op jit(solution)/shard_map/ppermute | solution.py:344
  9.6 2.0 %collective-permute-start = (bf16[80,1024]{1,0:T(8,128)(2,1)}, bf16[80,1024]{1,0:T(8,128)(2,1)S(1)}, u32[]{:S(2)}, u32[]{:S(2)}) collective-permute-start(bf16[80,1024]{1,0:T(8,128)(2,1)} %pack.1), channel_id=1, source_target_pairs={{0,0},{1,2},{2,1},{3,3},{4,4},{5,6},{6,5},{7,7},{8,8},{9,10},{10,9... | collective-permute-start | bytes 491528 | tf_op jit(solution)/shard_map/ppermute | solution.py:344
  11.7 3.5 %collective-permute-start.4 = (bf16[64,1024]{1,0:T(8,128)(2,1)}, bf16[64,1024]{1,0:T(8,128)(2,1)S(1)}, u32[]{:S(2)}, u32[]{:S(2)}) collective-permute-start(bf16[64,1024]{1,0:T(8,128)(2,1)} %param.9), channel_id=1, source_target_pairs={{0,0},{1,2},{2,1},{3,3},{4,4},{5,6},{6,5},{7,7},{8,8},{9,10},{10,9... | collective-permute-start | bytes 393224 | tf_op jit(solution)/shard_map/ppermute | solution.py:344
  15.2 5.3 %collective-permute-done.4.refs_0_ = bf16[64,1024]{1,0:T(8,128)(2,1)S(1)} collective-permute-done((bf16[64,1024]{1,0:T(8,128)(2,1)}, bf16[64,1024]{1,0:T(8,128)(2,1)S(1)}, u32[]{:S(2)}, u32[]{:S(2)}) %collective-permute-start.4) | collective-permute-done | bytes 131104 | tf_op jit(solution)/shard_map/ppermute | solution.py:344
  25.7 7.3 %x_first.1 = (bf16[8,160,384]{2,1,0:T(8,128)(2,1)}, f32[16,512]{1,0:T(8,128)S(1)}, f32[16,512]{1,0:T(8,128)S(1)}) custom-call(s32[3]{0:T(128)S(1)} %add_add_fusion.1.s_ref, bf16[80,1024]{1,0:T(8,128)(2,1)} %copy-done.5, bf16[80,1024]{1,0:T(8,128)(2,1)} %copy-done.4, bf16[80,1024]{1,0:T(8,128)(2,1)} %copy-done.3, bf16[80,1024]{1,0:T(8,128)(2,1)} %copy-done.2, ...), custom_call_target="tpu_custom_call" | custom-call | flops 1677721600 | bytes 12582912 | tf_op jit(solution)/shard_map/x_first/pallas_call | solution.py:360
  34.6 2.5 %collective-permute-start.10 = (bf16[64,1024]{1,0:T(8,128)(2,1)S(1)}, bf16[64,1024]{1,0:T(8,128)(2,1)S(1)}, u32[]{:S(2)}, u32[]{:S(2)}) collective-permute-start(bf16[64,1024]{1,0:T(8,128)(2,1)S(1)} %collective-permute-done.4.refs_0_), channel_id=1, source_target_pairs={{0,8},{4,12},{8,0},{12,4},{1,9},{5,13},{9,1},{13,5},{2,10},{6,14},... | collective-permute-start | bytes 393224 | tf_op jit(solution)/shard_map/ppermute | solution.py:347
  38.4 6.1 %x_mine.1.au_m = f32[8,160,384]{2,1,0:T(8,128)S(1)} custom-call(s32[3]{0:T(128)S(1)} %add_add_fusion.s_ref, bf16[80,1024]{1,0:T(8,128)(2,1)} %copy-done.5, bf16[80,1024]{1,0:T(8,128)(2,1)} %copy-done.4, bf16[80,1024]{1,0:T(8,128)(2,1)} %copy-done.3, bf16[80,1024]{1,0:T(8,128)(2,1)} %copy-done.2, bf16[80,1024]{1,0:T(8,128)(2,1)} %copy-done.6, ...), custom_call_target="tpu_custom_call" | custom-call | flops 1677721600 | bytes 12582912 | tf_op jit(solution)/shard_map/x_mine/pallas_call | solution.py:360
  44.6 4.1 %collective-permute-done.10.refs_2_ = bf16[64,1024]{1,0:T(8,128)(2,1)S(1)} collective-permute-done((bf16[64,1024]{1,0:T(8,128)(2,1)S(1)}, bf16[64,1024]{1,0:T(8,128)(2,1)S(1)}, u32[]{:S(2)}, u32[]{:S(2)}) %collective-permute-start.10) | collective-permute-done | bytes 131104 | tf_op jit(solution)/shard_map/ppermute | solution.py:347
  51.9 5.8 %y_first.1 = (bf16[4,80,384]{2,1,0:T(8,128)(2,1)S(1)}, bf16[16,80,1024]{2,1,0:T(8,128)(2,1)}) custom-call(s32[3]{0:T(128)S(1)} %add_add_fusion.1.s_ref, bf16[64,1024]{1,0:T(8,128)(2,1)} %copy-done.10, bf16[64,1024]{1,0:T(8,128)(2,1)} %copy-done.13, bf16[64,1024]{1,0:T(8,128)(2,1)} %copy-done.12, bf16[64,1024]{1,0:T(8,128)(2,1)} %copy-done.11, ...), custom_call_target="tpu_custom_call" | custom-call | flops 1593835520 | bytes 3145728 | tf_op jit(solution)/shard_map/y_first/pallas_call | solution.py:360
  58.2 3.3 %y_other.1 = bf16[4,80,384]{2,1,0:T(8,128)(2,1)S(1)} custom-call(s32[3]{0:T(128)S(1)} %add_add_fusion.2.s_ref, bf16[16,80,1024]{2,1,0:T(8,128)(2,1)} %get-tuple-element.55.yin_ref, bf16[16,384,1024]{2,1,0:T(8,128)(2,1)} %down_ref.3), custom_call_target="tpu_custom_call" | custom-call | flops 251658240 | bytes 3145728 | tf_op jit(solution)/shard_map/y_other/pallas_call | solution.py:360
  62.7 4.9 %y_mine.1.dh_m = f32[8,80,384]{2,1,0:T(8,128)S(1)} custom-call(s32[3]{0:T(128)S(1)} %add_add_fusion.s_ref, bf16[16,80,1024]{2,1,0:T(8,128)(2,1)} %get-tuple-element.55.yin_ref, bf16[16,384,1024]{2,1,0:T(8,128)(2,1)} %down_ref.3), custom_call_target="tpu_custom_call" | custom-call | flops 503316480 | bytes 6291456 | tf_op jit(solution)/shard_map/y_mine/pallas_call | solution.py:360
  68.6 1.9 %collective-permute-done.18.dh_r = bf16[4,80,384]{2,1,0:T(8,128)(2,1)S(1)} collective-permute-done((bf16[4,80,384]{2,1,0:T(8,128)(2,1)S(1)}, bf16[4,80,384]{2,1,0:T(8,128)(2,1)S(1)}, u32[]{:S(2)}, u32[]{:S(2)}) %collective-permute-start.18) | collective-permute-done | bytes 245792 | tf_op jit(solution)/shard_map/ppermute | solution.py:335
  70.9 4.4 %mine_parts.2.refs_0_ = bf16[320,1024]{1,0:T(8,128)(2,1)S(1)} custom-call(s32[3]{0:T(128)S(1)} %add_add_fusion.s_ref, bf16[4,160,384]{2,1,0:T(8,128)(2,1)S(1)} %get-tuple-element.64.refs_0_, bf16[16,1024,384]{2,1,0:T(8,128)(2,1)} %gate_ref.3, bf16[16,1024,384]{2,1,0:T(8,128)(2,1)} %up_ref.3), custom_call_target="tpu_custom_call" | custom-call | flops 503316480 | bytes 6291456 | tf_op jit(solution)/shard_map/mine_parts/pallas_call | solution.py:360
  75.3 1.8 %final.3 = (bf16[4,160,384]{2,1,0:T(8,128)(2,1)}, f32[4,1,384]{2,1,0:T(1,128)S(1)}) custom-call(s32[3]{0:T(128)S(1)} %add_add_fusion.s_ref, f32[8,160,384]{2,1,0:T(8,128)S(1)} %x_mine.1.au_m, f32[8,80,384]{2,1,0:T(8,128)S(1)} %y_mine.1.dh_m, bf16[8,160,384]{2,1,0:T(8,128)(2,1)S(1)} %collective-permute-done.16.au_r, ...), custom_call_target="tpu_custom_call" | custom-call | flops 4915200 | bytes 3686400 | tf_op jit(solution)/shard_map/final/pallas_call | solution.py:360
  78.8 4.9 %mine_parts.3.refs_1_ = bf16[320,1024]{1,0:T(8,128)(2,1)S(1)} custom-call(s32[3]{0:T(128)S(1)} %add_add_fusion.3.s_ref, bf16[4,160,384]{2,1,0:T(8,128)(2,1)} %get-tuple-element.67.refs_0_, bf16[16,1024,384]{2,1,0:T(8,128)(2,1)} %gate_ref.3, bf16[16,1024,384]{2,1,0:T(8,128)(2,1)} %up_ref.3), custom_call_target="tpu_custom_call" | custom-call | flops 503316480 | bytes 6291456 | tf_op jit(solution)/shard_map/mine_parts/pallas_call | solution.py:360
  83.8 5.8 %combine.2.refs_0_ = f32[512,1024]{1,0:T(8,128)S(1)} custom-call(s32[3]{0:T(128)S(1)} %add_add_fusion.1.s_ref, bf16[4,160,384]{2,1,0:T(8,128)(2,1)} %collective-permute-done.19.d_ref, bf16[16,1024,384]{2,1,0:T(8,128)(2,1)} %gate_ref.3, bf16[16,1024,384]{2,1,0:T(8,128)(2,1)} %up_ref.3, f32[16,512]{1,0:T(8,128)S(1)} %get-tuple-element.45.refs_8_.place_ref, ...), custom_call_target="tpu_custom_call" | custom-call | flops 1509949440 | bytes 6291456 | tf_op jit(solution)/shard_map/combine/pallas_call | solution.py:360
  89.6 3.4 %collective-permute-done.20 = f32[8,384]{1,0:T(8,128)S(1)} collective-permute-done((f32[8,384]{1,0:T(8,128)S(1)}, f32[8,384]{1,0:T(8,128)S(1)}, u32[]{:S(2)}, u32[]{:S(2)}) %collective-permute-start.20) | collective-permute-done | bytes 12320 | tf_op jit(solution)/shard_map/ppermute | solution.py:335
  93.0 5.3 %combine.3 = (f32[4,64,1024]{2,1,0:T(8,128)S(1)}, bf16[4,64,1024]{2,1,0:T(8,128)(2,1)S(1)}) custom-call(s32[3]{0:T(128)S(1)} %add_add_fusion.1.s_ref, bf16[4,160,384]{2,1,0:T(8,128)(2,1)S(1)} %collective-permute-done.21.d_ref, bf16[16,1024,384]{2,1,0:T(8,128)(2,1)} %gate_ref.3, bf16[16,1024,384]{2,1,0:T(8,128)(2,1)} %up_ref.3, ...), custom_call_target="tpu_custom_call" | custom-call | flops 838860800 | bytes 6291456 | tf_op jit(solution)/shard_map/combine/pallas_call | solution.py:360
  98.3 2.0 %collective-permute-start.22 = (bf16[4,64,1024]{2,1,0:T(8,128)(2,1)S(1)}, bf16[4,64,1024]{2,1,0:T(8,128)(2,1)S(1)}, u32[]{:S(2)}, u32[]{:S(2)}) collective-permute-start(bf16[4,64,1024]{2,1,0:T(8,128)(2,1)S(1)} %get-tuple-element.71), channel_id=1, source_target_pairs={{0,1},{1,0},{2,3},{3,2},{4,5},{5,4},{6,7},{7,6},{8,9},{9,8},{10,11... | collective-permute-start | bytes 1572872 | tf_op jit(solution)/shard_map/ppermute | solution.py:335
  102.0 2.6 %collective-permute-start.23 = (bf16[64,1024]{1,0:T(8,128)(2,1)S(1)}, bf16[64,1024]{1,0:T(8,128)(2,1)S(1)}, u32[]{:S(2)}, u32[]{:S(2)}) collective-permute-start(bf16[64,1024]{1,0:T(8,128)(2,1)S(1)} %get-tuple-element.72), channel_id=1, source_target_pairs={{0,0},{1,2},{2,1},{3,3},{4,4},{5,6},{6,5},{7,7},{8,8},{9,10},{10,9... | collective-permute-start | bytes 393224 | tf_op jit(solution)/shard_map/ppermute | solution.py:344
  104.9 4.2 %collective-permute-start.24 = (bf16[64,1024]{1,0:T(8,128)(2,1)S(1)}, bf16[64,1024]{1,0:T(8,128)(2,1)S(1)}, u32[]{:S(2)}, u32[]{:S(2)}) collective-permute-start(bf16[64,1024]{1,0:T(8,128)(2,1)S(1)} %get-tuple-element.75), channel_id=1, source_target_pairs={{0,12},{1,14},{2,13},{3,15},{4,0},{5,2},{6,1},{7,3},{8,4},{9,6},{1... | collective-permute-start | bytes 393224 | tf_op jit(solution)/shard_map/ppermute | solution.py:344
  109.7 3.0 %collective-permute-done.26 = bf16[64,1024]{1,0:T(8,128)(2,1)S(1)} collective-permute-done((bf16[64,1024]{1,0:T(8,128)(2,1)S(1)}, bf16[64,1024]{1,0:T(8,128)(2,1)S(1)}, u32[]{:S(2)}, u32[]{:S(2)}) %collective-permute-start.26) | collective-permute-done | bytes 131104 | tf_op jit(solution)/shard_map/ppermute | solution.py:344
  112.7 2.9 %collective-permute-done.25 = bf16[64,1024]{1,0:T(8,128)(2,1)S(1)} collective-permute-done((bf16[64,1024]{1,0:T(8,128)(2,1)S(1)}, bf16[64,1024]{1,0:T(8,128)(2,1)S(1)}, u32[]{:S(2)}, u32[]{:S(2)}) %collective-permute-start.25) | collective-permute-done | bytes 131104 | tf_op jit(solution)/shard_map/ppermute | solution.py:344
  (81 shorter events, 21.0 us)
Async XLA Ops:
  2.4 18.1 %collective-permute-start.3 = (bf16[80,1024]{1,0:T(8,128)(2,1)}, bf16[80,1024]{1,0:T(8,128)(2,1)S(1)}, u32[]{:S(2)}, u32[]{:S(2)}) collective-permute-start(bf16[80,1024]{1,0:T(8,128)(2,1)} %pack.1), channel_id=1, source_target_pairs={{0,12},{1,14},{2,13},{3,15},{4,0},{5,2},{6,1},{7,3},{8,4},{9,6},{1... | collective-permute-start | bytes 491528 | tf_op jit(solution)/shard_map/ppermute | solution.py:344
  8.0 13.8 %collective-permute-start.2 = (bf16[80,1024]{1,0:T(8,128)(2,1)}, bf16[80,1024]{1,0:T(8,128)(2,1)S(1)}, u32[]{:S(2)}, u32[]{:S(2)}) collective-permute-start(bf16[80,1024]{1,0:T(8,128)(2,1)} %pack.1), channel_id=1, source_target_pairs={{0,8},{1,10},{2,9},{3,11},{4,12},{5,14},{6,13},{7,15},{8,0},{9,2},... | collective-permute-start | bytes 491528 | tf_op jit(solution)/shard_map/ppermute | solution.py:344
  8.0 13.8 %collective-permute-start.1 = (bf16[80,1024]{1,0:T(8,128)(2,1)}, bf16[80,1024]{1,0:T(8,128)(2,1)S(1)}, u32[]{:S(2)}, u32[]{:S(2)}) collective-permute-start(bf16[80,1024]{1,0:T(8,128)(2,1)} %pack.1), channel_id=1, source_target_pairs={{0,4},{1,6},{2,5},{3,7},{4,8},{5,10},{6,9},{7,11},{8,12},{9,14},{1... | collective-permute-start | bytes 491528 | tf_op jit(solution)/shard_map/ppermute | solution.py:344
  9.6 12.2 %collective-permute-start = (bf16[80,1024]{1,0:T(8,128)(2,1)}, bf16[80,1024]{1,0:T(8,128)(2,1)S(1)}, u32[]{:S(2)}, u32[]{:S(2)}) collective-permute-start(bf16[80,1024]{1,0:T(8,128)(2,1)} %pack.1), channel_id=1, source_target_pairs={{0,0},{1,2},{2,1},{3,3},{4,4},{5,6},{6,5},{7,7},{8,8},{9,10},{10,9... | collective-permute-start | bytes 491528 | tf_op jit(solution)/shard_map/ppermute | solution.py:344
  11.7 8.8 %collective-permute-start.4 = (bf16[64,1024]{1,0:T(8,128)(2,1)}, bf16[64,1024]{1,0:T(8,128)(2,1)S(1)}, u32[]{:S(2)}, u32[]{:S(2)}) collective-permute-start(bf16[64,1024]{1,0:T(8,128)(2,1)} %param.9), channel_id=1, source_target_pairs={{0,0},{1,2},{2,1},{3,3},{4,4},{5,6},{6,5},{7,7},{8,8},{9,10},{10,9... | collective-permute-start | bytes 393224 | tf_op jit(solution)/shard_map/ppermute | solution.py:344
  21.8 2.0 %collective-permute-start.5 = (bf16[80,1024]{1,0:T(8,128)(2,1)S(1)}, bf16[80,1024]{1,0:T(8,128)(2,1)S(1)}, u32[]{:S(2)}, u32[]{:S(2)}) collective-permute-start(bf16[80,1024]{1,0:T(8,128)(2,1)S(1)} %collective-permute-done.refs_0_), channel_id=1, source_target_pairs={{0,1},{1,0},{2,3},{3,2},{4,5},{5,4},{6,7},{7,6},{8,9},{9,8},{10,11... | collective-permute-start | bytes 491528 | tf_op jit(solution)/shard_map/ppermute | solution.py:335
  22.9 1.6 %collective-permute-start.7 = (bf16[80,1024]{1,0:T(8,128)(2,1)S(1)}, bf16[80,1024]{1,0:T(8,128)(2,1)S(1)}, u32[]{:S(2)}, u32[]{:S(2)}) collective-permute-start(bf16[80,1024]{1,0:T(8,128)(2,1)S(1)} %collective-permute-done.2.refs_2_), channel_id=1, source_target_pairs={{0,1},{1,0},{2,3},{3,2},{4,5},{5,4},{6,7},{7,6},{8,9},{9,8},{10,11... | collective-permute-start | bytes 491528 | tf_op jit(solution)/shard_map/ppermute | solution.py:335
  33.1 25.2 %collective-permute-start.16 = (bf16[8,160,384]{2,1,0:T(8,128)(2,1)}, bf16[8,160,384]{2,1,0:T(8,128)(2,1)S(1)}, u32[]{:S(2)}, u32[]{:S(2)}) collective-permute-start(bf16[8,160,384]{2,1,0:T(8,128)(2,1)} %get-tuple-element.53), channel_id=1, source_target_pairs={{0,2},{2,0},{1,3},{3,1},{4,6},{6,4},{5,7},{7,5},{8,10},{10,8},{9,1... | collective-permute-start | bytes 2949128 | tf_op jit(solution)/shard_map/ppermute | solution.py:335
  34.3 10.2 %collective-permute-start.11 = (bf16[64,1024]{1,0:T(8,128)(2,1)S(1)}, bf16[64,1024]{1,0:T(8,128)(2,1)S(1)}, u32[]{:S(2)}, u32[]{:S(2)}) collective-permute-start(bf16[64,1024]{1,0:T(8,128)(2,1)S(1)} %collective-permute-done.4.refs_0_), channel_id=1, source_target_pairs={{0,12},{4,0},{8,4},{12,8},{1,13},{5,1},{9,5},{13,9},{2,14},{6,2},{... | collective-permute-start | bytes 393224 | tf_op jit(solution)/shard_map/ppermute | solution.py:347
  34.6 14.2 %collective-permute-start.10 = (bf16[64,1024]{1,0:T(8,128)(2,1)S(1)}, bf16[64,1024]{1,0:T(8,128)(2,1)S(1)}, u32[]{:S(2)}, u32[]{:S(2)}) collective-permute-start(bf16[64,1024]{1,0:T(8,128)(2,1)S(1)} %collective-permute-done.4.refs_0_), channel_id=1, source_target_pairs={{0,8},{4,12},{8,0},{12,4},{1,9},{5,13},{9,1},{13,5},{2,10},{6,14},... | collective-permute-start | bytes 393224 | tf_op jit(solution)/shard_map/ppermute | solution.py:347
  37.0 11.7 %collective-permute-start.9 = (bf16[64,1024]{1,0:T(8,128)(2,1)S(1)}, bf16[64,1024]{1,0:T(8,128)(2,1)S(1)}, u32[]{:S(2)}, u32[]{:S(2)}) collective-permute-start(bf16[64,1024]{1,0:T(8,128)(2,1)S(1)} %collective-permute-done.4.refs_0_), channel_id=1, source_target_pairs={{0,4},{4,8},{8,12},{12,0},{1,5},{5,9},{9,13},{13,1},{2,6},{6,10},{... | collective-permute-start | bytes 393224 | tf_op jit(solution)/shard_map/ppermute | solution.py:347
  48.8 2.3 %collective-permute-start.12 = (bf16[64,1024]{1,0:T(8,128)(2,1)S(1)}, bf16[64,1024]{1,0:T(8,128)(2,1)}, u32[]{:S(2)}, u32[]{:S(2)}) collective-permute-start(bf16[64,1024]{1,0:T(8,128)(2,1)S(1)} %collective-permute-done.4.refs_0_), channel_id=1, source_target_pairs={{0,1},{1,0},{2,3},{3,2},{4,5},{5,4},{6,7},{7,6},{8,9},{9,8},{10,11... | collective-permute-start | bytes 393224 | tf_op jit(solution)/shard_map/ppermute | solution.py:335
  49.9 1.5 %collective-permute-start.13 = (bf16[64,1024]{1,0:T(8,128)(2,1)S(1)}, bf16[64,1024]{1,0:T(8,128)(2,1)}, u32[]{:S(2)}, u32[]{:S(2)}) collective-permute-start(bf16[64,1024]{1,0:T(8,128)(2,1)S(1)} %collective-permute-done.9.refs_1_), channel_id=1, source_target_pairs={{0,1},{1,0},{2,3},{3,2},{4,5},{5,4},{6,7},{7,6},{8,9},{9,8},{10,11... | collective-permute-start | bytes 393224 | tf_op jit(solution)/shard_map/ppermute | solution.py:335
  50.0 1.6 %collective-permute-start.14 = (bf16[64,1024]{1,0:T(8,128)(2,1)S(1)}, bf16[64,1024]{1,0:T(8,128)(2,1)}, u32[]{:S(2)}, u32[]{:S(2)}) collective-permute-start(bf16[64,1024]{1,0:T(8,128)(2,1)S(1)} %collective-permute-done.10.refs_2_), channel_id=1, source_target_pairs={{0,1},{1,0},{2,3},{3,2},{4,5},{5,4},{6,7},{7,6},{8,9},{9,8},{10,11... | collective-permute-start | bytes 393224 | tf_op jit(solution)/shard_map/ppermute | solution.py:335
  57.8 9.9 %collective-permute-start.17 = (bf16[4,80,384]{2,1,0:T(8,128)(2,1)S(1)}, bf16[4,80,384]{2,1,0:T(8,128)(2,1)S(1)}, u32[]{:S(2)}, u32[]{:S(2)}) collective-permute-start(bf16[4,80,384]{2,1,0:T(8,128)(2,1)S(1)} %get-tuple-element.57), channel_id=1, source_target_pairs={{0,2},{2,0},{1,3},{3,1},{4,6},{6,4},{5,7},{7,5},{8,10},{10,8},{9,1... | collective-permute-start | bytes 737288 | tf_op jit(solution)/shard_map/ppermute | solution.py:335
  61.6 8.9 %collective-permute-start.18 = (bf16[4,80,384]{2,1,0:T(8,128)(2,1)S(1)}, bf16[4,80,384]{2,1,0:T(8,128)(2,1)S(1)}, u32[]{:S(2)}, u32[]{:S(2)}) collective-permute-start(bf16[4,80,384]{2,1,0:T(8,128)(2,1)S(1)} %y_other.1), channel_id=1, source_target_pairs={{0,2},{2,0},{1,3},{3,1},{4,6},{6,4},{5,7},{7,5},{8,10},{10,8},{9,1... | collective-permute-start | bytes 737288 | tf_op jit(solution)/shard_map/ppermute | solution.py:335
  70.5 13.3 %collective-permute-start.19 = (bf16[4,160,384]{2,1,0:T(8,128)(2,1)S(1)}, bf16[4,160,384]{2,1,0:T(8,128)(2,1)}, u32[]{:S(2)}, u32[]{:S(2)}) collective-permute-start(bf16[4,160,384]{2,1,0:T(8,128)(2,1)S(1)} %get-tuple-element.64.refs_0_), channel_id=1, source_target_pairs={{0,2},{2,0},{1,3},{3,1},{4,6},{6,4},{5,7},{7,5},{8,10},{10,8},{9,1... | collective-permute-start | bytes 1474568 | tf_op jit(solution)/shard_map/ppermute | solution.py:335
  77.1 15.9 %collective-permute-start.21 = (bf16[4,160,384]{2,1,0:T(8,128)(2,1)}, bf16[4,160,384]{2,1,0:T(8,128)(2,1)S(1)}, u32[]{:S(2)}, u32[]{:S(2)}) collective-permute-start(bf16[4,160,384]{2,1,0:T(8,128)(2,1)} %get-tuple-element.67.refs_0_), channel_id=1, source_target_pairs={{0,2},{2,0},{1,3},{3,1},{4,6},{6,4},{5,7},{7,5},{8,10},{10,8},{9,1... | collective-permute-start | bytes 1474568 | tf_op jit(solution)/shard_map/ppermute | solution.py:335
  78.3 14.7 %collective-permute-start.20 = (f32[8,384]{1,0:T(8,128)S(1)}, f32[8,384]{1,0:T(8,128)S(1)}, u32[]{:S(2)}, u32[]{:S(2)}) collective-permute-start(f32[8,384]{1,0:T(8,128)S(1)} %bitcast.25), channel_id=1, source_target_pairs={{0,2},{2,0},{1,3},{3,1},{4,6},{6,4},{5,7},{7,5},{8,10},{10,8},{9,1... | collective-permute-start | bytes 36872 | tf_op jit(solution)/shard_map/ppermute | solution.py:335
  98.3 3.5 %collective-permute-start.22 = (bf16[4,64,1024]{2,1,0:T(8,128)(2,1)S(1)}, bf16[4,64,1024]{2,1,0:T(8,128)(2,1)S(1)}, u32[]{:S(2)}, u32[]{:S(2)}) collective-permute-start(bf16[4,64,1024]{2,1,0:T(8,128)(2,1)S(1)} %get-tuple-element.71), channel_id=1, source_target_pairs={{0,1},{1,0},{2,3},{3,2},{4,5},{5,4},{6,7},{7,6},{8,9},{9,8},{10,11... | collective-permute-start | bytes 1572872 | tf_op jit(solution)/shard_map/ppermute | solution.py:335
  102.0 7.7 %collective-permute-start.23 = (bf16[64,1024]{1,0:T(8,128)(2,1)S(1)}, bf16[64,1024]{1,0:T(8,128)(2,1)S(1)}, u32[]{:S(2)}, u32[]{:S(2)}) collective-permute-start(bf16[64,1024]{1,0:T(8,128)(2,1)S(1)} %get-tuple-element.72), channel_id=1, source_target_pairs={{0,0},{1,2},{2,1},{3,3},{4,4},{5,6},{6,5},{7,7},{8,8},{9,10},{10,9... | collective-permute-start | bytes 393224 | tf_op jit(solution)/shard_map/ppermute | solution.py:344
  104.6 8.1 %collective-permute-start.26 = (bf16[64,1024]{1,0:T(8,128)(2,1)S(1)}, bf16[64,1024]{1,0:T(8,128)(2,1)S(1)}, u32[]{:S(2)}, u32[]{:S(2)}) collective-permute-start(bf16[64,1024]{1,0:T(8,128)(2,1)S(1)} %get-tuple-element.73), channel_id=1, source_target_pairs={{0,4},{1,6},{2,5},{3,7},{4,8},{5,10},{6,9},{7,11},{8,12},{9,14},{1... | collective-permute-start | bytes 393224 | tf_op jit(solution)/shard_map/ppermute | solution.py:344
  104.7 11.0 %collective-permute-start.25 = (bf16[64,1024]{1,0:T(8,128)(2,1)S(1)}, bf16[64,1024]{1,0:T(8,128)(2,1)S(1)}, u32[]{:S(2)}, u32[]{:S(2)}) collective-permute-start(bf16[64,1024]{1,0:T(8,128)(2,1)S(1)} %get-tuple-element.74), channel_id=1, source_target_pairs={{0,8},{1,10},{2,9},{3,11},{4,12},{5,14},{6,13},{7,15},{8,0},{9,2},... | collective-permute-start | bytes 393224 | tf_op jit(solution)/shard_map/ppermute | solution.py:344
  104.9 10.8 %collective-permute-start.24 = (bf16[64,1024]{1,0:T(8,128)(2,1)S(1)}, bf16[64,1024]{1,0:T(8,128)(2,1)S(1)}, u32[]{:S(2)}, u32[]{:S(2)}) collective-permute-start(bf16[64,1024]{1,0:T(8,128)(2,1)S(1)} %get-tuple-element.75), channel_id=1, source_target_pairs={{0,12},{1,14},{2,13},{3,15},{4,0},{5,2},{6,1},{7,3},{8,4},{9,6},{1... | collective-permute-start | bytes 393224 | tf_op jit(solution)/shard_map/ppermute | solution.py:344
  (17 other events, 72.4 us)

commit v7 on v6

--- a/solution.py
+++ b/solution.py
@@ -213,10 +213,10 @@
     forward(rows, count, 0, copies, rows_ref, (gate, up), au_ref)
 
 
-def back_dots(count, first, arrived, ys, down, out_ref):
+def back_dots(count, arrived, ys, down, out_ref):
     def body(j):
         arrived(j)
-        out_ref[j] = lax.dot_general(ys[first + j], down[j], NT, preferred_element_type=F32).astype(out_ref.dtype)
+        out_ref[j] = lax.dot_general(ys[j], down[j], NT, preferred_element_type=F32).astype(out_ref.dtype)
 
     each(count, body)
 
@@ -229,16 +229,28 @@
     filling, _ = fill(tok_ref, tokens, s_ref[1], tok, tok_sem)
     copies = load((down_ref,), s_ref[0], count, (down,), sem)
     ready(filling)
-    dispatch(rows, 0, experts, group, place_ref, tok_ref, hot_ref, rows_ref, level_ref)
+    dispatch(rows, s_ref[0], experts // 2, group, place_ref, tok_ref, hot_ref, rows_ref, level_ref)
     leaving = pltpu.make_async_copy(rows_ref, yin_ref, out_sem)
     leaving.start()
-    back_dots(count, s_ref[0], copies, rows_ref, down, dh_ref)
+    back_dots(count, copies, rows_ref, down, dh_ref)
     leaving.wait()
 
 
-def y2_kernel(count, s_ref, yin_ref, down_ref, dh_ref, ys, down, sem):
-    arrived = load((yin_ref, down_ref), s_ref[0], count, (ys, down), sem)
-    back_dots(count, 0, arrived, ys, down, dh_ref)
+def y2_kernel(start, count, s_ref, yin_ref, down_ref, dh_ref, ys, down, sem, row_sem):
+    rows_here = load((yin_ref,), start, count, (ys,), row_sem)
+    arrived = load((down_ref,), s_ref[0], count, (down,), sem)
+    each(count, rows_here)
+    back_dots(count, arrived, ys, down, dh_ref)
+
+
+def y3_kernel(cfg, count, s_ref, *refs):
+    zs, tok, experts, rows, group = cfg
+    place_ref, level_ref, down_ref, dh_ref, tok_ref, hot_ref, rows_ref, down, sem, tok_sem = refs[2 * zs :]
+    filling, _ = fill(tok_ref, refs[: 2 * zs], s_ref[1], tok, tok_sem)
+    copies = load((down_ref,), s_ref[0], count, (down,), sem)
+    ready(filling)
+    dispatch(rows, s_ref[0], count, group, place_ref, tok_ref, hot_ref, rows_ref, level_ref)
+    back_dots(count, copies, rows_ref, down, dh_ref)
 
 
 def final_kernel(rows, scale, at, off, s_ref, au_m, dh_m, au_r, dh_r, d_ref, score_ref):
@@ -394,9 +406,8 @@
         return pltpu.VMEM((count, ff, width), BF16)
 
     place_shape = sds((experts, all_tok), F32)
-    rows_shape = pltpu.HBM((experts, rows, width), BF16)
+    rows_shape = pltpu.HBM((half, rows, width), BF16)
     half_rows = pltpu.VMEM((half, rows, width), BF16)
-    rows_scratch = pltpu.VMEM((experts, rows, width), BF16)
     def pinned(*arrays):
         return tuple(pltpu.with_memory_space_constraint(v, pltpu.HBM) for v in arrays)
 
@@ -437,29 +448,36 @@
         s,
         [(anywhere, pinned(*y_own, *y_other)), (vmem, (place, level)), (anywhere, (down_weight,))],
         [sds((first, rows, ff), BF16), rows_shape],
-        [tok_scratch, hot, rows_scratch, tall(first), dma((first,)), dma((2 * zs,)), dma],
-        first * flop + dflop,
+        [tok_scratch, hot, half_rows, tall(first), dma((first,)), dma((2 * zs,)), dma],
+        first * flop + dflop // 2,
         first * wbytes,
         "y_first",
     )
 
-    def y_call(first, n, dtype, name):
-        return call(
-            functools.partial(y2_kernel, n),
-            first,
-            s,
-            [(anywhere, pinned(yin, down_weight))],
-            sds((n, rows, ff), dtype),
-            [pltpu.VMEM((n, rows, width), BF16), tall(n), dma((2 * n,))],
-            n * flop,
-            n * wbytes,
-            name,
-        )
-
     yin, au_recv = lax.optimization_barrier((yin, au_recv))
-    dh_rest = y_call(other0 + first, rest, BF16, "y_other")
-    yin, dh_rest = lax.optimization_barrier((yin, dh_rest))
-    dh_mine = y_call(mine0, half, F32, "y_mine")
+    dh_rest = call(
+        functools.partial(y2_kernel, first, rest),
+        other0 + first,
+        s,
+        [(anywhere, pinned(yin, down_weight))],
+        sds((rest, rows, ff), BF16),
+        [pltpu.VMEM((rest, rows, width), BF16), tall(rest), dma((rest,)), dma((rest,))],
+        rest * flop,
+        rest * wbytes,
+        "y_other",
+    )
+    place_y, dh_rest = lax.optimization_barrier((place, dh_rest))
+    dh_mine = call(
+        functools.partial(y3_kernel, cfg, half),
+        mine0,
+        s,
+        [(anywhere, pinned(*y_own, *y_other)), (vmem, (place_y, level)), (anywhere, (down_weight,))],
+        sds((half, rows, ff), F32),
+        [tok_scratch, hot, half_rows, tall(half), dma((half,)), dma((2 * zs,))],
+        half * flop + dflop // 2,
+        half * wbytes,
+        "y_mine",
+    )
     dh_recv = [flip(v, "dp") for v in (dh_first, dh_rest)]
     scale = LOCAL_EXPERTS / (all_tok * TOPK)
     last = 0

time: 117 us -> 115 us (0.983)
  Pallas kernels: 52.5 us -> 50.5 us
  waiting for transfers between devices: 26.1 us -> 24.9 us
    pallas_call x11, Pallas kernels: 50.8 us -> 48.8 us  [call(): pl.pallas_call(body, out_shape=outs, in_specs=[smem] + ins, out_specs=jax...]
  transfers between devices with their start and end apart: 27 -> 27, of which waited for: 16 -> 16; matrix products, arithmetic and copies ran while one was open for 1% -> 1% of each run, Pallas kernels for 33% -> 32%
where the time goes in v7:
time: 115 us; the launch traced here: 114 us
  Pallas kernels  50.5 us (44%)
  starting transfers between devices  35.1 us (31%)
  waiting for transfers between devices  24.9 us (22%)
  other arithmetic  1.74 us (2%)
  local copies, waits for them, and re-layouts  1.32 us (1%)
    pallas_call x11, Pallas kernels, call(): pl.pallas_call(body, out_shape=outs, in_specs=[smem] + ins, out_specs=jax...  48.8 us
    ppermute x9, starting transfers between devices, turn(): return lax.ppermute(v, ('expert', 'dp', 'sub'), pairs)  20.9 us
    ppermute x9, waiting for transfers between devices, turn(): return lax.ppermute(v, ('expert', 'dp', 'sub'), pairs)  11.7 us
    ppermute x15, starting transfers between devices, flip(): return lax.ppermute(v, axis, [(0, 1), (1, 0)])  10.1 us
    ppermute x15, waiting for transfers between devices, flip(): return lax.ppermute(v, axis, [(0, 1), (1, 0)])  9.02 us
    ppermute x3, waiting for transfers between devices, shift(): return lax.ppermute(v, 'expert', [(i, (i + d) % zs) for i in range(zs)])  4.2 us
    ppermute x3, starting transfers between devices, shift(): return lax.ppermute(v, 'expert', [(i, (i + d) % zs) for i in range(zs)])  4.1 us
  transfers between devices with their start and end apart: 27, of which 16 were waited for; matrix products, arithmetic and copies ran while one was open for 1% of the time, Pallas kernels for 32%

profile of v7, /device:TPU:1, one launch (start us, length us, event | category | flops | bytes accessed | tf_op | source)
XLA Modules:
  0.0 114.4 jit_solution(3874802934861242580)
XLA Ops:
  0.6 1.7 %pack.1 = bf16[80,1024]{1,0:T(8,128)(2,1)} custom-call(s32[1]{0:T(128)} %bitcast.3.p_ref, bf16[64,1024]{1,0:T(8,128)(2,1)} %tokens_ref.1, s32[8,64]{1,0:T(8,128)} %bitcast.26, s32[8,64]{1,0:T(8,128)} %bitcast.27, f32[8,64]{1,0:T(8,128)} %bitcast.28), custom_call_target="tpu_custom_call" | custom-call | tf_op jit(solution)/shard_map/pack/pallas_call | solution.py:383
  2.4 5.6 %collective-permute-start.3 = (bf16[80,1024]{1,0:T(8,128)(2,1)}, bf16[80,1024]{1,0:T(8,128)(2,1)S(1)}, u32[]{:S(2)}, u32[]{:S(2)}) collective-permute-start(bf16[80,1024]{1,0:T(8,128)(2,1)} %pack.1), channel_id=1, source_target_pairs={{0,12},{1,14},{2,13},{3,15},{4,0},{5,2},{6,1},{7,3},{8,4},{9,6},{1... | collective-permute-start | bytes 491528 | tf_op jit(solution)/shard_map/ppermute | solution.py:356
  8.0 1.6 %collective-permute-start.1 = (bf16[80,1024]{1,0:T(8,128)(2,1)}, bf16[80,1024]{1,0:T(8,128)(2,1)S(1)}, u32[]{:S(2)}, u32[]{:S(2)}) collective-permute-start(bf16[80,1024]{1,0:T(8,128)(2,1)} %pack.1), channel_id=1, source_target_pairs={{0,4},{1,6},{2,5},{3,7},{4,8},{5,10},{6,9},{7,11},{8,12},{9,14},{1... | collective-permute-start | bytes 491528 | tf_op jit(solution)/shard_map/ppermute | solution.py:356
  9.6 2.0 %collective-permute-start = (bf16[80,1024]{1,0:T(8,128)(2,1)}, bf16[80,1024]{1,0:T(8,128)(2,1)S(1)}, u32[]{:S(2)}, u32[]{:S(2)}) collective-permute-start(bf16[80,1024]{1,0:T(8,128)(2,1)} %pack.1), channel_id=1, source_target_pairs={{0,0},{1,2},{2,1},{3,3},{4,4},{5,6},{6,5},{7,7},{8,8},{9,10},{10,9... | collective-permute-start | bytes 491528 | tf_op jit(solution)/shard_map/ppermute | solution.py:356
  11.7 3.5 %collective-permute-start.4 = (bf16[64,1024]{1,0:T(8,128)(2,1)}, bf16[64,1024]{1,0:T(8,128)(2,1)S(1)}, u32[]{:S(2)}, u32[]{:S(2)}) collective-permute-start(bf16[64,1024]{1,0:T(8,128)(2,1)} %param.9), channel_id=1, source_target_pairs={{0,0},{1,2},{2,1},{3,3},{4,4},{5,6},{6,5},{7,7},{8,8},{9,10},{10,9... | collective-permute-start | bytes 393224 | tf_op jit(solution)/shard_map/ppermute | solution.py:356
  15.2 5.3 %collective-permute-done.4.refs_0_ = bf16[64,1024]{1,0:T(8,128)(2,1)S(1)} collective-permute-done((bf16[64,1024]{1,0:T(8,128)(2,1)}, bf16[64,1024]{1,0:T(8,128)(2,1)S(1)}, u32[]{:S(2)}, u32[]{:S(2)}) %collective-permute-start.4) | collective-permute-done | bytes 131104 | tf_op jit(solution)/shard_map/ppermute | solution.py:356
  25.4 6.3 %x_first.1 = (bf16[8,160,384]{2,1,0:T(8,128)(2,1)S(1)}, f32[16,512]{1,0:T(8,128)S(1)}, f32[16,512]{1,0:T(8,128)S(1)}) custom-call(s32[3]{0:T(128)S(1)} %get-tuple-element.78.s_ref, bf16[80,1024]{1,0:T(8,128)(2,1)} %copy-done.3, bf16[80,1024]{1,0:T(8,128)(2,1)} %copy-done.2, bf16[80,1024]{1,0:T(8,128)(2,1)} %copy-done.1, bf16[80,1024]{1,0:T(8,128)(2,1)} %copy-done, ...), custom_call_target="tpu_custom_call" | custom-call | flops 1677721600 | bytes 12582912 | tf_op jit(solution)/shard_map/x_first/pallas_call | solution.py:372
  33.2 2.5 %collective-permute-start.10 = (bf16[64,1024]{1,0:T(8,128)(2,1)S(1)}, bf16[64,1024]{1,0:T(8,128)(2,1)S(1)}, u32[]{:S(2)}, u32[]{:S(2)}) collective-permute-start(bf16[64,1024]{1,0:T(8,128)(2,1)S(1)} %collective-permute-done.4.refs_0_), channel_id=1, source_target_pairs={{0,8},{4,12},{8,0},{12,4},{1,9},{5,13},{9,1},{13,5},{2,10},{6,14},... | collective-permute-start | bytes 393224 | tf_op jit(solution)/shard_map/ppermute | solution.py:359
  37.1 6.1 %x_mine.1.au_m = f32[8,160,384]{2,1,0:T(8,128)S(1)} custom-call(s32[3]{0:T(128)S(1)} %add_add_fusion.s_ref, bf16[80,1024]{1,0:T(8,128)(2,1)} %copy-done.3, bf16[80,1024]{1,0:T(8,128)(2,1)} %copy-done.2, bf16[80,1024]{1,0:T(8,128)(2,1)} %copy-done.1, bf16[80,1024]{1,0:T(8,128)(2,1)} %copy-done, bf16[80,1024]{1,0:T(8,128)(2,1)} %copy-done.4, ...), custom_call_target="tpu_custom_call" | custom-call | flops 1677721600 | bytes 12582912 | tf_op jit(solution)/shard_map/x_mine/pallas_call | solution.py:372
  43.3 4.2 %collective-permute-done.10.refs_2_ = bf16[64,1024]{1,0:T(8,128)(2,1)S(1)} collective-permute-done((bf16[64,1024]{1,0:T(8,128)(2,1)S(1)}, bf16[64,1024]{1,0:T(8,128)(2,1)S(1)}, u32[]{:S(2)}, u32[]{:S(2)}) %collective-permute-start.10) | collective-permute-done | bytes 131104 | tf_op jit(solution)/shard_map/ppermute | solution.py:359
  51.1 4.6 %y_first.1 = (bf16[4,80,384]{2,1,0:T(8,128)(2,1)S(1)}, bf16[8,80,1024]{2,1,0:T(8,128)(2,1)}) custom-call(s32[3]{0:T(128)S(1)} %get-tuple-element.78.s_ref, bf16[64,1024]{1,0:T(8,128)(2,1)} %copy-done.8, bf16[64,1024]{1,0:T(8,128)(2,1)} %copy-done.11, bf16[64,1024]{1,0:T(8,128)(2,1)} %copy-done.10, bf16[64,1024]{1,0:T(8,128)(2,1)} %copy-done.9, ...), custom_call_target="tpu_custom_call" | custom-call | flops 922746880 | bytes 3145728 | tf_op jit(solution)/shard_map/y_first/pallas_call | solution.py:372
  56.1 3.6 %y_other.1 = bf16[4,80,384]{2,1,0:T(8,128)(2,1)S(1)} custom-call(s32[3]{0:T(128)S(1)} %get-tuple-element.79.s_ref, bf16[8,80,1024]{2,1,0:T(8,128)(2,1)} %get-tuple-element.54.yin_ref, bf16[16,384,1024]{2,1,0:T(8,128)(2,1)} %refs_10_.5), custom_call_target="tpu_custom_call" | custom-call | flops 251658240 | bytes 3145728 | tf_op jit(solution)/shard_map/y_other/pallas_call | solution.py:372
  60.9 6.1 %y_mine.1.dh_m = f32[8,80,384]{2,1,0:T(8,128)S(1)} custom-call(s32[3]{0:T(128)S(1)} %add_add_fusion.s_ref, bf16[64,1024]{1,0:T(8,128)(2,1)} %copy-done.8, bf16[64,1024]{1,0:T(8,128)(2,1)} %copy-done.11, bf16[64,1024]{1,0:T(8,128)(2,1)} %copy-done.10, bf16[64,1024]{1,0:T(8,128)(2,1)} %copy-done.9, bf16[64,1024]{1,0:T(8,128)(2,1)} %copy-done.12, ...), custom_call_target="tpu_custom_call" | custom-call | flops 1174405120 | bytes 6291456 | tf_op jit(solution)/shard_map/y_mine/pallas_call | solution.py:372
  68.9 4.4 %mine_parts.2.refs_0_ = bf16[320,1024]{1,0:T(8,128)(2,1)S(1)} custom-call(s32[3]{0:T(128)S(1)} %add_add_fusion.s_ref, bf16[4,160,384]{2,1,0:T(8,128)(2,1)S(1)} %get-tuple-element.64.refs_0_, bf16[16,1024,384]{2,1,0:T(8,128)(2,1)} %gate_ref.3, bf16[16,1024,384]{2,1,0:T(8,128)(2,1)} %up_ref.3), custom_call_target="tpu_custom_call" | custom-call | flops 503316480 | bytes 6291456 | tf_op jit(solution)/shard_map/mine_parts/pallas_call | solution.py:372
  76.0 4.4 %mine_parts.3.refs_1_ = bf16[320,1024]{1,0:T(8,128)(2,1)S(1)} custom-call(s32[3]{0:T(128)S(1)} %add_add_fusion.3.s_ref, bf16[4,160,384]{2,1,0:T(8,128)(2,1)S(1)} %get-tuple-element.67.refs_0_, bf16[16,1024,384]{2,1,0:T(8,128)(2,1)} %gate_ref.3, bf16[16,1024,384]{2,1,0:T(8,128)(2,1)} %up_ref.3), custom_call_target="tpu_custom_call" | custom-call | flops 503316480 | bytes 6291456 | tf_op jit(solution)/shard_map/mine_parts/pallas_call | solution.py:372
  80.5 5.9 %combine.2.refs_0_ = f32[512,1024]{1,0:T(8,128)S(1)} custom-call(s32[3]{0:T(128)S(1)} %get-tuple-element.78.s_ref, bf16[4,160,384]{2,1,0:T(8,128)(2,1)} %collective-permute-done.19.d_ref, bf16[16,1024,384]{2,1,0:T(8,128)(2,1)} %gate_ref.3, bf16[16,1024,384]{2,1,0:T(8,128)(2,1)} %up_ref.3, f32[16,512]{1,0:T(8,128)S(1)} %get-tuple-element.55.refs_8_.place_ref, ...), custom_call_target="tpu_custom_call" | custom-call | flops 1509949440 | bytes 6291456 | tf_op jit(solution)/shard_map/combine/pallas_call | solution.py:372
  86.4 4.6 %collective-permute-done.20 = f32[8,384]{1,0:T(8,128)S(1)} collective-permute-done((f32[8,384]{1,0:T(8,128)S(1)}, f32[8,384]{1,0:T(8,128)S(1)}, u32[]{:S(2)}, u32[]{:S(2)}) %collective-permute-start.20) | collective-permute-done | bytes 12320 | tf_op jit(solution)/shard_map/ppermute | solution.py:347
  90.9 5.3 %combine.3 = (f32[4,64,1024]{2,1,0:T(8,128)S(1)}, bf16[4,64,1024]{2,1,0:T(8,128)(2,1)S(1)}) custom-call(s32[3]{0:T(128)S(1)} %get-tuple-element.78.s_ref, bf16[4,160,384]{2,1,0:T(8,128)(2,1)S(1)} %collective-permute-done.21.d_ref, bf16[16,1024,384]{2,1,0:T(8,128)(2,1)} %gate_ref.3, bf16[16,1024,384]{2,1,0:T(8,128)(2,1)} %up_ref.3, ...), custom_call_target="tpu_custom_call" | custom-call | flops 838860800 | bytes 6291456 | tf_op jit(solution)/shard_map/combine/pallas_call | solution.py:372
  96.2 2.0 %collective-permute-start.22 = (bf16[4,64,1024]{2,1,0:T(8,128)(2,1)S(1)}, bf16[4,64,1024]{2,1,0:T(8,128)(2,1)S(1)}, u32[]{:S(2)}, u32[]{:S(2)}) collective-permute-start(bf16[4,64,1024]{2,1,0:T(8,128)(2,1)S(1)} %get-tuple-element.71), channel_id=1, source_target_pairs={{0,1},{1,0},{2,3},{3,2},{4,5},{5,4},{6,7},{7,6},{8,9},{9,8},{10,11... | collective-permute-start | bytes 1572872 | tf_op jit(solution)/shard_map/ppermute | solution.py:347
  100.0 2.7 %collective-permute-start.23 = (bf16[64,1024]{1,0:T(8,128)(2,1)S(1)}, bf16[64,1024]{1,0:T(8,128)(2,1)S(1)}, u32[]{:S(2)}, u32[]{:S(2)}) collective-permute-start(bf16[64,1024]{1,0:T(8,128)(2,1)S(1)} %get-tuple-element.72), channel_id=1, source_target_pairs={{0,0},{1,2},{2,1},{3,3},{4,4},{5,6},{6,5},{7,7},{8,8},{9,10},{10,9... | collective-permute-start | bytes 393224 | tf_op jit(solution)/shard_map/ppermute | solution.py:356
  102.7 1.9 %collective-permute-start.25 = (bf16[64,1024]{1,0:T(8,128)(2,1)S(1)}, bf16[64,1024]{1,0:T(8,128)(2,1)S(1)}, u32[]{:S(2)}, u32[]{:S(2)}) collective-permute-start(bf16[64,1024]{1,0:T(8,128)(2,1)S(1)} %get-tuple-element.74), channel_id=1, source_target_pairs={{0,8},{1,10},{2,9},{3,11},{4,12},{5,14},{6,13},{7,15},{8,0},{9,2},... | collective-permute-start | bytes 393224 | tf_op jit(solution)/shard_map/ppermute | solution.py:356
  104.6 3.5 %collective-permute-start.24 = (bf16[64,1024]{1,0:T(8,128)(2,1)S(1)}, bf16[64,1024]{1,0:T(8,128)(2,1)S(1)}, u32[]{:S(2)}, u32[]{:S(2)}) collective-permute-start(bf16[64,1024]{1,0:T(8,128)(2,1)S(1)} %get-tuple-element.75), channel_id=1, source_target_pairs={{0,12},{1,14},{2,13},{3,15},{4,0},{5,2},{6,1},{7,3},{8,4},{9,6},{1... | collective-permute-start | bytes 393224 | tf_op jit(solution)/shard_map/ppermute | solution.py:356
  108.6 2.1 %collective-permute-done.26 = bf16[64,1024]{1,0:T(8,128)(2,1)S(1)} collective-permute-done((bf16[64,1024]{1,0:T(8,128)(2,1)S(1)}, bf16[64,1024]{1,0:T(8,128)(2,1)S(1)}, u32[]{:S(2)}, u32[]{:S(2)}) %collective-permute-start.26) | collective-permute-done | bytes 131104 | tf_op jit(solution)/shard_map/ppermute | solution.py:356
  110.8 2.9 %collective-permute-done.25 = bf16[64,1024]{1,0:T(8,128)(2,1)S(1)} collective-permute-done((bf16[64,1024]{1,0:T(8,128)(2,1)S(1)}, bf16[64,1024]{1,0:T(8,128)(2,1)S(1)}, u32[]{:S(2)}, u32[]{:S(2)}) %collective-permute-start.25) | collective-permute-done | bytes 131104 | tf_op jit(solution)/shard_map/ppermute | solution.py:356
  (84 shorter events, 20.7 us)
Async XLA Ops:
  2.4 18.1 %collective-permute-start.3 = (bf16[80,1024]{1,0:T(8,128)(2,1)}, bf16[80,1024]{1,0:T(8,128)(2,1)S(1)}, u32[]{:S(2)}, u32[]{:S(2)}) collective-permute-start(bf16[80,1024]{1,0:T(8,128)(2,1)} %pack.1), channel_id=1, source_target_pairs={{0,12},{1,14},{2,13},{3,15},{4,0},{5,2},{6,1},{7,3},{8,4},{9,6},{1... | collective-permute-start | bytes 491528 | tf_op jit(solution)/shard_map/ppermute | solution.py:356
  8.0 13.8 %collective-permute-start.2 = (bf16[80,1024]{1,0:T(8,128)(2,1)}, bf16[80,1024]{1,0:T(8,128)(2,1)S(1)}, u32[]{:S(2)}, u32[]{:S(2)}) collective-permute-start(bf16[80,1024]{1,0:T(8,128)(2,1)} %pack.1), channel_id=1, source_target_pairs={{0,8},{1,10},{2,9},{3,11},{4,12},{5,14},{6,13},{7,15},{8,0},{9,2},... | collective-permute-start | bytes 491528 | tf_op jit(solution)/shard_map/ppermute | solution.py:356
  8.0 13.8 %collective-permute-start.1 = (bf16[80,1024]{1,0:T(8,128)(2,1)}, bf16[80,1024]{1,0:T(8,128)(2,1)S(1)}, u32[]{:S(2)}, u32[]{:S(2)}) collective-permute-start(bf16[80,1024]{1,0:T(8,128)(2,1)} %pack.1), channel_id=1, source_target_pairs={{0,4},{1,6},{2,5},{3,7},{4,8},{5,10},{6,9},{7,11},{8,12},{9,14},{1... | collective-permute-start | bytes 491528 | tf_op jit(solution)/shard_map/ppermute | solution.py:356
  9.6 12.2 %collective-permute-start = (bf16[80,1024]{1,0:T(8,128)(2,1)}, bf16[80,1024]{1,0:T(8,128)(2,1)S(1)}, u32[]{:S(2)}, u32[]{:S(2)}) collective-permute-start(bf16[80,1024]{1,0:T(8,128)(2,1)} %pack.1), channel_id=1, source_target_pairs={{0,0},{1,2},{2,1},{3,3},{4,4},{5,6},{6,5},{7,7},{8,8},{9,10},{10,9... | collective-permute-start | bytes 491528 | tf_op jit(solution)/shard_map/ppermute | solution.py:356
  11.7 8.8 %collective-permute-start.4 = (bf16[64,1024]{1,0:T(8,128)(2,1)}, bf16[64,1024]{1,0:T(8,128)(2,1)S(1)}, u32[]{:S(2)}, u32[]{:S(2)}) collective-permute-start(bf16[64,1024]{1,0:T(8,128)(2,1)} %param.9), channel_id=1, source_target_pairs={{0,0},{1,2},{2,1},{3,3},{4,4},{5,6},{6,5},{7,7},{8,8},{9,10},{10,9... | collective-permute-start | bytes 393224 | tf_op jit(solution)/shard_map/ppermute | solution.py:356
  21.8 2.0 %collective-permute-start.5 = (bf16[80,1024]{1,0:T(8,128)(2,1)S(1)}, bf16[80,1024]{1,0:T(8,128)(2,1)S(1)}, u32[]{:S(2)}, u32[]{:S(2)}) collective-permute-start(bf16[80,1024]{1,0:T(8,128)(2,1)S(1)} %collective-permute-done.refs_0_), channel_id=1, source_target_pairs={{0,1},{1,0},{2,3},{3,2},{4,5},{5,4},{6,7},{7,6},{8,9},{9,8},{10,11... | collective-permute-start | bytes 491528 | tf_op jit(solution)/shard_map/ppermute | solution.py:347
  22.9 1.6 %collective-permute-start.7 = (bf16[80,1024]{1,0:T(8,128)(2,1)S(1)}, bf16[80,1024]{1,0:T(8,128)(2,1)S(1)}, u32[]{:S(2)}, u32[]{:S(2)}) collective-permute-start(bf16[80,1024]{1,0:T(8,128)(2,1)S(1)} %collective-permute-done.2.refs_2_), channel_id=1, source_target_pairs={{0,1},{1,0},{2,3},{3,2},{4,5},{5,4},{6,7},{7,6},{8,9},{9,8},{10,11... | collective-permute-start | bytes 491528 | tf_op jit(solution)/shard_map/ppermute | solution.py:347
  23.3 1.4 %collective-permute-start.8 = (bf16[80,1024]{1,0:T(8,128)(2,1)S(1)}, bf16[80,1024]{1,0:T(8,128)(2,1)S(1)}, u32[]{:S(2)}, u32[]{:S(2)}) collective-permute-start(bf16[80,1024]{1,0:T(8,128)(2,1)S(1)} %collective-permute-done.3.refs_3_), channel_id=1, source_target_pairs={{0,1},{1,0},{2,3},{3,2},{4,5},{5,4},{6,7},{7,6},{8,9},{9,8},{10,11... | collective-permute-start | bytes 491528 | tf_op jit(solution)/shard_map/ppermute | solution.py:347
  31.7 24.4 %collective-permute-start.16 = (bf16[8,160,384]{2,1,0:T(8,128)(2,1)S(1)}, bf16[8,160,384]{2,1,0:T(8,128)(2,1)S(1)}, u32[]{:S(2)}, u32[]{:S(2)}) collective-permute-start(bf16[8,160,384]{2,1,0:T(8,128)(2,1)S(1)} %get-tuple-element.53), channel_id=1, source_target_pairs={{0,2},{2,0},{1,3},{3,1},{4,6},{6,4},{5,7},{7,5},{8,10},{10,8},{9,1... | collective-permute-start | bytes 2949128 | tf_op jit(solution)/shard_map/ppermute | solution.py:347
  33.0 10.3 %collective-permute-start.11 = (bf16[64,1024]{1,0:T(8,128)(2,1)S(1)}, bf16[64,1024]{1,0:T(8,128)(2,1)S(1)}, u32[]{:S(2)}, u32[]{:S(2)}) collective-permute-start(bf16[64,1024]{1,0:T(8,128)(2,1)S(1)} %collective-permute-done.4.refs_0_), channel_id=1, source_target_pairs={{0,12},{4,0},{8,4},{12,8},{1,13},{5,1},{9,5},{13,9},{2,14},{6,2},{... | collective-permute-start | bytes 393224 | tf_op jit(solution)/shard_map/ppermute | solution.py:359
  33.2 14.2 %collective-permute-start.10 = (bf16[64,1024]{1,0:T(8,128)(2,1)S(1)}, bf16[64,1024]{1,0:T(8,128)(2,1)S(1)}, u32[]{:S(2)}, u32[]{:S(2)}) collective-permute-start(bf16[64,1024]{1,0:T(8,128)(2,1)S(1)} %collective-permute-done.4.refs_0_), channel_id=1, source_target_pairs={{0,8},{4,12},{8,0},{12,4},{1,9},{5,13},{9,1},{13,5},{2,10},{6,14},... | collective-permute-start | bytes 393224 | tf_op jit(solution)/shard_map/ppermute | solution.py:359
  35.7 11.8 %collective-permute-start.9 = (bf16[64,1024]{1,0:T(8,128)(2,1)S(1)}, bf16[64,1024]{1,0:T(8,128)(2,1)S(1)}, u32[]{:S(2)}, u32[]{:S(2)}) collective-permute-start(bf16[64,1024]{1,0:T(8,128)(2,1)S(1)} %collective-permute-done.4.refs_0_), channel_id=1, source_target_pairs={{0,4},{4,8},{8,12},{12,0},{1,5},{5,9},{9,13},{13,1},{2,6},{6,10},{... | collective-permute-start | bytes 393224 | tf_op jit(solution)/shard_map/ppermute | solution.py:359
  47.5 2.1 %collective-permute-start.12 = (bf16[64,1024]{1,0:T(8,128)(2,1)S(1)}, bf16[64,1024]{1,0:T(8,128)(2,1)S(1)}, u32[]{:S(2)}, u32[]{:S(2)}) collective-permute-start(bf16[64,1024]{1,0:T(8,128)(2,1)S(1)} %collective-permute-done.4.refs_0_), channel_id=1, source_target_pairs={{0,1},{1,0},{2,3},{3,2},{4,5},{5,4},{6,7},{7,6},{8,9},{9,8},{10,11... | collective-permute-start | bytes 393224 | tf_op jit(solution)/shard_map/ppermute | solution.py:347
  48.6 1.5 %collective-permute-start.14 = (bf16[64,1024]{1,0:T(8,128)(2,1)S(1)}, bf16[64,1024]{1,0:T(8,128)(2,1)S(1)}, u32[]{:S(2)}, u32[]{:S(2)}) collective-permute-start(bf16[64,1024]{1,0:T(8,128)(2,1)S(1)} %collective-permute-done.10.refs_2_), channel_id=1, source_target_pairs={{0,1},{1,0},{2,3},{3,2},{4,5},{5,4},{6,7},{7,6},{8,9},{9,8},{10,11... | collective-permute-start | bytes 393224 | tf_op jit(solution)/shard_map/ppermute | solution.py:347
  55.7 11.3 %collective-permute-start.17 = (bf16[4,80,384]{2,1,0:T(8,128)(2,1)S(1)}, bf16[4,80,384]{2,1,0:T(8,128)(2,1)S(1)}, u32[]{:S(2)}, u32[]{:S(2)}) collective-permute-start(bf16[4,80,384]{2,1,0:T(8,128)(2,1)S(1)} %get-tuple-element.57), channel_id=1, source_target_pairs={{0,2},{2,0},{1,3},{3,1},{4,6},{6,4},{5,7},{7,5},{8,10},{10,8},{9,1... | collective-permute-start | bytes 737288 | tf_op jit(solution)/shard_map/ppermute | solution.py:347
  59.7 8.7 %collective-permute-start.18 = (bf16[4,80,384]{2,1,0:T(8,128)(2,1)S(1)}, bf16[4,80,384]{2,1,0:T(8,128)(2,1)S(1)}, u32[]{:S(2)}, u32[]{:S(2)}) collective-permute-start(bf16[4,80,384]{2,1,0:T(8,128)(2,1)S(1)} %y_other.1), channel_id=1, source_target_pairs={{0,2},{2,0},{1,3},{3,1},{4,6},{6,4},{5,7},{7,5},{8,10},{10,8},{9,1... | collective-permute-start | bytes 737288 | tf_op jit(solution)/shard_map/ppermute | solution.py:347
  68.4 12.1 %collective-permute-start.19 = (bf16[4,160,384]{2,1,0:T(8,128)(2,1)S(1)}, bf16[4,160,384]{2,1,0:T(8,128)(2,1)}, u32[]{:S(2)}, u32[]{:S(2)}) collective-permute-start(bf16[4,160,384]{2,1,0:T(8,128)(2,1)S(1)} %get-tuple-element.64.refs_0_), channel_id=1, source_target_pairs={{0,2},{2,0},{1,3},{3,1},{4,6},{6,4},{5,7},{7,5},{8,10},{10,8},{9,1... | collective-permute-start | bytes 1474568 | tf_op jit(solution)/shard_map/ppermute | solution.py:347
  74.3 16.6 %collective-permute-start.21 = (bf16[4,160,384]{2,1,0:T(8,128)(2,1)S(1)}, bf16[4,160,384]{2,1,0:T(8,128)(2,1)S(1)}, u32[]{:S(2)}, u32[]{:S(2)}) collective-permute-start(bf16[4,160,384]{2,1,0:T(8,128)(2,1)S(1)} %get-tuple-element.67.refs_0_), channel_id=1, source_target_pairs={{0,2},{2,0},{1,3},{3,1},{4,6},{6,4},{5,7},{7,5},{8,10},{10,8},{9,1... | collective-permute-start | bytes 1474568 | tf_op jit(solution)/shard_map/ppermute | solution.py:347
  75.5 15.4 %collective-permute-start.20 = (f32[8,384]{1,0:T(8,128)S(1)}, f32[8,384]{1,0:T(8,128)S(1)}, u32[]{:S(2)}, u32[]{:S(2)}) collective-permute-start(f32[8,384]{1,0:T(8,128)S(1)} %bitcast.25), channel_id=1, source_target_pairs={{0,2},{2,0},{1,3},{3,1},{4,6},{6,4},{5,7},{7,5},{8,10},{10,8},{9,1... | collective-permute-start | bytes 36872 | tf_op jit(solution)/shard_map/ppermute | solution.py:347
  96.2 3.5 %collective-permute-start.22 = (bf16[4,64,1024]{2,1,0:T(8,128)(2,1)S(1)}, bf16[4,64,1024]{2,1,0:T(8,128)(2,1)S(1)}, u32[]{:S(2)}, u32[]{:S(2)}) collective-permute-start(bf16[4,64,1024]{2,1,0:T(8,128)(2,1)S(1)} %get-tuple-element.71), channel_id=1, source_target_pairs={{0,1},{1,0},{2,3},{3,2},{4,5},{5,4},{6,7},{7,6},{8,9},{9,8},{10,11... | collective-permute-start | bytes 1572872 | tf_op jit(solution)/shard_map/ppermute | solution.py:347
  100.0 8.7 %collective-permute-start.23 = (bf16[64,1024]{1,0:T(8,128)(2,1)S(1)}, bf16[64,1024]{1,0:T(8,128)(2,1)S(1)}, u32[]{:S(2)}, u32[]{:S(2)}) collective-permute-start(bf16[64,1024]{1,0:T(8,128)(2,1)S(1)} %get-tuple-element.72), channel_id=1, source_target_pairs={{0,0},{1,2},{2,1},{3,3},{4,4},{5,6},{6,5},{7,7},{8,8},{9,10},{10,9... | collective-permute-start | bytes 393224 | tf_op jit(solution)/shard_map/ppermute | solution.py:356
  102.6 8.1 %collective-permute-start.26 = (bf16[64,1024]{1,0:T(8,128)(2,1)S(1)}, bf16[64,1024]{1,0:T(8,128)(2,1)S(1)}, u32[]{:S(2)}, u32[]{:S(2)}) collective-permute-start(bf16[64,1024]{1,0:T(8,128)(2,1)S(1)} %get-tuple-element.73), channel_id=1, source_target_pairs={{0,4},{1,6},{2,5},{3,7},{4,8},{5,10},{6,9},{7,11},{8,12},{9,14},{1... | collective-permute-start | bytes 393224 | tf_op jit(solution)/shard_map/ppermute | solution.py:356
  102.7 11.0 %collective-permute-start.25 = (bf16[64,1024]{1,0:T(8,128)(2,1)S(1)}, bf16[64,1024]{1,0:T(8,128)(2,1)S(1)}, u32[]{:S(2)}, u32[]{:S(2)}) collective-permute-start(bf16[64,1024]{1,0:T(8,128)(2,1)S(1)} %get-tuple-element.74), channel_id=1, source_target_pairs={{0,8},{1,10},{2,9},{3,11},{4,12},{5,14},{6,13},{7,15},{8,0},{9,2},... | collective-permute-start | bytes 393224 | tf_op jit(solution)/shard_map/ppermute | solution.py:356
  104.6 9.2 %collective-permute-start.24 = (bf16[64,1024]{1,0:T(8,128)(2,1)S(1)}, bf16[64,1024]{1,0:T(8,128)(2,1)S(1)}, u32[]{:S(2)}, u32[]{:S(2)}) collective-permute-start(bf16[64,1024]{1,0:T(8,128)(2,1)S(1)} %get-tuple-element.75), channel_id=1, source_target_pairs={{0,12},{1,14},{2,13},{3,15},{4,0},{5,2},{6,1},{7,3},{8,4},{9,6},{1... | collective-permute-start | bytes 393224 | tf_op jit(solution)/shard_map/ppermute | solution.py:356
  (19 other events, 65.9 us)

commit v8 on v7

--- a/solution.py
+++ b/solution.py
@@ -293,7 +293,7 @@
     if at == 0:
         *mine_refs, acc, gate, up, part_ref, hot_ref, sem = refs
     elif last:
-        acc_in, keep_ref, send_ref, gate, up, part_ref, hot_ref, acc, sem = refs
+        acc_in, keep_ref, send_ref, gate, up, part_ref, hot_ref, sem = refs
     else:
         acc_in, acc, gate, up, part_ref, hot_ref, sem = refs
     copies = load((gate_ref, up_ref), first, count, (gate, up), sem)
@@ -320,13 +320,14 @@
     if at == 0:
         acc[...] += total
         return
-    acc[...] = total + acc_in[...]
+    total = total + acc_in[...]
     if not last:
+        acc[...] = total
         return
-    side = s_ref[1]
     for d in range(zs):
-        keep_ref[d] = acc[pl.ds(pl.multiple_of(2 * d * tok + side * tok, tok), tok), :]
-        send_ref[d] = acc[pl.ds(pl.multiple_of(2 * d * tok + (1 - side) * tok, tok), tok), :].astype(BF16)
+        low, high = total[2 * d * tok : (2 * d + 1) * tok], total[(2 * d + 1) * tok : 2 * (d + 1) * tok]
+        keep_ref[d] = jnp.where(s_ref[1] == 0, low, high)
+        send_ref[d] = jnp.where(s_ref[1] == 0, high, low).astype(BF16)
 
 
 def stationary(tokens, out_grad, gates, expert_ids, slots, gate_weight, up_weight, down_weight):
@@ -497,10 +498,7 @@
             "final",
         )
         scores.append(score)
-        if k == 0:
-            sent, dh_recv[1] = lax.optimization_barrier((d, dh_recv[1]))
-        else:
-            sent = d
+        sent = d
         back.append(flip(sent, "dp"))
         return d
 
@@ -539,7 +537,6 @@
             [(vmem, (back[k],)), weights, (vmem, (place, *given))],
             [sds(zshape, F32), sds(zshape, BF16)] if final else [sds(acc_shape, F32)],
             [wide(n), wide(n), pltpu.VMEM((n * rows, width), BF16), pltpu.VMEM((used * rows, all_tok), BF16)]
-            + ([pltpu.VMEM(acc_shape, F32)] if final else [])
             + [dma((2 * n,))],
             2 * n * flop + 2 * used * rows * width * all_tok,
             2 * n * wbytes,

time: 115 us -> 115 us (level)
  transfers between devices with their start and end apart: 27 -> 27, of which waited for: 16 -> 16; matrix products, arithmetic and copies ran while one was open for 1% -> 1% of each run, Pallas kernels for 32% -> 33%
where the time goes in v8:
time: 115 us; the launch traced here: 114 us
  Pallas kernels  50.4 us (44%)
  starting transfers between devices  35 us (30%)
  waiting for transfers between devices  24.4 us (21%)
  other arithmetic  1.74 us (2%)
  local copies, waits for them, and re-layouts  1.32 us (1%)
    pallas_call x11, Pallas kernels, call(): pl.pallas_call(body, out_shape=outs, in_specs=[smem] + ins, out_specs=jax...  48.7 us
    ppermute x9, starting transfers between devices, turn(): return lax.ppermute(v, ('expert', 'dp', 'sub'), pairs)  21.2 us
    ppermute x9, waiting for transfers between devices, turn(): return lax.ppermute(v, ('expert', 'dp', 'sub'), pairs)  11.2 us
    ppermute x15, starting transfers between devices, flip(): return lax.ppermute(v, axis, [(0, 1), (1, 0)])  9.76 us
    ppermute x15, waiting for transfers between devices, flip(): return lax.ppermute(v, axis, [(0, 1), (1, 0)])  9.04 us
    ppermute x3, waiting for transfers between devices, shift(): return lax.ppermute(v, 'expert', [(i, (i + d) % zs) for i in range(zs)])  4.2 us
    ppermute x3, starting transfers between devices, shift(): return lax.ppermute(v, 'expert', [(i, (i + d) % zs) for i in range(zs)])  4.1 us
  transfers between devices with their start and end apart: 27, of which 16 were waited for; matrix products, arithmetic and copies ran while one was open for 1% of the time, Pallas kernels for 33%

profile of v8, /device:TPU:1, one launch (start us, length us, event | category | flops | bytes accessed | tf_op | source)
XLA Modules:
  0.0 113.9 jit_solution(6274987971679305762)
XLA Ops:
  0.6 1.7 %pack.1 = bf16[80,1024]{1,0:T(8,128)(2,1)} custom-call(s32[1]{0:T(128)} %bitcast.3.p_ref, bf16[64,1024]{1,0:T(8,128)(2,1)} %tokens_ref.1, s32[8,64]{1,0:T(8,128)} %bitcast.26, s32[8,64]{1,0:T(8,128)} %bitcast.27, f32[8,64]{1,0:T(8,128)} %bitcast.28), custom_call_target="tpu_custom_call" | custom-call | tf_op jit(solution)/shard_map/pack/pallas_call | solution.py:384
  2.4 5.6 %collective-permute-start.3 = (bf16[80,1024]{1,0:T(8,128)(2,1)}, bf16[80,1024]{1,0:T(8,128)(2,1)S(1)}, u32[]{:S(2)}, u32[]{:S(2)}) collective-permute-start(bf16[80,1024]{1,0:T(8,128)(2,1)} %pack.1), channel_id=1, source_target_pairs={{0,12},{1,14},{2,13},{3,15},{4,0},{5,2},{6,1},{7,3},{8,4},{9,6},{1... | collective-permute-start | bytes 491528 | tf_op jit(solution)/shard_map/ppermute | solution.py:357
  8.0 1.6 %collective-permute-start.1 = (bf16[80,1024]{1,0:T(8,128)(2,1)}, bf16[80,1024]{1,0:T(8,128)(2,1)S(1)}, u32[]{:S(2)}, u32[]{:S(2)}) collective-permute-start(bf16[80,1024]{1,0:T(8,128)(2,1)} %pack.1), channel_id=1, source_target_pairs={{0,4},{1,6},{2,5},{3,7},{4,8},{5,10},{6,9},{7,11},{8,12},{9,14},{1... | collective-permute-start | bytes 491528 | tf_op jit(solution)/shard_map/ppermute | solution.py:357
  9.6 2.0 %collective-permute-start = (bf16[80,1024]{1,0:T(8,128)(2,1)}, bf16[80,1024]{1,0:T(8,128)(2,1)S(1)}, u32[]{:S(2)}, u32[]{:S(2)}) collective-permute-start(bf16[80,1024]{1,0:T(8,128)(2,1)} %pack.1), channel_id=1, source_target_pairs={{0,0},{1,2},{2,1},{3,3},{4,4},{5,6},{6,5},{7,7},{8,8},{9,10},{10,9... | collective-permute-start | bytes 491528 | tf_op jit(solution)/shard_map/ppermute | solution.py:357
  11.7 3.5 %collective-permute-start.4 = (bf16[64,1024]{1,0:T(8,128)(2,1)}, bf16[64,1024]{1,0:T(8,128)(2,1)S(1)}, u32[]{:S(2)}, u32[]{:S(2)}) collective-permute-start(bf16[64,1024]{1,0:T(8,128)(2,1)} %param.9), channel_id=1, source_target_pairs={{0,0},{1,2},{2,1},{3,3},{4,4},{5,6},{6,5},{7,7},{8,8},{9,10},{10,9... | collective-permute-start | bytes 393224 | tf_op jit(solution)/shard_map/ppermute | solution.py:357
  15.2 5.3 %collective-permute-done.4.refs_0_ = bf16[64,1024]{1,0:T(8,128)(2,1)S(1)} collective-permute-done((bf16[64,1024]{1,0:T(8,128)(2,1)}, bf16[64,1024]{1,0:T(8,128)(2,1)S(1)}, u32[]{:S(2)}, u32[]{:S(2)}) %collective-permute-start.4) | collective-permute-done | bytes 131104 | tf_op jit(solution)/shard_map/ppermute | solution.py:357
  25.4 6.3 %x_first.1 = (bf16[8,160,384]{2,1,0:T(8,128)(2,1)S(1)}, f32[16,512]{1,0:T(8,128)S(1)}, f32[16,512]{1,0:T(8,128)S(1)}) custom-call(s32[3]{0:T(128)S(1)} %get-tuple-element.74.s_ref, bf16[80,1024]{1,0:T(8,128)(2,1)} %copy-done.3, bf16[80,1024]{1,0:T(8,128)(2,1)} %copy-done.2, bf16[80,1024]{1,0:T(8,128)(2,1)} %copy-done.1, bf16[80,1024]{1,0:T(8,128)(2,1)} %copy-done, ...), custom_call_target="tpu_custom_call" | custom-call | flops 1677721600 | bytes 12582912 | tf_op jit(solution)/shard_map/x_first/pallas_call | solution.py:373
  33.2 2.5 %collective-permute-start.10 = (bf16[64,1024]{1,0:T(8,128)(2,1)S(1)}, bf16[64,1024]{1,0:T(8,128)(2,1)S(1)}, u32[]{:S(2)}, u32[]{:S(2)}) collective-permute-start(bf16[64,1024]{1,0:T(8,128)(2,1)S(1)} %collective-permute-done.4.refs_0_), channel_id=1, source_target_pairs={{0,8},{4,12},{8,0},{12,4},{1,9},{5,13},{9,1},{13,5},{2,10},{6,14},... | collective-permute-start | bytes 393224 | tf_op jit(solution)/shard_map/ppermute | solution.py:360
  37.1 6.1 %x_mine.1.au_m = f32[8,160,384]{2,1,0:T(8,128)S(1)} custom-call(s32[3]{0:T(128)S(1)} %add_add_fusion.s_ref, bf16[80,1024]{1,0:T(8,128)(2,1)} %copy-done.3, bf16[80,1024]{1,0:T(8,128)(2,1)} %copy-done.2, bf16[80,1024]{1,0:T(8,128)(2,1)} %copy-done.1, bf16[80,1024]{1,0:T(8,128)(2,1)} %copy-done, bf16[80,1024]{1,0:T(8,128)(2,1)} %copy-done.4, ...), custom_call_target="tpu_custom_call" | custom-call | flops 1677721600 | bytes 12582912 | tf_op jit(solution)/shard_map/x_mine/pallas_call | solution.py:373
  43.3 4.2 %collective-permute-done.10.refs_2_ = bf16[64,1024]{1,0:T(8,128)(2,1)S(1)} collective-permute-done((bf16[64,1024]{1,0:T(8,128)(2,1)S(1)}, bf16[64,1024]{1,0:T(8,128)(2,1)S(1)}, u32[]{:S(2)}, u32[]{:S(2)}) %collective-permute-start.10) | collective-permute-done | bytes 131104 | tf_op jit(solution)/shard_map/ppermute | solution.py:360
  51.1 4.6 %y_first.1 = (bf16[4,80,384]{2,1,0:T(8,128)(2,1)S(1)}, bf16[8,80,1024]{2,1,0:T(8,128)(2,1)}) custom-call(s32[3]{0:T(128)S(1)} %get-tuple-element.74.s_ref, bf16[64,1024]{1,0:T(8,128)(2,1)} %copy-done.8, bf16[64,1024]{1,0:T(8,128)(2,1)} %copy-done.11, bf16[64,1024]{1,0:T(8,128)(2,1)} %copy-done.10, bf16[64,1024]{1,0:T(8,128)(2,1)} %copy-done.9, ...), custom_call_target="tpu_custom_call" | custom-call | flops 922746880 | bytes 3145728 | tf_op jit(solution)/shard_map/y_first/pallas_call | solution.py:373
  56.1 3.6 %y_other.1 = bf16[4,80,384]{2,1,0:T(8,128)(2,1)S(1)} custom-call(s32[3]{0:T(128)S(1)} %get-tuple-element.75.s_ref, bf16[8,80,1024]{2,1,0:T(8,128)(2,1)} %get-tuple-element.52.yin_ref, bf16[16,384,1024]{2,1,0:T(8,128)(2,1)} %refs_10_.5), custom_call_target="tpu_custom_call" | custom-call | flops 251658240 | bytes 3145728 | tf_op jit(solution)/shard_map/y_other/pallas_call | solution.py:373
  60.9 6.1 %y_mine.1.dh_m = f32[8,80,384]{2,1,0:T(8,128)S(1)} custom-call(s32[3]{0:T(128)S(1)} %add_add_fusion.s_ref, bf16[64,1024]{1,0:T(8,128)(2,1)} %copy-done.8, bf16[64,1024]{1,0:T(8,128)(2,1)} %copy-done.11, bf16[64,1024]{1,0:T(8,128)(2,1)} %copy-done.10, bf16[64,1024]{1,0:T(8,128)(2,1)} %copy-done.9, bf16[64,1024]{1,0:T(8,128)(2,1)} %copy-done.12, ...), custom_call_target="tpu_custom_call" | custom-call | flops 1174405120 | bytes 6291456 | tf_op jit(solution)/shard_map/y_mine/pallas_call | solution.py:373
  68.4 4.4 %mine_parts.2.refs_0_ = bf16[320,1024]{1,0:T(8,128)(2,1)S(1)} custom-call(s32[3]{0:T(128)S(1)} %add_add_fusion.s_ref, bf16[4,160,384]{2,1,0:T(8,128)(2,1)S(1)} %get-tuple-element.57.refs_0_, bf16[16,1024,384]{2,1,0:T(8,128)(2,1)} %gate_ref.3, bf16[16,1024,384]{2,1,0:T(8,128)(2,1)} %up_ref.3), custom_call_target="tpu_custom_call" | custom-call | flops 503316480 | bytes 6291456 | tf_op jit(solution)/shard_map/mine_parts/pallas_call | solution.py:373
  75.6 4.4 %mine_parts.3.refs_1_ = bf16[320,1024]{1,0:T(8,128)(2,1)S(1)} custom-call(s32[3]{0:T(128)S(1)} %add_add_fusion.3.s_ref, bf16[4,160,384]{2,1,0:T(8,128)(2,1)S(1)} %get-tuple-element.63.refs_0_, bf16[16,1024,384]{2,1,0:T(8,128)(2,1)} %gate_ref.3, bf16[16,1024,384]{2,1,0:T(8,128)(2,1)} %up_ref.3), custom_call_target="tpu_custom_call" | custom-call | flops 503316480 | bytes 6291456 | tf_op jit(solution)/shard_map/mine_parts/pallas_call | solution.py:373
  80.2 5.8 %combine.2.refs_0_ = f32[512,1024]{1,0:T(8,128)S(1)} custom-call(s32[3]{0:T(128)S(1)} %get-tuple-element.74.s_ref, bf16[4,160,384]{2,1,0:T(8,128)(2,1)} %collective-permute-done.19.d_ref, bf16[16,1024,384]{2,1,0:T(8,128)(2,1)} %gate_ref.3, bf16[16,1024,384]{2,1,0:T(8,128)(2,1)} %up_ref.3, f32[16,512]{1,0:T(8,128)S(1)} %get-tuple-element.53.refs_8_.place_ref, ...), custom_call_target="tpu_custom_call" | custom-call | flops 1509949440 | bytes 6291456 | tf_op jit(solution)/shard_map/combine/pallas_call | solution.py:373
  86.0 4.8 %collective-permute-done.20 = f32[8,384]{1,0:T(8,128)S(1)} collective-permute-done((f32[8,384]{1,0:T(8,128)S(1)}, f32[8,384]{1,0:T(8,128)S(1)}, u32[]{:S(2)}, u32[]{:S(2)}) %collective-permute-start.20) | collective-permute-done | bytes 12320 | tf_op jit(solution)/shard_map/ppermute | solution.py:348
  90.9 5.2 %combine.3 = (f32[4,64,1024]{2,1,0:T(8,128)S(1)}, bf16[4,64,1024]{2,1,0:T(8,128)(2,1)S(1)}) custom-call(s32[3]{0:T(128)S(1)} %get-tuple-element.74.s_ref, bf16[4,160,384]{2,1,0:T(8,128)(2,1)S(1)} %collective-permute-done.21.d_ref, bf16[16,1024,384]{2,1,0:T(8,128)(2,1)} %gate_ref.3, bf16[16,1024,384]{2,1,0:T(8,128)(2,1)} %up_ref.3, ...), custom_call_target="tpu_custom_call" | custom-call | flops 838860800 | bytes 6291456 | tf_op jit(solution)/shard_map/combine/pallas_call | solution.py:373
  96.1 1.7 %collective-permute-start.22 = (bf16[4,64,1024]{2,1,0:T(8,128)(2,1)S(1)}, bf16[4,64,1024]{2,1,0:T(8,128)(2,1)S(1)}, u32[]{:S(2)}, u32[]{:S(2)}) collective-permute-start(bf16[4,64,1024]{2,1,0:T(8,128)(2,1)S(1)} %get-tuple-element.67), channel_id=1, source_target_pairs={{0,1},{1,0},{2,3},{3,2},{4,5},{5,4},{6,7},{7,6},{8,9},{9,8},{10,11... | collective-permute-start | bytes 1572872 | tf_op jit(solution)/shard_map/ppermute | solution.py:348
  99.5 2.5 %collective-permute-start.23 = (bf16[64,1024]{1,0:T(8,128)(2,1)S(1)}, bf16[64,1024]{1,0:T(8,128)(2,1)S(1)}, u32[]{:S(2)}, u32[]{:S(2)}) collective-permute-start(bf16[64,1024]{1,0:T(8,128)(2,1)S(1)} %get-tuple-element.68), channel_id=1, source_target_pairs={{0,0},{1,2},{2,1},{3,3},{4,4},{5,6},{6,5},{7,7},{8,8},{9,10},{10,9... | collective-permute-start | bytes 393224 | tf_op jit(solution)/shard_map/ppermute | solution.py:357
  102.1 2.3 %collective-permute-start.25 = (bf16[64,1024]{1,0:T(8,128)(2,1)S(1)}, bf16[64,1024]{1,0:T(8,128)(2,1)S(1)}, u32[]{:S(2)}, u32[]{:S(2)}) collective-permute-start(bf16[64,1024]{1,0:T(8,128)(2,1)S(1)} %get-tuple-element.70), channel_id=1, source_target_pairs={{0,8},{1,10},{2,9},{3,11},{4,12},{5,14},{6,13},{7,15},{8,0},{9,2},... | collective-permute-start | bytes 393224 | tf_op jit(solution)/shard_map/ppermute | solution.py:357
  104.4 3.5 %collective-permute-start.24 = (bf16[64,1024]{1,0:T(8,128)(2,1)S(1)}, bf16[64,1024]{1,0:T(8,128)(2,1)S(1)}, u32[]{:S(2)}, u32[]{:S(2)}) collective-permute-start(bf16[64,1024]{1,0:T(8,128)(2,1)S(1)} %get-tuple-element.71), channel_id=1, source_target_pairs={{0,12},{1,14},{2,13},{3,15},{4,0},{5,2},{6,1},{7,3},{8,4},{9,6},{1... | collective-permute-start | bytes 393224 | tf_op jit(solution)/shard_map/ppermute | solution.py:357
  108.5 1.7 %collective-permute-done.26 = bf16[64,1024]{1,0:T(8,128)(2,1)S(1)} collective-permute-done((bf16[64,1024]{1,0:T(8,128)(2,1)S(1)}, bf16[64,1024]{1,0:T(8,128)(2,1)S(1)}, u32[]{:S(2)}, u32[]{:S(2)}) %collective-permute-start.26) | collective-permute-done | bytes 131104 | tf_op jit(solution)/shard_map/ppermute | solution.py:357
  110.2 2.9 %collective-permute-done.25 = bf16[64,1024]{1,0:T(8,128)(2,1)S(1)} collective-permute-done((bf16[64,1024]{1,0:T(8,128)(2,1)S(1)}, bf16[64,1024]{1,0:T(8,128)(2,1)S(1)}, u32[]{:S(2)}, u32[]{:S(2)}) %collective-permute-start.25) | collective-permute-done | bytes 131104 | tf_op jit(solution)/shard_map/ppermute | solution.py:357
  (84 shorter events, 20.4 us)
Async XLA Ops:
  2.4 18.1 %collective-permute-start.3 = (bf16[80,1024]{1,0:T(8,128)(2,1)}, bf16[80,1024]{1,0:T(8,128)(2,1)S(1)}, u32[]{:S(2)}, u32[]{:S(2)}) collective-permute-start(bf16[80,1024]{1,0:T(8,128)(2,1)} %pack.1), channel_id=1, source_target_pairs={{0,12},{1,14},{2,13},{3,15},{4,0},{5,2},{6,1},{7,3},{8,4},{9,6},{1... | collective-permute-start | bytes 491528 | tf_op jit(solution)/shard_map/ppermute | solution.py:357
  8.0 13.8 %collective-permute-start.2 = (bf16[80,1024]{1,0:T(8,128)(2,1)}, bf16[80,1024]{1,0:T(8,128)(2,1)S(1)}, u32[]{:S(2)}, u32[]{:S(2)}) collective-permute-start(bf16[80,1024]{1,0:T(8,128)(2,1)} %pack.1), channel_id=1, source_target_pairs={{0,8},{1,10},{2,9},{3,11},{4,12},{5,14},{6,13},{7,15},{8,0},{9,2},... | collective-permute-start | bytes 491528 | tf_op jit(solution)/shard_map/ppermute | solution.py:357
  8.0 13.8 %collective-permute-start.1 = (bf16[80,1024]{1,0:T(8,128)(2,1)}, bf16[80,1024]{1,0:T(8,128)(2,1)S(1)}, u32[]{:S(2)}, u32[]{:S(2)}) collective-permute-start(bf16[80,1024]{1,0:T(8,128)(2,1)} %pack.1), channel_id=1, source_target_pairs={{0,4},{1,6},{2,5},{3,7},{4,8},{5,10},{6,9},{7,11},{8,12},{9,14},{1... | collective-permute-start | bytes 491528 | tf_op jit(solution)/shard_map/ppermute | solution.py:357
  9.6 12.2 %collective-permute-start = (bf16[80,1024]{1,0:T(8,128)(2,1)}, bf16[80,1024]{1,0:T(8,128)(2,1)S(1)}, u32[]{:S(2)}, u32[]{:S(2)}) collective-permute-start(bf16[80,1024]{1,0:T(8,128)(2,1)} %pack.1), channel_id=1, source_target_pairs={{0,0},{1,2},{2,1},{3,3},{4,4},{5,6},{6,5},{7,7},{8,8},{9,10},{10,9... | collective-permute-start | bytes 491528 | tf_op jit(solution)/shard_map/ppermute | solution.py:357
  11.7 8.8 %collective-permute-start.4 = (bf16[64,1024]{1,0:T(8,128)(2,1)}, bf16[64,1024]{1,0:T(8,128)(2,1)S(1)}, u32[]{:S(2)}, u32[]{:S(2)}) collective-permute-start(bf16[64,1024]{1,0:T(8,128)(2,1)} %param.9), channel_id=1, source_target_pairs={{0,0},{1,2},{2,1},{3,3},{4,4},{5,6},{6,5},{7,7},{8,8},{9,10},{10,9... | collective-permute-start | bytes 393224 | tf_op jit(solution)/shard_map/ppermute | solution.py:357
  21.8 2.0 %collective-permute-start.5 = (bf16[80,1024]{1,0:T(8,128)(2,1)S(1)}, bf16[80,1024]{1,0:T(8,128)(2,1)S(1)}, u32[]{:S(2)}, u32[]{:S(2)}) collective-permute-start(bf16[80,1024]{1,0:T(8,128)(2,1)S(1)} %collective-permute-done.refs_0_), channel_id=1, source_target_pairs={{0,1},{1,0},{2,3},{3,2},{4,5},{5,4},{6,7},{7,6},{8,9},{9,8},{10,11... | collective-permute-start | bytes 491528 | tf_op jit(solution)/shard_map/ppermute | solution.py:348
  22.8 1.4 %collective-permute-start.6 = (bf16[80,1024]{1,0:T(8,128)(2,1)S(1)}, bf16[80,1024]{1,0:T(8,128)(2,1)S(1)}, u32[]{:S(2)}, u32[]{:S(2)}) collective-permute-start(bf16[80,1024]{1,0:T(8,128)(2,1)S(1)} %collective-permute-done.1.refs_1_), channel_id=1, source_target_pairs={{0,1},{1,0},{2,3},{3,2},{4,5},{5,4},{6,7},{7,6},{8,9},{9,8},{10,11... | collective-permute-start | bytes 491528 | tf_op jit(solution)/shard_map/ppermute | solution.py:348
  22.9 1.6 %collective-permute-start.7 = (bf16[80,1024]{1,0:T(8,128)(2,1)S(1)}, bf16[80,1024]{1,0:T(8,128)(2,1)S(1)}, u32[]{:S(2)}, u32[]{:S(2)}) collective-permute-start(bf16[80,1024]{1,0:T(8,128)(2,1)S(1)} %collective-permute-done.2.refs_2_), channel_id=1, source_target_pairs={{0,1},{1,0},{2,3},{3,2},{4,5},{5,4},{6,7},{7,6},{8,9},{9,8},{10,11... | collective-permute-start | bytes 491528 | tf_op jit(solution)/shard_map/ppermute | solution.py:348
  31.7 24.4 %collective-permute-start.16 = (bf16[8,160,384]{2,1,0:T(8,128)(2,1)S(1)}, bf16[8,160,384]{2,1,0:T(8,128)(2,1)S(1)}, u32[]{:S(2)}, u32[]{:S(2)}) collective-permute-start(bf16[8,160,384]{2,1,0:T(8,128)(2,1)S(1)} %get-tuple-element.51), channel_id=1, source_target_pairs={{0,2},{2,0},{1,3},{3,1},{4,6},{6,4},{5,7},{7,5},{8,10},{10,8},{9,1... | collective-permute-start | bytes 2949128 | tf_op jit(solution)/shard_map/ppermute | solution.py:348
  33.0 10.3 %collective-permute-start.11 = (bf16[64,1024]{1,0:T(8,128)(2,1)S(1)}, bf16[64,1024]{1,0:T(8,128)(2,1)S(1)}, u32[]{:S(2)}, u32[]{:S(2)}) collective-permute-start(bf16[64,1024]{1,0:T(8,128)(2,1)S(1)} %collective-permute-done.4.refs_0_), channel_id=1, source_target_pairs={{0,12},{4,0},{8,4},{12,8},{1,13},{5,1},{9,5},{13,9},{2,14},{6,2},{... | collective-permute-start | bytes 393224 | tf_op jit(solution)/shard_map/ppermute | solution.py:360
  33.2 14.2 %collective-permute-start.10 = (bf16[64,1024]{1,0:T(8,128)(2,1)S(1)}, bf16[64,1024]{1,0:T(8,128)(2,1)S(1)}, u32[]{:S(2)}, u32[]{:S(2)}) collective-permute-start(bf16[64,1024]{1,0:T(8,128)(2,1)S(1)} %collective-permute-done.4.refs_0_), channel_id=1, source_target_pairs={{0,8},{4,12},{8,0},{12,4},{1,9},{5,13},{9,1},{13,5},{2,10},{6,14},... | collective-permute-start | bytes 393224 | tf_op jit(solution)/shard_map/ppermute | solution.py:360
  35.7 11.8 %collective-permute-start.9 = (bf16[64,1024]{1,0:T(8,128)(2,1)S(1)}, bf16[64,1024]{1,0:T(8,128)(2,1)S(1)}, u32[]{:S(2)}, u32[]{:S(2)}) collective-permute-start(bf16[64,1024]{1,0:T(8,128)(2,1)S(1)} %collective-permute-done.4.refs_0_), channel_id=1, source_target_pairs={{0,4},{4,8},{8,12},{12,0},{1,5},{5,9},{9,13},{13,1},{2,6},{6,10},{... | collective-permute-start | bytes 393224 | tf_op jit(solution)/shard_map/ppermute | solution.py:360
  47.5 2.1 %collective-permute-start.12 = (bf16[64,1024]{1,0:T(8,128)(2,1)S(1)}, bf16[64,1024]{1,0:T(8,128)(2,1)S(1)}, u32[]{:S(2)}, u32[]{:S(2)}) collective-permute-start(bf16[64,1024]{1,0:T(8,128)(2,1)S(1)} %collective-permute-done.4.refs_0_), channel_id=1, source_target_pairs={{0,1},{1,0},{2,3},{3,2},{4,5},{5,4},{6,7},{7,6},{8,9},{9,8},{10,11... | collective-permute-start | bytes 393224 | tf_op jit(solution)/shard_map/ppermute | solution.py:348
  48.6 1.5 %collective-permute-start.14 = (bf16[64,1024]{1,0:T(8,128)(2,1)S(1)}, bf16[64,1024]{1,0:T(8,128)(2,1)S(1)}, u32[]{:S(2)}, u32[]{:S(2)}) collective-permute-start(bf16[64,1024]{1,0:T(8,128)(2,1)S(1)} %collective-permute-done.10.refs_2_), channel_id=1, source_target_pairs={{0,1},{1,0},{2,3},{3,2},{4,5},{5,4},{6,7},{7,6},{8,9},{9,8},{10,11... | collective-permute-start | bytes 393224 | tf_op jit(solution)/shard_map/ppermute | solution.py:348
  55.7 11.3 %collective-permute-start.17 = (bf16[4,80,384]{2,1,0:T(8,128)(2,1)S(1)}, bf16[4,80,384]{2,1,0:T(8,128)(2,1)S(1)}, u32[]{:S(2)}, u32[]{:S(2)}) collective-permute-start(bf16[4,80,384]{2,1,0:T(8,128)(2,1)S(1)} %get-tuple-element.55), channel_id=1, source_target_pairs={{0,2},{2,0},{1,3},{3,1},{4,6},{6,4},{5,7},{7,5},{8,10},{10,8},{9,1... | collective-permute-start | bytes 737288 | tf_op jit(solution)/shard_map/ppermute | solution.py:348
  59.7 13.2 %collective-permute-start.18 = (bf16[4,80,384]{2,1,0:T(8,128)(2,1)S(1)}, bf16[4,80,384]{2,1,0:T(8,128)(2,1)S(1)}, u32[]{:S(2)}, u32[]{:S(2)}) collective-permute-start(bf16[4,80,384]{2,1,0:T(8,128)(2,1)S(1)} %y_other.1), channel_id=1, source_target_pairs={{0,2},{2,0},{1,3},{3,1},{4,6},{6,4},{5,7},{7,5},{8,10},{10,8},{9,1... | collective-permute-start | bytes 737288 | tf_op jit(solution)/shard_map/ppermute | solution.py:348
  68.0 12.2 %collective-permute-start.19 = (bf16[4,160,384]{2,1,0:T(8,128)(2,1)S(1)}, bf16[4,160,384]{2,1,0:T(8,128)(2,1)}, u32[]{:S(2)}, u32[]{:S(2)}) collective-permute-start(bf16[4,160,384]{2,1,0:T(8,128)(2,1)S(1)} %get-tuple-element.57.refs_0_), channel_id=1, source_target_pairs={{0,2},{2,0},{1,3},{3,1},{4,6},{6,4},{5,7},{7,5},{8,10},{10,8},{9,1... | collective-permute-start | bytes 1474568 | tf_op jit(solution)/shard_map/ppermute | solution.py:348
  73.9 17.0 %collective-permute-start.21 = (bf16[4,160,384]{2,1,0:T(8,128)(2,1)S(1)}, bf16[4,160,384]{2,1,0:T(8,128)(2,1)S(1)}, u32[]{:S(2)}, u32[]{:S(2)}) collective-permute-start(bf16[4,160,384]{2,1,0:T(8,128)(2,1)S(1)} %get-tuple-element.63.refs_0_), channel_id=1, source_target_pairs={{0,2},{2,0},{1,3},{3,1},{4,6},{6,4},{5,7},{7,5},{8,10},{10,8},{9,1... | collective-permute-start | bytes 1474568 | tf_op jit(solution)/shard_map/ppermute | solution.py:348
  75.2 15.7 %collective-permute-start.20 = (f32[8,384]{1,0:T(8,128)S(1)}, f32[8,384]{1,0:T(8,128)S(1)}, u32[]{:S(2)}, u32[]{:S(2)}) collective-permute-start(f32[8,384]{1,0:T(8,128)S(1)} %bitcast.25), channel_id=1, source_target_pairs={{0,2},{2,0},{1,3},{3,1},{4,6},{6,4},{5,7},{7,5},{8,10},{10,8},{9,1... | collective-permute-start | bytes 36872 | tf_op jit(solution)/shard_map/ppermute | solution.py:348
  96.1 3.2 %collective-permute-start.22 = (bf16[4,64,1024]{2,1,0:T(8,128)(2,1)S(1)}, bf16[4,64,1024]{2,1,0:T(8,128)(2,1)S(1)}, u32[]{:S(2)}, u32[]{:S(2)}) collective-permute-start(bf16[4,64,1024]{2,1,0:T(8,128)(2,1)S(1)} %get-tuple-element.67), channel_id=1, source_target_pairs={{0,1},{1,0},{2,3},{3,2},{4,5},{5,4},{6,7},{7,6},{8,9},{9,8},{10,11... | collective-permute-start | bytes 1572872 | tf_op jit(solution)/shard_map/ppermute | solution.py:348
  99.5 9.0 %collective-permute-start.23 = (bf16[64,1024]{1,0:T(8,128)(2,1)S(1)}, bf16[64,1024]{1,0:T(8,128)(2,1)S(1)}, u32[]{:S(2)}, u32[]{:S(2)}) collective-permute-start(bf16[64,1024]{1,0:T(8,128)(2,1)S(1)} %get-tuple-element.68), channel_id=1, source_target_pairs={{0,0},{1,2},{2,1},{3,3},{4,4},{5,6},{6,5},{7,7},{8,8},{9,10},{10,9... | collective-permute-start | bytes 393224 | tf_op jit(solution)/shard_map/ppermute | solution.py:357
  102.0 8.2 %collective-permute-start.26 = (bf16[64,1024]{1,0:T(8,128)(2,1)S(1)}, bf16[64,1024]{1,0:T(8,128)(2,1)S(1)}, u32[]{:S(2)}, u32[]{:S(2)}) collective-permute-start(bf16[64,1024]{1,0:T(8,128)(2,1)S(1)} %get-tuple-element.69), channel_id=1, source_target_pairs={{0,4},{1,6},{2,5},{3,7},{4,8},{5,10},{6,9},{7,11},{8,12},{9,14},{1... | collective-permute-start | bytes 393224 | tf_op jit(solution)/shard_map/ppermute | solution.py:357
  102.1 11.0 %collective-permute-start.25 = (bf16[64,1024]{1,0:T(8,128)(2,1)S(1)}, bf16[64,1024]{1,0:T(8,128)(2,1)S(1)}, u32[]{:S(2)}, u32[]{:S(2)}) collective-permute-start(bf16[64,1024]{1,0:T(8,128)(2,1)S(1)} %get-tuple-element.70), channel_id=1, source_target_pairs={{0,8},{1,10},{2,9},{3,11},{4,12},{5,14},{6,13},{7,15},{8,0},{9,2},... | collective-permute-start | bytes 393224 | tf_op jit(solution)/shard_map/ppermute | solution.py:357
  104.4 8.7 %collective-permute-start.24 = (bf16[64,1024]{1,0:T(8,128)(2,1)S(1)}, bf16[64,1024]{1,0:T(8,128)(2,1)S(1)}, u32[]{:S(2)}, u32[]{:S(2)}) collective-permute-start(bf16[64,1024]{1,0:T(8,128)(2,1)S(1)} %get-tuple-element.71), channel_id=1, source_target_pairs={{0,12},{1,14},{2,13},{3,15},{4,0},{5,2},{6,1},{7,3},{8,4},{9,6},{1... | collective-permute-start | bytes 393224 | tf_op jit(solution)/shard_map/ppermute | solution.py:357
  (19 other events, 65.9 us)

commit v9 on v8

--- a/solution.py
+++ b/solution.py
@@ -337,7 +337,7 @@
     rows = 2 * zs * CAP
     all_tok = 2 * zs * tok
     half = experts // 2
-    group = 4 if half % 4 == 0 else 1
+    group = half
     p, s, z = lax.axis_index("dp"), lax.axis_index("sub"), lax.axis_index("expert")
     mine0, other0 = half * p, half * (1 - p)
     first = half // 2

time: 115 us -> 114 us (level)
  transfers between devices with their start and end apart: 27 -> 27, of which waited for: 16 -> 16; matrix products, arithmetic and copies ran while one was open for 1% -> 1% of each run, Pallas kernels for 33% -> 32%
where the time goes in v9:
time: 114 us; the launch traced here: 113 us
  Pallas kernels  49.8 us (44%)
  starting transfers between devices  35.3 us (31%)
  waiting for transfers between devices  24.2 us (21%)
  other arithmetic  1.74 us (2%)
  local copies, waits for them, and re-layouts  1.32 us (1%)
    pallas_call x11, Pallas kernels, call(): pl.pallas_call(body, out_shape=outs, in_specs=[smem] + ins, out_specs=jax...  48.1 us
    ppermute x9, starting transfers between devices, turn(): return lax.ppermute(v, ('expert', 'dp', 'sub'), pairs)  21.5 us
    ppermute x9, waiting for transfers between devices, turn(): return lax.ppermute(v, ('expert', 'dp', 'sub'), pairs)  11 us
    ppermute x15, starting transfers between devices, flip(): return lax.ppermute(v, axis, [(0, 1), (1, 0)])  9.77 us
    ppermute x15, waiting for transfers between devices, flip(): return lax.ppermute(v, axis, [(0, 1), (1, 0)])  9.02 us
    ppermute x3, waiting for transfers between devices, shift(): return lax.ppermute(v, 'expert', [(i, (i + d) % zs) for i in range(zs)])  4.2 us
    ppermute x3, starting transfers between devices, shift(): return lax.ppermute(v, 'expert', [(i, (i + d) % zs) for i in range(zs)])  4.1 us
  transfers between devices with their start and end apart: 27, of which 16 were waited for; matrix products, arithmetic and copies ran while one was open for 1% of the time, Pallas kernels for 32%

profile of v9, /device:TPU:1, one launch (start us, length us, event | category | flops | bytes accessed | tf_op | source)
XLA Modules:
  0.0 113.3 jit_solution(5595790610623088491)
XLA Ops:
  0.6 1.7 %pack.1 = bf16[80,1024]{1,0:T(8,128)(2,1)} custom-call(s32[1]{0:T(128)} %bitcast.3.p_ref, bf16[64,1024]{1,0:T(8,128)(2,1)} %tokens_ref.1, s32[8,64]{1,0:T(8,128)} %bitcast.26, s32[8,64]{1,0:T(8,128)} %bitcast.27, f32[8,64]{1,0:T(8,128)} %bitcast.28), custom_call_target="tpu_custom_call" | custom-call | tf_op jit(solution)/shard_map/pack/pallas_call | solution.py:384
  2.4 5.6 %collective-permute-start.3 = (bf16[80,1024]{1,0:T(8,128)(2,1)}, bf16[80,1024]{1,0:T(8,128)(2,1)S(1)}, u32[]{:S(2)}, u32[]{:S(2)}) collective-permute-start(bf16[80,1024]{1,0:T(8,128)(2,1)} %pack.1), channel_id=1, source_target_pairs={{0,12},{1,14},{2,13},{3,15},{4,0},{5,2},{6,1},{7,3},{8,4},{9,6},{1... | collective-permute-start | bytes 491528 | tf_op jit(solution)/shard_map/ppermute | solution.py:357
  8.0 1.6 %collective-permute-start.1 = (bf16[80,1024]{1,0:T(8,128)(2,1)}, bf16[80,1024]{1,0:T(8,128)(2,1)S(1)}, u32[]{:S(2)}, u32[]{:S(2)}) collective-permute-start(bf16[80,1024]{1,0:T(8,128)(2,1)} %pack.1), channel_id=1, source_target_pairs={{0,4},{1,6},{2,5},{3,7},{4,8},{5,10},{6,9},{7,11},{8,12},{9,14},{1... | collective-permute-start | bytes 491528 | tf_op jit(solution)/shard_map/ppermute | solution.py:357
  9.6 2.0 %collective-permute-start = (bf16[80,1024]{1,0:T(8,128)(2,1)}, bf16[80,1024]{1,0:T(8,128)(2,1)S(1)}, u32[]{:S(2)}, u32[]{:S(2)}) collective-permute-start(bf16[80,1024]{1,0:T(8,128)(2,1)} %pack.1), channel_id=1, source_target_pairs={{0,0},{1,2},{2,1},{3,3},{4,4},{5,6},{6,5},{7,7},{8,8},{9,10},{10,9... | collective-permute-start | bytes 491528 | tf_op jit(solution)/shard_map/ppermute | solution.py:357
  11.7 3.5 %collective-permute-start.4 = (bf16[64,1024]{1,0:T(8,128)(2,1)}, bf16[64,1024]{1,0:T(8,128)(2,1)S(1)}, u32[]{:S(2)}, u32[]{:S(2)}) collective-permute-start(bf16[64,1024]{1,0:T(8,128)(2,1)} %param.9), channel_id=1, source_target_pairs={{0,0},{1,2},{2,1},{3,3},{4,4},{5,6},{6,5},{7,7},{8,8},{9,10},{10,9... | collective-permute-start | bytes 393224 | tf_op jit(solution)/shard_map/ppermute | solution.py:357
  15.2 5.3 %collective-permute-done.4.refs_0_ = bf16[64,1024]{1,0:T(8,128)(2,1)S(1)} collective-permute-done((bf16[64,1024]{1,0:T(8,128)(2,1)}, bf16[64,1024]{1,0:T(8,128)(2,1)S(1)}, u32[]{:S(2)}, u32[]{:S(2)}) %collective-permute-start.4) | collective-permute-done | bytes 131104 | tf_op jit(solution)/shard_map/ppermute | solution.py:357
  25.4 6.3 %x_first.1 = (bf16[8,160,384]{2,1,0:T(8,128)(2,1)S(1)}, f32[16,512]{1,0:T(8,128)S(1)}, f32[16,512]{1,0:T(8,128)S(1)}) custom-call(s32[3]{0:T(128)S(1)} %get-tuple-element.74.s_ref, bf16[80,1024]{1,0:T(8,128)(2,1)} %copy-done.3, bf16[80,1024]{1,0:T(8,128)(2,1)} %copy-done.2, bf16[80,1024]{1,0:T(8,128)(2,1)} %copy-done.1, bf16[80,1024]{1,0:T(8,128)(2,1)} %copy-done, ...), custom_call_target="tpu_custom_call" | custom-call | flops 1677721600 | bytes 12582912 | tf_op jit(solution)/shard_map/x_first/pallas_call | solution.py:373
  33.2 2.5 %collective-permute-start.10 = (bf16[64,1024]{1,0:T(8,128)(2,1)S(1)}, bf16[64,1024]{1,0:T(8,128)(2,1)S(1)}, u32[]{:S(2)}, u32[]{:S(2)}) collective-permute-start(bf16[64,1024]{1,0:T(8,128)(2,1)S(1)} %collective-permute-done.4.refs_0_), channel_id=1, source_target_pairs={{0,8},{4,12},{8,0},{12,4},{1,9},{5,13},{9,1},{13,5},{2,10},{6,14},... | collective-permute-start | bytes 393224 | tf_op jit(solution)/shard_map/ppermute | solution.py:360
  37.0 6.1 %x_mine.1.au_m = f32[8,160,384]{2,1,0:T(8,128)S(1)} custom-call(s32[3]{0:T(128)S(1)} %add_add_fusion.s_ref, bf16[80,1024]{1,0:T(8,128)(2,1)} %copy-done.3, bf16[80,1024]{1,0:T(8,128)(2,1)} %copy-done.2, bf16[80,1024]{1,0:T(8,128)(2,1)} %copy-done.1, bf16[80,1024]{1,0:T(8,128)(2,1)} %copy-done, bf16[80,1024]{1,0:T(8,128)(2,1)} %copy-done.4, ...), custom_call_target="tpu_custom_call" | custom-call | flops 1677721600 | bytes 12582912 | tf_op jit(solution)/shard_map/x_mine/pallas_call | solution.py:373
  43.2 4.2 %collective-permute-done.10.refs_2_ = bf16[64,1024]{1,0:T(8,128)(2,1)S(1)} collective-permute-done((bf16[64,1024]{1,0:T(8,128)(2,1)S(1)}, bf16[64,1024]{1,0:T(8,128)(2,1)S(1)}, u32[]{:S(2)}, u32[]{:S(2)}) %collective-permute-start.10) | collective-permute-done | bytes 131104 | tf_op jit(solution)/shard_map/ppermute | solution.py:360
  51.0 4.4 %y_first.1 = (bf16[4,80,384]{2,1,0:T(8,128)(2,1)S(1)}, bf16[8,80,1024]{2,1,0:T(8,128)(2,1)}) custom-call(s32[3]{0:T(128)S(1)} %get-tuple-element.74.s_ref, bf16[64,1024]{1,0:T(8,128)(2,1)} %copy-done.8, bf16[64,1024]{1,0:T(8,128)(2,1)} %copy-done.11, bf16[64,1024]{1,0:T(8,128)(2,1)} %copy-done.10, bf16[64,1024]{1,0:T(8,128)(2,1)} %copy-done.9, ...), custom_call_target="tpu_custom_call" | custom-call | flops 922746880 | bytes 3145728 | tf_op jit(solution)/shard_map/y_first/pallas_call | solution.py:373
  55.8 3.6 %y_other.1 = bf16[4,80,384]{2,1,0:T(8,128)(2,1)S(1)} custom-call(s32[3]{0:T(128)S(1)} %get-tuple-element.75.s_ref, bf16[8,80,1024]{2,1,0:T(8,128)(2,1)} %get-tuple-element.52.yin_ref, bf16[16,384,1024]{2,1,0:T(8,128)(2,1)} %refs_10_.5), custom_call_target="tpu_custom_call" | custom-call | flops 251658240 | bytes 3145728 | tf_op jit(solution)/shard_map/y_other/pallas_call | solution.py:373
  60.6 5.9 %y_mine.1.dh_m = f32[8,80,384]{2,1,0:T(8,128)S(1)} custom-call(s32[3]{0:T(128)S(1)} %add_add_fusion.s_ref, bf16[64,1024]{1,0:T(8,128)(2,1)} %copy-done.8, bf16[64,1024]{1,0:T(8,128)(2,1)} %copy-done.11, bf16[64,1024]{1,0:T(8,128)(2,1)} %copy-done.10, bf16[64,1024]{1,0:T(8,128)(2,1)} %copy-done.9, bf16[64,1024]{1,0:T(8,128)(2,1)} %copy-done.12, ...), custom_call_target="tpu_custom_call" | custom-call | flops 1174405120 | bytes 6291456 | tf_op jit(solution)/shard_map/y_mine/pallas_call | solution.py:373
  67.9 4.4 %mine_parts.2.refs_0_ = bf16[320,1024]{1,0:T(8,128)(2,1)S(1)} custom-call(s32[3]{0:T(128)S(1)} %add_add_fusion.s_ref, bf16[4,160,384]{2,1,0:T(8,128)(2,1)S(1)} %get-tuple-element.57.refs_0_, bf16[16,1024,384]{2,1,0:T(8,128)(2,1)} %gate_ref.3, bf16[16,1024,384]{2,1,0:T(8,128)(2,1)} %up_ref.3), custom_call_target="tpu_custom_call" | custom-call | flops 503316480 | bytes 6291456 | tf_op jit(solution)/shard_map/mine_parts/pallas_call | solution.py:373
  75.0 4.4 %mine_parts.3.refs_1_ = bf16[320,1024]{1,0:T(8,128)(2,1)S(1)} custom-call(s32[3]{0:T(128)S(1)} %add_add_fusion.3.s_ref, bf16[4,160,384]{2,1,0:T(8,128)(2,1)S(1)} %get-tuple-element.63.refs_0_, bf16[16,1024,384]{2,1,0:T(8,128)(2,1)} %gate_ref.3, bf16[16,1024,384]{2,1,0:T(8,128)(2,1)} %up_ref.3), custom_call_target="tpu_custom_call" | custom-call | flops 503316480 | bytes 6291456 | tf_op jit(solution)/shard_map/mine_parts/pallas_call | solution.py:373
  79.7 5.9 %combine.2.refs_0_ = f32[512,1024]{1,0:T(8,128)S(1)} custom-call(s32[3]{0:T(128)S(1)} %get-tuple-element.74.s_ref, bf16[4,160,384]{2,1,0:T(8,128)(2,1)} %collective-permute-done.19.d_ref, bf16[16,1024,384]{2,1,0:T(8,128)(2,1)} %gate_ref.3, bf16[16,1024,384]{2,1,0:T(8,128)(2,1)} %up_ref.3, f32[16,512]{1,0:T(8,128)S(1)} %get-tuple-element.53.refs_8_.place_ref, ...), custom_call_target="tpu_custom_call" | custom-call | flops 1509949440 | bytes 6291456 | tf_op jit(solution)/shard_map/combine/pallas_call | solution.py:373
  85.5 4.8 %collective-permute-done.20 = f32[8,384]{1,0:T(8,128)S(1)} collective-permute-done((f32[8,384]{1,0:T(8,128)S(1)}, f32[8,384]{1,0:T(8,128)S(1)}, u32[]{:S(2)}, u32[]{:S(2)}) %collective-permute-start.20) | collective-permute-done | bytes 12320 | tf_op jit(solution)/shard_map/ppermute | solution.py:348
  90.3 5.2 %combine.3 = (f32[4,64,1024]{2,1,0:T(8,128)S(1)}, bf16[4,64,1024]{2,1,0:T(8,128)(2,1)S(1)}) custom-call(s32[3]{0:T(128)S(1)} %get-tuple-element.74.s_ref, bf16[4,160,384]{2,1,0:T(8,128)(2,1)S(1)} %collective-permute-done.21.d_ref, bf16[16,1024,384]{2,1,0:T(8,128)(2,1)} %gate_ref.3, bf16[16,1024,384]{2,1,0:T(8,128)(2,1)} %up_ref.3, ...), custom_call_target="tpu_custom_call" | custom-call | flops 838860800 | bytes 6291456 | tf_op jit(solution)/shard_map/combine/pallas_call | solution.py:373
  95.5 1.7 %collective-permute-start.22 = (bf16[4,64,1024]{2,1,0:T(8,128)(2,1)S(1)}, bf16[4,64,1024]{2,1,0:T(8,128)(2,1)S(1)}, u32[]{:S(2)}, u32[]{:S(2)}) collective-permute-start(bf16[4,64,1024]{2,1,0:T(8,128)(2,1)S(1)} %get-tuple-element.67), channel_id=1, source_target_pairs={{0,1},{1,0},{2,3},{3,2},{4,5},{5,4},{6,7},{7,6},{8,9},{9,8},{10,11... | collective-permute-start | bytes 1572872 | tf_op jit(solution)/shard_map/ppermute | solution.py:348
  97.2 1.5 %collective-permute-done.22 = bf16[4,64,1024]{2,1,0:T(8,128)(2,1)S(1)} collective-permute-done((bf16[4,64,1024]{2,1,0:T(8,128)(2,1)S(1)}, bf16[4,64,1024]{2,1,0:T(8,128)(2,1)S(1)}, u32[]{:S(2)}, u32[]{:S(2)}) %collective-permute-start.22) | collective-permute-done | bytes 524320 | tf_op jit(solution)/shard_map/ppermute | solution.py:348
  99.0 2.5 %collective-permute-start.23 = (bf16[64,1024]{1,0:T(8,128)(2,1)S(1)}, bf16[64,1024]{1,0:T(8,128)(2,1)S(1)}, u32[]{:S(2)}, u32[]{:S(2)}) collective-permute-start(bf16[64,1024]{1,0:T(8,128)(2,1)S(1)} %get-tuple-element.68), channel_id=1, source_target_pairs={{0,0},{1,2},{2,1},{3,3},{4,4},{5,6},{6,5},{7,7},{8,8},{9,10},{10,9... | collective-permute-start | bytes 393224 | tf_op jit(solution)/shard_map/ppermute | solution.py:357
  101.6 2.6 %collective-permute-start.25 = (bf16[64,1024]{1,0:T(8,128)(2,1)S(1)}, bf16[64,1024]{1,0:T(8,128)(2,1)S(1)}, u32[]{:S(2)}, u32[]{:S(2)}) collective-permute-start(bf16[64,1024]{1,0:T(8,128)(2,1)S(1)} %get-tuple-element.70), channel_id=1, source_target_pairs={{0,8},{1,10},{2,9},{3,11},{4,12},{5,14},{6,13},{7,15},{8,0},{9,2},... | collective-permute-start | bytes 393224 | tf_op jit(solution)/shard_map/ppermute | solution.py:357
  104.1 3.5 %collective-permute-start.24 = (bf16[64,1024]{1,0:T(8,128)(2,1)S(1)}, bf16[64,1024]{1,0:T(8,128)(2,1)S(1)}, u32[]{:S(2)}, u32[]{:S(2)}) collective-permute-start(bf16[64,1024]{1,0:T(8,128)(2,1)S(1)} %get-tuple-element.71), channel_id=1, source_target_pairs={{0,12},{1,14},{2,13},{3,15},{4,0},{5,2},{6,1},{7,3},{8,4},{9,6},{1... | collective-permute-start | bytes 393224 | tf_op jit(solution)/shard_map/ppermute | solution.py:357
  109.7 2.9 %collective-permute-done.25 = bf16[64,1024]{1,0:T(8,128)(2,1)S(1)} collective-permute-done((bf16[64,1024]{1,0:T(8,128)(2,1)S(1)}, bf16[64,1024]{1,0:T(8,128)(2,1)S(1)}, u32[]{:S(2)}, u32[]{:S(2)}) %collective-permute-start.25) | collective-permute-done | bytes 131104 | tf_op jit(solution)/shard_map/ppermute | solution.py:357
  (84 shorter events, 20.2 us)
Async XLA Ops:
  2.4 18.1 %collective-permute-start.3 = (bf16[80,1024]{1,0:T(8,128)(2,1)}, bf16[80,1024]{1,0:T(8,128)(2,1)S(1)}, u32[]{:S(2)}, u32[]{:S(2)}) collective-permute-start(bf16[80,1024]{1,0:T(8,128)(2,1)} %pack.1), channel_id=1, source_target_pairs={{0,12},{1,14},{2,13},{3,15},{4,0},{5,2},{6,1},{7,3},{8,4},{9,6},{1... | collective-permute-start | bytes 491528 | tf_op jit(solution)/shard_map/ppermute | solution.py:357
  8.0 13.8 %collective-permute-start.2 = (bf16[80,1024]{1,0:T(8,128)(2,1)}, bf16[80,1024]{1,0:T(8,128)(2,1)S(1)}, u32[]{:S(2)}, u32[]{:S(2)}) collective-permute-start(bf16[80,1024]{1,0:T(8,128)(2,1)} %pack.1), channel_id=1, source_target_pairs={{0,8},{1,10},{2,9},{3,11},{4,12},{5,14},{6,13},{7,15},{8,0},{9,2},... | collective-permute-start | bytes 491528 | tf_op jit(solution)/shard_map/ppermute | solution.py:357
  8.0 13.8 %collective-permute-start.1 = (bf16[80,1024]{1,0:T(8,128)(2,1)}, bf16[80,1024]{1,0:T(8,128)(2,1)S(1)}, u32[]{:S(2)}, u32[]{:S(2)}) collective-permute-start(bf16[80,1024]{1,0:T(8,128)(2,1)} %pack.1), channel_id=1, source_target_pairs={{0,4},{1,6},{2,5},{3,7},{4,8},{5,10},{6,9},{7,11},{8,12},{9,14},{1... | collective-permute-start | bytes 491528 | tf_op jit(solution)/shard_map/ppermute | solution.py:357
  9.6 12.2 %collective-permute-start = (bf16[80,1024]{1,0:T(8,128)(2,1)}, bf16[80,1024]{1,0:T(8,128)(2,1)S(1)}, u32[]{:S(2)}, u32[]{:S(2)}) collective-permute-start(bf16[80,1024]{1,0:T(8,128)(2,1)} %pack.1), channel_id=1, source_target_pairs={{0,0},{1,2},{2,1},{3,3},{4,4},{5,6},{6,5},{7,7},{8,8},{9,10},{10,9... | collective-permute-start | bytes 491528 | tf_op jit(solution)/shard_map/ppermute | solution.py:357
  11.7 8.8 %collective-permute-start.4 = (bf16[64,1024]{1,0:T(8,128)(2,1)}, bf16[64,1024]{1,0:T(8,128)(2,1)S(1)}, u32[]{:S(2)}, u32[]{:S(2)}) collective-permute-start(bf16[64,1024]{1,0:T(8,128)(2,1)} %param.9), channel_id=1, source_target_pairs={{0,0},{1,2},{2,1},{3,3},{4,4},{5,6},{6,5},{7,7},{8,8},{9,10},{10,9... | collective-permute-start | bytes 393224 | tf_op jit(solution)/shard_map/ppermute | solution.py:357
  21.8 2.0 %collective-permute-start.5 = (bf16[80,1024]{1,0:T(8,128)(2,1)S(1)}, bf16[80,1024]{1,0:T(8,128)(2,1)S(1)}, u32[]{:S(2)}, u32[]{:S(2)}) collective-permute-start(bf16[80,1024]{1,0:T(8,128)(2,1)S(1)} %collective-permute-done.refs_0_), channel_id=1, source_target_pairs={{0,1},{1,0},{2,3},{3,2},{4,5},{5,4},{6,7},{7,6},{8,9},{9,8},{10,11... | collective-permute-start | bytes 491528 | tf_op jit(solution)/shard_map/ppermute | solution.py:348
  22.9 1.6 %collective-permute-start.7 = (bf16[80,1024]{1,0:T(8,128)(2,1)S(1)}, bf16[80,1024]{1,0:T(8,128)(2,1)S(1)}, u32[]{:S(2)}, u32[]{:S(2)}) collective-permute-start(bf16[80,1024]{1,0:T(8,128)(2,1)S(1)} %collective-permute-done.2.refs_2_), channel_id=1, source_target_pairs={{0,1},{1,0},{2,3},{3,2},{4,5},{5,4},{6,7},{7,6},{8,9},{9,8},{10,11... | collective-permute-start | bytes 491528 | tf_op jit(solution)/shard_map/ppermute | solution.py:348
  23.3 1.4 %collective-permute-start.8 = (bf16[80,1024]{1,0:T(8,128)(2,1)S(1)}, bf16[80,1024]{1,0:T(8,128)(2,1)S(1)}, u32[]{:S(2)}, u32[]{:S(2)}) collective-permute-start(bf16[80,1024]{1,0:T(8,128)(2,1)S(1)} %collective-permute-done.3.refs_3_), channel_id=1, source_target_pairs={{0,1},{1,0},{2,3},{3,2},{4,5},{5,4},{6,7},{7,6},{8,9},{9,8},{10,11... | collective-permute-start | bytes 491528 | tf_op jit(solution)/shard_map/ppermute | solution.py:348
  31.7 24.2 %collective-permute-start.16 = (bf16[8,160,384]{2,1,0:T(8,128)(2,1)S(1)}, bf16[8,160,384]{2,1,0:T(8,128)(2,1)S(1)}, u32[]{:S(2)}, u32[]{:S(2)}) collective-permute-start(bf16[8,160,384]{2,1,0:T(8,128)(2,1)S(1)} %get-tuple-element.51), channel_id=1, source_target_pairs={{0,2},{2,0},{1,3},{3,1},{4,6},{6,4},{5,7},{7,5},{8,10},{10,8},{9,1... | collective-permute-start | bytes 2949128 | tf_op jit(solution)/shard_map/ppermute | solution.py:348
  32.9 10.3 %collective-permute-start.11 = (bf16[64,1024]{1,0:T(8,128)(2,1)S(1)}, bf16[64,1024]{1,0:T(8,128)(2,1)S(1)}, u32[]{:S(2)}, u32[]{:S(2)}) collective-permute-start(bf16[64,1024]{1,0:T(8,128)(2,1)S(1)} %collective-permute-done.4.refs_0_), channel_id=1, source_target_pairs={{0,12},{4,0},{8,4},{12,8},{1,13},{5,1},{9,5},{13,9},{2,14},{6,2},{... | collective-permute-start | bytes 393224 | tf_op jit(solution)/shard_map/ppermute | solution.py:360
  33.2 14.2 %collective-permute-start.10 = (bf16[64,1024]{1,0:T(8,128)(2,1)S(1)}, bf16[64,1024]{1,0:T(8,128)(2,1)S(1)}, u32[]{:S(2)}, u32[]{:S(2)}) collective-permute-start(bf16[64,1024]{1,0:T(8,128)(2,1)S(1)} %collective-permute-done.4.refs_0_), channel_id=1, source_target_pairs={{0,8},{4,12},{8,0},{12,4},{1,9},{5,13},{9,1},{13,5},{2,10},{6,14},... | collective-permute-start | bytes 393224 | tf_op jit(solution)/shard_map/ppermute | solution.py:360
  35.6 11.8 %collective-permute-start.9 = (bf16[64,1024]{1,0:T(8,128)(2,1)S(1)}, bf16[64,1024]{1,0:T(8,128)(2,1)S(1)}, u32[]{:S(2)}, u32[]{:S(2)}) collective-permute-start(bf16[64,1024]{1,0:T(8,128)(2,1)S(1)} %collective-permute-done.4.refs_0_), channel_id=1, source_target_pairs={{0,4},{4,8},{8,12},{12,0},{1,5},{5,9},{9,13},{13,1},{2,6},{6,10},{... | collective-permute-start | bytes 393224 | tf_op jit(solution)/shard_map/ppermute | solution.py:360
  47.4 2.1 %collective-permute-start.12 = (bf16[64,1024]{1,0:T(8,128)(2,1)S(1)}, bf16[64,1024]{1,0:T(8,128)(2,1)S(1)}, u32[]{:S(2)}, u32[]{:S(2)}) collective-permute-start(bf16[64,1024]{1,0:T(8,128)(2,1)S(1)} %collective-permute-done.4.refs_0_), channel_id=1, source_target_pairs={{0,1},{1,0},{2,3},{3,2},{4,5},{5,4},{6,7},{7,6},{8,9},{9,8},{10,11... | collective-permute-start | bytes 393224 | tf_op jit(solution)/shard_map/ppermute | solution.py:348
  48.6 1.5 %collective-permute-start.14 = (bf16[64,1024]{1,0:T(8,128)(2,1)S(1)}, bf16[64,1024]{1,0:T(8,128)(2,1)S(1)}, u32[]{:S(2)}, u32[]{:S(2)}) collective-permute-start(bf16[64,1024]{1,0:T(8,128)(2,1)S(1)} %collective-permute-done.10.refs_2_), channel_id=1, source_target_pairs={{0,1},{1,0},{2,3},{3,2},{4,5},{5,4},{6,7},{7,6},{8,9},{9,8},{10,11... | collective-permute-start | bytes 393224 | tf_op jit(solution)/shard_map/ppermute | solution.py:348
  55.4 11.1 %collective-permute-start.17 = (bf16[4,80,384]{2,1,0:T(8,128)(2,1)S(1)}, bf16[4,80,384]{2,1,0:T(8,128)(2,1)S(1)}, u32[]{:S(2)}, u32[]{:S(2)}) collective-permute-start(bf16[4,80,384]{2,1,0:T(8,128)(2,1)S(1)} %get-tuple-element.55), channel_id=1, source_target_pairs={{0,2},{2,0},{1,3},{3,1},{4,6},{6,4},{5,7},{7,5},{8,10},{10,8},{9,1... | collective-permute-start | bytes 737288 | tf_op jit(solution)/shard_map/ppermute | solution.py:348
  59.4 12.9 %collective-permute-start.18 = (bf16[4,80,384]{2,1,0:T(8,128)(2,1)S(1)}, bf16[4,80,384]{2,1,0:T(8,128)(2,1)S(1)}, u32[]{:S(2)}, u32[]{:S(2)}) collective-permute-start(bf16[4,80,384]{2,1,0:T(8,128)(2,1)S(1)} %y_other.1), channel_id=1, source_target_pairs={{0,2},{2,0},{1,3},{3,1},{4,6},{6,4},{5,7},{7,5},{8,10},{10,8},{9,1... | collective-permute-start | bytes 737288 | tf_op jit(solution)/shard_map/ppermute | solution.py:348
  67.5 12.2 %collective-permute-start.19 = (bf16[4,160,384]{2,1,0:T(8,128)(2,1)S(1)}, bf16[4,160,384]{2,1,0:T(8,128)(2,1)}, u32[]{:S(2)}, u32[]{:S(2)}) collective-permute-start(bf16[4,160,384]{2,1,0:T(8,128)(2,1)S(1)} %get-tuple-element.57.refs_0_), channel_id=1, source_target_pairs={{0,2},{2,0},{1,3},{3,1},{4,6},{6,4},{5,7},{7,5},{8,10},{10,8},{9,1... | collective-permute-start | bytes 1474568 | tf_op jit(solution)/shard_map/ppermute | solution.py:348
  73.3 17.0 %collective-permute-start.21 = (bf16[4,160,384]{2,1,0:T(8,128)(2,1)S(1)}, bf16[4,160,384]{2,1,0:T(8,128)(2,1)S(1)}, u32[]{:S(2)}, u32[]{:S(2)}) collective-permute-start(bf16[4,160,384]{2,1,0:T(8,128)(2,1)S(1)} %get-tuple-element.63.refs_0_), channel_id=1, source_target_pairs={{0,2},{2,0},{1,3},{3,1},{4,6},{6,4},{5,7},{7,5},{8,10},{10,8},{9,1... | collective-permute-start | bytes 1474568 | tf_op jit(solution)/shard_map/ppermute | solution.py:348
  74.6 15.7 %collective-permute-start.20 = (f32[8,384]{1,0:T(8,128)S(1)}, f32[8,384]{1,0:T(8,128)S(1)}, u32[]{:S(2)}, u32[]{:S(2)}) collective-permute-start(f32[8,384]{1,0:T(8,128)S(1)} %bitcast.25), channel_id=1, source_target_pairs={{0,2},{2,0},{1,3},{3,1},{4,6},{6,4},{5,7},{7,5},{8,10},{10,8},{9,1... | collective-permute-start | bytes 36872 | tf_op jit(solution)/shard_map/ppermute | solution.py:348
  95.5 3.2 %collective-permute-start.22 = (bf16[4,64,1024]{2,1,0:T(8,128)(2,1)S(1)}, bf16[4,64,1024]{2,1,0:T(8,128)(2,1)S(1)}, u32[]{:S(2)}, u32[]{:S(2)}) collective-permute-start(bf16[4,64,1024]{2,1,0:T(8,128)(2,1)S(1)} %get-tuple-element.67), channel_id=1, source_target_pairs={{0,1},{1,0},{2,3},{3,2},{4,5},{5,4},{6,7},{7,6},{8,9},{9,8},{10,11... | collective-permute-start | bytes 1572872 | tf_op jit(solution)/shard_map/ppermute | solution.py:348
  99.0 9.3 %collective-permute-start.23 = (bf16[64,1024]{1,0:T(8,128)(2,1)S(1)}, bf16[64,1024]{1,0:T(8,128)(2,1)S(1)}, u32[]{:S(2)}, u32[]{:S(2)}) collective-permute-start(bf16[64,1024]{1,0:T(8,128)(2,1)S(1)} %get-tuple-element.68), channel_id=1, source_target_pairs={{0,0},{1,2},{2,1},{3,3},{4,4},{5,6},{6,5},{7,7},{8,8},{9,10},{10,9... | collective-permute-start | bytes 393224 | tf_op jit(solution)/shard_map/ppermute | solution.py:357
  101.5 8.1 %collective-permute-start.26 = (bf16[64,1024]{1,0:T(8,128)(2,1)S(1)}, bf16[64,1024]{1,0:T(8,128)(2,1)S(1)}, u32[]{:S(2)}, u32[]{:S(2)}) collective-permute-start(bf16[64,1024]{1,0:T(8,128)(2,1)S(1)} %get-tuple-element.69), channel_id=1, source_target_pairs={{0,4},{1,6},{2,5},{3,7},{4,8},{5,10},{6,9},{7,11},{8,12},{9,14},{1... | collective-permute-start | bytes 393224 | tf_op jit(solution)/shard_map/ppermute | solution.py:357
  101.6 11.0 %collective-permute-start.25 = (bf16[64,1024]{1,0:T(8,128)(2,1)S(1)}, bf16[64,1024]{1,0:T(8,128)(2,1)S(1)}, u32[]{:S(2)}, u32[]{:S(2)}) collective-permute-start(bf16[64,1024]{1,0:T(8,128)(2,1)S(1)} %get-tuple-element.70), channel_id=1, source_target_pairs={{0,8},{1,10},{2,9},{3,11},{4,12},{5,14},{6,13},{7,15},{8,0},{9,2},... | collective-permute-start | bytes 393224 | tf_op jit(solution)/shard_map/ppermute | solution.py:357
  104.1 8.4 %collective-permute-start.24 = (bf16[64,1024]{1,0:T(8,128)(2,1)S(1)}, bf16[64,1024]{1,0:T(8,128)(2,1)S(1)}, u32[]{:S(2)}, u32[]{:S(2)}) collective-permute-start(bf16[64,1024]{1,0:T(8,128)(2,1)S(1)} %get-tuple-element.71), channel_id=1, source_target_pairs={{0,12},{1,14},{2,13},{3,15},{4,0},{5,2},{6,1},{7,3},{8,4},{9,6},{1... | collective-permute-start | bytes 393224 | tf_op jit(solution)/shard_map/ppermute | solution.py:357
  (19 other events, 65.8 us)
